TPU v7x, 128 devices: a whole 4x4x4 slice. The times are simulated.
128 devices in a mesh: dp: 16 (over z, x), expert: 8 (over y, core).
Axes of the slice: x: 4, y: 4, z: 4, core: 2. Of those that a mesh axis runs over, the one named last changes fastest.
Arguments:
- local_grads: bfloat16 [16, 8, 4, 1048576], P('dp', 'expert')
- master_weights: float32 [8, 4, 1048576], P('expert', None, 'dp'), may hold values from -6 to 6
- first_moment: float32 [8, 4, 1048576], P('expert', None, 'dp')
- second_moment: float32 [8, 4, 1048576], P('expert', None, 'dp')
Outputs:
- new_params: bfloat16 [8, 4, 1048576], P('expert')
- new_master: float32 [8, 4, 1048576], P('expert', None, 'dp')
- new_first: float32 [8, 4, 1048576], P('expert', None, 'dp')
- new_second: float32 [8, 4, 1048576], P('expert', None, 'dp')
All inputs are finite; a program needn't handle non-finite values.
Results may differ from a plain program's by a relative error of at most 0.0013.
Values may be sent and summed in bfloat16 or wider, within the bound.
No kernel may reach another device: no remote copies, remote signals or barrier semaphores. Data moves between devices by JAX's collectives and lax.ppermute only.
A program may use at most 128 MiB of HBM per device.

v0:
```python
import functools

import jax
import jax.numpy as jnp
from jax import lax
from jax.sharding import Mesh
from jax.sharding import PartitionSpec as P

DP = ("dp_0", "dp_1")
DP_EXPERT = ("dp_0", "dp_1", "expert_0", "expert_1")
EXPERT = ("expert_0", "expert_1")


beta_first = 0.9
beta_second = 0.95
correct_first = 1.0 - 0.9**10
correct_second = 1.0 - 0.95**10
learn_rate = 0.05
decay_rate = 0.1
clip_limit = 1.0
tiny_eps = 1e-08
norm_eps = 1e-06


def by_axis(x, axes):
    return functools.reduce(lax.psum, axes, x)


def adam_update(gradient, master, first, second, clip_factor):
    scaled = clip_factor * gradient
    new_first = beta_first * first + (1.0 - beta_first) * scaled
    new_second = beta_second * second + (1.0 - beta_second) * scaled * scaled
    direction = new_first / correct_first / (jnp.sqrt(new_second / correct_second) + tiny_eps)
    new_master = master - learn_rate * (decay_rate * master + direction)
    return (new_master, new_first, new_second)


def shards(local_grads, master_weights, first_moment, second_moment):
    replicas = lax.axis_size(DP)
    own_grads = local_grads[0, 0]
    layer_count = own_grads.shape[0]
    share = own_grads.shape[1] // replicas
    pieces_all = own_grads.reshape(layer_count, replicas, share)
    arrived = lax.all_to_all(pieces_all, DP, split_axis=1, concat_axis=1, tiled=True)
    reduced = jnp.sum(arrived.astype(jnp.float32), axis=1)
    mean_grad = reduced / replicas
    squares = jnp.sum(mean_grad * mean_grad)
    total_squares = by_axis(squares, DP_EXPERT)
    grad_norm = jnp.sqrt(total_squares)
    clip_factor = jnp.minimum(1.0, clip_limit / (grad_norm + norm_eps))
    new_master, new_first, new_second = adam_update(
        mean_grad, master_weights[0], first_moment[0], second_moment[0], clip_factor
    )
    rounded = new_master.astype(jnp.bfloat16)
    gathered = lax.all_gather(rounded, DP, axis=1, tiled=True)
    return (gathered[None], new_master[None], new_first[None], new_second[None])


def solution(mesh):
    torus = Mesh(mesh.devices.reshape(4, 4, 4, 2), ("dp_0", "dp_1", "expert_0", "expert_1"))
    return jax.shard_map(
        shards,
        mesh=torus,
        in_specs=(
            P(DP, EXPERT, None, None),
            P(EXPERT, None, DP),
            P(EXPERT, None, DP),
            P(EXPERT, None, DP),
        ),
        out_specs=(
            P(EXPERT, None, None),
            P(EXPERT, None, DP),
            P(EXPERT, None, DP),
            P(EXPERT, None, DP),
        ),
        check_vma=False,
    )
```

profile of v0, /device:TPU:0, one launch (start us, length us, event | category | flops | bytes accessed | tf_op | source)
XLA Modules:
  0.0 238.0 jit_solution(16362549095326047776)
XLA Ops:
  7.2 0.0 all-gather.2.cloned.1.call-start
  7.2 103.9 %all_to_all.5 = bf16[4,16,65536]{2,0,1:T(4,128)(2,1)} all-to-all(bf16[4,16,65536]{2,0,1:T(4,128)(2,1)} %bitcast.32), channel_id=1, replica_groups=mesh['dp_0'=4,'dp_1'=4,'expert_0'=4,'expert_1'=2] {'dp_0','dp_1'}, dimensions={1} | all-to-all | bytes 16777216 | tf_op jit(solution)/shard_map/all_to_all | solution.py:44
  111.1 0.0 copy-start
  111.1 0.0 copy-start.1
  111.1 7.2 %convert_reduce_fusion = f32[4,65536]{1,0:T(4,128)S(1)} fusion(bf16[4,16,65536]{2,0,1:T(4,128)(2,1)} %all_to_all.5), kind=kLoop, calls=%fused_computation | loop fusion | flops 8126464 | bytes 9437184 | tf_op jit(solution)/shard_map/reduce_sum | solution.py:45
  118.3 1.1 multiply_reduce_fusion
  119.5 9.2 %psum.28 = f32[]{:T(128)} all-reduce(f32[]{:T(128)} %multiply_reduce_fusion), channel_id=1, replica_groups=mesh['dp_0'=4,'dp_1'=4,'expert_0'=4,'expert_1'=2] {'dp_0'}, use_global_device_ids=true, to_apply=%region_2.0 | all-reduce | flops 1 | bytes 8 | tf_op jit(solution)/shard_map/psum | solution.py:26
  128.7 9.2 %psum.29 = f32[]{:T(128)} all-reduce(f32[]{:T(128)} %psum.28), channel_id=1, replica_groups=mesh['dp_0'=4,'dp_1'=4,'expert_0'=4,'expert_1'=2] {'dp_1'}, use_global_device_ids=true, to_apply=%region_3.0 | all-reduce | flops 1 | bytes 8 | tf_op jit(solution)/shard_map/psum | solution.py:26
  137.9 11.3 %psum.30 = f32[]{:T(128)} all-reduce(f32[]{:T(128)} %psum.29), channel_id=1, replica_groups=mesh['dp_0'=4,'dp_1'=4,'expert_0'=4,'expert_1'=2] {'expert_0'}, use_global_device_ids=true, to_apply=%region_4.0 | all-reduce | flops 1 | bytes 8 | tf_op jit(solution)/shard_map/psum | solution.py:26
  149.2 3.1 %psum.31 = f32[]{:T(128)} all-reduce(f32[]{:T(128)} %psum.30), channel_id=1, replica_groups=mesh['dp_0'=4,'dp_1'=4,'expert_0'=4,'expert_1'=2] {'expert_1'}, use_global_device_ids=true, to_apply=%region_5.0 | all-reduce | flops 1 | bytes 8 | tf_op jit(solution)/shard_map/psum | solution.py:26
  153.0 0.0 copy-done
  153.1 0.0 copy-done.1
  153.1 3.7 %fusion.10 = bf16[4,65536]{1,0:T(4,128)(2,1)} fusion(f32[1,4,65536]{2,1,0:T(4,128)S(1)} %copy-done, f32[1,4,65536]{2,1,0:T(4,128)S(1)} %copy-done.1, f32[1,4,65536]{2,1,0:T(4,128)} %param.6, f32[4,65536]{1,0:T(4,128)S(1)} %convert_reduce_fusion, f32[]{:T(128)S(6)} %mul.104), kind=kLoop, calls=%fused_computation.17 | loop fusion | flops 4456448 | bytes 4718596 | tf_op jit(solution)/shard_map/convert_element_type | solution.py:54
  156.8 0.0 all-gather.2.cloned.1.call-update
  156.8 4.5 %multiply_subtract_fusion = (f32[1,4,65536]{2,1,0:T(4,128)}, f32[1,4,65536]{2,1,0:T(4,128)}, f32[1,4,65536]{2,1,0:T(4,128)}) fusion(f32[1,4,65536]{2,1,0:T(4,128)S(1)} %copy-done, f32[4,65536]{1,0:T(4,128)S(1)} %convert_reduce_fusion, f32[]{:T(128)S(6)} %mul.104, f32[1,4,65536]{2,1,0:T(4,128)} %param.6, f32[1,4,65536]{2,1,0:T(4,128)S(1)} %copy-done.1), kind=kLoop, calls=%fused_computation.18 | loop fusion | flops 4194304 | bytes 7340036 | tf_op jit(solution)/shard_map/sub | solution.py:34
  161.3 61.9 %all-gather.2.cloned.1.call-done = bf16[4,1048576]{1,0:T(4,128)(2,1)} async-done(((bf16[4,65536]{1,0:T(4,128)(2,1)}), bf16[4,1048576]{1,0:T(4,128)(2,1)}) %all-gather.2.cloned.1.call-update) | async-done | bytes 8388624 | tf_op jit(solution)/shard_map/all_gather | solution.py:55
  223.1 8.1 %copy.9 = bf16[1,4,1048576]{2,1,0:T(4,128)(2,1)} copy(bf16[1,4,1048576]{2,1,0:T(4,128)(2,1)} %bitcast.33) | data formatting | bytes 16777216
Async XLA Ops:
  7.2 216.0 %all-gather.2.cloned.1.call-start = ((), (), s32[]{:S(2)}) async-start(), calls=%async_computation.1 | async-start | bytes 8912896 | tf_op jit(solution)/shard_map/all_gather | solution.py:55
  111.1 42.0 %copy-start = (f32[1,4,65536]{2,1,0:T(4,128)S(1)}, f32[1,4,65536]{2,1,0:T(4,128)}, u32[]{:S(2)}) copy-start(f32[1,4,65536]{2,1,0:T(4,128)} %param.5) | copy-start | bytes 3145732
  111.1 42.0 %copy-start.1 = (f32[1,4,65536]{2,1,0:T(4,128)S(1)}, f32[1,4,65536]{2,1,0:T(4,128)}, u32[]{:S(2)}) copy-start(f32[1,4,65536]{2,1,0:T(4,128)} %param.7) | copy-start | bytes 3145732
Sparse Core Ops, SparseCore 0:
  156.9 66.1 all-gather.1
where the time goes:
time: 239 us; the launch traced here: 238 us
  blocking collectives  137 us (57%)
  waiting for transfers between devices  61.9 us (26%)
  other arithmetic  16.6 us (7%)
  between operations  14.8 us (6%)
  local copies, waits for them, and re-layouts  8.06 us (3%)
    all_to_all x1, blocking collectives, shards(): lax.all_to_all(pieces_all, DP, split_axis=1, concat_axis=1, tiled=True)  104 us
    all_gather x1, waiting for transfers between devices, shards(): gathered = lax.all_gather(rounded, DP, axis=1, tiled=True)  61.9 us
    psum x4, blocking collectives, by_axis(): return functools.reduce(lax.psum, axes, x)  32.8 us
    unnamed x5, local copies, waits for them, and re-layouts  8.06 us
    reduce_sum x1, other arithmetic, shards(): reduced = jnp.sum(arrived.astype(jnp.float32), axis=1)  7.25 us
  transfers between devices with their start and end apart: 1, of which 1 were waited for; matrix products, arithmetic and copies ran while one was open for 2% of the time, Pallas kernels for 0%

commit v1 on v0

v1 whole, which is shorter than its diff:
```python
import functools

import jax
import jax.numpy as jnp
from jax import lax
from jax.experimental import pallas as pl
from jax.experimental.pallas import tpu as pltpu
from jax.sharding import Mesh
from jax.sharding import PartitionSpec as P

Z, X, Y, CORE = "z", "x", "y", "core"
beta_first = 0.9
beta_second = 0.95
correct_first = 1.0 - 0.9**10
correct_second = 1.0 - 0.95**10
learn_rate = 0.05
decay_rate = 0.1
clip_limit = 1.0
tiny_eps = 1e-08
norm_eps = 1e-06

LANES = 128
BLOCK = 256
VMEM_LIMIT = 12 * 2**20
f32, bf16 = jnp.float32, jnp.bfloat16


def shift(value, axis, by):
    size = lax.axis_size(axis)
    return lax.ppermute(value, axis, [(i, (i + by) % size) for i in range(size)])


def cost(flops, moved):
    return pl.CostEstimate(flops=flops, bytes_accessed=moved, transcendentals=0)


def first_sum_kernel(where, own, one, two, three, *outs):
    mine = where[1]
    for ahead, out in enumerate(outs):
        at = lax.rem(mine + ahead, 4)
        total = own[at].astype(f32)
        for part in (one, two, three):
            total += part[at].astype(f32)
        out[...] = total


def first_sum(pieces, arrived, where, along_z):
    half = arrived[0].shape[1]
    steps = half // BLOCK
    if along_z:
        own = pl.BlockSpec((None, 4, BLOCK, LANES), lambda i, w: (w[0], 0, i, 0))
    else:
        own = pl.BlockSpec((4, None, BLOCK, LANES), lambda i, w: (0, w[0], steps + i, 0))
    part = pl.BlockSpec((4, BLOCK, LANES), lambda i, w: (0, i, 0))
    out = pl.BlockSpec((BLOCK, LANES), lambda i, w: (i, 0))
    return pl.pallas_call(
        first_sum_kernel,
        grid_spec=pltpu.PrefetchScalarGridSpec(
            num_scalar_prefetch=1, grid=(steps,), in_specs=[own, part, part, part], out_specs=[out] * 4
        ),
        out_shape=[jax.ShapeDtypeStruct((half, LANES), f32)] * 4,
        compiler_params=pltpu.CompilerParams(vmem_limit_bytes=VMEM_LIMIT),
        cost_estimate=cost(16 * half * LANES, 4 * 4 * half * LANES * 3),
    )(where, pieces, *arrived)


def last_sum_kernel(*refs):
    parts_a, parts_b, (mean_a, mean_b, squares) = refs[:4], refs[4:8], refs[8:]

    @pl.when(pl.program_id(0) == 0)
    def _():
        squares[...] = jnp.zeros_like(squares)

    for parts, mean in ((parts_a, mean_a), (parts_b, mean_b)):
        total = (parts[0][...] + parts[1][...] + parts[2][...] + parts[3][...]) * (1.0 / 16.0)
        mean[...] = total
        squares[...] += jnp.sum((total * total).reshape(BLOCK // 8, 8, LANES), axis=0)


def last_sum(parts_a, parts_b):
    half = parts_a[0].shape[0]
    block = pl.BlockSpec((BLOCK, LANES), lambda i: (i, 0))
    return pl.pallas_call(
        last_sum_kernel,
        grid=(half // BLOCK,),
        in_specs=[block] * 8,
        out_specs=[block, block, pl.BlockSpec((8, LANES), lambda i: (0, 0))],
        out_shape=[jax.ShapeDtypeStruct((half, LANES), f32)] * 2 + [jax.ShapeDtypeStruct((8, LANES), f32)],
        compiler_params=pltpu.CompilerParams(vmem_limit_bytes=VMEM_LIMIT),
        cost_estimate=cost(16 * half * LANES, 10 * 4 * half * LANES),
    )(*parts_a, *parts_b)


def adam_update(gradient, master, first, second, clip_factor):
    scaled = clip_factor * gradient
    new_first = beta_first * first + (1.0 - beta_first) * scaled
    new_second = beta_second * second + (1.0 - beta_second) * scaled * scaled
    direction = new_first / correct_first / (jnp.sqrt(new_second / correct_second) + tiny_eps)
    new_master = master - learn_rate * (decay_rate * master + direction)
    return (new_master, new_first, new_second)


def clip_of(squares):
    total = jnp.sum(jnp.sum(squares[...], axis=0, keepdims=True), axis=1, keepdims=True)
    return jnp.minimum(1.0, clip_limit / (jnp.sqrt(total) + norm_eps))


def params_kernel(squares, *refs):
    clip_factor = clip_of(squares)
    for ins, out in ((refs[0:4], refs[8]), (refs[4:8], refs[9])):
        new_master, _, _ = adam_update(*(r[...] for r in ins), clip_factor)
        out[...] = new_master.astype(bf16)


def new_params(squares, means, states):
    half = means[0].shape[0]
    steps = half // BLOCK
    whole = pl.BlockSpec((8, LANES), lambda i: (0, 0))
    low = pl.BlockSpec((BLOCK, LANES), lambda i: (i, 0))
    high = pl.BlockSpec((BLOCK, LANES), lambda i: (steps + i, 0))
    return pl.pallas_call(
        params_kernel,
        grid=(steps,),
        in_specs=[whole, low, low, low, low, low, high, high, high],
        out_specs=[low, low],
        out_shape=[jax.ShapeDtypeStruct((half, LANES), bf16)] * 2,
        compiler_params=pltpu.CompilerParams(vmem_limit_bytes=VMEM_LIMIT),
        cost_estimate=cost(40 * half * LANES, 36 * half * LANES),
    )(squares, means[0], *states, means[1], *states)


def states_both_kernel(squares, mean_a, mean_b, master, first, second, *outs):
    clip_factor = clip_of(squares)
    for at, mean in enumerate((mean_a, mean_b)):
        values = adam_update(mean[...], master[at], first[at], second[at], clip_factor)
        for out, value in zip(outs, values):
            out[at] = value


def both_states(squares, means, states):
    half = means[0].shape[0]
    whole = pl.BlockSpec((8, LANES), lambda i: (0, 0))
    low = pl.BlockSpec((BLOCK, LANES), lambda i: (i, 0))
    pair = pl.BlockSpec((2, BLOCK, LANES), lambda i: (0, i, 0))
    return pl.pallas_call(
        states_both_kernel,
        grid=(half // BLOCK,),
        in_specs=[whole, low, low, pair, pair, pair],
        out_specs=[pair] * 3,
        out_shape=[jax.ShapeDtypeStruct((2, half, LANES), f32)] * 3,
        compiler_params=pltpu.CompilerParams(vmem_limit_bytes=VMEM_LIMIT),
        cost_estimate=cost(40 * half * LANES, 60 * half * LANES),
    )(squares, *means, *(s.reshape(2, half, LANES) for s in states))


def place_kernel(moves, n_parts, where, *refs):
    parts, out, sems = refs[:n_parts], refs[-2], refs[-1]
    copies = []
    for k, (source, target) in enumerate(moves):
        src = source(parts)
        dst = target(out, where)
        copies.append(pltpu.make_async_copy(src, dst, sems.at[k]))
    for copy in copies:
        copy.start()
    for copy in copies:
        copy.wait()


def place(out, where, parts, moves, shape):
    extra = [] if out is None else [out]
    any_ = pl.BlockSpec(memory_space=pl.ANY)
    return pl.pallas_call(
        functools.partial(place_kernel, moves, len(parts)),
        grid_spec=pltpu.PrefetchScalarGridSpec(
            num_scalar_prefetch=1,
            grid=(),
            in_specs=[any_] * (len(parts) + len(extra)),
            out_specs=any_,
            scratch_shapes=[pltpu.SemaphoreType.DMA((len(moves),))],
        ),
        out_shape=jax.ShapeDtypeStruct(shape, bf16),
        input_output_aliases={} if out is None else {len(parts) + 1: 0},
        compiler_params=pltpu.CompilerParams(vmem_limit_bytes=VMEM_LIMIT),
        cost_estimate=cost(0, 2 * sum(p.size for p in parts) * 2),
    )(where, *parts, *extra)


def shards(local_grads, master_weights, first_moment, second_moment):
    layers, flat = local_grads.shape[2:]
    rows = layers * flat // LANES // 16
    half = rows // 2
    z, x = lax.axis_index(Z), lax.axis_index(X)

    def to_rows(value):
        return value.reshape(layers, -1, LANES).transpose(1, 0, 2).reshape(-1, LANES)

    def from_rows(value):
        return value.reshape(-1, layers, LANES).transpose(1, 0, 2).reshape(1, layers, -1)

    pieces = to_rows(local_grads[0, 0]).reshape(4, 4, rows, LANES)
    states = [to_rows(s[0]) for s in (master_weights, first_moment, second_moment)]
    zx = jnp.stack([z, x]).astype(jnp.int32)
    xz = jnp.stack([x, z]).astype(jnp.int32)

    def for_z(by):
        at = lax.rem(z + by, 4)
        return lax.dynamic_slice(pieces, (at, 0, 0, 0), (1, 4, half, LANES)).reshape(4, half, LANES)

    def for_x(by):
        at = lax.rem(x + by, 4)
        return lax.dynamic_slice(pieces, (0, at, half, 0), (4, 1, half, LANES)).reshape(4, half, LANES)

    shifts = (1, 3, 2)
    got_z = [shift(for_z(s), Z, s) for s in shifts]
    got_x = [shift(for_x(s), X, s) for s in shifts]
    sums_a = first_sum(pieces, got_z, zx, True)
    sums_b = first_sum(pieces, got_x, xz, False)
    parts_a = [sums_a[0]] + [shift(sums_a[s], X, s) for s in shifts]
    parts_b = [sums_b[0]] + [shift(sums_b[s], Z, s) for s in shifts]
    mean_a, mean_b, squares = last_sum(parts_a, parts_b)

    for axis in (Z, X, Y):
        squares = squares + shift(squares, axis, 1) + shift(squares, axis, 3) + shift(squares, axis, 2)
    squares = squares + shift(squares, CORE, 1)

    par_a, par_b = new_params(squares, (mean_a, mean_b), states)
    outs = both_states(squares, (mean_a, mean_b), states)
    outs = [from_rows(o.reshape(rows, LANES)) for o in outs]

    def turn(i, by):
        return lax.rem(i + by, 4)

    row_a = [par_a] + [shift(par_a, X, s) for s in (1, 2, 3)]
    row_b = [par_b] + [shift(par_b, Z, s) for s in (1, 2, 3)]
    shape = (4, half, LANES)
    moves = [(lambda p, s=s: p[s], lambda o, w, s=s: o.at[turn(w[1], 4 - s)]) for s in range(4)]
    line_a = place(None, zx, row_a, moves, shape)
    line_b = place(None, xz, row_b, moves, shape)
    full = (4, 4, 2, half, LANES)

    def to_a(by, lo=0, n=half):
        return lambda o, w: o.at[turn(w[0], by), :, 0, pl.ds(lo, n)]

    def to_b(by, lo=0, n=half):
        return lambda o, w: o.at[:, turn(w[1], by), 1, pl.ds(lo, n)]

    out = place(None, zx, [line_a, line_b], [(lambda p: p[0], to_a(0)), (lambda p: p[1], to_b(0))], full)
    near = [shift(line_a, Z, 1), shift(line_a, Z, 3), shift(line_b, X, 1), shift(line_b, X, 3)]
    q = half // 2
    far = [
        shift(near[0][:, :q], Z, 1),
        shift(near[1][:, q:], Z, 3),
        shift(near[2][:, :q], X, 1),
        shift(near[3][:, q:], X, 3),
    ]
    out = place(
        out, zx, near,
        [(lambda p: p[0], to_a(3)), (lambda p: p[1], to_a(1)), (lambda p: p[2], to_b(3)), (lambda p: p[3], to_b(1))],
        full,
    )
    out = place(
        out, zx, far,
        [
            (lambda p: p[0], to_a(2, 0, q)),
            (lambda p: p[1], to_a(2, q, q)),
            (lambda p: p[2], to_b(2, 0, q)),
            (lambda p: p[3], to_b(2, q, q)),
        ],
        full,
    )
    return (from_rows(out.reshape(-1, LANES)), *outs)


def solution(mesh):
    torus = Mesh(mesh.devices.reshape(4, 4, 4, 2), (Z, X, Y, CORE))
    dp, expert = (Z, X), (Y, CORE)
    return jax.shard_map(
        shards,
        mesh=torus,
        in_specs=(P(dp, expert, None, None), P(expert, None, dp), P(expert, None, dp), P(expert, None, dp)),
        out_specs=(P(expert, None, None), P(expert, None, dp), P(expert, None, dp), P(expert, None, dp)),
        check_vma=False,
    )
```

time: 239 us -> 189 us (0.79)
  blocking collectives: 137 us -> 0 us
  starting transfers between devices: 0.04 us -> 58.3 us
  waiting for transfers between devices: 61.9 us -> 104 us
  other arithmetic: 16.6 us -> 0.17 us
  Pallas kernels: 0 us -> 16 us
  between operations: 14.8 us -> 1.05 us
    ppermute x0 -> x36, waiting for transfers between devices: none -> 104 us  [shift(): lax.ppermute(value, axis, [(i, (i + by) % size) for i in range(size)])]
    all_to_all x1 -> x0, blocking collectives: 104 us -> none  [shards(): lax.all_to_all(pieces_all, DP, split_axis=1, concat_axis=1, tiled=True)]
    all_gather x1 -> x0, waiting for transfers between devices: 61.9 us -> none  [shards(): gathered = lax.all_gather(rounded, DP, axis=1, tiled=True)]
    ppermute x0 -> x36, starting transfers between devices: none -> 58.3 us  [shift(): lax.ppermute(value, axis, [(i, (i + by) % size) for i in range(size)])]
    psum x4 -> x0, blocking collectives: 32.8 us -> none  [by_axis(): return functools.reduce(lax.psum, axes, x)]
    pallas_call x0 -> x10, Pallas kernels: none -> 16 us  [the longest x5 7.7 us: place(): pl.pallas_call(functools.partial(place_kernel, moves, len(parts)), grid_s...]
    reduce_sum x2 -> x0, other arithmetic: 8.38 us -> none  [the longest x1 7.25 us: shards(): reduced = jnp.sum(arrived.astype(jnp.float32), axis=1)]
    reshape x0 -> x2, local copies, waits for them, and re-layouts: none -> 5.66 us  [the longest x1 3.6 us: for_x(): lax.dynamic_slice(pieces, (0, at, half, 0), (4, 1, half, LANES))]
  transfers between devices with their start and end apart: 1 -> 36, of which waited for: 1 -> 17; matrix products, arithmetic and copies ran while one was open for 2% -> 1% of each run, Pallas kernels for 0% -> 6%
where the time goes in v1:
time: 189 us
  waiting for transfers between devices  104 us (55%)
  starting transfers between devices  58.3 us (31%)
  Pallas kernels  16 us (8%)
  local copies, waits for them, and re-layouts  9.2 us (5%)
    ppermute x36, waiting for transfers between devices, shift(): lax.ppermute(value, axis, [(i, (i + by) % size) for i in range(size)])  104 us
    ppermute x36, starting transfers between devices, shift(): lax.ppermute(value, axis, [(i, (i + by) % size) for i in range(size)])  58.3 us
    pallas_call x5, Pallas kernels, place(): pl.pallas_call(functools.partial(place_kernel, moves, len(parts)), grid_s...  7.7 us
  transfers between devices with their start and end apart: 36, of which 17 were waited for; matrix products, arithmetic and copies ran while one was open for 1% of the time, Pallas kernels for 6%

profile of v1, /device:TPU:0, one launch (start us, length us, event | category | flops | bytes accessed | tf_op | source)
XLA Modules:
  0.0 188.9 jit_solution(10881649819009648199)
XLA Ops:
  0.7 3.6 %dynamic-slice_bitcast_fusion = (bf16[4,1024,128]{2,1,0:T(8,128)(2,1)}, bf16[4,1024,128]{2,1,0:T(8,128)(2,1)}, bf16[4,1024,128]{2,1,0:T(8,128)(2,1)}) fusion(bf16[4,4,2048,128]{3,2,1,0:T(8,128)(2,1)} %bitcast.60, s32[]{:T(128)S(6)} %select_n.23, s32[]{:T(128)S(6)} %select_n.22, s32[]{:T(128)S(6)} %select_n.21), kind=kLoop, calls=%fused_computation | loop fusion | bytes 6291468 | tf_op jit(solution)/shard_map/reshape | solution.py:211
  4.3 1.6 collective-permute-start.6
  5.8 1.7 collective-permute-start.7
  7.5 1.9 %collective-permute-start.8 = (bf16[4,1024,128]{2,1,0:T(8,128)(2,1)}, bf16[4,1024,128]{2,1,0:T(8,128)(2,1)S(1)}, u32[]{:S(2)}, u32[]{:S(2)}) collective-permute-start(bf16[4,1024,128]{2,1,0:T(8,128)(2,1)} %get-tuple-element.36), channel_id=1, source_target_pairs={{0,16},{8,24},{16,0},{24,8},{1,17},{9,25},{17,1},{25,9},{2,18},{10... | collective-permute-start | bytes 3145736 | tf_op jit(solution)/shard_map/ppermute | solution.py:30
  9.4 2.1 %dynamic-slice_bitcast_fusion.3 = (bf16[4,1024,128]{2,1,0:T(8,128)(2,1)S(1)}, bf16[4,1024,128]{2,1,0:T(8,128)(2,1)S(1)}, bf16[4,1024,128]{2,1,0:T(8,128)(2,1)S(1)}) fusion(bf16[4,4,2048,128]{3,2,1,0:T(8,128)(2,1)} %bitcast.61, s32[]{:T(128)S(6)} %select_n.20, s32[]{:T(128)S(6)} %select_n.19, s32[]{:T(128)S(6)} %select_n.18), kind=kLoop, calls=%fused_computation.3 | loop fusion | bytes 6291468 | tf_op jit(solution)/shard_map/reshape | solution.py:207
  11.5 2.0 %collective-permute-start = (bf16[4,1024,128]{2,1,0:T(8,128)(2,1)S(1)}, bf16[4,1024,128]{2,1,0:T(8,128)(2,1)S(1)}, u32[]{:S(2)}, u32[]{:S(2)}) collective-permute-start(bf16[4,1024,128]{2,1,0:T(8,128)(2,1)S(1)} %get-tuple-element.41), channel_id=1, source_target_pairs={{0,32},{32,64},{64,96},{96,0},{1,33},{33,65},{65,97},{97,1},{2,34}... | collective-permute-start | bytes 3145736 | tf_op jit(solution)/shard_map/ppermute | solution.py:30
  13.4 2.2 %collective-permute-start.1 = (bf16[4,1024,128]{2,1,0:T(8,128)(2,1)S(1)}, bf16[4,1024,128]{2,1,0:T(8,128)(2,1)S(1)}, u32[]{:S(2)}, u32[]{:S(2)}) collective-permute-start(bf16[4,1024,128]{2,1,0:T(8,128)(2,1)S(1)} %get-tuple-element.40), channel_id=1, source_target_pairs={{0,96},{32,0},{64,32},{96,64},{1,97},{33,1},{65,33},{97,65},{2,98}... | collective-permute-start | bytes 3145736 | tf_op jit(solution)/shard_map/ppermute | solution.py:30
  15.6 14.8 %collective-permute-done.6.one = bf16[4,1024,128]{2,1,0:T(8,128)(2,1)S(1)} collective-permute-done((bf16[4,1024,128]{2,1,0:T(8,128)(2,1)}, bf16[4,1024,128]{2,1,0:T(8,128)(2,1)S(1)}, u32[]{:S(2)}, u32[]{:S(2)}) %collective-permute-start.6) | collective-permute-done | bytes 1048608 | tf_op jit(solution)/shard_map/ppermute | solution.py:30
  30.5 4.2 %collective-permute-start.2 = (bf16[4,1024,128]{2,1,0:T(8,128)(2,1)S(1)}, bf16[4,1024,128]{2,1,0:T(8,128)(2,1)S(1)}, u32[]{:S(2)}, u32[]{:S(2)}) collective-permute-start(bf16[4,1024,128]{2,1,0:T(8,128)(2,1)S(1)} %get-tuple-element.39), channel_id=1, source_target_pairs={{0,64},{32,96},{64,0},{96,32},{1,65},{33,97},{65,1},{97,33},{2,66}... | collective-permute-start | bytes 3145736 | tf_op jit(solution)/shard_map/ppermute | solution.py:30
  34.8 19.3 %collective-permute-done.8.three = bf16[4,1024,128]{2,1,0:T(8,128)(2,1)S(1)} collective-permute-done((bf16[4,1024,128]{2,1,0:T(8,128)(2,1)}, bf16[4,1024,128]{2,1,0:T(8,128)(2,1)S(1)}, u32[]{:S(2)}, u32[]{:S(2)}) %collective-permute-start.8) | collective-permute-done | bytes 1048608 | tf_op jit(solution)/shard_map/ppermute | solution.py:30
  54.1 3.4 %copy-done = bf16[1,1,4,1048576]{3,2,1,0:T(4,128)(2,1)S(1)} copy-done((bf16[1,1,4,1048576]{3,2,1,0:T(4,128)(2,1)S(1)}, bf16[1,1,4,1048576]{3,2,1,0:T(4,128)(2,1)}, u32[]{:S(2)}) %copy-start) | copy-done | bytes 8388632
  57.5 1.5 shard_map.76
  59.0 4.1 %collective-permute-start.10 = (f32[1024,128]{1,0:T(8,128)S(1)}, f32[1024,128]{1,0:T(8,128)S(1)}, u32[]{:S(2)}, u32[]{:S(2)}) collective-permute-start(f32[1024,128]{1,0:T(8,128)S(1)} %get-tuple-element.26), channel_id=1, source_target_pairs={{0,96},{32,0},{64,32},{96,64},{1,97},{33,1},{65,33},{97,65},{2,98}... | collective-permute-start | bytes 1572872 | tf_op jit(solution)/shard_map/ppermute | solution.py:30
  63.2 1.2 collective-permute-start.9
  64.5 1.5 shard_map.75
  66.0 1.2 collective-permute-start.3
  67.2 2.1 %collective-permute-start.4 = (f32[1024,128]{1,0:T(8,128)S(1)}, f32[1024,128]{1,0:T(8,128)S(1)}, u32[]{:S(2)}, u32[]{:S(2)}) collective-permute-start(f32[1024,128]{1,0:T(8,128)S(1)} %get-tuple-element.22), channel_id=1, source_target_pairs={{0,24},{8,0},{16,8},{24,16},{1,25},{9,1},{17,9},{25,17},{2,26},{10... | collective-permute-start | bytes 1572872 | tf_op jit(solution)/shard_map/ppermute | solution.py:30
  69.3 15.4 %collective-permute-done.10.refs_6_ = f32[1024,128]{1,0:T(8,128)S(1)} collective-permute-done((f32[1024,128]{1,0:T(8,128)S(1)}, f32[1024,128]{1,0:T(8,128)S(1)}, u32[]{:S(2)}, u32[]{:S(2)}) %collective-permute-start.10) | collective-permute-done | bytes 524320 | tf_op jit(solution)/shard_map/ppermute | solution.py:30
  85.5 2.8 %collective-permute-done.9.refs_5_ = f32[1024,128]{1,0:T(8,128)S(1)} collective-permute-done((f32[1024,128]{1,0:T(8,128)S(1)}, f32[1024,128]{1,0:T(8,128)S(1)}, u32[]{:S(2)}, u32[]{:S(2)}) %collective-permute-start.9) | collective-permute-done | bytes 524320 | tf_op jit(solution)/shard_map/ppermute | solution.py:30
  88.3 7.1 %collective-permute-done.5.refs_3_ = f32[1024,128]{1,0:T(8,128)S(1)} collective-permute-done((f32[1024,128]{1,0:T(8,128)S(1)}, f32[1024,128]{1,0:T(8,128)S(1)}, u32[]{:S(2)}, u32[]{:S(2)}) %collective-permute-start.5) | collective-permute-done | bytes 524320 | tf_op jit(solution)/shard_map/ppermute | solution.py:30
  95.9 6.4 %collective-permute-start.13 = (f32[8,128]{1,0:T(8,128)S(1)}, f32[8,128]{1,0:T(8,128)S(1)}, u32[]{:S(2)}, u32[]{:S(2)}) collective-permute-start(f32[8,128]{1,0:T(8,128)S(1)} %get-tuple-element.28), channel_id=1, source_target_pairs={{0,96},{32,0},{64,32},{96,64},{1,97},{33,1},{65,33},{97,65},{2,98}... | collective-permute-start | bytes 12296 | tf_op jit(solution)/shard_map/ppermute | solution.py:30
  102.3 1.4 collective-permute-start.14
  103.8 3.6 %collective-permute-done.14 = f32[8,128]{1,0:T(8,128)S(1)} collective-permute-done((f32[8,128]{1,0:T(8,128)S(1)}, f32[8,128]{1,0:T(8,128)S(1)}, u32[]{:S(2)}, u32[]{:S(2)}) %collective-permute-start.14) | collective-permute-done | bytes 4128 | tf_op jit(solution)/shard_map/ppermute | solution.py:30
  107.4 3.2 %collective-permute-start.16 = (f32[8,128]{1,0:T(8,128)S(1)}, f32[8,128]{1,0:T(8,128)S(1)}, u32[]{:S(2)}, u32[]{:S(2)}) collective-permute-start(f32[8,128]{1,0:T(8,128)S(1)} %add_add_fusion.2), channel_id=1, source_target_pairs={{0,24},{8,0},{16,8},{24,16},{1,25},{9,1},{17,9},{25,17},{2,26},{10... | collective-permute-start | bytes 12296 | tf_op jit(solution)/shard_map/ppermute | solution.py:30
  110.7 1.6 collective-permute-done.15
  112.3 3.5 %collective-permute-done.17 = f32[8,128]{1,0:T(8,128)S(1)} collective-permute-done((f32[8,128]{1,0:T(8,128)S(1)}, f32[8,128]{1,0:T(8,128)S(1)}, u32[]{:S(2)}, u32[]{:S(2)}) %collective-permute-start.17) | collective-permute-done | bytes 4128 | tf_op jit(solution)/shard_map/ppermute | solution.py:30
  115.8 1.6 collective-permute-start.18
  117.4 1.7 collective-permute-start.19
  119.0 2.0 %collective-permute-start.20 = (f32[8,128]{1,0:T(8,128)S(1)}, f32[8,128]{1,0:T(8,128)S(1)}, u32[]{:S(2)}, u32[]{:S(2)}) collective-permute-start(f32[8,128]{1,0:T(8,128)S(1)} %add_add_fusion.1), channel_id=1, source_target_pairs={{0,4},{2,6},{4,0},{6,2},{1,5},{3,7},{5,1},{7,3},{8,12},{10,14},{12... | collective-permute-start | bytes 12296 | tf_op jit(solution)/shard_map/ppermute | solution.py:30
  121.0 3.1 %collective-permute-done.20 = f32[8,128]{1,0:T(8,128)S(1)} collective-permute-done((f32[8,128]{1,0:T(8,128)S(1)}, f32[8,128]{1,0:T(8,128)S(1)}, u32[]{:S(2)}, u32[]{:S(2)}) %collective-permute-start.20) | collective-permute-done | bytes 4128 | tf_op jit(solution)/shard_map/ppermute | solution.py:30
  124.2 1.2 collective-permute-done.21
  125.3 1.7 shard_map.78
  127.1 3.4 %collective-permute-start.30 = (bf16[1024,128]{1,0:T(8,128)(2,1)S(1)}, bf16[1024,128]{1,0:T(8,128)(2,1)S(1)}, u32[]{:S(2)}, u32[]{:S(2)}) collective-permute-start(bf16[1024,128]{1,0:T(8,128)(2,1)S(1)} %get-tuple-element.32.refs_0_), channel_id=1, source_target_pairs={{0,64},{32,96},{64,0},{96,32},{1,65},{33,97},{65,1},{97,33},{2,66}... | collective-permute-start | bytes 786440 | tf_op jit(solution)/shard_map/ppermute | solution.py:30
  131.1 1.5 collective-permute-start.23
  132.6 4.7 %collective-permute-done.29.refs_1_ = bf16[1024,128]{1,0:T(8,128)(2,1)S(1)} collective-permute-done((bf16[1024,128]{1,0:T(8,128)(2,1)S(1)}, bf16[1024,128]{1,0:T(8,128)(2,1)S(1)}, u32[]{:S(2)}, u32[]{:S(2)}) %collective-permute-start.29) | collective-permute-done | bytes 262176 | tf_op jit(solution)/shard_map/ppermute | solution.py:30
  137.3 5.2 %collective-permute-done.30.refs_2_ = bf16[1024,128]{1,0:T(8,128)(2,1)S(1)} collective-permute-done((bf16[1024,128]{1,0:T(8,128)(2,1)S(1)}, bf16[1024,128]{1,0:T(8,128)(2,1)S(1)}, u32[]{:S(2)}, u32[]{:S(2)}) %collective-permute-start.30) | collective-permute-done | bytes 262176 | tf_op jit(solution)/shard_map/ppermute | solution.py:30
  143.7 3.2 %collective-permute-start.34 = (bf16[4,1024,128]{2,1,0:T(8,128)(2,1)S(1)}, bf16[4,1024,128]{2,1,0:T(8,128)(2,1)S(1)}, u32[]{:S(2)}, u32[]{:S(2)}) collective-permute-start(bf16[4,1024,128]{2,1,0:T(8,128)(2,1)S(1)} %shard_map.80.refs_1_), channel_id=1, source_target_pairs={{0,24},{8,0},{16,8},{24,16},{1,25},{9,1},{17,9},{25,17},{2,26},{10... | collective-permute-start | bytes 3145736 | tf_op jit(solution)/shard_map/ppermute | solution.py:30
  147.6 0.8 collective-permute-start.25
  148.4 2.5 %collective-permute-start.27 = (bf16[4,1024,128]{2,1,0:T(8,128)(2,1)S(1)}, bf16[4,1024,128]{2,1,0:T(8,128)(2,1)S(1)}, u32[]{:S(2)}, u32[]{:S(2)}) collective-permute-start(bf16[4,1024,128]{2,1,0:T(8,128)(2,1)S(1)} %shard_map.79.refs_0_), channel_id=1, source_target_pairs={{0,96},{32,0},{64,32},{96,64},{1,97},{33,1},{65,33},{97,65},{2,98}... | collective-permute-start | bytes 3145736 | tf_op jit(solution)/shard_map/ppermute | solution.py:30
  150.9 18.1 %collective-permute-done.32.refs_2_ = bf16[4,1024,128]{2,1,0:T(8,128)(2,1)S(1)} collective-permute-done((bf16[4,1024,128]{2,1,0:T(8,128)(2,1)S(1)}, bf16[4,1024,128]{2,1,0:T(8,128)(2,1)S(1)}, u32[]{:S(2)}, u32[]{:S(2)}) %collective-permute-start.32) | collective-permute-done | bytes 1048608 | tf_op jit(solution)/shard_map/ppermute | solution.py:30
  169.1 3.3 %collective-permute-start.35 = (bf16[4,512,128]{2,1,0:T(8,128)(2,1)S(1)}, bf16[4,512,128]{2,1,0:T(8,128)(2,1)S(1)}, u32[]{:S(2)}, u32[]{:S(2)}) collective-permute-start(bf16[4,512,128]{2,1,0:T(8,128)(2,1)S(1)} %slice.19), channel_id=1, source_target_pairs={{0,24},{8,0},{16,8},{24,16},{1,25},{9,1},{17,9},{25,17},{2,26},{10... | collective-permute-start | bytes 1572872 | tf_op jit(solution)/shard_map/ppermute | solution.py:30
  173.1 1.1 collective-permute-start.26
  174.3 2.2 %collective-permute-start.28 = (bf16[4,512,128]{2,1,0:T(8,128)(2,1)S(1)}, bf16[4,512,128]{2,1,0:T(8,128)(2,1)S(1)}, u32[]{:S(2)}, u32[]{:S(2)}) collective-permute-start(bf16[4,512,128]{2,1,0:T(8,128)(2,1)S(1)} %slice.17), channel_id=1, source_target_pairs={{0,96},{32,0},{64,32},{96,64},{1,97},{33,1},{65,33},{97,65},{2,98}... | collective-permute-start | bytes 1572872 | tf_op jit(solution)/shard_map/ppermute | solution.py:30
  176.5 3.2 %shard_map.84 = (f32[2,1024,128]{2,1,0:T(8,128)}, f32[2,1024,128]{2,1,0:T(8,128)}, f32[2,1024,128]{2,1,0:T(8,128)}) custom-call(f32[8,128]{1,0:T(8,128)S(1)} %add.87.squares, f32[1024,128]{1,0:T(8,128)S(1)} %get-tuple-element.29.refs_0_.mean_a, f32[1024,128]{1,0:T(8,128)S(1)} %get-tuple-element.30.refs_4_.mean_b, f32[2,1024,128]{2,1,0:T(8,128)S(1)} %bitcast.66, ...), custom_call_target="tpu_custom_call" | custom-call | flops 5242880 | bytes 7864320 | tf_op jit(solution)/shard_map/pallas_call | solution.py:145
  179.8 1.9 shard_map.81.refs_4_
  181.6 2.6 %shard_map.82.refs_4_ = bf16[4,4,2,1024,128]{4,3,2,1,0:T(8,128)(2,1)} custom-call(s32[2]{0:T(128)S(1)} %pad_add_fusion.where, bf16[4,1024,128]{2,1,0:T(8,128)(2,1)S(1)} %collective-permute-done.25.refs_0_, bf16[4,1024,128]{2,1,0:T(8,128)(2,1)S(1)} %collective-permute-done.27.refs_1_, ...), custom_call_target="tpu_custom_call", output_to_operand_aliasing={{}: (5, {})} | custom-call | bytes 8388608 | tf_op jit(solution)/shard_map/pallas_call | solution.py:172
  184.3 2.6 %collective-permute-done.26.refs_0_ = bf16[4,512,128]{2,1,0:T(8,128)(2,1)S(1)} collective-permute-done((bf16[4,512,128]{2,1,0:T(8,128)(2,1)S(1)}, bf16[4,512,128]{2,1,0:T(8,128)(2,1)S(1)}, u32[]{:S(2)}, u32[]{:S(2)}) %collective-permute-start.26) | collective-permute-done | bytes 524320 | tf_op jit(solution)/shard_map/ppermute | solution.py:30
  186.9 1.9 %shard_map.83 = bf16[4,4,2,1024,128]{4,3,2,1,0:T(8,128)(2,1)} custom-call(s32[2]{0:T(128)S(1)} %pad_add_fusion.where, bf16[4,512,128]{2,1,0:T(8,128)(2,1)S(1)} %collective-permute-done.26.refs_0_, bf16[4,512,128]{2,1,0:T(8,128)(2,1)S(1)} %collective-permute-done.28.refs_1_, ...), custom_call_target="tpu_custom_call", output_to_operand_aliasing={{}: (5, {})} | custom-call | bytes 4194304 | tf_op jit(solution)/shard_map/pallas_call | solution.py:172
  (54 shorter events, 5.1 us)
Async XLA Ops:
  4.3 26.2 %collective-permute-start.6 = (bf16[4,1024,128]{2,1,0:T(8,128)(2,1)}, bf16[4,1024,128]{2,1,0:T(8,128)(2,1)S(1)}, u32[]{:S(2)}, u32[]{:S(2)}) collective-permute-start(bf16[4,1024,128]{2,1,0:T(8,128)(2,1)} %get-tuple-element.38), channel_id=1, source_target_pairs={{0,8},{8,16},{16,24},{24,0},{1,9},{9,17},{17,25},{25,1},{2,10},{10... | collective-permute-start | bytes 3145736 | tf_op jit(solution)/shard_map/ppermute | solution.py:30
  5.8 28.9 %collective-permute-start.7 = (bf16[4,1024,128]{2,1,0:T(8,128)(2,1)}, bf16[4,1024,128]{2,1,0:T(8,128)(2,1)S(1)}, u32[]{:S(2)}, u32[]{:S(2)}) collective-permute-start(bf16[4,1024,128]{2,1,0:T(8,128)(2,1)} %get-tuple-element.37), channel_id=1, source_target_pairs={{0,24},{8,0},{16,8},{24,16},{1,25},{9,1},{17,9},{25,17},{2,26},{10... | collective-permute-start | bytes 3145736 | tf_op jit(solution)/shard_map/ppermute | solution.py:30
  7.5 46.6 %collective-permute-start.8 = (bf16[4,1024,128]{2,1,0:T(8,128)(2,1)}, bf16[4,1024,128]{2,1,0:T(8,128)(2,1)S(1)}, u32[]{:S(2)}, u32[]{:S(2)}) collective-permute-start(bf16[4,1024,128]{2,1,0:T(8,128)(2,1)} %get-tuple-element.36), channel_id=1, source_target_pairs={{0,16},{8,24},{16,0},{24,8},{1,17},{9,25},{17,1},{25,9},{2,18},{10... | collective-permute-start | bytes 3145736 | tf_op jit(solution)/shard_map/ppermute | solution.py:30
  11.5 51.8 %collective-permute-start = (bf16[4,1024,128]{2,1,0:T(8,128)(2,1)S(1)}, bf16[4,1024,128]{2,1,0:T(8,128)(2,1)S(1)}, u32[]{:S(2)}, u32[]{:S(2)}) collective-permute-start(bf16[4,1024,128]{2,1,0:T(8,128)(2,1)S(1)} %get-tuple-element.41), channel_id=1, source_target_pairs={{0,32},{32,64},{64,96},{96,0},{1,33},{33,65},{65,97},{97,1},{2,34}... | collective-permute-start | bytes 3145736 | tf_op jit(solution)/shard_map/ppermute | solution.py:30
  13.4 51.0 %collective-permute-start.1 = (bf16[4,1024,128]{2,1,0:T(8,128)(2,1)S(1)}, bf16[4,1024,128]{2,1,0:T(8,128)(2,1)S(1)}, u32[]{:S(2)}, u32[]{:S(2)}) collective-permute-start(bf16[4,1024,128]{2,1,0:T(8,128)(2,1)S(1)} %get-tuple-element.40), channel_id=1, source_target_pairs={{0,96},{32,0},{64,32},{96,64},{1,97},{33,1},{65,33},{97,65},{2,98}... | collective-permute-start | bytes 3145736 | tf_op jit(solution)/shard_map/ppermute | solution.py:30
  30.5 34.0 %collective-permute-start.2 = (bf16[4,1024,128]{2,1,0:T(8,128)(2,1)S(1)}, bf16[4,1024,128]{2,1,0:T(8,128)(2,1)S(1)}, u32[]{:S(2)}, u32[]{:S(2)}) collective-permute-start(bf16[4,1024,128]{2,1,0:T(8,128)(2,1)S(1)} %get-tuple-element.39), channel_id=1, source_target_pairs={{0,64},{32,96},{64,0},{96,32},{1,65},{33,97},{65,1},{97,33},{2,66}... | collective-permute-start | bytes 3145736 | tf_op jit(solution)/shard_map/ppermute | solution.py:30
  54.1 3.4 %copy-start = (bf16[1,1,4,1048576]{3,2,1,0:T(4,128)(2,1)S(1)}, bf16[1,1,4,1048576]{3,2,1,0:T(4,128)(2,1)}, u32[]{:S(2)}) copy-start(bf16[1,1,4,1048576]{3,2,1,0:T(4,128)(2,1)} %param.4) | copy-start | bytes 25165828
  59.0 66.3 %copy-start.1 = (f32[1,4,65536]{2,1,0:T(4,128)S(1)}, f32[1,4,65536]{2,1,0:T(4,128)}, u32[]{:S(2)}) copy-start(f32[1,4,65536]{2,1,0:T(4,128)} %param.5) | copy-start | bytes 3145732
  59.0 66.3 %copy-start.2 = (f32[1,4,65536]{2,1,0:T(4,128)S(1)}, f32[1,4,65536]{2,1,0:T(4,128)}, u32[]{:S(2)}) copy-start(f32[1,4,65536]{2,1,0:T(4,128)} %param.6) | copy-start | bytes 3145732
  59.0 66.3 %copy-start.3 = (f32[1,4,65536]{2,1,0:T(4,128)S(1)}, f32[1,4,65536]{2,1,0:T(4,128)}, u32[]{:S(2)}) copy-start(f32[1,4,65536]{2,1,0:T(4,128)} %param.7) | copy-start | bytes 3145732
  59.0 25.7 %collective-permute-start.10 = (f32[1024,128]{1,0:T(8,128)S(1)}, f32[1024,128]{1,0:T(8,128)S(1)}, u32[]{:S(2)}, u32[]{:S(2)}) collective-permute-start(f32[1024,128]{1,0:T(8,128)S(1)} %get-tuple-element.26), channel_id=1, source_target_pairs={{0,96},{32,0},{64,32},{96,64},{1,97},{33,1},{65,33},{97,65},{2,98}... | collective-permute-start | bytes 1572872 | tf_op jit(solution)/shard_map/ppermute | solution.py:30
  63.2 22.3 %collective-permute-start.11 = (f32[1024,128]{1,0:T(8,128)S(1)}, f32[1024,128]{1,0:T(8,128)S(1)}, u32[]{:S(2)}, u32[]{:S(2)}) collective-permute-start(f32[1024,128]{1,0:T(8,128)S(1)} %get-tuple-element.27), channel_id=1, source_target_pairs={{0,64},{32,96},{64,0},{96,32},{1,65},{33,97},{65,1},{97,33},{2,66}... | collective-permute-start | bytes 1572872 | tf_op jit(solution)/shard_map/ppermute | solution.py:30
  63.2 25.0 %collective-permute-start.9 = (f32[1024,128]{1,0:T(8,128)S(1)}, f32[1024,128]{1,0:T(8,128)S(1)}, u32[]{:S(2)}, u32[]{:S(2)}) collective-permute-start(f32[1024,128]{1,0:T(8,128)S(1)} %get-tuple-element.25), channel_id=1, source_target_pairs={{0,32},{32,64},{64,96},{96,0},{1,33},{33,65},{65,97},{97,1},{2,34}... | collective-permute-start | bytes 1572872 | tf_op jit(solution)/shard_map/ppermute | solution.py:30
  66.0 22.3 %collective-permute-start.3 = (f32[1024,128]{1,0:T(8,128)S(1)}, f32[1024,128]{1,0:T(8,128)S(1)}, u32[]{:S(2)}, u32[]{:S(2)}) collective-permute-start(f32[1024,128]{1,0:T(8,128)S(1)} %get-tuple-element.21), channel_id=1, source_target_pairs={{0,8},{8,16},{16,24},{24,0},{1,9},{9,17},{17,25},{25,1},{2,10},{10... | collective-permute-start | bytes 1572872 | tf_op jit(solution)/shard_map/ppermute | solution.py:30
  67.2 21.1 %collective-permute-start.4 = (f32[1024,128]{1,0:T(8,128)S(1)}, f32[1024,128]{1,0:T(8,128)S(1)}, u32[]{:S(2)}, u32[]{:S(2)}) collective-permute-start(f32[1024,128]{1,0:T(8,128)S(1)} %get-tuple-element.22), channel_id=1, source_target_pairs={{0,24},{8,0},{16,8},{24,16},{1,25},{9,1},{17,9},{25,17},{2,26},{10... | collective-permute-start | bytes 1572872 | tf_op jit(solution)/shard_map/ppermute | solution.py:30
  84.7 10.7 %collective-permute-start.5 = (f32[1024,128]{1,0:T(8,128)S(1)}, f32[1024,128]{1,0:T(8,128)S(1)}, u32[]{:S(2)}, u32[]{:S(2)}) collective-permute-start(f32[1024,128]{1,0:T(8,128)S(1)} %get-tuple-element.23), channel_id=1, source_target_pairs={{0,16},{8,24},{16,0},{24,8},{1,17},{9,25},{17,1},{25,9},{2,18},{10... | collective-permute-start | bytes 1572872 | tf_op jit(solution)/shard_map/ppermute | solution.py:30
  95.8 8.0 %collective-permute-start.12 = (f32[8,128]{1,0:T(8,128)S(1)}, f32[8,128]{1,0:T(8,128)S(1)}, u32[]{:S(2)}, u32[]{:S(2)}) collective-permute-start(f32[8,128]{1,0:T(8,128)S(1)} %get-tuple-element.28), channel_id=1, source_target_pairs={{0,32},{32,64},{64,96},{96,0},{1,33},{33,65},{65,97},{97,1},{2,34}... | collective-permute-start | bytes 12296 | tf_op jit(solution)/shard_map/ppermute | solution.py:30
  95.9 8.0 %collective-permute-start.13 = (f32[8,128]{1,0:T(8,128)S(1)}, f32[8,128]{1,0:T(8,128)S(1)}, u32[]{:S(2)}, u32[]{:S(2)}) collective-permute-start(f32[8,128]{1,0:T(8,128)S(1)} %get-tuple-element.28), channel_id=1, source_target_pairs={{0,96},{32,0},{64,32},{96,64},{1,97},{33,1},{65,33},{97,65},{2,98}... | collective-permute-start | bytes 12296 | tf_op jit(solution)/shard_map/ppermute | solution.py:30
  102.3 5.1 %collective-permute-start.14 = (f32[8,128]{1,0:T(8,128)S(1)}, f32[8,128]{1,0:T(8,128)S(1)}, u32[]{:S(2)}, u32[]{:S(2)}) collective-permute-start(f32[8,128]{1,0:T(8,128)S(1)} %get-tuple-element.28), channel_id=1, source_target_pairs={{0,64},{32,96},{64,0},{96,32},{1,65},{33,97},{65,1},{97,33},{2,66}... | collective-permute-start | bytes 12296 | tf_op jit(solution)/shard_map/ppermute | solution.py:30
  107.4 4.8 %collective-permute-start.15 = (f32[8,128]{1,0:T(8,128)S(1)}, f32[8,128]{1,0:T(8,128)S(1)}, u32[]{:S(2)}, u32[]{:S(2)}) collective-permute-start(f32[8,128]{1,0:T(8,128)S(1)} %add_add_fusion.2), channel_id=1, source_target_pairs={{0,8},{8,16},{16,24},{24,0},{1,9},{9,17},{17,25},{25,1},{2,10},{10... | collective-permute-start | bytes 12296 | tf_op jit(solution)/shard_map/ppermute | solution.py:30
  107.4 4.8 %collective-permute-start.16 = (f32[8,128]{1,0:T(8,128)S(1)}, f32[8,128]{1,0:T(8,128)S(1)}, u32[]{:S(2)}, u32[]{:S(2)}) collective-permute-start(f32[8,128]{1,0:T(8,128)S(1)} %add_add_fusion.2), channel_id=1, source_target_pairs={{0,24},{8,0},{16,8},{24,16},{1,25},{9,1},{17,9},{25,17},{2,26},{10... | collective-permute-start | bytes 12296 | tf_op jit(solution)/shard_map/ppermute | solution.py:30
  110.7 5.1 %collective-permute-start.17 = (f32[8,128]{1,0:T(8,128)S(1)}, f32[8,128]{1,0:T(8,128)S(1)}, u32[]{:S(2)}, u32[]{:S(2)}) collective-permute-start(f32[8,128]{1,0:T(8,128)S(1)} %add_add_fusion.2), channel_id=1, source_target_pairs={{0,16},{8,24},{16,0},{24,8},{1,17},{9,25},{17,1},{25,9},{2,18},{10... | collective-permute-start | bytes 12296 | tf_op jit(solution)/shard_map/ppermute | solution.py:30
  115.8 5.2 %collective-permute-start.18 = (f32[8,128]{1,0:T(8,128)S(1)}, f32[8,128]{1,0:T(8,128)S(1)}, u32[]{:S(2)}, u32[]{:S(2)}) collective-permute-start(f32[8,128]{1,0:T(8,128)S(1)} %add_add_fusion.1), channel_id=1, source_target_pairs={{0,2},{2,4},{4,6},{6,0},{1,3},{3,5},{5,7},{7,1},{8,10},{10,12},{12... | collective-permute-start | bytes 12296 | tf_op jit(solution)/shard_map/ppermute | solution.py:30
  117.4 3.7 %collective-permute-start.19 = (f32[8,128]{1,0:T(8,128)S(1)}, f32[8,128]{1,0:T(8,128)S(1)}, u32[]{:S(2)}, u32[]{:S(2)}) collective-permute-start(f32[8,128]{1,0:T(8,128)S(1)} %add_add_fusion.1), channel_id=1, source_target_pairs={{0,6},{2,0},{4,2},{6,4},{1,7},{3,1},{5,3},{7,5},{8,14},{10,8},{12,... | collective-permute-start | bytes 12296 | tf_op jit(solution)/shard_map/ppermute | solution.py:30
  119.0 5.1 %collective-permute-start.20 = (f32[8,128]{1,0:T(8,128)S(1)}, f32[8,128]{1,0:T(8,128)S(1)}, u32[]{:S(2)}, u32[]{:S(2)}) collective-permute-start(f32[8,128]{1,0:T(8,128)S(1)} %add_add_fusion.1), channel_id=1, source_target_pairs={{0,4},{2,6},{4,0},{6,2},{1,5},{3,7},{5,1},{7,3},{8,12},{10,14},{12... | collective-permute-start | bytes 12296 | tf_op jit(solution)/shard_map/ppermute | solution.py:30
  124.1 1.2 collective-permute-start.21
  127.0 10.3 %collective-permute-start.29 = (bf16[1024,128]{1,0:T(8,128)(2,1)S(1)}, bf16[1024,128]{1,0:T(8,128)(2,1)S(1)}, u32[]{:S(2)}, u32[]{:S(2)}) collective-permute-start(bf16[1024,128]{1,0:T(8,128)(2,1)S(1)} %get-tuple-element.32.refs_0_), channel_id=1, source_target_pairs={{0,32},{32,64},{64,96},{96,0},{1,33},{33,65},{65,97},{97,1},{2,34}... | collective-permute-start | bytes 786440 | tf_op jit(solution)/shard_map/ppermute | solution.py:30
  127.1 15.4 %collective-permute-start.30 = (bf16[1024,128]{1,0:T(8,128)(2,1)S(1)}, bf16[1024,128]{1,0:T(8,128)(2,1)S(1)}, u32[]{:S(2)}, u32[]{:S(2)}) collective-permute-start(bf16[1024,128]{1,0:T(8,128)(2,1)S(1)} %get-tuple-element.32.refs_0_), channel_id=1, source_target_pairs={{0,64},{32,96},{64,0},{96,32},{1,65},{33,97},{65,1},{97,33},{2,66}... | collective-permute-start | bytes 786440 | tf_op jit(solution)/shard_map/ppermute | solution.py:30
  130.5 12.4 %collective-permute-start.31 = (bf16[1024,128]{1,0:T(8,128)(2,1)S(1)}, bf16[1024,128]{1,0:T(8,128)(2,1)S(1)}, u32[]{:S(2)}, u32[]{:S(2)}) collective-permute-start(bf16[1024,128]{1,0:T(8,128)(2,1)S(1)} %get-tuple-element.32.refs_0_), channel_id=1, source_target_pairs={{0,96},{32,0},{64,32},{96,64},{1,97},{33,1},{65,33},{97,65},{2,98}... | collective-permute-start | bytes 786440 | tf_op jit(solution)/shard_map/ppermute | solution.py:30
  131.1 15.8 %collective-permute-start.22 = (bf16[1024,128]{1,0:T(8,128)(2,1)S(1)}, bf16[1024,128]{1,0:T(8,128)(2,1)S(1)}, u32[]{:S(2)}, u32[]{:S(2)}) collective-permute-start(bf16[1024,128]{1,0:T(8,128)(2,1)S(1)} %get-tuple-element.31.refs_0_), channel_id=1, source_target_pairs={{0,8},{8,16},{16,24},{24,0},{1,9},{9,17},{17,25},{25,1},{2,10},{10... | collective-permute-start | bytes 786440 | tf_op jit(solution)/shard_map/ppermute | solution.py:30
  131.1 15.8 %collective-permute-start.23 = (bf16[1024,128]{1,0:T(8,128)(2,1)S(1)}, bf16[1024,128]{1,0:T(8,128)(2,1)S(1)}, u32[]{:S(2)}, u32[]{:S(2)}) collective-permute-start(bf16[1024,128]{1,0:T(8,128)(2,1)S(1)} %get-tuple-element.31.refs_0_), channel_id=1, source_target_pairs={{0,16},{8,24},{16,0},{24,8},{1,17},{9,25},{17,1},{25,9},{2,18},{10... | collective-permute-start | bytes 786440 | tf_op jit(solution)/shard_map/ppermute | solution.py:30
  137.3 9.6 %collective-permute-start.24 = (bf16[1024,128]{1,0:T(8,128)(2,1)S(1)}, bf16[1024,128]{1,0:T(8,128)(2,1)S(1)}, u32[]{:S(2)}, u32[]{:S(2)}) collective-permute-start(bf16[1024,128]{1,0:T(8,128)(2,1)S(1)} %get-tuple-element.31.refs_0_), channel_id=1, source_target_pairs={{0,24},{8,0},{16,8},{24,16},{1,25},{9,1},{17,9},{25,17},{2,26},{10... | collective-permute-start | bytes 786440 | tf_op jit(solution)/shard_map/ppermute | solution.py:30
  143.6 25.4 %collective-permute-start.32 = (bf16[4,1024,128]{2,1,0:T(8,128)(2,1)S(1)}, bf16[4,1024,128]{2,1,0:T(8,128)(2,1)S(1)}, u32[]{:S(2)}, u32[]{:S(2)}) collective-permute-start(bf16[4,1024,128]{2,1,0:T(8,128)(2,1)S(1)} %shard_map.80.refs_1_), channel_id=1, source_target_pairs={{0,8},{8,16},{16,24},{24,0},{1,9},{9,17},{17,25},{25,1},{2,10},{10... | collective-permute-start | bytes 3145736 | tf_op jit(solution)/shard_map/ppermute | solution.py:30
  143.7 25.4 %collective-permute-start.34 = (bf16[4,1024,128]{2,1,0:T(8,128)(2,1)S(1)}, bf16[4,1024,128]{2,1,0:T(8,128)(2,1)S(1)}, u32[]{:S(2)}, u32[]{:S(2)}) collective-permute-start(bf16[4,1024,128]{2,1,0:T(8,128)(2,1)S(1)} %shard_map.80.refs_1_), channel_id=1, source_target_pairs={{0,24},{8,0},{16,8},{24,16},{1,25},{9,1},{17,9},{25,17},{2,26},{10... | collective-permute-start | bytes 3145736 | tf_op jit(solution)/shard_map/ppermute | solution.py:30
  147.6 25.5 %collective-permute-start.25 = (bf16[4,1024,128]{2,1,0:T(8,128)(2,1)S(1)}, bf16[4,1024,128]{2,1,0:T(8,128)(2,1)S(1)}, u32[]{:S(2)}, u32[]{:S(2)}) collective-permute-start(bf16[4,1024,128]{2,1,0:T(8,128)(2,1)S(1)} %shard_map.79.refs_0_), channel_id=1, source_target_pairs={{0,32},{32,64},{64,96},{96,0},{1,33},{33,65},{65,97},{97,1},{2,34}... | collective-permute-start | bytes 3145736 | tf_op jit(solution)/shard_map/ppermute | solution.py:30
  148.4 25.8 %collective-permute-start.27 = (bf16[4,1024,128]{2,1,0:T(8,128)(2,1)S(1)}, bf16[4,1024,128]{2,1,0:T(8,128)(2,1)S(1)}, u32[]{:S(2)}, u32[]{:S(2)}) collective-permute-start(bf16[4,1024,128]{2,1,0:T(8,128)(2,1)S(1)} %shard_map.79.refs_0_), channel_id=1, source_target_pairs={{0,96},{32,0},{64,32},{96,64},{1,97},{33,1},{65,33},{97,65},{2,98}... | collective-permute-start | bytes 3145736 | tf_op jit(solution)/shard_map/ppermute | solution.py:30
  169.0 15.2 %collective-permute-start.33 = (bf16[4,512,128]{2,1,0:T(8,128)(2,1)S(1)}, bf16[4,512,128]{2,1,0:T(8,128)(2,1)S(1)}, u32[]{:S(2)}, u32[]{:S(2)}) collective-permute-start(bf16[4,512,128]{2,1,0:T(8,128)(2,1)S(1)} %slice.18), channel_id=1, source_target_pairs={{0,8},{8,16},{16,24},{24,0},{1,9},{9,17},{17,25},{25,1},{2,10},{10... | collective-permute-start | bytes 1572872 | tf_op jit(solution)/shard_map/ppermute | solution.py:30
  169.1 15.1 %collective-permute-start.35 = (bf16[4,512,128]{2,1,0:T(8,128)(2,1)S(1)}, bf16[4,512,128]{2,1,0:T(8,128)(2,1)S(1)}, u32[]{:S(2)}, u32[]{:S(2)}) collective-permute-start(bf16[4,512,128]{2,1,0:T(8,128)(2,1)S(1)} %slice.19), channel_id=1, source_target_pairs={{0,24},{8,0},{16,8},{24,16},{1,25},{9,1},{17,9},{25,17},{2,26},{10... | collective-permute-start | bytes 1572872 | tf_op jit(solution)/shard_map/ppermute | solution.py:30
  173.1 13.7 %collective-permute-start.26 = (bf16[4,512,128]{2,1,0:T(8,128)(2,1)S(1)}, bf16[4,512,128]{2,1,0:T(8,128)(2,1)S(1)}, u32[]{:S(2)}, u32[]{:S(2)}) collective-permute-start(bf16[4,512,128]{2,1,0:T(8,128)(2,1)S(1)} %slice.16), channel_id=1, source_target_pairs={{0,32},{32,64},{64,96},{96,0},{1,33},{33,65},{65,97},{97,1},{2,34}... | collective-permute-start | bytes 1572872 | tf_op jit(solution)/shard_map/ppermute | solution.py:30
  174.3 12.6 %collective-permute-start.28 = (bf16[4,512,128]{2,1,0:T(8,128)(2,1)S(1)}, bf16[4,512,128]{2,1,0:T(8,128)(2,1)S(1)}, u32[]{:S(2)}, u32[]{:S(2)}) collective-permute-start(bf16[4,512,128]{2,1,0:T(8,128)(2,1)S(1)} %slice.17), channel_id=1, source_target_pairs={{0,96},{32,0},{64,32},{96,64},{1,97},{33,1},{65,33},{97,65},{2,98}... | collective-permute-start | bytes 1572872 | tf_op jit(solution)/shard_map/ppermute | solution.py:30

commit v2 on v1

--- a/solution.py
+++ b/solution.py
@@ -34,58 +34,178 @@
     return pl.CostEstimate(flops=flops, bytes_accessed=moved, transcendentals=0)
 
 
-def first_sum_kernel(where, own, one, two, three, *outs):
-    mine = where[1]
-    for ahead, out in enumerate(outs):
-        at = lax.rem(mine + ahead, 4)
-        total = own[at].astype(f32)
-        for part in (one, two, three):
-            total += part[at].astype(f32)
-        out[...] = total
-
-
-def first_sum(pieces, arrived, where, along_z):
-    half = arrived[0].shape[1]
-    steps = half // BLOCK
-    if along_z:
-        own = pl.BlockSpec((None, 4, BLOCK, LANES), lambda i, w: (w[0], 0, i, 0))
+def pick_kernel(along_z, by, where, pieces, out, sems):
+    quarter = out.shape[1] // 2
+    low = 0 if along_z else 2 * quarter
+    far_low = low if by == 1 else low + quarter
+    near, far = lax.rem(where[0] + by, 4), lax.rem(where[0] + 2, 4)
+
+    def source(at, start, count):
+        rows = pl.ds(start, count)
+        return pieces.at[at, :, rows] if along_z else pieces.at[:, at, rows]
+
+    copies = [pltpu.make_async_copy(source(near, low, 2 * quarter), out.at[pl.ds(0, 4)], sems.at[0])]
+    for j in range(4):
+        rows = pl.ds(far_low, quarter)
+        piece = pieces.at[far, j, rows] if along_z else pieces.at[j, far, rows]
+        copies.append(pltpu.make_async_copy(piece, out.at[4 + j // 2, pl.ds(j % 2 * quarter, quarter)], sems.at[1 + j]))
+    for copy in copies:
+        copy.start()
+    for copy in copies:
+        copy.wait()
+
+
+def pick(pieces, where, along_z, by):
+    half = pieces.shape[2] // 2
+    return pl.pallas_call(
+        functools.partial(pick_kernel, along_z, by),
+        grid_spec=pltpu.PrefetchScalarGridSpec(
+            num_scalar_prefetch=1,
+            grid=(),
+            in_specs=[pl.BlockSpec(memory_space=pl.ANY)],
+            out_specs=pl.BlockSpec(memory_space=pl.ANY),
+            scratch_shapes=[pltpu.SemaphoreType.DMA((5,))],
+        ),
+        out_shape=jax.ShapeDtypeStruct((6, half, LANES), bf16),
+        compiler_params=pltpu.CompilerParams(vmem_limit_bytes=VMEM_LIMIT),
+        cost_estimate=cost(0, 24 * half * LANES),
+    )(where, pieces)
+
+
+def own_kernel(where, pieces, out_a, out_b, sems):
+    half = out_a.shape[1]
+    copies = [
+        pltpu.make_async_copy(pieces.at[where[0], :, pl.ds(0, half)], out_a, sems.at[0]),
+        pltpu.make_async_copy(pieces.at[:, where[1], pl.ds(half, half)], out_b, sems.at[1]),
+    ]
+    for copy in copies:
+        copy.start()
+    for copy in copies:
+        copy.wait()
+
+
+def own_pieces(pieces, zx):
+    half = pieces.shape[2] // 2
+    return pl.pallas_call(
+        own_kernel,
+        grid_spec=pltpu.PrefetchScalarGridSpec(
+            num_scalar_prefetch=1,
+            grid=(),
+            in_specs=[pl.BlockSpec(memory_space=pl.ANY)],
+            out_specs=[pl.BlockSpec(memory_space=pl.ANY)] * 2,
+            scratch_shapes=[pltpu.SemaphoreType.DMA((2,))],
+        ),
+        out_shape=[jax.ShapeDtypeStruct((4, half, LANES), bf16)] * 2,
+        compiler_params=pltpu.CompilerParams(vmem_limit_bytes=VMEM_LIMIT),
+        cost_estimate=cost(0, 32 * half * LANES),
+    )(zx, pieces)
+
+
+def total_of(refs, at, far):
+    own, behind, ahead = refs
+    return own[at].astype(f32) + behind[at].astype(f32) + ahead[at].astype(f32) + far[at].astype(f32)
+
+
+def far_sum_kernel(where, own, behind, ahead, far_low, far_high, low, high):
+    at = lax.rem(where[1] + 2, 4)
+
+    @pl.when(pl.program_id(0) < pl.num_programs(0) // 2)
+    def _():
+        low[...] = total_of((own, behind, ahead), at, far_low)
+
+    @pl.when(pl.program_id(0) >= pl.num_programs(0) // 2)
+    def _():
+        high[...] = total_of((own, behind, ahead), at, far_high)
+
+
+def near_sum_kernel(where, own, behind, ahead, far_low, far_high, *outs):
+    def write(far):
+        for by, out in zip((0, 1, 3), outs):
+            out[...] = total_of((own, behind, ahead), lax.rem(where[1] + by, 4), far)
+
+    pl.when(pl.program_id(0) < pl.num_programs(0) // 2)(lambda: write(far_low))
+    pl.when(pl.program_id(0) >= pl.num_programs(0) // 2)(lambda: write(far_high))
+
+
+def first_sum(where, own, behind, ahead, far_low, far_high, only_far):
+    half = own.shape[1]
+    quarter, steps = half // 2, half // BLOCK
+    lower = lambda i: jnp.minimum(i, steps // 2 - 1)
+    upper = lambda i: jnp.maximum(i - steps // 2, 0)
+    part = pl.BlockSpec((4, BLOCK, LANES), lambda i, w: (0, i, 0))
+    in_specs = [part] * 3 + [
+        pl.BlockSpec((4, BLOCK, LANES), lambda i, w: (0, lower(i), 0)),
+        pl.BlockSpec((4, BLOCK, LANES), lambda i, w: (0, upper(i), 0)),
+    ]
+    if only_far:
+        out_specs = [
+            pl.BlockSpec((BLOCK, LANES), lambda i, w: (lower(i), 0)),
+            pl.BlockSpec((BLOCK, LANES), lambda i, w: (upper(i), 0)),
+        ]
+        out_shape = [jax.ShapeDtypeStruct((quarter, LANES), f32)] * 2
     else:
-        own = pl.BlockSpec((4, None, BLOCK, LANES), lambda i, w: (0, w[0], steps + i, 0))
-    part = pl.BlockSpec((4, BLOCK, LANES), lambda i, w: (0, i, 0))
-    out = pl.BlockSpec((BLOCK, LANES), lambda i, w: (i, 0))
-    return pl.pallas_call(
-        first_sum_kernel,
+        out_specs = [pl.BlockSpec((BLOCK, LANES), lambda i, w: (i, 0))] * 3
+        out_shape = [jax.ShapeDtypeStruct((half, LANES), f32)] * 3
+    return pl.pallas_call(
+        far_sum_kernel if only_far else near_sum_kernel,
         grid_spec=pltpu.PrefetchScalarGridSpec(
-            num_scalar_prefetch=1, grid=(steps,), in_specs=[own, part, part, part], out_specs=[out] * 4
+            num_scalar_prefetch=1, grid=(steps,), in_specs=in_specs, out_specs=out_specs
         ),
-        out_shape=[jax.ShapeDtypeStruct((half, LANES), f32)] * 4,
+        out_shape=out_shape,
         compiler_params=pltpu.CompilerParams(vmem_limit_bytes=VMEM_LIMIT),
         cost_estimate=cost(16 * half * LANES, 4 * 4 * half * LANES * 3),
-    )(where, pieces, *arrived)
+    )(where, own, behind, ahead, far_low.reshape(4, quarter, LANES), far_high.reshape(4, quarter, LANES))
+
+
+def add_kernel(next_part, low, last_part, high, next_out, last_out):
+    next_out[...] = next_part[...] + low[...]
+    last_out[...] = last_part[...] + high[...]
+
+
+def add_far(to_next, low, to_last, high):
+    quarter = low.shape[0]
+    steps = quarter // BLOCK
+    first = pl.BlockSpec((BLOCK, LANES), lambda i: (i, 0))
+    second = pl.BlockSpec((BLOCK, LANES), lambda i: (steps + i, 0))
+    return pl.pallas_call(
+        add_kernel,
+        grid=(steps,),
+        in_specs=[first, first, second, first],
+        out_specs=[first, second],
+        out_shape=[jax.ShapeDtypeStruct(to_next.shape, f32)] * 2,
+        input_output_aliases={0: 0, 2: 1},
+        compiler_params=pltpu.CompilerParams(vmem_limit_bytes=VMEM_LIMIT),
+        cost_estimate=cost(2 * quarter * LANES, 24 * quarter * LANES),
+    )(to_next, low, to_last, high)
 
 
 def last_sum_kernel(*refs):
-    parts_a, parts_b, (mean_a, mean_b, squares) = refs[:4], refs[4:8], refs[8:]
+    parts_a, parts_b, (mean_a, mean_b, squares, held) = refs[:3], refs[3:6], refs[6:]
 
     @pl.when(pl.program_id(0) == 0)
     def _():
-        squares[...] = jnp.zeros_like(squares)
+        held[...] = jnp.zeros_like(held)
 
     for parts, mean in ((parts_a, mean_a), (parts_b, mean_b)):
-        total = (parts[0][...] + parts[1][...] + parts[2][...] + parts[3][...]) * (1.0 / 16.0)
+        total = (parts[0][...] + parts[1][...] + parts[2][...]) * (1.0 / 16.0)
         mean[...] = total
-        squares[...] += jnp.sum((total * total).reshape(BLOCK // 8, 8, LANES), axis=0)
-
-
-def last_sum(parts_a, parts_b):
+        held[...] += jnp.sum((total * total).reshape(BLOCK // 8, 8, LANES), axis=0)
+
+    @pl.when(pl.program_id(0) == pl.num_programs(0) - 1)
+    def _():
+        squares[...] = jnp.broadcast_to(jnp.sum(held[...], axis=0, keepdims=True), squares.shape)
+
+
+def last_sum(parts_a, parts_b, devices):
     half = parts_a[0].shape[0]
     block = pl.BlockSpec((BLOCK, LANES), lambda i: (i, 0))
     return pl.pallas_call(
         last_sum_kernel,
         grid=(half // BLOCK,),
-        in_specs=[block] * 8,
-        out_specs=[block, block, pl.BlockSpec((8, LANES), lambda i: (0, 0))],
-        out_shape=[jax.ShapeDtypeStruct((half, LANES), f32)] * 2 + [jax.ShapeDtypeStruct((8, LANES), f32)],
+        in_specs=[block] * 6,
+        out_specs=[block, block, pl.BlockSpec((devices, LANES), lambda i: (0, 0))],
+        out_shape=[jax.ShapeDtypeStruct((half, LANES), f32)] * 2 + [jax.ShapeDtypeStruct((devices, LANES), f32)],
+        scratch_shapes=[pltpu.VMEM((8, LANES), f32)],
         compiler_params=pltpu.CompilerParams(vmem_limit_bytes=VMEM_LIMIT),
         cost_estimate=cost(16 * half * LANES, 10 * 4 * half * LANES),
     )(*parts_a, *parts_b)
@@ -115,7 +235,7 @@
 def new_params(squares, means, states):
     half = means[0].shape[0]
     steps = half // BLOCK
-    whole = pl.BlockSpec((8, LANES), lambda i: (0, 0))
+    whole = pl.BlockSpec(squares.shape, lambda i: (0, 0))
     low = pl.BlockSpec((BLOCK, LANES), lambda i: (i, 0))
     high = pl.BlockSpec((BLOCK, LANES), lambda i: (steps + i, 0))
     return pl.pallas_call(
@@ -139,7 +259,7 @@
 
 def both_states(squares, means, states):
     half = means[0].shape[0]
-    whole = pl.BlockSpec((8, LANES), lambda i: (0, 0))
+    whole = pl.BlockSpec(squares.shape, lambda i: (0, 0))
     low = pl.BlockSpec((BLOCK, LANES), lambda i: (i, 0))
     pair = pl.BlockSpec((2, BLOCK, LANES), lambda i: (0, i, 0))
     return pl.pallas_call(
@@ -202,26 +322,27 @@
     zx = jnp.stack([z, x]).astype(jnp.int32)
     xz = jnp.stack([x, z]).astype(jnp.int32)
 
-    def for_z(by):
-        at = lax.rem(z + by, 4)
-        return lax.dynamic_slice(pieces, (at, 0, 0, 0), (1, 4, half, LANES)).reshape(4, half, LANES)
-
-    def for_x(by):
-        at = lax.rem(x + by, 4)
-        return lax.dynamic_slice(pieces, (0, at, half, 0), (4, 1, half, LANES)).reshape(4, half, LANES)
-
-    shifts = (1, 3, 2)
-    got_z = [shift(for_z(s), Z, s) for s in shifts]
-    got_x = [shift(for_x(s), X, s) for s in shifts]
-    sums_a = first_sum(pieces, got_z, zx, True)
-    sums_b = first_sum(pieces, got_x, xz, False)
-    parts_a = [sums_a[0]] + [shift(sums_a[s], X, s) for s in shifts]
-    parts_b = [sums_b[0]] + [shift(sums_b[s], Z, s) for s in shifts]
-    mean_a, mean_b, squares = last_sum(parts_a, parts_b)
-
-    for axis in (Z, X, Y):
-        squares = squares + shift(squares, axis, 1) + shift(squares, axis, 3) + shift(squares, axis, 2)
-    squares = squares + shift(squares, CORE, 1)
+    own_a, own_b = own_pieces(pieces, zx)
+    sends = [pick(pieces, zx, True, 1), pick(pieces, zx, True, 3), pick(pieces, xz, False, 1), pick(pieces, xz, False, 3)]
+    axes = (Z, Z, X, X)
+    ways = (1, 3, 1, 3)
+    got = [shift(v, axis, by) for v, axis, by in zip(sends, axes, ways)]
+    far = [shift(v[4:], axis, by) for v, axis, by in zip(got, axes, ways)]
+    set_a = (zx, own_a, got[0], got[1], far[0], far[1])
+    set_b = (xz, own_b, got[2], got[3], far[2], far[3])
+    low_a, high_a = first_sum(*set_a, True)
+    low_b, high_b = first_sum(*set_b, True)
+    low_a, high_a = shift(low_a, X, 1), shift(high_a, X, 3)
+    low_b, high_b = shift(low_b, Z, 1), shift(high_b, Z, 3)
+    here_a, next_a, last_a = first_sum(*set_a, False)
+    here_b, next_b, last_b = first_sum(*set_b, False)
+    next_a, last_a = add_far(next_a, low_a, last_a, high_a)
+    next_b, last_b = add_far(next_b, low_b, last_b, high_b)
+    parts_a = here_a, shift(next_a, X, 1), shift(last_a, X, 3)
+    parts_b = here_b, shift(next_b, Z, 1), shift(last_b, Z, 3)
+    devices = lax.axis_size((Z, X, Y, CORE))
+    mean_a, mean_b, squares = last_sum(parts_a, parts_b, devices)
+    squares = lax.all_to_all(squares, (Z, X, Y, CORE), 0, 0, tiled=True)
 
     par_a, par_b = new_params(squares, (mean_a, mean_b), states)
     outs = both_states(squares, (mean_a, mean_b), states)

time: 189 us -> 171 us (0.905)
  waiting for transfers between devices: 104 us -> 73 us
  blocking collectives: 0 us -> 18.4 us
  starting transfers between devices: 58.3 us -> 49.6 us
  Pallas kernels: 16 us -> 24.6 us
  local copies, waits for them, and re-layouts: 9.2 us -> 3.68 us
    ppermute x36 -> x30, waiting for transfers between devices: 104 us -> 73 us  [shift(): lax.ppermute(value, axis, [(i, (i + by) % size) for i in range(size)])]
    all_to_all x0 -> x1, blocking collectives: none -> 18.4 us  [shards(): squares = lax.all_to_all(squares, (Z, X, Y, CORE), 0, 0, tiled=True)]
    ppermute x36 -> x30, starting transfers between devices: 58.3 us -> 49.6 us  [shift(): lax.ppermute(value, axis, [(i, (i + by) % size) for i in range(size)])]
    pallas_call x2 -> x11, Pallas kernels: 2.99 us -> 11.6 us  [the longest x4 5.38 us: pick(): pl.pallas_call(functools.partial(pick_kernel, along_z, by), grid_spec=plt...]
    reshape x2 -> x0, local copies, waits for them, and re-layouts: 5.66 us -> none  [the longest x1 3.6 us: for_x(): lax.dynamic_slice(pieces, (0, at, half, 0), (4, 1, half, LANES))]
  transfers between devices with their start and end apart: 36 -> 30, of which waited for: 17 -> 13; matrix products, arithmetic and copies ran while one was open for 1% -> 0% of each run, Pallas kernels for 6% -> 11%
where the time goes in v2:
time: 171 us
  waiting for transfers between devices  73 us (43%)
  starting transfers between devices  49.6 us (29%)
  Pallas kernels  24.6 us (14%)
  blocking collectives  18.4 us (11%)
  local copies, waits for them, and re-layouts  3.68 us (2%)
    ppermute x30, waiting for transfers between devices, shift(): lax.ppermute(value, axis, [(i, (i + by) % size) for i in range(size)])  73 us
    ppermute x30, starting transfers between devices, shift(): lax.ppermute(value, axis, [(i, (i + by) % size) for i in range(size)])  49.6 us
    all_to_all x1, blocking collectives, shards(): squares = lax.all_to_all(squares, (Z, X, Y, CORE), 0, 0, tiled=True)  18.4 us
    pallas_call x5, Pallas kernels, place(): pl.pallas_call(functools.partial(place_kernel, moves, len(parts)), grid_s...  7.69 us
    pallas_call x4, Pallas kernels, pick(): pl.pallas_call(functools.partial(pick_kernel, along_z, by), grid_spec=plt...  5.38 us
    pallas_call x4, Pallas kernels, first_sum(): pl.pallas_call(far_sum_kernel if only_far else near_sum_kernel, grid_spec...  5.3 us
  transfers between devices with their start and end apart: 30, of which 13 were waited for; matrix products, arithmetic and copies ran while one was open for 0% of the time, Pallas kernels for 11%

profile of v2, /device:TPU:0, one launch (start us, length us, event | category | flops | bytes accessed | tf_op | source)
XLA Modules:
  0.0 170.6 jit_solution(10529990292093746352)
XLA Ops:
  0.7 3.4 %copy-done = bf16[1,1,4,1048576]{3,2,1,0:T(4,128)(2,1)S(1)} copy-done((bf16[1,1,4,1048576]{3,2,1,0:T(4,128)(2,1)S(1)}, bf16[1,1,4,1048576]{3,2,1,0:T(4,128)(2,1)}, u32[]{:S(2)}) %copy-start) | copy-done | bytes 8388632
  4.1 1.3 shard_map.82
  5.5 2.9 %collective-permute-start.9 = (bf16[6,1024,128]{2,1,0:T(8,128)(2,1)S(1)}, bf16[6,1024,128]{2,1,0:T(8,128)(2,1)S(1)}, u32[]{:S(2)}, u32[]{:S(2)}) collective-permute-start(bf16[6,1024,128]{2,1,0:T(8,128)(2,1)S(1)} %shard_map.82), channel_id=1, source_target_pairs={{0,24},{8,0},{16,8},{24,16},{1,25},{9,1},{17,9},{25,17},{2,26},{10... | collective-permute-start | bytes 4718600 | tf_op jit(solution)/shard_map/ppermute | solution.py:30
  8.4 1.3 shard_map.81
  9.9 1.3 shard_map.76
  11.2 2.0 %collective-permute-start = (bf16[6,1024,128]{2,1,0:T(8,128)(2,1)S(1)}, bf16[6,1024,128]{2,1,0:T(8,128)(2,1)S(1)}, u32[]{:S(2)}, u32[]{:S(2)}) collective-permute-start(bf16[6,1024,128]{2,1,0:T(8,128)(2,1)S(1)} %shard_map.76), channel_id=1, source_target_pairs={{0,32},{32,64},{64,96},{96,0},{1,33},{33,65},{65,97},{97,1},{2,34}... | collective-permute-start | bytes 4718600 | tf_op jit(solution)/shard_map/ppermute | solution.py:30
  13.2 1.3 shard_map.77
  14.6 2.2 %collective-permute-start.1 = (bf16[6,1024,128]{2,1,0:T(8,128)(2,1)S(1)}, bf16[6,1024,128]{2,1,0:T(8,128)(2,1)S(1)}, u32[]{:S(2)}, u32[]{:S(2)}) collective-permute-start(bf16[6,1024,128]{2,1,0:T(8,128)(2,1)S(1)} %shard_map.77), channel_id=1, source_target_pairs={{0,96},{32,0},{64,32},{96,64},{1,97},{33,1},{65,33},{97,65},{2,98}... | collective-permute-start | bytes 4718600 | tf_op jit(solution)/shard_map/ppermute | solution.py:30
  16.8 25.2 %collective-permute-done.9.ahead = bf16[6,1024,128]{2,1,0:T(8,128)(2,1)S(1)} collective-permute-done((bf16[6,1024,128]{2,1,0:T(8,128)(2,1)S(1)}, bf16[6,1024,128]{2,1,0:T(8,128)(2,1)S(1)}, u32[]{:S(2)}, u32[]{:S(2)}) %collective-permute-start.9) | collective-permute-done | bytes 1572896 | tf_op jit(solution)/shard_map/ppermute | solution.py:30
  42.1 3.8 %collective-permute-start.11 = (bf16[2,1024,128]{2,1,0:T(8,128)(2,1)S(1)}, bf16[2,1024,128]{2,1,0:T(8,128)(2,1)S(1)}, u32[]{:S(2)}, u32[]{:S(2)}) collective-permute-start(bf16[2,1024,128]{2,1,0:T(8,128)(2,1)S(1)} %slice.35), channel_id=1, source_target_pairs={{0,24},{8,0},{16,8},{24,16},{1,25},{9,1},{17,9},{25,17},{2,26},{10... | collective-permute-start | bytes 1572872 | tf_op jit(solution)/shard_map/ppermute | solution.py:30
  45.8 1.0 collective-permute-done.8.behind
  47.0 2.5 %collective-permute-done.behind = bf16[6,1024,128]{2,1,0:T(8,128)(2,1)S(1)} collective-permute-done((bf16[6,1024,128]{2,1,0:T(8,128)(2,1)S(1)}, bf16[6,1024,128]{2,1,0:T(8,128)(2,1)S(1)}, u32[]{:S(2)}, u32[]{:S(2)}) %collective-permute-start) | collective-permute-done | bytes 1572896 | tf_op jit(solution)/shard_map/ppermute | solution.py:30
  49.6 0.8 collective-permute-done.1.ahead
  50.5 3.5 %collective-permute-start.3 = (bf16[2,1024,128]{2,1,0:T(8,128)(2,1)S(1)}, bf16[2,1024,128]{2,1,0:T(8,128)(2,1)S(1)}, u32[]{:S(2)}, u32[]{:S(2)}) collective-permute-start(bf16[2,1024,128]{2,1,0:T(8,128)(2,1)S(1)} %slice.33), channel_id=1, source_target_pairs={{0,96},{32,0},{64,32},{96,64},{1,97},{33,1},{65,33},{97,65},{2,98}... | collective-permute-start | bytes 1572872 | tf_op jit(solution)/shard_map/ppermute | solution.py:30
  54.7 1.5 collective-permute-done.11
  56.1 4.5 %collective-permute-done.10 = bf16[2,1024,128]{2,1,0:T(8,128)(2,1)S(1)} collective-permute-done((bf16[2,1024,128]{2,1,0:T(8,128)(2,1)S(1)}, bf16[2,1024,128]{2,1,0:T(8,128)(2,1)S(1)}, u32[]{:S(2)}, u32[]{:S(2)}) %collective-permute-start.10) | collective-permute-done | bytes 524320 | tf_op jit(solution)/shard_map/ppermute | solution.py:30
  60.7 1.2 shard_map.84
  61.9 2.0 %collective-permute-start.12 = (f32[512,128]{1,0:T(8,128)S(1)}, f32[512,128]{1,0:T(8,128)S(1)}, u32[]{:S(2)}, u32[]{:S(2)}) collective-permute-start(f32[512,128]{1,0:T(8,128)S(1)} %get-tuple-element.39), channel_id=1, source_target_pairs={{0,32},{32,64},{64,96},{96,0},{1,33},{33,65},{65,97},{97,1},{2,34}... | collective-permute-start | bytes 786440 | tf_op jit(solution)/shard_map/ppermute | solution.py:30
  63.9 2.2 %collective-permute-start.13 = (f32[512,128]{1,0:T(8,128)S(1)}, f32[512,128]{1,0:T(8,128)S(1)}, u32[]{:S(2)}, u32[]{:S(2)}) collective-permute-start(f32[512,128]{1,0:T(8,128)S(1)} %get-tuple-element.41), channel_id=1, source_target_pairs={{0,96},{32,0},{64,32},{96,64},{1,97},{33,1},{65,33},{97,65},{2,98}... | collective-permute-start | bytes 786440 | tf_op jit(solution)/shard_map/ppermute | solution.py:30
  66.1 1.2 shard_map.79
  67.4 3.3 %collective-permute-start.5 = (f32[512,128]{1,0:T(8,128)S(1)}, f32[512,128]{1,0:T(8,128)S(1)}, u32[]{:S(2)}, u32[]{:S(2)}) collective-permute-start(f32[512,128]{1,0:T(8,128)S(1)} %get-tuple-element.33), channel_id=1, source_target_pairs={{0,24},{8,0},{16,8},{24,16},{1,25},{9,1},{17,9},{25,17},{2,26},{10... | collective-permute-start | bytes 786440 | tf_op jit(solution)/shard_map/ppermute | solution.py:30
  70.7 1.4 shard_map.83
  72.1 1.4 shard_map.78
  73.8 3.8 %collective-permute-start.15 = (f32[1024,128]{1,0:T(8,128)S(1)}, f32[1024,128]{1,0:T(8,128)S(1)}, u32[]{:S(2)}, u32[]{:S(2)}) collective-permute-start(f32[1024,128]{1,0:T(8,128)S(1)} %get-tuple-element.43), channel_id=1, source_target_pairs={{0,96},{32,0},{64,32},{96,64},{1,97},{33,1},{65,33},{97,65},{2,98}... | collective-permute-start | bytes 1572872 | tf_op jit(solution)/shard_map/ppermute | solution.py:30
  77.7 3.2 %collective-permute-start.7 = (f32[1024,128]{1,0:T(8,128)S(1)}, f32[1024,128]{1,0:T(8,128)S(1)}, u32[]{:S(2)}, u32[]{:S(2)}) collective-permute-start(f32[1024,128]{1,0:T(8,128)S(1)} %get-tuple-element.35), channel_id=1, source_target_pairs={{0,24},{8,0},{16,8},{24,16},{1,25},{9,1},{17,9},{25,17},{2,26},{10... | collective-permute-start | bytes 1572872 | tf_op jit(solution)/shard_map/ppermute | solution.py:30
  80.9 4.7 %collective-permute-done.14.refs_4_ = f32[1024,128]{1,0:T(8,128)S(1)} collective-permute-done((f32[1024,128]{1,0:T(8,128)S(1)}, f32[1024,128]{1,0:T(8,128)S(1)}, u32[]{:S(2)}, u32[]{:S(2)}) %collective-permute-start.14) | collective-permute-done | bytes 524320 | tf_op jit(solution)/shard_map/ppermute | solution.py:30
  85.6 2.8 %collective-permute-done.6.refs_1_ = f32[1024,128]{1,0:T(8,128)S(1)} collective-permute-done((f32[1024,128]{1,0:T(8,128)S(1)}, f32[1024,128]{1,0:T(8,128)S(1)}, u32[]{:S(2)}, u32[]{:S(2)}) %collective-permute-start.6) | collective-permute-done | bytes 524320 | tf_op jit(solution)/shard_map/ppermute | solution.py:30
  88.9 18.4 %all_to_all.11 = f32[128,1,128]{2,1,0:T(1,128)S(1)} all-to-all(f32[128,1,128]{2,1,0:T(1,128)S(1)} %bitcast.82), channel_id=1, replica_groups=mesh['z'=4,'x'=4,'y'=4,'core'=2] {'z','x','y','core'}, dimensions={0} | all-to-all | bytes 131072 | tf_op jit(solution)/shard_map/all_to_all | solution.py:345
  107.3 1.7 %shard_map.87 = (bf16[1024,128]{1,0:T(8,128)(2,1)S(1)}, bf16[1024,128]{1,0:T(8,128)(2,1)S(1)}) custom-call(f32[128,128]{1,0:T(8,128)S(1)} %bitcast.80, f32[1024,128]{1,0:T(8,128)S(1)} %get-tuple-element.45.refs_0_.mean_a, f32[2048,128]{1,0:T(8,128)S(1)} %bitcast.63, f32[2048,128]{1,0:T(8,128)S(1)} %bitcast.66, f32[2048,128]{1,0:T(8,128)S(1)} %bitcast.69, ...), custom_call_target="tpu_custom_call" | custom-call | flops 5242880 | bytes 4718592 | tf_op jit(solution)/shard_map/pallas_call | solution.py:241
  109.0 0.9 collective-permute-start.23
  109.9 1.5 collective-permute-start.24
  111.4 1.6 collective-permute-start.25
  113.6 1.6 collective-permute-start.17
  115.2 8.6 %collective-permute-done.23.refs_1_ = bf16[1024,128]{1,0:T(8,128)(2,1)S(1)} collective-permute-done((bf16[1024,128]{1,0:T(8,128)(2,1)S(1)}, bf16[1024,128]{1,0:T(8,128)(2,1)S(1)}, u32[]{:S(2)}, u32[]{:S(2)}) %collective-permute-start.23) | collective-permute-done | bytes 262176 | tf_op jit(solution)/shard_map/ppermute | solution.py:30
  123.8 1.2 collective-permute-start.18
  125.7 0.9 collective-permute-start.26
  126.6 2.4 %collective-permute-start.28 = (bf16[4,1024,128]{2,1,0:T(8,128)(2,1)S(1)}, bf16[4,1024,128]{2,1,0:T(8,128)(2,1)S(1)}, u32[]{:S(2)}, u32[]{:S(2)}) collective-permute-start(bf16[4,1024,128]{2,1,0:T(8,128)(2,1)S(1)} %shard_map.89.refs_1_), channel_id=1, source_target_pairs={{0,24},{8,0},{16,8},{24,16},{1,25},{9,1},{17,9},{25,17},{2,26},{10... | collective-permute-start | bytes 3145736 | tf_op jit(solution)/shard_map/ppermute | solution.py:30
  129.1 3.9 %collective-permute-done.18.refs_3_ = bf16[1024,128]{1,0:T(8,128)(2,1)S(1)} collective-permute-done((bf16[1024,128]{1,0:T(8,128)(2,1)S(1)}, bf16[1024,128]{1,0:T(8,128)(2,1)S(1)}, u32[]{:S(2)}, u32[]{:S(2)}) %collective-permute-start.18) | collective-permute-done | bytes 262176 | tf_op jit(solution)/shard_map/ppermute | solution.py:30
  133.7 3.2 %collective-permute-start.21 = (bf16[4,1024,128]{2,1,0:T(8,128)(2,1)S(1)}, bf16[4,1024,128]{2,1,0:T(8,128)(2,1)S(1)}, u32[]{:S(2)}, u32[]{:S(2)}) collective-permute-start(bf16[4,1024,128]{2,1,0:T(8,128)(2,1)S(1)} %shard_map.88.refs_0_), channel_id=1, source_target_pairs={{0,96},{32,0},{64,32},{96,64},{1,97},{33,1},{65,33},{97,65},{2,98}... | collective-permute-start | bytes 3145736 | tf_op jit(solution)/shard_map/ppermute | solution.py:30
  136.9 13.5 %collective-permute-done.26.refs_2_ = bf16[4,1024,128]{2,1,0:T(8,128)(2,1)S(1)} collective-permute-done((bf16[4,1024,128]{2,1,0:T(8,128)(2,1)S(1)}, bf16[4,1024,128]{2,1,0:T(8,128)(2,1)S(1)}, u32[]{:S(2)}, u32[]{:S(2)}) %collective-permute-start.26) | collective-permute-done | bytes 1048608 | tf_op jit(solution)/shard_map/ppermute | solution.py:30
  150.6 1.8 %collective-permute-done.28.refs_3_ = bf16[4,1024,128]{2,1,0:T(8,128)(2,1)S(1)} collective-permute-done((bf16[4,1024,128]{2,1,0:T(8,128)(2,1)S(1)}, bf16[4,1024,128]{2,1,0:T(8,128)(2,1)S(1)}, u32[]{:S(2)}, u32[]{:S(2)}) %collective-permute-start.28) | collective-permute-done | bytes 1048608 | tf_op jit(solution)/shard_map/ppermute | solution.py:30
  152.4 2.8 %collective-permute-start.29 = (bf16[4,512,128]{2,1,0:T(8,128)(2,1)S(1)}, bf16[4,512,128]{2,1,0:T(8,128)(2,1)S(1)}, u32[]{:S(2)}, u32[]{:S(2)}) collective-permute-start(bf16[4,512,128]{2,1,0:T(8,128)(2,1)S(1)} %slice.39), channel_id=1, source_target_pairs={{0,24},{8,0},{16,8},{24,16},{1,25},{9,1},{17,9},{25,17},{2,26},{10... | collective-permute-start | bytes 1572872 | tf_op jit(solution)/shard_map/ppermute | solution.py:30
  156.0 2.7 %collective-permute-start.22 = (bf16[4,512,128]{2,1,0:T(8,128)(2,1)S(1)}, bf16[4,512,128]{2,1,0:T(8,128)(2,1)S(1)}, u32[]{:S(2)}, u32[]{:S(2)}) collective-permute-start(bf16[4,512,128]{2,1,0:T(8,128)(2,1)S(1)} %slice.37), channel_id=1, source_target_pairs={{0,96},{32,0},{64,32},{96,64},{1,97},{33,1},{65,33},{97,65},{2,98}... | collective-permute-start | bytes 1572872 | tf_op jit(solution)/shard_map/ppermute | solution.py:30
  158.7 3.3 %shard_map.93 = (f32[2,1024,128]{2,1,0:T(8,128)}, f32[2,1024,128]{2,1,0:T(8,128)}, f32[2,1024,128]{2,1,0:T(8,128)}) custom-call(f32[128,128]{1,0:T(8,128)S(1)} %bitcast.81, f32[1024,128]{1,0:T(8,128)S(1)} %get-tuple-element.45.refs_0_.mean_a, f32[1024,128]{1,0:T(8,128)S(1)} %get-tuple-element.46.refs_4_.mean_b, f32[2,1024,128]{2,1,0:T(8,128)S(1)} %bitcast.65, ...), custom_call_target="tpu_custom_call" | custom-call | flops 5242880 | bytes 7864320 | tf_op jit(solution)/shard_map/pallas_call | solution.py:265
  161.9 1.9 %shard_map.90.refs_4_ = bf16[4,4,2,1024,128]{4,3,2,1,0:T(8,128)(2,1)} custom-call(s32[2]{0:T(128)S(1)} %pad_add_fusion.where, bf16[4,1024,128]{2,1,0:T(8,128)(2,1)S(1)} %shard_map.88.refs_0_, bf16[4,1024,128]{2,1,0:T(8,128)(2,1)S(1)} %shard_map.89.refs_1_), custom_call_target="tpu_custom_call" | custom-call | bytes 4194304 | tf_op jit(solution)/shard_map/pallas_call | solution.py:292
  163.8 2.6 %shard_map.91.refs_4_ = bf16[4,4,2,1024,128]{4,3,2,1,0:T(8,128)(2,1)} custom-call(s32[2]{0:T(128)S(1)} %pad_add_fusion.where, bf16[4,1024,128]{2,1,0:T(8,128)(2,1)S(1)} %collective-permute-done.19.refs_0_, bf16[4,1024,128]{2,1,0:T(8,128)(2,1)S(1)} %collective-permute-done.21.refs_1_, ...), custom_call_target="tpu_custom_call", output_to_operand_aliasing={{}: (5, {})} | custom-call | bytes 8388608 | tf_op jit(solution)/shard_map/pallas_call | solution.py:292
  166.4 2.1 %collective-permute-done.20.refs_0_ = bf16[4,512,128]{2,1,0:T(8,128)(2,1)S(1)} collective-permute-done((bf16[4,512,128]{2,1,0:T(8,128)(2,1)S(1)}, bf16[4,512,128]{2,1,0:T(8,128)(2,1)S(1)}, u32[]{:S(2)}, u32[]{:S(2)}) %collective-permute-start.20) | collective-permute-done | bytes 524320 | tf_op jit(solution)/shard_map/ppermute | solution.py:30
  168.5 1.9 %shard_map.92 = bf16[4,4,2,1024,128]{4,3,2,1,0:T(8,128)(2,1)} custom-call(s32[2]{0:T(128)S(1)} %pad_add_fusion.where, bf16[4,512,128]{2,1,0:T(8,128)(2,1)S(1)} %collective-permute-done.20.refs_0_, bf16[4,512,128]{2,1,0:T(8,128)(2,1)S(1)} %collective-permute-done.22.refs_1_, ...), custom_call_target="tpu_custom_call", output_to_operand_aliasing={{}: (5, {})} | custom-call | bytes 4194304 | tf_op jit(solution)/shard_map/pallas_call | solution.py:292
  (55 shorter events, 5.0 us)
Async XLA Ops:
  0.7 3.4 %copy-start = (bf16[1,1,4,1048576]{3,2,1,0:T(4,128)(2,1)S(1)}, bf16[1,1,4,1048576]{3,2,1,0:T(4,128)(2,1)}, u32[]{:S(2)}) copy-start(bf16[1,1,4,1048576]{3,2,1,0:T(4,128)(2,1)} %param.4) | copy-start | bytes 25165828
  4.1 5.8 %slice-start = ((s8[8388608]{0:T(1024)(128)(4,1)}), s8[4194304]{0:T(1024)(128)(4,1)S(1)}, s32[]{:S(2)}) async-start(s8[8388608]{0:T(1024)(128)(4,1)} %bitcast.58), calls=%async_computation.1 | async-start | bytes 8388608
  5.4 4.4 %slice-start.1 = ((s8[8388608]{0:T(1024)(128)(4,1)}), s8[4194304]{0:T(1024)(128)(4,1)S(1)}, s32[]{:S(2)}) async-start(s8[8388608]{0:T(1024)(128)(4,1)} %bitcast.58), calls=%async_computation.2 | async-start | bytes 8388608
  5.5 36.6 %collective-permute-start.9 = (bf16[6,1024,128]{2,1,0:T(8,128)(2,1)S(1)}, bf16[6,1024,128]{2,1,0:T(8,128)(2,1)S(1)}, u32[]{:S(2)}, u32[]{:S(2)}) collective-permute-start(bf16[6,1024,128]{2,1,0:T(8,128)(2,1)S(1)} %shard_map.82), channel_id=1, source_target_pairs={{0,24},{8,0},{16,8},{24,16},{1,25},{9,1},{17,9},{25,17},{2,26},{10... | collective-permute-start | bytes 4718600 | tf_op jit(solution)/shard_map/ppermute | solution.py:30
  9.7 37.1 %collective-permute-start.8 = (bf16[6,1024,128]{2,1,0:T(8,128)(2,1)S(1)}, bf16[6,1024,128]{2,1,0:T(8,128)(2,1)S(1)}, u32[]{:S(2)}, u32[]{:S(2)}) collective-permute-start(bf16[6,1024,128]{2,1,0:T(8,128)(2,1)S(1)} %shard_map.81), channel_id=1, source_target_pairs={{0,8},{8,16},{16,24},{24,0},{1,9},{9,17},{17,25},{25,1},{2,10},{10... | collective-permute-start | bytes 4718600 | tf_op jit(solution)/shard_map/ppermute | solution.py:30
  11.2 38.2 %collective-permute-start = (bf16[6,1024,128]{2,1,0:T(8,128)(2,1)S(1)}, bf16[6,1024,128]{2,1,0:T(8,128)(2,1)S(1)}, u32[]{:S(2)}, u32[]{:S(2)}) collective-permute-start(bf16[6,1024,128]{2,1,0:T(8,128)(2,1)S(1)} %shard_map.76), channel_id=1, source_target_pairs={{0,32},{32,64},{64,96},{96,0},{1,33},{33,65},{65,97},{97,1},{2,34}... | collective-permute-start | bytes 4718600 | tf_op jit(solution)/shard_map/ppermute | solution.py:30
  14.6 35.8 %collective-permute-start.1 = (bf16[6,1024,128]{2,1,0:T(8,128)(2,1)S(1)}, bf16[6,1024,128]{2,1,0:T(8,128)(2,1)S(1)}, u32[]{:S(2)}, u32[]{:S(2)}) collective-permute-start(bf16[6,1024,128]{2,1,0:T(8,128)(2,1)S(1)} %shard_map.77), channel_id=1, source_target_pairs={{0,96},{32,0},{64,32},{96,64},{1,97},{33,1},{65,33},{97,65},{2,98}... | collective-permute-start | bytes 4718600 | tf_op jit(solution)/shard_map/ppermute | solution.py:30
  42.1 14.1 %collective-permute-start.11 = (bf16[2,1024,128]{2,1,0:T(8,128)(2,1)S(1)}, bf16[2,1024,128]{2,1,0:T(8,128)(2,1)S(1)}, u32[]{:S(2)}, u32[]{:S(2)}) collective-permute-start(bf16[2,1024,128]{2,1,0:T(8,128)(2,1)S(1)} %slice.35), channel_id=1, source_target_pairs={{0,24},{8,0},{16,8},{24,16},{1,25},{9,1},{17,9},{25,17},{2,26},{10... | collective-permute-start | bytes 1572872 | tf_op jit(solution)/shard_map/ppermute | solution.py:30
  46.9 13.8 %collective-permute-start.10 = (bf16[2,1024,128]{2,1,0:T(8,128)(2,1)S(1)}, bf16[2,1024,128]{2,1,0:T(8,128)(2,1)S(1)}, u32[]{:S(2)}, u32[]{:S(2)}) collective-permute-start(bf16[2,1024,128]{2,1,0:T(8,128)(2,1)S(1)} %slice.34), channel_id=1, source_target_pairs={{0,8},{8,16},{16,24},{24,0},{1,9},{9,17},{17,25},{25,1},{2,10},{10... | collective-permute-start | bytes 1572872 | tf_op jit(solution)/shard_map/ppermute | solution.py:30
  49.5 16.6 %collective-permute-start.2 = (bf16[2,1024,128]{2,1,0:T(8,128)(2,1)S(1)}, bf16[2,1024,128]{2,1,0:T(8,128)(2,1)S(1)}, u32[]{:S(2)}, u32[]{:S(2)}) collective-permute-start(bf16[2,1024,128]{2,1,0:T(8,128)(2,1)S(1)} %slice.32), channel_id=1, source_target_pairs={{0,32},{32,64},{64,96},{96,0},{1,33},{33,65},{65,97},{97,1},{2,34}... | collective-permute-start | bytes 1572872 | tf_op jit(solution)/shard_map/ppermute | solution.py:30
  50.5 15.6 %collective-permute-start.3 = (bf16[2,1024,128]{2,1,0:T(8,128)(2,1)S(1)}, bf16[2,1024,128]{2,1,0:T(8,128)(2,1)S(1)}, u32[]{:S(2)}, u32[]{:S(2)}) collective-permute-start(bf16[2,1024,128]{2,1,0:T(8,128)(2,1)S(1)} %slice.33), channel_id=1, source_target_pairs={{0,96},{32,0},{64,32},{96,64},{1,97},{33,1},{65,33},{97,65},{2,98}... | collective-permute-start | bytes 1572872 | tf_op jit(solution)/shard_map/ppermute | solution.py:30
  61.9 11.7 %collective-permute-start.12 = (f32[512,128]{1,0:T(8,128)S(1)}, f32[512,128]{1,0:T(8,128)S(1)}, u32[]{:S(2)}, u32[]{:S(2)}) collective-permute-start(f32[512,128]{1,0:T(8,128)S(1)} %get-tuple-element.39), channel_id=1, source_target_pairs={{0,32},{32,64},{64,96},{96,0},{1,33},{33,65},{65,97},{97,1},{2,34}... | collective-permute-start | bytes 786440 | tf_op jit(solution)/shard_map/ppermute | solution.py:30
  63.9 9.7 %collective-permute-start.13 = (f32[512,128]{1,0:T(8,128)S(1)}, f32[512,128]{1,0:T(8,128)S(1)}, u32[]{:S(2)}, u32[]{:S(2)}) collective-permute-start(f32[512,128]{1,0:T(8,128)S(1)} %get-tuple-element.41), channel_id=1, source_target_pairs={{0,96},{32,0},{64,32},{96,64},{1,97},{33,1},{65,33},{97,65},{2,98}... | collective-permute-start | bytes 786440 | tf_op jit(solution)/shard_map/ppermute | solution.py:30
  67.3 10.2 %collective-permute-start.4 = (f32[512,128]{1,0:T(8,128)S(1)}, f32[512,128]{1,0:T(8,128)S(1)}, u32[]{:S(2)}, u32[]{:S(2)}) collective-permute-start(f32[512,128]{1,0:T(8,128)S(1)} %get-tuple-element.31), channel_id=1, source_target_pairs={{0,8},{8,16},{16,24},{24,0},{1,9},{9,17},{17,25},{25,1},{2,10},{10... | collective-permute-start | bytes 786440 | tf_op jit(solution)/shard_map/ppermute | solution.py:30
  67.4 10.1 %collective-permute-start.5 = (f32[512,128]{1,0:T(8,128)S(1)}, f32[512,128]{1,0:T(8,128)S(1)}, u32[]{:S(2)}, u32[]{:S(2)}) collective-permute-start(f32[512,128]{1,0:T(8,128)S(1)} %get-tuple-element.33), channel_id=1, source_target_pairs={{0,24},{8,0},{16,8},{24,16},{1,25},{9,1},{17,9},{25,17},{2,26},{10... | collective-permute-start | bytes 786440 | tf_op jit(solution)/shard_map/ppermute | solution.py:30
  73.7 11.9 %collective-permute-start.14 = (f32[1024,128]{1,0:T(8,128)S(1)}, f32[1024,128]{1,0:T(8,128)S(1)}, u32[]{:S(2)}, u32[]{:S(2)}) collective-permute-start(f32[1024,128]{1,0:T(8,128)S(1)} %get-tuple-element.42), channel_id=1, source_target_pairs={{0,32},{32,64},{64,96},{96,0},{1,33},{33,65},{65,97},{97,1},{2,34}... | collective-permute-start | bytes 1572872 | tf_op jit(solution)/shard_map/ppermute | solution.py:30
  73.8 11.9 %collective-permute-start.15 = (f32[1024,128]{1,0:T(8,128)S(1)}, f32[1024,128]{1,0:T(8,128)S(1)}, u32[]{:S(2)}, u32[]{:S(2)}) collective-permute-start(f32[1024,128]{1,0:T(8,128)S(1)} %get-tuple-element.43), channel_id=1, source_target_pairs={{0,96},{32,0},{64,32},{96,64},{1,97},{33,1},{65,33},{97,65},{2,98}... | collective-permute-start | bytes 1572872 | tf_op jit(solution)/shard_map/ppermute | solution.py:30
  77.6 10.8 %collective-permute-start.6 = (f32[1024,128]{1,0:T(8,128)S(1)}, f32[1024,128]{1,0:T(8,128)S(1)}, u32[]{:S(2)}, u32[]{:S(2)}) collective-permute-start(f32[1024,128]{1,0:T(8,128)S(1)} %get-tuple-element.34), channel_id=1, source_target_pairs={{0,8},{8,16},{16,24},{24,0},{1,9},{9,17},{17,25},{25,1},{2,10},{10... | collective-permute-start | bytes 1572872 | tf_op jit(solution)/shard_map/ppermute | solution.py:30
  77.7 10.8 %collective-permute-start.7 = (f32[1024,128]{1,0:T(8,128)S(1)}, f32[1024,128]{1,0:T(8,128)S(1)}, u32[]{:S(2)}, u32[]{:S(2)}) collective-permute-start(f32[1024,128]{1,0:T(8,128)S(1)} %get-tuple-element.35), channel_id=1, source_target_pairs={{0,24},{8,0},{16,8},{24,16},{1,25},{9,1},{17,9},{25,17},{2,26},{10... | collective-permute-start | bytes 1572872 | tf_op jit(solution)/shard_map/ppermute | solution.py:30
  88.5 18.8 %copy-start.1 = (f32[1,4,65536]{2,1,0:T(4,128)S(1)}, f32[1,4,65536]{2,1,0:T(4,128)}, u32[]{:S(2)}) copy-start(f32[1,4,65536]{2,1,0:T(4,128)} %param.5) | copy-start | bytes 3145732
  88.5 18.8 %copy-start.2 = (f32[1,4,65536]{2,1,0:T(4,128)S(1)}, f32[1,4,65536]{2,1,0:T(4,128)}, u32[]{:S(2)}) copy-start(f32[1,4,65536]{2,1,0:T(4,128)} %param.6) | copy-start | bytes 3145732
  88.5 18.8 %copy-start.3 = (f32[1,4,65536]{2,1,0:T(4,128)S(1)}, f32[1,4,65536]{2,1,0:T(4,128)}, u32[]{:S(2)}) copy-start(f32[1,4,65536]{2,1,0:T(4,128)} %param.7) | copy-start | bytes 3145732
  109.0 14.8 %collective-permute-start.23 = (bf16[1024,128]{1,0:T(8,128)(2,1)S(1)}, bf16[1024,128]{1,0:T(8,128)(2,1)S(1)}, u32[]{:S(2)}, u32[]{:S(2)}) collective-permute-start(bf16[1024,128]{1,0:T(8,128)(2,1)S(1)} %get-tuple-element.48.refs_0_), channel_id=1, source_target_pairs={{0,32},{32,64},{64,96},{96,0},{1,33},{33,65},{65,97},{97,1},{2,34}... | collective-permute-start | bytes 786440 | tf_op jit(solution)/shard_map/ppermute | solution.py:30
  109.9 15.2 %collective-permute-start.24 = (bf16[1024,128]{1,0:T(8,128)(2,1)S(1)}, bf16[1024,128]{1,0:T(8,128)(2,1)S(1)}, u32[]{:S(2)}, u32[]{:S(2)}) collective-permute-start(bf16[1024,128]{1,0:T(8,128)(2,1)S(1)} %get-tuple-element.48.refs_0_), channel_id=1, source_target_pairs={{0,64},{32,96},{64,0},{96,32},{1,65},{33,97},{65,1},{97,33},{2,66}... | collective-permute-start | bytes 786440 | tf_op jit(solution)/shard_map/ppermute | solution.py:30
  111.4 13.6 %collective-permute-start.25 = (bf16[1024,128]{1,0:T(8,128)(2,1)S(1)}, bf16[1024,128]{1,0:T(8,128)(2,1)S(1)}, u32[]{:S(2)}, u32[]{:S(2)}) collective-permute-start(bf16[1024,128]{1,0:T(8,128)(2,1)S(1)} %get-tuple-element.48.refs_0_), channel_id=1, source_target_pairs={{0,96},{32,0},{64,32},{96,64},{1,97},{33,1},{65,33},{97,65},{2,98}... | collective-permute-start | bytes 786440 | tf_op jit(solution)/shard_map/ppermute | solution.py:30
  113.0 16.0 %collective-permute-start.16 = (bf16[1024,128]{1,0:T(8,128)(2,1)S(1)}, bf16[1024,128]{1,0:T(8,128)(2,1)S(1)}, u32[]{:S(2)}, u32[]{:S(2)}) collective-permute-start(bf16[1024,128]{1,0:T(8,128)(2,1)S(1)} %get-tuple-element.47.refs_0_), channel_id=1, source_target_pairs={{0,8},{8,16},{16,24},{24,0},{1,9},{9,17},{17,25},{25,1},{2,10},{10... | collective-permute-start | bytes 786440 | tf_op jit(solution)/shard_map/ppermute | solution.py:30
  113.6 15.4 %collective-permute-start.17 = (bf16[1024,128]{1,0:T(8,128)(2,1)S(1)}, bf16[1024,128]{1,0:T(8,128)(2,1)S(1)}, u32[]{:S(2)}, u32[]{:S(2)}) collective-permute-start(bf16[1024,128]{1,0:T(8,128)(2,1)S(1)} %get-tuple-element.47.refs_0_), channel_id=1, source_target_pairs={{0,16},{8,24},{16,0},{24,8},{1,17},{9,25},{17,1},{25,9},{2,18},{10... | collective-permute-start | bytes 786440 | tf_op jit(solution)/shard_map/ppermute | solution.py:30
  123.8 9.1 %collective-permute-start.18 = (bf16[1024,128]{1,0:T(8,128)(2,1)S(1)}, bf16[1024,128]{1,0:T(8,128)(2,1)S(1)}, u32[]{:S(2)}, u32[]{:S(2)}) collective-permute-start(bf16[1024,128]{1,0:T(8,128)(2,1)S(1)} %get-tuple-element.47.refs_0_), channel_id=1, source_target_pairs={{0,24},{8,0},{16,8},{24,16},{1,25},{9,1},{17,9},{25,17},{2,26},{10... | collective-permute-start | bytes 786440 | tf_op jit(solution)/shard_map/ppermute | solution.py:30
  125.7 24.7 %collective-permute-start.26 = (bf16[4,1024,128]{2,1,0:T(8,128)(2,1)S(1)}, bf16[4,1024,128]{2,1,0:T(8,128)(2,1)S(1)}, u32[]{:S(2)}, u32[]{:S(2)}) collective-permute-start(bf16[4,1024,128]{2,1,0:T(8,128)(2,1)S(1)} %shard_map.89.refs_1_), channel_id=1, source_target_pairs={{0,8},{8,16},{16,24},{24,0},{1,9},{9,17},{17,25},{25,1},{2,10},{10... | collective-permute-start | bytes 3145736 | tf_op jit(solution)/shard_map/ppermute | solution.py:30
  126.6 25.7 %collective-permute-start.28 = (bf16[4,1024,128]{2,1,0:T(8,128)(2,1)S(1)}, bf16[4,1024,128]{2,1,0:T(8,128)(2,1)S(1)}, u32[]{:S(2)}, u32[]{:S(2)}) collective-permute-start(bf16[4,1024,128]{2,1,0:T(8,128)(2,1)S(1)} %shard_map.89.refs_1_), channel_id=1, source_target_pairs={{0,24},{8,0},{16,8},{24,16},{1,25},{9,1},{17,9},{25,17},{2,26},{10... | collective-permute-start | bytes 3145736 | tf_op jit(solution)/shard_map/ppermute | solution.py:30
  133.6 21.6 %collective-permute-start.19 = (bf16[4,1024,128]{2,1,0:T(8,128)(2,1)S(1)}, bf16[4,1024,128]{2,1,0:T(8,128)(2,1)S(1)}, u32[]{:S(2)}, u32[]{:S(2)}) collective-permute-start(bf16[4,1024,128]{2,1,0:T(8,128)(2,1)S(1)} %shard_map.88.refs_0_), channel_id=1, source_target_pairs={{0,32},{32,64},{64,96},{96,0},{1,33},{33,65},{65,97},{97,1},{2,34}... | collective-permute-start | bytes 3145736 | tf_op jit(solution)/shard_map/ppermute | solution.py:30
  133.7 22.2 %collective-permute-start.21 = (bf16[4,1024,128]{2,1,0:T(8,128)(2,1)S(1)}, bf16[4,1024,128]{2,1,0:T(8,128)(2,1)S(1)}, u32[]{:S(2)}, u32[]{:S(2)}) collective-permute-start(bf16[4,1024,128]{2,1,0:T(8,128)(2,1)S(1)} %shard_map.88.refs_0_), channel_id=1, source_target_pairs={{0,96},{32,0},{64,32},{96,64},{1,97},{33,1},{65,33},{97,65},{2,98}... | collective-permute-start | bytes 3145736 | tf_op jit(solution)/shard_map/ppermute | solution.py:30
  150.5 15.9 %collective-permute-start.27 = (bf16[4,512,128]{2,1,0:T(8,128)(2,1)S(1)}, bf16[4,512,128]{2,1,0:T(8,128)(2,1)S(1)}, u32[]{:S(2)}, u32[]{:S(2)}) collective-permute-start(bf16[4,512,128]{2,1,0:T(8,128)(2,1)S(1)} %slice.38), channel_id=1, source_target_pairs={{0,8},{8,16},{16,24},{24,0},{1,9},{9,17},{17,25},{25,1},{2,10},{10... | collective-permute-start | bytes 1572872 | tf_op jit(solution)/shard_map/ppermute | solution.py:30
  152.4 14.1 %collective-permute-start.29 = (bf16[4,512,128]{2,1,0:T(8,128)(2,1)S(1)}, bf16[4,512,128]{2,1,0:T(8,128)(2,1)S(1)}, u32[]{:S(2)}, u32[]{:S(2)}) collective-permute-start(bf16[4,512,128]{2,1,0:T(8,128)(2,1)S(1)} %slice.39), channel_id=1, source_target_pairs={{0,24},{8,0},{16,8},{24,16},{1,25},{9,1},{17,9},{25,17},{2,26},{10... | collective-permute-start | bytes 1572872 | tf_op jit(solution)/shard_map/ppermute | solution.py:30
  155.3 13.2 %collective-permute-start.20 = (bf16[4,512,128]{2,1,0:T(8,128)(2,1)S(1)}, bf16[4,512,128]{2,1,0:T(8,128)(2,1)S(1)}, u32[]{:S(2)}, u32[]{:S(2)}) collective-permute-start(bf16[4,512,128]{2,1,0:T(8,128)(2,1)S(1)} %slice.36), channel_id=1, source_target_pairs={{0,32},{32,64},{64,96},{96,0},{1,33},{33,65},{65,97},{97,1},{2,34}... | collective-permute-start | bytes 1572872 | tf_op jit(solution)/shard_map/ppermute | solution.py:30
  156.0 12.5 %collective-permute-start.22 = (bf16[4,512,128]{2,1,0:T(8,128)(2,1)S(1)}, bf16[4,512,128]{2,1,0:T(8,128)(2,1)S(1)}, u32[]{:S(2)}, u32[]{:S(2)}) collective-permute-start(bf16[4,512,128]{2,1,0:T(8,128)(2,1)S(1)} %slice.37), channel_id=1, source_target_pairs={{0,96},{32,0},{64,32},{96,64},{1,97},{33,1},{65,33},{97,65},{2,98}... | collective-permute-start | bytes 1572872 | tf_op jit(solution)/shard_map/ppermute | solution.py:30

commit v3 on v2

--- a/solution.py
+++ b/solution.py
@@ -34,42 +34,44 @@
     return pl.CostEstimate(flops=flops, bytes_accessed=moved, transcendentals=0)
 
 
-def pick_kernel(along_z, by, where, pieces, out, sems):
-    quarter = out.shape[1] // 2
-    low = 0 if along_z else 2 * quarter
-    far_low = low if by == 1 else low + quarter
-    near, far = lax.rem(where[0] + by, 4), lax.rem(where[0] + 2, 4)
-
-    def source(at, start, count):
-        rows = pl.ds(start, count)
-        return pieces.at[at, :, rows] if along_z else pieces.at[:, at, rows]
-
-    copies = [pltpu.make_async_copy(source(near, low, 2 * quarter), out.at[pl.ds(0, 4)], sems.at[0])]
-    for j in range(4):
-        rows = pl.ds(far_low, quarter)
-        piece = pieces.at[far, j, rows] if along_z else pieces.at[j, far, rows]
-        copies.append(pltpu.make_async_copy(piece, out.at[4 + j // 2, pl.ds(j % 2 * quarter, quarter)], sems.at[1 + j]))
+def pick_kernel(along_z, where, pieces, *refs):
+    outs, sems = refs[:2], refs[2]
+    quarter = outs[0].shape[1] // 2
+    copies = []
+    for k, (out, by) in enumerate(zip(outs, (1, 3))):
+        me = where[0] if along_z else where[1]
+        low = 0 if along_z else 2 * quarter
+        far_low = low if by == 1 else low + quarter
+        near, far = lax.rem(me + by, 4), lax.rem(me + 2, 4)
+        rows = pl.ds(low, 2 * quarter)
+        piece = pieces.at[near, :, rows] if along_z else pieces.at[:, near, rows]
+        copies.append(pltpu.make_async_copy(piece, out.at[pl.ds(0, 4)], sems.at[k, 0]))
+        for j in range(4):
+            rows = pl.ds(far_low, quarter)
+            piece = pieces.at[far, j, rows] if along_z else pieces.at[j, far, rows]
+            target = out.at[4 + j // 2, pl.ds(j % 2 * quarter, quarter)]
+            copies.append(pltpu.make_async_copy(piece, target, sems.at[k, 1 + j]))
     for copy in copies:
         copy.start()
     for copy in copies:
         copy.wait()
 
 
-def pick(pieces, where, along_z, by):
+def pick(pieces, zx, along_z):
     half = pieces.shape[2] // 2
     return pl.pallas_call(
-        functools.partial(pick_kernel, along_z, by),
+        functools.partial(pick_kernel, along_z),
         grid_spec=pltpu.PrefetchScalarGridSpec(
             num_scalar_prefetch=1,
             grid=(),
             in_specs=[pl.BlockSpec(memory_space=pl.ANY)],
-            out_specs=pl.BlockSpec(memory_space=pl.ANY),
-            scratch_shapes=[pltpu.SemaphoreType.DMA((5,))],
+            out_specs=[pl.BlockSpec(memory_space=pl.ANY)] * 2,
+            scratch_shapes=[pltpu.SemaphoreType.DMA((2, 5))],
         ),
-        out_shape=jax.ShapeDtypeStruct((6, half, LANES), bf16),
-        compiler_params=pltpu.CompilerParams(vmem_limit_bytes=VMEM_LIMIT),
-        cost_estimate=cost(0, 24 * half * LANES),
-    )(where, pieces)
+        out_shape=[jax.ShapeDtypeStruct((6, half, LANES), bf16)] * 2,
+        compiler_params=pltpu.CompilerParams(vmem_limit_bytes=VMEM_LIMIT),
+        cost_estimate=cost(0, 48 * half * LANES),
+    )(zx, pltpu.with_memory_space_constraint(pieces, pltpu.HBM))
 
 
 def own_kernel(where, pieces, out_a, out_b, sems):
@@ -98,7 +100,7 @@
         out_shape=[jax.ShapeDtypeStruct((4, half, LANES), bf16)] * 2,
         compiler_params=pltpu.CompilerParams(vmem_limit_bytes=VMEM_LIMIT),
         cost_estimate=cost(0, 32 * half * LANES),
-    )(zx, pieces)
+    )(zx, pltpu.with_memory_space_constraint(pieces, pltpu.HBM))
 
 
 def total_of(refs, at, far):
@@ -225,28 +227,32 @@
     return jnp.minimum(1.0, clip_limit / (jnp.sqrt(total) + norm_eps))
 
 
-def params_kernel(squares, *refs):
+def params_kernel(squares, mean_a, mean_b, master, first, second, *outs):
     clip_factor = clip_of(squares)
-    for ins, out in ((refs[0:4], refs[8]), (refs[4:8], refs[9])):
-        new_master, _, _ = adam_update(*(r[...] for r in ins), clip_factor)
+    for at, out in enumerate(outs):
+        mean = (mean_a, mean_b)[at // 2]
+        new_master, _, _ = adam_update(mean[at % 2], master[at], first[at], second[at], clip_factor)
         out[...] = new_master.astype(bf16)
 
 
 def new_params(squares, means, states):
-    half = means[0].shape[0]
-    steps = half // BLOCK
+    quarter = means[0].shape[0] // 2
     whole = pl.BlockSpec(squares.shape, lambda i: (0, 0))
-    low = pl.BlockSpec((BLOCK, LANES), lambda i: (i, 0))
-    high = pl.BlockSpec((BLOCK, LANES), lambda i: (steps + i, 0))
+    two = pl.BlockSpec((2, BLOCK, LANES), lambda i: (0, i, 0))
+    four = pl.BlockSpec((4, BLOCK, LANES), lambda i: (0, i, 0))
     return pl.pallas_call(
         params_kernel,
-        grid=(steps,),
-        in_specs=[whole, low, low, low, low, low, high, high, high],
-        out_specs=[low, low],
-        out_shape=[jax.ShapeDtypeStruct((half, LANES), bf16)] * 2,
-        compiler_params=pltpu.CompilerParams(vmem_limit_bytes=VMEM_LIMIT),
-        cost_estimate=cost(40 * half * LANES, 36 * half * LANES),
-    )(squares, means[0], *states, means[1], *states)
+        grid=(quarter // BLOCK,),
+        in_specs=[whole, two, two, four, four, four],
+        out_specs=[pl.BlockSpec((BLOCK, LANES), lambda i: (i, 0))] * 4,
+        out_shape=[jax.ShapeDtypeStruct((quarter, LANES), bf16)] * 4,
+        compiler_params=pltpu.CompilerParams(vmem_limit_bytes=VMEM_LIMIT),
+        cost_estimate=cost(160 * quarter * LANES, 72 * quarter * LANES),
+    )(
+        squares,
+        *(m.reshape(2, quarter, LANES) for m in means),
+        *(s.reshape(4, quarter, LANES) for s in states),
+    )
 
 
 def states_both_kernel(squares, mean_a, mean_b, master, first, second, *outs):
@@ -273,36 +279,88 @@
     )(squares, *means, *(s.reshape(2, half, LANES) for s in states))
 
 
-def place_kernel(moves, n_parts, where, *refs):
+DIMS = {"zA": (Z, 1), "zB": (Z, 3), "xA": (X, 1), "xB": (X, 3)}
+ORDERS = (("zA", "xA", "zB", "xB"), ("xA", "zB", "xB", "zA"), ("zB", "xB", "zA", "xA"), ("xB", "zA", "xA", "zB"))
+
+
+def partner(value, dim):
+    axis, mask = DIMS[dim]
+    return lax.ppermute(value, axis, [(i, i ^ mask) for i in range(4)])
+
+
+def join_kernel(one, two, out, sems):
+    size = one.shape[0]
+    copies = [
+        pltpu.make_async_copy(one, out.at[pl.ds(0, size)], sems.at[0]),
+        pltpu.make_async_copy(two, out.at[pl.ds(size, size)], sems.at[1]),
+    ]
+    for copy in copies:
+        copy.start()
+    for copy in copies:
+        copy.wait()
+
+
+def join(one, two):
+    any_ = pl.BlockSpec(memory_space=pl.ANY)
+    return pl.pallas_call(
+        join_kernel,
+        in_specs=[any_, any_],
+        out_specs=any_,
+        scratch_shapes=[pltpu.SemaphoreType.DMA((2,))],
+        out_shape=jax.ShapeDtypeStruct((2 * one.shape[0],) + one.shape[1:], one.dtype),
+        compiler_params=pltpu.CompilerParams(vmem_limit_bytes=VMEM_LIMIT),
+        cost_estimate=cost(0, 4 * one.size),
+    )(one, two)
+
+
+def masks_of(order):
+    found = [(0, 0)]
+    for dim in order:
+        axis, mask = DIMS[dim]
+        found += [(mz ^ mask, mx) if axis == Z else (mz, mx ^ mask) for mz, mx in found]
+    return found
+
+
+def set_kernel(jobs, n_parts, *refs):
     parts, out, sems = refs[:n_parts], refs[-2], refs[-1]
+    z, x = lax.axis_index(Z), lax.axis_index(X)
     copies = []
-    for k, (source, target) in enumerate(moves):
-        src = source(parts)
-        dst = target(out, where)
-        copies.append(pltpu.make_async_copy(src, dst, sems.at[k]))
+    for k, (part, entry, chain, mz, mx) in enumerate(jobs):
+        target = out.at[lax.bitwise_xor(z, mz), lax.bitwise_xor(x, mx), chain]
+        copies.append(pltpu.make_async_copy(parts[part].at[entry], target, sems.at[k]))
     for copy in copies:
         copy.start()
     for copy in copies:
         copy.wait()
 
 
-def place(out, where, parts, moves, shape):
+def set_blocks(out, parts, jobs, shape):
     extra = [] if out is None else [out]
     any_ = pl.BlockSpec(memory_space=pl.ANY)
     return pl.pallas_call(
-        functools.partial(place_kernel, moves, len(parts)),
-        grid_spec=pltpu.PrefetchScalarGridSpec(
-            num_scalar_prefetch=1,
-            grid=(),
-            in_specs=[any_] * (len(parts) + len(extra)),
-            out_specs=any_,
-            scratch_shapes=[pltpu.SemaphoreType.DMA((len(moves),))],
-        ),
+        functools.partial(set_kernel, jobs, len(parts)),
+        in_specs=[any_] * (len(parts) + len(extra)),
+        out_specs=any_,
+        scratch_shapes=[pltpu.SemaphoreType.DMA((len(jobs),))],
         out_shape=jax.ShapeDtypeStruct(shape, bf16),
-        input_output_aliases={} if out is None else {len(parts) + 1: 0},
-        compiler_params=pltpu.CompilerParams(vmem_limit_bytes=VMEM_LIMIT),
-        cost_estimate=cost(0, 2 * sum(p.size for p in parts) * 2),
-    )(where, *parts, *extra)
+        input_output_aliases={} if out is None else {len(parts): 0},
+        compiler_params=pltpu.CompilerParams(vmem_limit_bytes=VMEM_LIMIT),
+        cost_estimate=cost(0, 4 * sum(p.size for p in parts)),
+    )(*parts, *extra)
+
+
+def gather_blocks(blocks):
+    held = [b[None] for b in blocks]
+    for step in range(3):
+        sent = [partner(h, order[step]) for h, order in zip(held, ORDERS)]
+        held = [join(h, s) for h, s in zip(held, sent)]
+    sent = [partner(h, order[3]) for h, order in zip(held, ORDERS)]
+    shape = (4, 4, 4) + blocks[0].shape
+    masks = [masks_of(order) for order in ORDERS]
+    out = set_blocks(None, held, [(c, e, c) + masks[c][e] for c in range(4) for e in range(8)], shape)
+    for c in range(4):
+        out = set_blocks(out, [sent[c]], [(0, e, c) + masks[c][8 + e] for e in range(8)], shape)
+    return out
 
 
 def shards(local_grads, master_weights, first_moment, second_moment):
@@ -323,7 +381,7 @@
     xz = jnp.stack([x, z]).astype(jnp.int32)
 
     own_a, own_b = own_pieces(pieces, zx)
-    sends = [pick(pieces, zx, True, 1), pick(pieces, zx, True, 3), pick(pieces, xz, False, 1), pick(pieces, xz, False, 3)]
+    sends = pick(pieces, zx, True) + pick(pieces, zx, False)
     axes = (Z, Z, X, X)
     ways = (1, 3, 1, 3)
     got = [shift(v, axis, by) for v, axis, by in zip(sends, axes, ways)]
@@ -344,51 +402,10 @@
     mean_a, mean_b, squares = last_sum(parts_a, parts_b, devices)
     squares = lax.all_to_all(squares, (Z, X, Y, CORE), 0, 0, tiled=True)
 
-    par_a, par_b = new_params(squares, (mean_a, mean_b), states)
+    blocks = new_params(squares, (mean_a, mean_b), states)
     outs = both_states(squares, (mean_a, mean_b), states)
     outs = [from_rows(o.reshape(rows, LANES)) for o in outs]
-
-    def turn(i, by):
-        return lax.rem(i + by, 4)
-
-    row_a = [par_a] + [shift(par_a, X, s) for s in (1, 2, 3)]
-    row_b = [par_b] + [shift(par_b, Z, s) for s in (1, 2, 3)]
-    shape = (4, half, LANES)
-    moves = [(lambda p, s=s: p[s], lambda o, w, s=s: o.at[turn(w[1], 4 - s)]) for s in range(4)]
-    line_a = place(None, zx, row_a, moves, shape)
-    line_b = place(None, xz, row_b, moves, shape)
-    full = (4, 4, 2, half, LANES)
-
-    def to_a(by, lo=0, n=half):
-        return lambda o, w: o.at[turn(w[0], by), :, 0, pl.ds(lo, n)]
-
-    def to_b(by, lo=0, n=half):
-        return lambda o, w: o.at[:, turn(w[1], by), 1, pl.ds(lo, n)]
-
-    out = place(None, zx, [line_a, line_b], [(lambda p: p[0], to_a(0)), (lambda p: p[1], to_b(0))], full)
-    near = [shift(line_a, Z, 1), shift(line_a, Z, 3), shift(line_b, X, 1), shift(line_b, X, 3)]
-    q = half // 2
-    far = [
-        shift(near[0][:, :q], Z, 1),
-        shift(near[1][:, q:], Z, 3),
-        shift(near[2][:, :q], X, 1),
-        shift(near[3][:, q:], X, 3),
-    ]
-    out = place(
-        out, zx, near,
-        [(lambda p: p[0], to_a(3)), (lambda p: p[1], to_a(1)), (lambda p: p[2], to_b(3)), (lambda p: p[3], to_b(1))],
-        full,
-    )
-    out = place(
-        out, zx, far,
-        [
-            (lambda p: p[0], to_a(2, 0, q)),
-            (lambda p: p[1], to_a(2, q, q)),
-            (lambda p: p[2], to_b(2, 0, q)),
-            (lambda p: p[3], to_b(2, q, q)),
-        ],
-        full,
-    )
+    out = gather_blocks(blocks)
     return (from_rows(out.reshape(-1, LANES)), *outs)
 
 

time: 171 us -> 161 us (0.942)
  starting transfers between devices: 49.6 us -> 42.8 us
  local copies, waits for them, and re-layouts: 3.68 us -> 0.15 us
    ppermute x30 -> x16, waiting for transfers between devices: 73 us -> 42.4 us  [shift(): lax.ppermute(value, axis, [(i, (i + by) % size) for i in range(size)])]
    ppermute x0 -> x16, waiting for transfers between devices: none -> 29.3 us  [partner(): return lax.ppermute(value, axis, [(i, i ^ mask) for i in range(4)])]
    ppermute x30 -> x16, starting transfers between devices: 49.6 us -> 27.5 us  [shift(): lax.ppermute(value, axis, [(i, (i + by) % size) for i in range(size)])]
    ppermute x0 -> x16, starting transfers between devices: none -> 15.3 us  [partner(): return lax.ppermute(value, axis, [(i, i ^ mask) for i in range(4)])]
    unnamed x12 -> x6, local copies, waits for them, and re-layouts: 3.4 us -> 0.01 us
    pallas_call x10 -> x20, Pallas kernels: 14.8 us -> 15 us  [the longest x5 6.41 us: set_blocks(): pl.pallas_call(functools.partial(set_kernel, jobs, len(parts)), in_specs=...]
  transfers between devices with their start and end apart: 30 -> 32, of which waited for: 13 -> 12; matrix products, arithmetic and copies ran while one was open for 0% -> 0% of each run, Pallas kernels for 11% -> 13%
where the time goes in v3:
time: 161 us; the launch traced here: 160 us
  waiting for transfers between devices  71.7 us (45%)
  starting transfers between devices  42.8 us (27%)
  Pallas kernels  26.3 us (16%)
  blocking collectives  18.1 us (11%)
    ppermute x16, waiting for transfers between devices, shift(): lax.ppermute(value, axis, [(i, (i + by) % size) for i in range(size)])  42.4 us
    ppermute x16, waiting for transfers between devices, partner(): return lax.ppermute(value, axis, [(i, i ^ mask) for i in range(4)])  29.3 us
    ppermute x16, starting transfers between devices, shift(): lax.ppermute(value, axis, [(i, (i + by) % size) for i in range(size)])  27.5 us
    all_to_all x1, blocking collectives, shards(): squares = lax.all_to_all(squares, (Z, X, Y, CORE), 0, 0, tiled=True)  18.1 us
    ppermute x16, starting transfers between devices, partner(): return lax.ppermute(value, axis, [(i, i ^ mask) for i in range(4)])  15.3 us
    pallas_call x5, Pallas kernels, set_blocks(): pl.pallas_call(functools.partial(set_kernel, jobs, len(parts)), in_specs=...  6.41 us
    pallas_call x4, Pallas kernels, first_sum(): pl.pallas_call(far_sum_kernel if only_far else near_sum_kernel, grid_spec...  5.3 us
    pallas_call x2, Pallas kernels, pick(): pl.pallas_call(functools.partial(pick_kernel, along_z), grid_spec=pltpu.P...  4.88 us
  transfers between devices with their start and end apart: 32, of which 12 were waited for; matrix products, arithmetic and copies ran while one was open for 0% of the time, Pallas kernels for 13%

profile of v3, /device:TPU:0, one launch (start us, length us, event | category | flops | bytes accessed | tf_op | source)
XLA Modules:
  0.0 160.4 jit_solution(3902705807945208435)
XLA Ops:
  0.7 2.4 %shard_map.76 = (bf16[6,1024,128]{2,1,0:T(8,128)(2,1)S(1)}, bf16[6,1024,128]{2,1,0:T(8,128)(2,1)S(1)}) custom-call(s32[2]{0:T(128)S(1)} %pad_add_fusion.where, bf16[4,4,2048,128]{3,2,1,0:T(8,128)(2,1)} %bitcast.90), custom_call_target="tpu_custom_call" | custom-call | bytes 6291456 | tf_op jit(solution)/shard_map/pallas_call | solution.py:62
  3.2 2.1 %collective-permute-start = (bf16[6,1024,128]{2,1,0:T(8,128)(2,1)S(1)}, bf16[6,1024,128]{2,1,0:T(8,128)(2,1)S(1)}, u32[]{:S(2)}, u32[]{:S(2)}) collective-permute-start(bf16[6,1024,128]{2,1,0:T(8,128)(2,1)S(1)} %get-tuple-element.35), channel_id=1, source_target_pairs={{0,32},{32,64},{64,96},{96,0},{1,33},{33,65},{65,97},{97,1},{2,34}... | collective-permute-start | bytes 4718600 | tf_op jit(solution)/shard_map/ppermute | solution.py:30
  5.2 2.2 %collective-permute-start.1 = (bf16[6,1024,128]{2,1,0:T(8,128)(2,1)S(1)}, bf16[6,1024,128]{2,1,0:T(8,128)(2,1)S(1)}, u32[]{:S(2)}, u32[]{:S(2)}) collective-permute-start(bf16[6,1024,128]{2,1,0:T(8,128)(2,1)S(1)} %get-tuple-element.36), channel_id=1, source_target_pairs={{0,96},{32,0},{64,32},{96,64},{1,97},{33,1},{65,33},{97,65},{2,98}... | collective-permute-start | bytes 4718600 | tf_op jit(solution)/shard_map/ppermute | solution.py:30
  7.4 2.4 %shard_map.80 = (bf16[6,1024,128]{2,1,0:T(8,128)(2,1)S(1)}, bf16[6,1024,128]{2,1,0:T(8,128)(2,1)S(1)}) custom-call(s32[2]{0:T(128)S(1)} %pad_add_fusion.where, bf16[4,4,2048,128]{3,2,1,0:T(8,128)(2,1)} %bitcast.91), custom_call_target="tpu_custom_call" | custom-call | bytes 6291456 | tf_op jit(solution)/shard_map/pallas_call | solution.py:62
  9.9 1.6 collective-permute-start.8
  11.4 1.7 %collective-permute-start.9 = (bf16[6,1024,128]{2,1,0:T(8,128)(2,1)S(1)}, bf16[6,1024,128]{2,1,0:T(8,128)(2,1)S(1)}, u32[]{:S(2)}, u32[]{:S(2)}) collective-permute-start(bf16[6,1024,128]{2,1,0:T(8,128)(2,1)S(1)} %get-tuple-element.46), channel_id=1, source_target_pairs={{0,24},{8,0},{16,8},{24,16},{1,25},{9,1},{17,9},{25,17},{2,26},{10... | collective-permute-start | bytes 4718600 | tf_op jit(solution)/shard_map/ppermute | solution.py:30
  13.2 28.6 %collective-permute-done.behind = bf16[6,1024,128]{2,1,0:T(8,128)(2,1)S(1)} collective-permute-done((bf16[6,1024,128]{2,1,0:T(8,128)(2,1)S(1)}, bf16[6,1024,128]{2,1,0:T(8,128)(2,1)S(1)}, u32[]{:S(2)}, u32[]{:S(2)}) %collective-permute-start) | collective-permute-done | bytes 1572896 | tf_op jit(solution)/shard_map/ppermute | solution.py:30
  41.9 3.3 %collective-permute-start.3 = (bf16[2,1024,128]{2,1,0:T(8,128)(2,1)S(1)}, bf16[2,1024,128]{2,1,0:T(8,128)(2,1)S(1)}, u32[]{:S(2)}, u32[]{:S(2)}) collective-permute-start(bf16[2,1024,128]{2,1,0:T(8,128)(2,1)S(1)} %slice.17), channel_id=1, source_target_pairs={{0,96},{32,0},{64,32},{96,64},{1,97},{33,1},{65,33},{97,65},{2,98}... | collective-permute-start | bytes 1572872 | tf_op jit(solution)/shard_map/ppermute | solution.py:30
  45.2 1.8 %collective-permute-done.8.behind = bf16[6,1024,128]{2,1,0:T(8,128)(2,1)S(1)} collective-permute-done((bf16[6,1024,128]{2,1,0:T(8,128)(2,1)S(1)}, bf16[6,1024,128]{2,1,0:T(8,128)(2,1)S(1)}, u32[]{:S(2)}, u32[]{:S(2)}) %collective-permute-start.8) | collective-permute-done | bytes 1572896 | tf_op jit(solution)/shard_map/ppermute | solution.py:30
  47.4 3.0 %collective-permute-start.11 = (bf16[2,1024,128]{2,1,0:T(8,128)(2,1)S(1)}, bf16[2,1024,128]{2,1,0:T(8,128)(2,1)S(1)}, u32[]{:S(2)}, u32[]{:S(2)}) collective-permute-start(bf16[2,1024,128]{2,1,0:T(8,128)(2,1)S(1)} %slice.19), channel_id=1, source_target_pairs={{0,24},{8,0},{16,8},{24,16},{1,25},{9,1},{17,9},{25,17},{2,26},{10... | collective-permute-start | bytes 1572872 | tf_op jit(solution)/shard_map/ppermute | solution.py:30
  50.5 2.1 %shard_map.75 = (bf16[4,1024,128]{2,1,0:T(8,128)(2,1)S(1)}, bf16[4,1024,128]{2,1,0:T(8,128)(2,1)S(1)}) custom-call(s32[2]{0:T(128)S(1)} %pad_add_fusion.where, bf16[4,4,2048,128]{3,2,1,0:T(8,128)(2,1)} %bitcast.92), custom_call_target="tpu_custom_call" | custom-call | bytes 4194304 | tf_op jit(solution)/shard_map/pallas_call | solution.py:91
  52.7 3.5 %collective-permute-done.2 = bf16[2,1024,128]{2,1,0:T(8,128)(2,1)S(1)} collective-permute-done((bf16[2,1024,128]{2,1,0:T(8,128)(2,1)S(1)}, bf16[2,1024,128]{2,1,0:T(8,128)(2,1)S(1)}, u32[]{:S(2)}, u32[]{:S(2)}) %collective-permute-start.2) | collective-permute-done | bytes 524320 | tf_op jit(solution)/shard_map/ppermute | solution.py:30
  56.2 1.2 shard_map.78
  57.4 1.6 collective-permute-start.4
  59.0 1.7 %collective-permute-start.5 = (f32[512,128]{1,0:T(8,128)S(1)}, f32[512,128]{1,0:T(8,128)S(1)}, u32[]{:S(2)}, u32[]{:S(2)}) collective-permute-start(f32[512,128]{1,0:T(8,128)S(1)} %get-tuple-element.41), channel_id=1, source_target_pairs={{0,24},{8,0},{16,8},{24,16},{1,25},{9,1},{17,9},{25,17},{2,26},{10... | collective-permute-start | bytes 786440 | tf_op jit(solution)/shard_map/ppermute | solution.py:30
  60.7 1.2 collective-permute-done.10
  61.9 1.2 shard_map.82
  63.2 3.2 %collective-permute-start.13 = (f32[512,128]{1,0:T(8,128)S(1)}, f32[512,128]{1,0:T(8,128)S(1)}, u32[]{:S(2)}, u32[]{:S(2)}) collective-permute-start(f32[512,128]{1,0:T(8,128)S(1)} %get-tuple-element.51), channel_id=1, source_target_pairs={{0,96},{32,0},{64,32},{96,64},{1,97},{33,1},{65,33},{97,65},{2,98}... | collective-permute-start | bytes 786440 | tf_op jit(solution)/shard_map/ppermute | solution.py:30
  66.4 1.4 shard_map.77
  67.9 1.4 shard_map.81
  69.6 3.2 %collective-permute-start.7 = (f32[1024,128]{1,0:T(8,128)S(1)}, f32[1024,128]{1,0:T(8,128)S(1)}, u32[]{:S(2)}, u32[]{:S(2)}) collective-permute-start(f32[1024,128]{1,0:T(8,128)S(1)} %get-tuple-element.43), channel_id=1, source_target_pairs={{0,24},{8,0},{16,8},{24,16},{1,25},{9,1},{17,9},{25,17},{2,26},{10... | collective-permute-start | bytes 1572872 | tf_op jit(solution)/shard_map/ppermute | solution.py:30
  73.0 3.2 %collective-permute-start.15 = (f32[1024,128]{1,0:T(8,128)S(1)}, f32[1024,128]{1,0:T(8,128)S(1)}, u32[]{:S(2)}, u32[]{:S(2)}) collective-permute-start(f32[1024,128]{1,0:T(8,128)S(1)} %get-tuple-element.53), channel_id=1, source_target_pairs={{0,96},{32,0},{64,32},{96,64},{1,97},{33,1},{65,33},{97,65},{2,98}... | collective-permute-start | bytes 1572872 | tf_op jit(solution)/shard_map/ppermute | solution.py:30
  76.2 4.4 %collective-permute-done.6.refs_1_ = f32[1024,128]{1,0:T(8,128)S(1)} collective-permute-done((f32[1024,128]{1,0:T(8,128)S(1)}, f32[1024,128]{1,0:T(8,128)S(1)}, u32[]{:S(2)}, u32[]{:S(2)}) %collective-permute-start.6) | collective-permute-done | bytes 524320 | tf_op jit(solution)/shard_map/ppermute | solution.py:30
  80.6 2.8 %collective-permute-done.14.refs_4_ = f32[1024,128]{1,0:T(8,128)S(1)} collective-permute-done((f32[1024,128]{1,0:T(8,128)S(1)}, f32[1024,128]{1,0:T(8,128)S(1)}, u32[]{:S(2)}, u32[]{:S(2)}) %collective-permute-start.14) | collective-permute-done | bytes 524320 | tf_op jit(solution)/shard_map/ppermute | solution.py:30
  83.9 18.1 %all_to_all.11 = f32[128,1,128]{2,1,0:T(1,128)S(1)} all-to-all(f32[128,1,128]{2,1,0:T(1,128)S(1)} %bitcast.88), channel_id=1, replica_groups=mesh['z'=4,'x'=4,'y'=4,'core'=2] {'z','x','y','core'}, dimensions={0} | all-to-all | bytes 131072 | tf_op jit(solution)/shard_map/all_to_all | solution.py:403
  102.1 1.8 %shard_map.85 = (bf16[512,128]{1,0:T(8,128)(2,1)S(1)}, bf16[512,128]{1,0:T(8,128)(2,1)S(1)}, bf16[512,128]{1,0:T(8,128)(2,1)S(1)}, bf16[512,128]{1,0:T(8,128)(2,1)S(1)}) custom-call(f32[128,128]{1,0:T(8,128)S(1)} %bitcast.78, f32[2,512,128]{2,1,0:T(8,128)S(1)} %bitcast.68, f32[2,512,128]{2,1,0:T(8,128)S(1)} %bitcast.69, f32[4,512,128]{2,1,0:T(8,128)S(1)} %bitcast.62, ...), custom_call_target="tpu_custom_call" | custom-call | flops 10485760 | bytes 4718592 | tf_op jit(solution)/shard_map/pallas_call | solution.py:243
  104.6 0.8 collective-permute-start.28
  105.4 1.1 collective-permute-start.20
  106.5 0.8 collective-permute-start.16
  107.3 1.8 %collective-permute-done.24.two = bf16[1,512,128]{2,1,0:T(8,128)(2,1)S(1)} collective-permute-done((bf16[1,512,128]{2,1,0:T(8,128)(2,1)S(1)}, bf16[1,512,128]{2,1,0:T(8,128)(2,1)S(1)}, u32[]{:S(2)}, u32[]{:S(2)}) %collective-permute-start.24) | collective-permute-done | bytes 131104 | tf_op jit(solution)/shard_map/ppermute | solution.py:288
  109.5 0.8 collective-permute-start.25
  110.6 0.8 collective-permute-start.29
  111.9 2.1 %collective-permute-start.21 = (bf16[2,512,128]{2,1,0:T(8,128)(2,1)S(1)}, bf16[2,512,128]{2,1,0:T(8,128)(2,1)S(1)}, u32[]{:S(2)}, u32[]{:S(2)}) collective-permute-start(bf16[2,512,128]{2,1,0:T(8,128)(2,1)S(1)} %shard_map.89.one), channel_id=1, source_target_pairs={{0,24},{8,16},{16,8},{24,0},{1,25},{9,17},{17,9},{25,1},{2,26},{10... | collective-permute-start | bytes 786440 | tf_op jit(solution)/shard_map/ppermute | solution.py:288
  114.4 3.4 %collective-permute-done.25.two = bf16[2,512,128]{2,1,0:T(8,128)(2,1)S(1)} collective-permute-done((bf16[2,512,128]{2,1,0:T(8,128)(2,1)S(1)}, bf16[2,512,128]{2,1,0:T(8,128)(2,1)S(1)}, u32[]{:S(2)}, u32[]{:S(2)}) %collective-permute-start.25) | collective-permute-done | bytes 262176 | tf_op jit(solution)/shard_map/ppermute | solution.py:288
  117.9 1.6 collective-permute-start.26
  119.5 1.1 collective-permute-start.30
  120.6 0.9 collective-permute-start.22
  121.7 0.8 collective-permute-start.18
  122.5 8.6 %collective-permute-done.26.two = bf16[4,512,128]{2,1,0:T(8,128)(2,1)S(1)} collective-permute-done((bf16[4,512,128]{2,1,0:T(8,128)(2,1)S(1)}, bf16[4,512,128]{2,1,0:T(8,128)(2,1)S(1)}, u32[]{:S(2)}, u32[]{:S(2)}) %collective-permute-start.26) | collective-permute-done | bytes 524320 | tf_op jit(solution)/shard_map/ppermute | solution.py:288
  132.5 1.9 %collective-permute-start.31 = (bf16[8,512,128]{2,1,0:T(8,128)(2,1)S(1)}, bf16[8,512,128]{2,1,0:T(8,128)(2,1)S(1)}, u32[]{:S(2)}, u32[]{:S(2)}) collective-permute-start(bf16[8,512,128]{2,1,0:T(8,128)(2,1)S(1)} %shard_map.97.refs_0_), channel_id=1, source_target_pairs={{0,24},{8,16},{16,8},{24,0},{1,25},{9,17},{17,9},{25,1},{2,26},{10... | collective-permute-start | bytes 3145736 | tf_op jit(solution)/shard_map/ppermute | solution.py:288
  134.7 1.2 collective-permute-start.19
  135.9 3.3 %shard_map.103 = (f32[2,1024,128]{2,1,0:T(8,128)}, f32[2,1024,128]{2,1,0:T(8,128)}, f32[2,1024,128]{2,1,0:T(8,128)}) custom-call(f32[128,128]{1,0:T(8,128)S(1)} %bitcast.79, f32[1024,128]{1,0:T(8,128)S(1)} %get-tuple-element.55.mean_a, f32[1024,128]{1,0:T(8,128)S(1)} %get-tuple-element.56.mean_b, f32[2,1024,128]{2,1,0:T(8,128)S(1)} %bitcast.63, ...), custom_call_target="tpu_custom_call" | custom-call | flops 5242880 | bytes 7864320 | tf_op jit(solution)/shard_map/pallas_call | solution.py:271
  139.2 2.3 %shard_map.98.refs_1_ = bf16[4,4,4,512,128]{4,3,2,1,0:T(8,128)(2,1)} custom-call(bf16[8,512,128]{2,1,0:T(8,128)(2,1)S(1)} %shard_map.97.refs_0_, bf16[8,512,128]{2,1,0:T(8,128)(2,1)S(1)} %shard_map.94.refs_1_, bf16[8,512,128]{2,1,0:T(8,128)(2,1)S(1)} %shard_map.91.refs_2_, bf16[8,512,128]{2,1,0:T(8,128)(2,1)S(1)} %shard_map.88.refs_3_), custom_call_target="tpu_custom_call" | custom-call | bytes 8388608 | tf_op jit(solution)/shard_map/pallas_call | solution.py:340
  141.4 14.6 %collective-permute-done.31.refs_0_ = bf16[8,512,128]{2,1,0:T(8,128)(2,1)S(1)} collective-permute-done((bf16[8,512,128]{2,1,0:T(8,128)(2,1)S(1)}, bf16[8,512,128]{2,1,0:T(8,128)(2,1)S(1)}, u32[]{:S(2)}, u32[]{:S(2)}) %collective-permute-start.31) | collective-permute-done | bytes 1048608 | tf_op jit(solution)/shard_map/ppermute | solution.py:288
  156.0 1.0 shard_map.99.refs_1_
  157.1 1.0 shard_map.100.refs_1_
  158.1 1.0 shard_map.101.refs_1_
  159.2 1.0 shard_map.102
  (58 shorter events, 5.7 us)
Async XLA Ops:
  3.2 38.6 %collective-permute-start = (bf16[6,1024,128]{2,1,0:T(8,128)(2,1)S(1)}, bf16[6,1024,128]{2,1,0:T(8,128)(2,1)S(1)}, u32[]{:S(2)}, u32[]{:S(2)}) collective-permute-start(bf16[6,1024,128]{2,1,0:T(8,128)(2,1)S(1)} %get-tuple-element.35), channel_id=1, source_target_pairs={{0,32},{32,64},{64,96},{96,0},{1,33},{33,65},{65,97},{97,1},{2,34}... | collective-permute-start | bytes 4718600 | tf_op jit(solution)/shard_map/ppermute | solution.py:30
  5.2 36.6 %collective-permute-start.1 = (bf16[6,1024,128]{2,1,0:T(8,128)(2,1)S(1)}, bf16[6,1024,128]{2,1,0:T(8,128)(2,1)S(1)}, u32[]{:S(2)}, u32[]{:S(2)}) collective-permute-start(bf16[6,1024,128]{2,1,0:T(8,128)(2,1)S(1)} %get-tuple-element.36), channel_id=1, source_target_pairs={{0,96},{32,0},{64,32},{96,64},{1,97},{33,1},{65,33},{97,65},{2,98}... | collective-permute-start | bytes 4718600 | tf_op jit(solution)/shard_map/ppermute | solution.py:30
  9.9 37.1 %collective-permute-start.8 = (bf16[6,1024,128]{2,1,0:T(8,128)(2,1)S(1)}, bf16[6,1024,128]{2,1,0:T(8,128)(2,1)S(1)}, u32[]{:S(2)}, u32[]{:S(2)}) collective-permute-start(bf16[6,1024,128]{2,1,0:T(8,128)(2,1)S(1)} %get-tuple-element.45), channel_id=1, source_target_pairs={{0,8},{8,16},{16,24},{24,0},{1,9},{9,17},{17,25},{25,1},{2,10},{10... | collective-permute-start | bytes 4718600 | tf_op jit(solution)/shard_map/ppermute | solution.py:30
  11.4 36.0 %collective-permute-start.9 = (bf16[6,1024,128]{2,1,0:T(8,128)(2,1)S(1)}, bf16[6,1024,128]{2,1,0:T(8,128)(2,1)S(1)}, u32[]{:S(2)}, u32[]{:S(2)}) collective-permute-start(bf16[6,1024,128]{2,1,0:T(8,128)(2,1)S(1)} %get-tuple-element.46), channel_id=1, source_target_pairs={{0,24},{8,0},{16,8},{24,16},{1,25},{9,1},{17,9},{25,17},{2,26},{10... | collective-permute-start | bytes 4718600 | tf_op jit(solution)/shard_map/ppermute | solution.py:30
  41.8 14.4 %collective-permute-start.2 = (bf16[2,1024,128]{2,1,0:T(8,128)(2,1)S(1)}, bf16[2,1024,128]{2,1,0:T(8,128)(2,1)S(1)}, u32[]{:S(2)}, u32[]{:S(2)}) collective-permute-start(bf16[2,1024,128]{2,1,0:T(8,128)(2,1)S(1)} %slice.16), channel_id=1, source_target_pairs={{0,32},{32,64},{64,96},{96,0},{1,33},{33,65},{65,97},{97,1},{2,34}... | collective-permute-start | bytes 1572872 | tf_op jit(solution)/shard_map/ppermute | solution.py:30
  41.9 14.3 %collective-permute-start.3 = (bf16[2,1024,128]{2,1,0:T(8,128)(2,1)S(1)}, bf16[2,1024,128]{2,1,0:T(8,128)(2,1)S(1)}, u32[]{:S(2)}, u32[]{:S(2)}) collective-permute-start(bf16[2,1024,128]{2,1,0:T(8,128)(2,1)S(1)} %slice.17), channel_id=1, source_target_pairs={{0,96},{32,0},{64,32},{96,64},{1,97},{33,1},{65,33},{97,65},{2,98}... | collective-permute-start | bytes 1572872 | tf_op jit(solution)/shard_map/ppermute | solution.py:30
  47.1 14.9 %collective-permute-start.10 = (bf16[2,1024,128]{2,1,0:T(8,128)(2,1)S(1)}, bf16[2,1024,128]{2,1,0:T(8,128)(2,1)S(1)}, u32[]{:S(2)}, u32[]{:S(2)}) collective-permute-start(bf16[2,1024,128]{2,1,0:T(8,128)(2,1)S(1)} %slice.18), channel_id=1, source_target_pairs={{0,8},{8,16},{16,24},{24,0},{1,9},{9,17},{17,25},{25,1},{2,10},{10... | collective-permute-start | bytes 1572872 | tf_op jit(solution)/shard_map/ppermute | solution.py:30
  47.4 14.5 %collective-permute-start.11 = (bf16[2,1024,128]{2,1,0:T(8,128)(2,1)S(1)}, bf16[2,1024,128]{2,1,0:T(8,128)(2,1)S(1)}, u32[]{:S(2)}, u32[]{:S(2)}) collective-permute-start(bf16[2,1024,128]{2,1,0:T(8,128)(2,1)S(1)} %slice.19), channel_id=1, source_target_pairs={{0,24},{8,0},{16,8},{24,16},{1,25},{9,1},{17,9},{25,17},{2,26},{10... | collective-permute-start | bytes 1572872 | tf_op jit(solution)/shard_map/ppermute | solution.py:30
  57.4 11.9 %collective-permute-start.4 = (f32[512,128]{1,0:T(8,128)S(1)}, f32[512,128]{1,0:T(8,128)S(1)}, u32[]{:S(2)}, u32[]{:S(2)}) collective-permute-start(f32[512,128]{1,0:T(8,128)S(1)} %get-tuple-element.39), channel_id=1, source_target_pairs={{0,8},{8,16},{16,24},{24,0},{1,9},{9,17},{17,25},{25,1},{2,10},{10... | collective-permute-start | bytes 786440 | tf_op jit(solution)/shard_map/ppermute | solution.py:30
  59.0 10.4 %collective-permute-start.5 = (f32[512,128]{1,0:T(8,128)S(1)}, f32[512,128]{1,0:T(8,128)S(1)}, u32[]{:S(2)}, u32[]{:S(2)}) collective-permute-start(f32[512,128]{1,0:T(8,128)S(1)} %get-tuple-element.41), channel_id=1, source_target_pairs={{0,24},{8,0},{16,8},{24,16},{1,25},{9,1},{17,9},{25,17},{2,26},{10... | collective-permute-start | bytes 786440 | tf_op jit(solution)/shard_map/ppermute | solution.py:30
  63.1 9.7 %collective-permute-start.12 = (f32[512,128]{1,0:T(8,128)S(1)}, f32[512,128]{1,0:T(8,128)S(1)}, u32[]{:S(2)}, u32[]{:S(2)}) collective-permute-start(f32[512,128]{1,0:T(8,128)S(1)} %get-tuple-element.49), channel_id=1, source_target_pairs={{0,32},{32,64},{64,96},{96,0},{1,33},{33,65},{65,97},{97,1},{2,34}... | collective-permute-start | bytes 786440 | tf_op jit(solution)/shard_map/ppermute | solution.py:30
  63.2 9.6 %collective-permute-start.13 = (f32[512,128]{1,0:T(8,128)S(1)}, f32[512,128]{1,0:T(8,128)S(1)}, u32[]{:S(2)}, u32[]{:S(2)}) collective-permute-start(f32[512,128]{1,0:T(8,128)S(1)} %get-tuple-element.51), channel_id=1, source_target_pairs={{0,96},{32,0},{64,32},{96,64},{1,97},{33,1},{65,33},{97,65},{2,98}... | collective-permute-start | bytes 786440 | tf_op jit(solution)/shard_map/ppermute | solution.py:30
  69.5 11.2 %collective-permute-start.6 = (f32[1024,128]{1,0:T(8,128)S(1)}, f32[1024,128]{1,0:T(8,128)S(1)}, u32[]{:S(2)}, u32[]{:S(2)}) collective-permute-start(f32[1024,128]{1,0:T(8,128)S(1)} %get-tuple-element.42), channel_id=1, source_target_pairs={{0,8},{8,16},{16,24},{24,0},{1,9},{9,17},{17,25},{25,1},{2,10},{10... | collective-permute-start | bytes 1572872 | tf_op jit(solution)/shard_map/ppermute | solution.py:30
  69.6 11.1 %collective-permute-start.7 = (f32[1024,128]{1,0:T(8,128)S(1)}, f32[1024,128]{1,0:T(8,128)S(1)}, u32[]{:S(2)}, u32[]{:S(2)}) collective-permute-start(f32[1024,128]{1,0:T(8,128)S(1)} %get-tuple-element.43), channel_id=1, source_target_pairs={{0,24},{8,0},{16,8},{24,16},{1,25},{9,1},{17,9},{25,17},{2,26},{10... | collective-permute-start | bytes 1572872 | tf_op jit(solution)/shard_map/ppermute | solution.py:30
  72.9 10.6 %collective-permute-start.14 = (f32[1024,128]{1,0:T(8,128)S(1)}, f32[1024,128]{1,0:T(8,128)S(1)}, u32[]{:S(2)}, u32[]{:S(2)}) collective-permute-start(f32[1024,128]{1,0:T(8,128)S(1)} %get-tuple-element.52), channel_id=1, source_target_pairs={{0,32},{32,64},{64,96},{96,0},{1,33},{33,65},{65,97},{97,1},{2,34}... | collective-permute-start | bytes 1572872 | tf_op jit(solution)/shard_map/ppermute | solution.py:30
  73.0 10.5 %collective-permute-start.15 = (f32[1024,128]{1,0:T(8,128)S(1)}, f32[1024,128]{1,0:T(8,128)S(1)}, u32[]{:S(2)}, u32[]{:S(2)}) collective-permute-start(f32[1024,128]{1,0:T(8,128)S(1)} %get-tuple-element.53), channel_id=1, source_target_pairs={{0,96},{32,0},{64,32},{96,64},{1,97},{33,1},{65,33},{97,65},{2,98}... | collective-permute-start | bytes 1572872 | tf_op jit(solution)/shard_map/ppermute | solution.py:30
  83.5 18.6 %copy-start = (f32[1,4,65536]{2,1,0:T(4,128)S(1)}, f32[1,4,65536]{2,1,0:T(4,128)}, u32[]{:S(2)}) copy-start(f32[1,4,65536]{2,1,0:T(4,128)} %param.5) | copy-start | bytes 3145732
  83.5 18.6 %copy-start.1 = (f32[1,4,65536]{2,1,0:T(4,128)S(1)}, f32[1,4,65536]{2,1,0:T(4,128)}, u32[]{:S(2)}) copy-start(f32[1,4,65536]{2,1,0:T(4,128)} %param.6) | copy-start | bytes 3145732
  83.5 18.6 %copy-start.2 = (f32[1,4,65536]{2,1,0:T(4,128)S(1)}, f32[1,4,65536]{2,1,0:T(4,128)}, u32[]{:S(2)}) copy-start(f32[1,4,65536]{2,1,0:T(4,128)} %param.7) | copy-start | bytes 3145732
  103.9 5.2 %collective-permute-start.24 = (bf16[1,512,128]{2,1,0:T(8,128)(2,1)S(1)}, bf16[1,512,128]{2,1,0:T(8,128)(2,1)S(1)}, u32[]{:S(2)}, u32[]{:S(2)}) collective-permute-start(bf16[1,512,128]{2,1,0:T(8,128)(2,1)S(1)} %bitcast.86), channel_id=1, source_target_pairs={{0,8},{8,0},{16,24},{24,16},{1,9},{9,1},{17,25},{25,17},{2,10},{10... | collective-permute-start | bytes 393224 | tf_op jit(solution)/shard_map/ppermute | solution.py:288
  104.6 5.7 %collective-permute-start.28 = (bf16[1,512,128]{2,1,0:T(8,128)(2,1)S(1)}, bf16[1,512,128]{2,1,0:T(8,128)(2,1)S(1)}, u32[]{:S(2)}, u32[]{:S(2)}) collective-permute-start(bf16[1,512,128]{2,1,0:T(8,128)(2,1)S(1)} %bitcast.84), channel_id=1, source_target_pairs={{0,32},{32,0},{64,96},{96,64},{1,33},{33,1},{65,97},{97,65},{2,34}... | collective-permute-start | bytes 393224 | tf_op jit(solution)/shard_map/ppermute | solution.py:288
  105.4 6.2 %collective-permute-start.20 = (bf16[1,512,128]{2,1,0:T(8,128)(2,1)S(1)}, bf16[1,512,128]{2,1,0:T(8,128)(2,1)S(1)}, u32[]{:S(2)}, u32[]{:S(2)}) collective-permute-start(bf16[1,512,128]{2,1,0:T(8,128)(2,1)S(1)} %bitcast.82), channel_id=1, source_target_pairs={{0,96},{32,64},{64,32},{96,0},{1,97},{33,65},{65,33},{97,1},{2,98}... | collective-permute-start | bytes 393224 | tf_op jit(solution)/shard_map/ppermute | solution.py:288
  106.5 7.5 %collective-permute-start.16 = (bf16[1,512,128]{2,1,0:T(8,128)(2,1)S(1)}, bf16[1,512,128]{2,1,0:T(8,128)(2,1)S(1)}, u32[]{:S(2)}, u32[]{:S(2)}) collective-permute-start(bf16[1,512,128]{2,1,0:T(8,128)(2,1)S(1)} %bitcast.80), channel_id=1, source_target_pairs={{0,24},{8,16},{16,8},{24,0},{1,25},{9,17},{17,9},{25,1},{2,26},{10... | collective-permute-start | bytes 393224 | tf_op jit(solution)/shard_map/ppermute | solution.py:288
  109.5 8.4 %collective-permute-start.25 = (bf16[2,512,128]{2,1,0:T(8,128)(2,1)S(1)}, bf16[2,512,128]{2,1,0:T(8,128)(2,1)S(1)}, u32[]{:S(2)}, u32[]{:S(2)}) collective-permute-start(bf16[2,512,128]{2,1,0:T(8,128)(2,1)S(1)} %shard_map.92.one), channel_id=1, source_target_pairs={{0,96},{32,64},{64,32},{96,0},{1,97},{33,65},{65,33},{97,1},{2,98}... | collective-permute-start | bytes 786440 | tf_op jit(solution)/shard_map/ppermute | solution.py:288
  110.6 8.8 %collective-permute-start.29 = (bf16[2,512,128]{2,1,0:T(8,128)(2,1)S(1)}, bf16[2,512,128]{2,1,0:T(8,128)(2,1)S(1)}, u32[]{:S(2)}, u32[]{:S(2)}) collective-permute-start(bf16[2,512,128]{2,1,0:T(8,128)(2,1)S(1)} %shard_map.95.one), channel_id=1, source_target_pairs={{0,8},{8,0},{16,24},{24,16},{1,9},{9,1},{17,25},{25,17},{2,10},{10... | collective-permute-start | bytes 786440 | tf_op jit(solution)/shard_map/ppermute | solution.py:288
  111.9 8.7 %collective-permute-start.21 = (bf16[2,512,128]{2,1,0:T(8,128)(2,1)S(1)}, bf16[2,512,128]{2,1,0:T(8,128)(2,1)S(1)}, u32[]{:S(2)}, u32[]{:S(2)}) collective-permute-start(bf16[2,512,128]{2,1,0:T(8,128)(2,1)S(1)} %shard_map.89.one), channel_id=1, source_target_pairs={{0,24},{8,16},{16,8},{24,0},{1,25},{9,17},{17,9},{25,1},{2,26},{10... | collective-permute-start | bytes 786440 | tf_op jit(solution)/shard_map/ppermute | solution.py:288
  114.3 7.3 %collective-permute-start.17 = (bf16[2,512,128]{2,1,0:T(8,128)(2,1)S(1)}, bf16[2,512,128]{2,1,0:T(8,128)(2,1)S(1)}, u32[]{:S(2)}, u32[]{:S(2)}) collective-permute-start(bf16[2,512,128]{2,1,0:T(8,128)(2,1)S(1)} %shard_map.86.one), channel_id=1, source_target_pairs={{0,32},{32,0},{64,96},{96,64},{1,33},{33,1},{65,97},{97,65},{2,34}... | collective-permute-start | bytes 786440 | tf_op jit(solution)/shard_map/ppermute | solution.py:288
  117.9 13.2 %collective-permute-start.26 = (bf16[4,512,128]{2,1,0:T(8,128)(2,1)S(1)}, bf16[4,512,128]{2,1,0:T(8,128)(2,1)S(1)}, u32[]{:S(2)}, u32[]{:S(2)}) collective-permute-start(bf16[4,512,128]{2,1,0:T(8,128)(2,1)S(1)} %shard_map.93.one), channel_id=1, source_target_pairs={{0,24},{8,16},{16,8},{24,0},{1,25},{9,17},{17,9},{25,1},{2,26},{10... | collective-permute-start | bytes 1572872 | tf_op jit(solution)/shard_map/ppermute | solution.py:288
  119.5 12.9 %collective-permute-start.30 = (bf16[4,512,128]{2,1,0:T(8,128)(2,1)S(1)}, bf16[4,512,128]{2,1,0:T(8,128)(2,1)S(1)}, u32[]{:S(2)}, u32[]{:S(2)}) collective-permute-start(bf16[4,512,128]{2,1,0:T(8,128)(2,1)S(1)} %shard_map.96.one), channel_id=1, source_target_pairs={{0,96},{32,64},{64,32},{96,0},{1,97},{33,65},{65,33},{97,1},{2,98}... | collective-permute-start | bytes 1572872 | tf_op jit(solution)/shard_map/ppermute | solution.py:288
  120.6 13.7 %collective-permute-start.22 = (bf16[4,512,128]{2,1,0:T(8,128)(2,1)S(1)}, bf16[4,512,128]{2,1,0:T(8,128)(2,1)S(1)}, u32[]{:S(2)}, u32[]{:S(2)}) collective-permute-start(bf16[4,512,128]{2,1,0:T(8,128)(2,1)S(1)} %shard_map.90.one), channel_id=1, source_target_pairs={{0,32},{32,0},{64,96},{96,64},{1,33},{33,1},{65,97},{97,65},{2,34}... | collective-permute-start | bytes 1572872 | tf_op jit(solution)/shard_map/ppermute | solution.py:288
  121.7 12.9 %collective-permute-start.18 = (bf16[4,512,128]{2,1,0:T(8,128)(2,1)S(1)}, bf16[4,512,128]{2,1,0:T(8,128)(2,1)S(1)}, u32[]{:S(2)}, u32[]{:S(2)}) collective-permute-start(bf16[4,512,128]{2,1,0:T(8,128)(2,1)S(1)} %shard_map.87.one), channel_id=1, source_target_pairs={{0,8},{8,0},{16,24},{24,16},{1,9},{9,1},{17,25},{25,17},{2,10},{10... | collective-permute-start | bytes 1572872 | tf_op jit(solution)/shard_map/ppermute | solution.py:288
  131.2 25.9 %collective-permute-start.27 = (bf16[8,512,128]{2,1,0:T(8,128)(2,1)S(1)}, bf16[8,512,128]{2,1,0:T(8,128)(2,1)S(1)}, u32[]{:S(2)}, u32[]{:S(2)}) collective-permute-start(bf16[8,512,128]{2,1,0:T(8,128)(2,1)S(1)} %shard_map.94.refs_1_), channel_id=1, source_target_pairs={{0,32},{32,0},{64,96},{96,64},{1,33},{33,1},{65,97},{97,65},{2,34}... | collective-permute-start | bytes 3145736 | tf_op jit(solution)/shard_map/ppermute | solution.py:288
  132.5 23.5 %collective-permute-start.31 = (bf16[8,512,128]{2,1,0:T(8,128)(2,1)S(1)}, bf16[8,512,128]{2,1,0:T(8,128)(2,1)S(1)}, u32[]{:S(2)}, u32[]{:S(2)}) collective-permute-start(bf16[8,512,128]{2,1,0:T(8,128)(2,1)S(1)} %shard_map.97.refs_0_), channel_id=1, source_target_pairs={{0,24},{8,16},{16,8},{24,0},{1,25},{9,17},{17,9},{25,1},{2,26},{10... | collective-permute-start | bytes 3145736 | tf_op jit(solution)/shard_map/ppermute | solution.py:288
  134.5 23.6 %collective-permute-start.23 = (bf16[8,512,128]{2,1,0:T(8,128)(2,1)S(1)}, bf16[8,512,128]{2,1,0:T(8,128)(2,1)S(1)}, u32[]{:S(2)}, u32[]{:S(2)}) collective-permute-start(bf16[8,512,128]{2,1,0:T(8,128)(2,1)S(1)} %shard_map.91.refs_2_), channel_id=1, source_target_pairs={{0,8},{8,0},{16,24},{24,16},{1,9},{9,1},{17,25},{25,17},{2,10},{10... | collective-permute-start | bytes 3145736 | tf_op jit(solution)/shard_map/ppermute | solution.py:288
  134.7 24.5 %collective-permute-start.19 = (bf16[8,512,128]{2,1,0:T(8,128)(2,1)S(1)}, bf16[8,512,128]{2,1,0:T(8,128)(2,1)S(1)}, u32[]{:S(2)}, u32[]{:S(2)}) collective-permute-start(bf16[8,512,128]{2,1,0:T(8,128)(2,1)S(1)} %shard_map.88.refs_3_), channel_id=1, source_target_pairs={{0,96},{32,64},{64,32},{96,0},{1,97},{33,65},{65,33},{97,1},{2,98}... | collective-permute-start | bytes 3145736 | tf_op jit(solution)/shard_map/ppermute | solution.py:288

commit v4 on v3

--- a/solution.py
+++ b/solution.py
@@ -34,12 +34,13 @@
     return pl.CostEstimate(flops=flops, bytes_accessed=moved, transcendentals=0)
 
 
-def pick_kernel(along_z, where, pieces, *refs):
-    outs, sems = refs[:2], refs[2]
+def pick_kernel(at_z, at_x, pieces, *refs):
+    outs, sems = refs[:4], refs[4]
     quarter = outs[0].shape[1] // 2
+    z, x = at_z[0], at_x[0]
     copies = []
-    for k, (out, by) in enumerate(zip(outs, (1, 3))):
-        me = where[0] if along_z else where[1]
+    for k, (out, along_z, by) in enumerate(zip(outs, (True, True, False, False), (1, 3, 1, 3))):
+        me = z if along_z else x
         low = 0 if along_z else 2 * quarter
         far_low = low if by == 1 else low + quarter
         near, far = lax.rem(me + by, 4), lax.rem(me + 2, 4)
@@ -57,128 +58,146 @@
         copy.wait()
 
 
-def pick(pieces, zx, along_z):
+def pick(pieces, z, x):
     half = pieces.shape[2] // 2
-    return pl.pallas_call(
-        functools.partial(pick_kernel, along_z),
+    any_ = pl.BlockSpec(memory_space=pl.ANY)
+    return pl.pallas_call(
+        pick_kernel,
+        grid_spec=pltpu.PrefetchScalarGridSpec(
+            num_scalar_prefetch=2,
+            grid=(),
+            in_specs=[any_],
+            out_specs=[any_] * 4,
+            scratch_shapes=[pltpu.SemaphoreType.DMA((4, 5))],
+        ),
+        out_shape=[jax.ShapeDtypeStruct((6, half, LANES), bf16)] * 4,
+        compiler_params=pltpu.CompilerParams(vmem_limit_bytes=VMEM_LIMIT),
+        cost_estimate=cost(0, 96 * half * LANES),
+    )(z.reshape(1), x.reshape(1), pltpu.with_memory_space_constraint(pieces, pltpu.HBM))
+
+
+def base_kernel(where, own, behind, ahead, out):
+    out[...] = own[...].astype(f32) + behind[...].astype(f32) + ahead[...].astype(f32)
+
+
+def base_sum(where, pieces, behind, ahead, along_z):
+    half = behind.shape[1]
+    steps = half // BLOCK
+    part = pl.BlockSpec((4, BLOCK, LANES), lambda i, w: (0, i, 0))
+    if along_z:
+        own = pl.BlockSpec((None, 4, BLOCK, LANES), lambda i, w: (w[0], 0, i, 0))
+    else:
+        own = pl.BlockSpec((4, None, BLOCK, LANES), lambda i, w: (0, w[0], steps + i, 0))
+    return pl.pallas_call(
+        base_kernel,
+        grid_spec=pltpu.PrefetchScalarGridSpec(
+            num_scalar_prefetch=1, grid=(steps,), in_specs=[own, part, part], out_specs=part
+        ),
+        out_shape=jax.ShapeDtypeStruct((4, half, LANES), f32),
+        compiler_params=pltpu.CompilerParams(vmem_limit_bytes=VMEM_LIMIT),
+        cost_estimate=cost(8 * half * LANES, 40 * half * LANES),
+    )(where, pltpu.with_memory_space_constraint(pieces, pltpu.HBM), behind, ahead)
+
+
+def on_half(low_part, high_part):
+    pl.when(pl.program_id(0) < pl.num_programs(0) // 2)(low_part)
+    pl.when(pl.program_id(0) >= pl.num_programs(0) // 2)(high_part)
+
+
+def far_sum_kernel(where, base, far_low, far_high, low, high):
+    def low_part():
+        low[...] = base[...] + far_low[...].astype(f32)
+
+    def high_part():
+        high[...] = base[...] + far_high[...].astype(f32)
+
+    on_half(low_part, high_part)
+
+
+def far_sum(where, base, far_low, far_high):
+    quarter = far_low.shape[1]
+    out = pl.BlockSpec((quarter, LANES), lambda i, w: (0, 0))
+    far = pl.BlockSpec((None, quarter, LANES), lambda i, w: (lax.rem(w[1] + 2, 4), 0, 0))
+    return pl.pallas_call(
+        far_sum_kernel,
         grid_spec=pltpu.PrefetchScalarGridSpec(
             num_scalar_prefetch=1,
-            grid=(),
-            in_specs=[pl.BlockSpec(memory_space=pl.ANY)],
-            out_specs=[pl.BlockSpec(memory_space=pl.ANY)] * 2,
-            scratch_shapes=[pltpu.SemaphoreType.DMA((2, 5))],
+            grid=(2,),
+            in_specs=[pl.BlockSpec((None, quarter, LANES), lambda i, w: (lax.rem(w[1] + 2, 4), i, 0)), far, far],
+            out_specs=[out, out],
         ),
-        out_shape=[jax.ShapeDtypeStruct((6, half, LANES), bf16)] * 2,
-        compiler_params=pltpu.CompilerParams(vmem_limit_bytes=VMEM_LIMIT),
-        cost_estimate=cost(0, 48 * half * LANES),
-    )(zx, pltpu.with_memory_space_constraint(pieces, pltpu.HBM))
-
-
-def own_kernel(where, pieces, out_a, out_b, sems):
-    half = out_a.shape[1]
-    copies = [
-        pltpu.make_async_copy(pieces.at[where[0], :, pl.ds(0, half)], out_a, sems.at[0]),
-        pltpu.make_async_copy(pieces.at[:, where[1], pl.ds(half, half)], out_b, sems.at[1]),
-    ]
-    for copy in copies:
-        copy.start()
-    for copy in copies:
-        copy.wait()
-
-
-def own_pieces(pieces, zx):
-    half = pieces.shape[2] // 2
-    return pl.pallas_call(
-        own_kernel,
+        out_shape=[jax.ShapeDtypeStruct((quarter, LANES), f32)] * 2,
+        compiler_params=pltpu.CompilerParams(vmem_limit_bytes=VMEM_LIMIT),
+        cost_estimate=cost(2 * quarter * LANES, 20 * quarter * LANES),
+    )(where, base, far_low, far_high)
+
+
+def near_sum_kernel(where, base_1, base_3, low_1, low_3, high_1, high_3, came_low, came_high, to_next, to_last):
+    def low_part():
+        to_next[...] = base_1[...] + low_1[...].astype(f32) + came_low[...]
+        to_last[...] = base_3[...] + low_3[...].astype(f32)
+
+    def high_part():
+        to_next[...] = base_1[...] + high_1[...].astype(f32)
+        to_last[...] = base_3[...] + high_3[...].astype(f32) + came_high[...]
+
+    on_half(low_part, high_part)
+
+
+def near_sum(where, base, far_low, far_high, came_low, came_high):
+    quarter = far_low.shape[1]
+    whole = pl.BlockSpec((quarter, LANES), lambda i, w: (0, 0))
+    out = pl.BlockSpec((quarter, LANES), lambda i, w: (i, 0))
+
+    def base_at(by):
+        return pl.BlockSpec((None, quarter, LANES), lambda i, w: (lax.rem(w[1] + by, 4), i, 0))
+
+    def far_at(by):
+        return pl.BlockSpec((None, quarter, LANES), lambda i, w: (lax.rem(w[1] + by, 4), 0, 0))
+
+    return pl.pallas_call(
+        near_sum_kernel,
         grid_spec=pltpu.PrefetchScalarGridSpec(
             num_scalar_prefetch=1,
-            grid=(),
-            in_specs=[pl.BlockSpec(memory_space=pl.ANY)],
-            out_specs=[pl.BlockSpec(memory_space=pl.ANY)] * 2,
-            scratch_shapes=[pltpu.SemaphoreType.DMA((2,))],
+            grid=(2,),
+            in_specs=[base_at(1), base_at(3), far_at(1), far_at(3), far_at(1), far_at(3), whole, whole],
+            out_specs=[out, out],
         ),
-        out_shape=[jax.ShapeDtypeStruct((4, half, LANES), bf16)] * 2,
-        compiler_params=pltpu.CompilerParams(vmem_limit_bytes=VMEM_LIMIT),
-        cost_estimate=cost(0, 32 * half * LANES),
-    )(zx, pltpu.with_memory_space_constraint(pieces, pltpu.HBM))
-
-
-def total_of(refs, at, far):
-    own, behind, ahead = refs
-    return own[at].astype(f32) + behind[at].astype(f32) + ahead[at].astype(f32) + far[at].astype(f32)
-
-
-def far_sum_kernel(where, own, behind, ahead, far_low, far_high, low, high):
-    at = lax.rem(where[1] + 2, 4)
-
-    @pl.when(pl.program_id(0) < pl.num_programs(0) // 2)
-    def _():
-        low[...] = total_of((own, behind, ahead), at, far_low)
-
-    @pl.when(pl.program_id(0) >= pl.num_programs(0) // 2)
-    def _():
-        high[...] = total_of((own, behind, ahead), at, far_high)
-
-
-def near_sum_kernel(where, own, behind, ahead, far_low, far_high, *outs):
-    def write(far):
-        for by, out in zip((0, 1, 3), outs):
-            out[...] = total_of((own, behind, ahead), lax.rem(where[1] + by, 4), far)
-
-    pl.when(pl.program_id(0) < pl.num_programs(0) // 2)(lambda: write(far_low))
-    pl.when(pl.program_id(0) >= pl.num_programs(0) // 2)(lambda: write(far_high))
-
-
-def first_sum(where, own, behind, ahead, far_low, far_high, only_far):
-    half = own.shape[1]
-    quarter, steps = half // 2, half // BLOCK
-    lower = lambda i: jnp.minimum(i, steps // 2 - 1)
-    upper = lambda i: jnp.maximum(i - steps // 2, 0)
-    part = pl.BlockSpec((4, BLOCK, LANES), lambda i, w: (0, i, 0))
-    in_specs = [part] * 3 + [
-        pl.BlockSpec((4, BLOCK, LANES), lambda i, w: (0, lower(i), 0)),
-        pl.BlockSpec((4, BLOCK, LANES), lambda i, w: (0, upper(i), 0)),
-    ]
-    if only_far:
-        out_specs = [
-            pl.BlockSpec((BLOCK, LANES), lambda i, w: (lower(i), 0)),
-            pl.BlockSpec((BLOCK, LANES), lambda i, w: (upper(i), 0)),
-        ]
-        out_shape = [jax.ShapeDtypeStruct((quarter, LANES), f32)] * 2
-    else:
-        out_specs = [pl.BlockSpec((BLOCK, LANES), lambda i, w: (i, 0))] * 3
-        out_shape = [jax.ShapeDtypeStruct((half, LANES), f32)] * 3
-    return pl.pallas_call(
-        far_sum_kernel if only_far else near_sum_kernel,
+        out_shape=[jax.ShapeDtypeStruct((2 * quarter, LANES), f32)] * 2,
+        compiler_params=pltpu.CompilerParams(vmem_limit_bytes=VMEM_LIMIT),
+        cost_estimate=cost(10 * quarter * LANES, 48 * quarter * LANES),
+    )(where, base, base, far_low, far_low, far_high, far_high, came_low, came_high)
+
+
+def here_sum_kernel(zx, *refs):
+    sets, outs = (refs[:3], refs[3:6]), refs[6:]
+
+    def add(which):
+        for parts, out in zip(sets, outs):
+            out[...] = parts[0][...] + parts[which][...].astype(f32)
+
+    on_half(lambda: add(1), lambda: add(2))
+
+
+def here_sum(zx, base_a, low_a, high_a, base_b, low_b, high_b):
+    quarter = low_a.shape[1]
+
+    def set_specs(at):
+        far = pl.BlockSpec((None, quarter, LANES), lambda i, w: (w[at], 0, 0))
+        return [pl.BlockSpec((None, quarter, LANES), lambda i, w: (w[at], i, 0)), far, far]
+
+    return pl.pallas_call(
+        here_sum_kernel,
         grid_spec=pltpu.PrefetchScalarGridSpec(
-            num_scalar_prefetch=1, grid=(steps,), in_specs=in_specs, out_specs=out_specs
+            num_scalar_prefetch=1,
+            grid=(2,),
+            in_specs=set_specs(1) + set_specs(0),
+            out_specs=[pl.BlockSpec((quarter, LANES), lambda i, w: (i, 0))] * 2,
         ),
-        out_shape=out_shape,
-        compiler_params=pltpu.CompilerParams(vmem_limit_bytes=VMEM_LIMIT),
-        cost_estimate=cost(16 * half * LANES, 4 * 4 * half * LANES * 3),
-    )(where, own, behind, ahead, far_low.reshape(4, quarter, LANES), far_high.reshape(4, quarter, LANES))
-
-
-def add_kernel(next_part, low, last_part, high, next_out, last_out):
-    next_out[...] = next_part[...] + low[...]
-    last_out[...] = last_part[...] + high[...]
-
-
-def add_far(to_next, low, to_last, high):
-    quarter = low.shape[0]
-    steps = quarter // BLOCK
-    first = pl.BlockSpec((BLOCK, LANES), lambda i: (i, 0))
-    second = pl.BlockSpec((BLOCK, LANES), lambda i: (steps + i, 0))
-    return pl.pallas_call(
-        add_kernel,
-        grid=(steps,),
-        in_specs=[first, first, second, first],
-        out_specs=[first, second],
-        out_shape=[jax.ShapeDtypeStruct(to_next.shape, f32)] * 2,
-        input_output_aliases={0: 0, 2: 1},
-        compiler_params=pltpu.CompilerParams(vmem_limit_bytes=VMEM_LIMIT),
-        cost_estimate=cost(2 * quarter * LANES, 24 * quarter * LANES),
-    )(to_next, low, to_last, high)
+        out_shape=[jax.ShapeDtypeStruct((2 * quarter, LANES), f32)] * 2,
+        compiler_params=pltpu.CompilerParams(vmem_limit_bytes=VMEM_LIMIT),
+        cost_estimate=cost(4 * quarter * LANES, 40 * quarter * LANES),
+    )(zx, base_a, low_a, high_a, base_b, low_b, high_b)
 
 
 def last_sum_kernel(*refs):
@@ -217,7 +236,7 @@
     scaled = clip_factor * gradient
     new_first = beta_first * first + (1.0 - beta_first) * scaled
     new_second = beta_second * second + (1.0 - beta_second) * scaled * scaled
-    direction = new_first / correct_first / (jnp.sqrt(new_second / correct_second) + tiny_eps)
+    direction = (new_first * (1.0 / correct_first)) / (jnp.sqrt(new_second * (1.0 / correct_second)) + tiny_eps)
     new_master = master - learn_rate * (decay_rate * master + direction)
     return (new_master, new_first, new_second)
 
@@ -380,22 +399,20 @@
     zx = jnp.stack([z, x]).astype(jnp.int32)
     xz = jnp.stack([x, z]).astype(jnp.int32)
 
-    own_a, own_b = own_pieces(pieces, zx)
-    sends = pick(pieces, zx, True) + pick(pieces, zx, False)
+    sends = pick(pieces, z, x)
     axes = (Z, Z, X, X)
     ways = (1, 3, 1, 3)
     got = [shift(v, axis, by) for v, axis, by in zip(sends, axes, ways)]
-    far = [shift(v[4:], axis, by) for v, axis, by in zip(got, axes, ways)]
-    set_a = (zx, own_a, got[0], got[1], far[0], far[1])
-    set_b = (xz, own_b, got[2], got[3], far[2], far[3])
-    low_a, high_a = first_sum(*set_a, True)
-    low_b, high_b = first_sum(*set_b, True)
+    far = [shift(v[4:], axis, by).reshape(4, half // 2, LANES) for v, axis, by in zip(got, axes, ways)]
+    base_a = base_sum(zx, pieces, got[0], got[1], True)
+    base_b = base_sum(xz, pieces, got[2], got[3], False)
+    low_a, high_a = far_sum(zx, base_a, far[0], far[1])
+    low_b, high_b = far_sum(xz, base_b, far[2], far[3])
     low_a, high_a = shift(low_a, X, 1), shift(high_a, X, 3)
     low_b, high_b = shift(low_b, Z, 1), shift(high_b, Z, 3)
-    here_a, next_a, last_a = first_sum(*set_a, False)
-    here_b, next_b, last_b = first_sum(*set_b, False)
-    next_a, last_a = add_far(next_a, low_a, last_a, high_a)
-    next_b, last_b = add_far(next_b, low_b, last_b, high_b)
+    next_a, last_a = near_sum(zx, base_a, far[0], far[1], low_a, high_a)
+    next_b, last_b = near_sum(xz, base_b, far[2], far[3], low_b, high_b)
+    here_a, here_b = here_sum(zx, base_a, far[0], far[1], base_b, far[2], far[3])
     parts_a = here_a, shift(next_a, X, 1), shift(last_a, X, 3)
     parts_b = here_b, shift(next_b, Z, 1), shift(last_b, Z, 3)
     devices = lax.axis_size((Z, X, Y, CORE))

time: 161 us -> 159 us (0.988)
    pallas_call x9 -> x8, Pallas kernels: 12.5 us -> 12.2 us  [the longest x2 5.86 us: base_sum(): pl.pallas_call(base_kernel, grid_spec=pltpu.PrefetchScalarGridSpec(num_sc...]
where the time goes in v4:
time: 159 us; the launch traced here: 158 us
  waiting for transfers between devices  70.3 us (44%)
  starting transfers between devices  43.1 us (27%)
  Pallas kernels  26 us (16%)
  blocking collectives  17.6 us (11%)
    ppermute x16, waiting for transfers between devices, shift(): lax.ppermute(value, axis, [(i, (i + by) % size) for i in range(size)])  41.2 us
    ppermute x16, waiting for transfers between devices, partner(): return lax.ppermute(value, axis, [(i, i ^ mask) for i in range(4)])  29.1 us
    ppermute x16, starting transfers between devices, shift(): lax.ppermute(value, axis, [(i, (i + by) % size) for i in range(size)])  27.5 us
    all_to_all x1, blocking collectives, shards(): squares = lax.all_to_all(squares, (Z, X, Y, CORE), 0, 0, tiled=True)  17.6 us
    ppermute x16, starting transfers between devices, partner(): return lax.ppermute(value, axis, [(i, i ^ mask) for i in range(4)])  15.6 us
    pallas_call x5, Pallas kernels, set_blocks(): pl.pallas_call(functools.partial(set_kernel, jobs, len(parts)), in_specs=...  6.41 us
    pallas_call x2, Pallas kernels, base_sum(): pl.pallas_call(base_kernel, grid_spec=pltpu.PrefetchScalarGridSpec(num_sc...  5.86 us
    pallas_call x1, Pallas kernels, both_states(): pl.pallas_call(states_both_kernel, grid=(half // BLOCK,), in_specs=[whole...  3.26 us
  transfers between devices with their start and end apart: 32, of which 12 were waited for; matrix products, arithmetic and copies ran while one was open for 0% of the time, Pallas kernels for 13%

profile of v4, /device:TPU:0, one launch (start us, length us, event | category | flops | bytes accessed | tf_op | source)
XLA Modules:
  0.0 158.4 jit_solution(14106388267648709940)
XLA Ops:
  0.6 2.9 %shard_map.75 = (bf16[6,1024,128]{2,1,0:T(8,128)(2,1)S(1)}, bf16[6,1024,128]{2,1,0:T(8,128)(2,1)S(1)}, bf16[6,1024,128]{2,1,0:T(8,128)(2,1)S(1)}, bf16[6,1024,128]{2,1,0:T(8,128)(2,1)S(1)}) custom-call(s32[1]{0:T(128)} %bitcast.at_z, s32[1]{0:T(128)} %bitcast.1.at_x, bf16[4,4,2048,128]{3,2,1,0:T(8,128)(2,1)} %bitcast.98), custom_call_target="tpu_custom_call" | custom-call | bytes 12582912 | tf_op jit(solution)/shard_map/pallas_call | solution.py:64
  3.6 2.1 %collective-permute-start = (bf16[6,1024,128]{2,1,0:T(8,128)(2,1)S(1)}, bf16[6,1024,128]{2,1,0:T(8,128)(2,1)S(1)}, u32[]{:S(2)}, u32[]{:S(2)}) collective-permute-start(bf16[6,1024,128]{2,1,0:T(8,128)(2,1)S(1)} %get-tuple-element.28), channel_id=1, source_target_pairs={{0,32},{32,64},{64,96},{96,0},{1,33},{33,65},{65,97},{97,1},{2,34}... | collective-permute-start | bytes 4718600 | tf_op jit(solution)/shard_map/ppermute | solution.py:30
  5.6 2.2 %collective-permute-start.1 = (bf16[6,1024,128]{2,1,0:T(8,128)(2,1)S(1)}, bf16[6,1024,128]{2,1,0:T(8,128)(2,1)S(1)}, u32[]{:S(2)}, u32[]{:S(2)}) collective-permute-start(bf16[6,1024,128]{2,1,0:T(8,128)(2,1)S(1)} %get-tuple-element.29), channel_id=1, source_target_pairs={{0,96},{32,0},{64,32},{96,64},{1,97},{33,1},{65,33},{97,65},{2,98}... | collective-permute-start | bytes 4718600 | tf_op jit(solution)/shard_map/ppermute | solution.py:30
  7.8 1.5 collective-permute-start.4
  9.3 1.7 %collective-permute-start.5 = (bf16[6,1024,128]{2,1,0:T(8,128)(2,1)S(1)}, bf16[6,1024,128]{2,1,0:T(8,128)(2,1)S(1)}, u32[]{:S(2)}, u32[]{:S(2)}) collective-permute-start(bf16[6,1024,128]{2,1,0:T(8,128)(2,1)S(1)} %get-tuple-element.31), channel_id=1, source_target_pairs={{0,24},{8,0},{16,8},{24,16},{1,25},{9,1},{17,9},{25,17},{2,26},{10... | collective-permute-start | bytes 4718600 | tf_op jit(solution)/shard_map/ppermute | solution.py:30
  11.1 31.1 %collective-permute-done.behind = bf16[6,1024,128]{2,1,0:T(8,128)(2,1)S(1)} collective-permute-done((bf16[6,1024,128]{2,1,0:T(8,128)(2,1)S(1)}, bf16[6,1024,128]{2,1,0:T(8,128)(2,1)S(1)}, u32[]{:S(2)}, u32[]{:S(2)}) %collective-permute-start) | collective-permute-done | bytes 1572896 | tf_op jit(solution)/shard_map/ppermute | solution.py:30
  42.3 3.3 %collective-permute-start.3 = (bf16[2,1024,128]{2,1,0:T(8,128)(2,1)S(1)}, bf16[2,1024,128]{2,1,0:T(8,128)(2,1)S(1)}, u32[]{:S(2)}, u32[]{:S(2)}) collective-permute-start(bf16[2,1024,128]{2,1,0:T(8,128)(2,1)S(1)} %slice.17), channel_id=1, source_target_pairs={{0,96},{32,0},{64,32},{96,64},{1,97},{33,1},{65,33},{97,65},{2,98}... | collective-permute-start | bytes 1572872 | tf_op jit(solution)/shard_map/ppermute | solution.py:30
  45.6 1.6 collective-permute-start.6
  47.2 1.8 %collective-permute-start.7 = (bf16[2,1024,128]{2,1,0:T(8,128)(2,1)S(1)}, bf16[2,1024,128]{2,1,0:T(8,128)(2,1)S(1)}, u32[]{:S(2)}, u32[]{:S(2)}) collective-permute-start(bf16[2,1024,128]{2,1,0:T(8,128)(2,1)S(1)} %slice.19), channel_id=1, source_target_pairs={{0,24},{8,0},{16,8},{24,16},{1,25},{9,1},{17,9},{25,17},{2,26},{10... | collective-permute-start | bytes 1572872 | tf_op jit(solution)/shard_map/ppermute | solution.py:30
  49.1 2.9 %shard_map.76.refs_0_.base.base_1.base_3 = f32[4,1024,128]{2,1,0:T(8,128)S(1)} custom-call(s32[2]{0:T(128)S(1)} %get-tuple-element.52.where.zx, bf16[4,4,2048,128]{3,2,1,0:T(8,128)(2,1)} %bitcast.99, bf16[6,1024,128]{2,1,0:T(8,128)(2,1)S(1)} %collective-permute-done.behind, bf16[6,1024,128]{2,1,0:T(8,128)(2,1)S(1)} %collective-permute-done.1.ahead), custom_call_target="tpu_custom_call" | custom-call | flops 1048576 | bytes 5242880 | tf_op jit(solution)/shard_map/pallas_call | solution.py:91
  52.1 2.9 %shard_map.77.refs_3_.base.base_1.base_3 = f32[4,1024,128]{2,1,0:T(8,128)S(1)} custom-call(s32[2]{0:T(128)S(1)} %get-tuple-element.53.where, bf16[4,4,2048,128]{3,2,1,0:T(8,128)(2,1)} %bitcast.100, bf16[6,1024,128]{2,1,0:T(8,128)(2,1)S(1)} %collective-permute-done.4.behind, bf16[6,1024,128]{2,1,0:T(8,128)(2,1)S(1)} %collective-permute-done.5.ahead), custom_call_target="tpu_custom_call" | custom-call | flops 1048576 | bytes 5242880 | tf_op jit(solution)/shard_map/pallas_call | solution.py:91
  55.0 1.6 collective-permute-done.2
  57.2 1.6 collective-permute-start.8
  58.8 1.7 %collective-permute-start.9 = (f32[512,128]{1,0:T(8,128)S(1)}, f32[512,128]{1,0:T(8,128)S(1)}, u32[]{:S(2)}, u32[]{:S(2)}) collective-permute-start(f32[512,128]{1,0:T(8,128)S(1)} %get-tuple-element.34), channel_id=1, source_target_pairs={{0,24},{8,0},{16,8},{24,16},{1,25},{9,1},{17,9},{25,17},{2,26},{10... | collective-permute-start | bytes 786440 | tf_op jit(solution)/shard_map/ppermute | solution.py:30
  61.3 3.2 %collective-permute-start.13 = (f32[512,128]{1,0:T(8,128)S(1)}, f32[512,128]{1,0:T(8,128)S(1)}, u32[]{:S(2)}, u32[]{:S(2)}) collective-permute-start(f32[512,128]{1,0:T(8,128)S(1)} %get-tuple-element.39), channel_id=1, source_target_pairs={{0,96},{32,0},{64,32},{96,64},{1,97},{33,1},{65,33},{97,65},{2,98}... | collective-permute-start | bytes 786440 | tf_op jit(solution)/shard_map/ppermute | solution.py:30
  65.2 0.7 shard_map.80
  65.9 1.6 collective-permute-start.10
  67.5 1.7 %collective-permute-start.11 = (f32[1024,128]{1,0:T(8,128)S(1)}, f32[1024,128]{1,0:T(8,128)S(1)}, u32[]{:S(2)}, u32[]{:S(2)}) collective-permute-start(f32[1024,128]{1,0:T(8,128)S(1)} %get-tuple-element.36), channel_id=1, source_target_pairs={{0,24},{8,0},{16,8},{24,16},{1,25},{9,1},{17,9},{25,17},{2,26},{10... | collective-permute-start | bytes 1572872 | tf_op jit(solution)/shard_map/ppermute | solution.py:30
  69.2 0.7 shard_map.82
  70.0 0.9 collective-permute-start.14
  70.9 2.4 %collective-permute-start.15 = (f32[1024,128]{1,0:T(8,128)S(1)}, f32[1024,128]{1,0:T(8,128)S(1)}, u32[]{:S(2)}, u32[]{:S(2)}) collective-permute-start(f32[1024,128]{1,0:T(8,128)S(1)} %get-tuple-element.41), channel_id=1, source_target_pairs={{0,96},{32,0},{64,32},{96,64},{1,97},{33,1},{65,33},{97,65},{2,98}... | collective-permute-start | bytes 1572872 | tf_op jit(solution)/shard_map/ppermute | solution.py:30
  74.0 4.4 %collective-permute-done.10.refs_1_ = f32[1024,128]{1,0:T(8,128)S(1)} collective-permute-done((f32[1024,128]{1,0:T(8,128)S(1)}, f32[1024,128]{1,0:T(8,128)S(1)}, u32[]{:S(2)}, u32[]{:S(2)}) %collective-permute-start.10) | collective-permute-done | bytes 524320 | tf_op jit(solution)/shard_map/ppermute | solution.py:30
  78.4 3.5 %collective-permute-done.14.refs_4_ = f32[1024,128]{1,0:T(8,128)S(1)} collective-permute-done((f32[1024,128]{1,0:T(8,128)S(1)}, f32[1024,128]{1,0:T(8,128)S(1)}, u32[]{:S(2)}, u32[]{:S(2)}) %collective-permute-start.14) | collective-permute-done | bytes 524320 | tf_op jit(solution)/shard_map/ppermute | solution.py:30
  82.2 17.6 %all_to_all.11 = f32[128,1,128]{2,1,0:T(1,128)S(1)} all-to-all(f32[128,1,128]{2,1,0:T(1,128)S(1)} %bitcast.96), channel_id=1, replica_groups=mesh['z'=4,'x'=4,'y'=4,'core'=2] {'z','x','y','core'}, dimensions={0} | all-to-all | bytes 131072 | tf_op jit(solution)/shard_map/all_to_all | solution.py:420
  99.9 1.8 %shard_map.84 = (bf16[512,128]{1,0:T(8,128)(2,1)S(1)}, bf16[512,128]{1,0:T(8,128)(2,1)S(1)}, bf16[512,128]{1,0:T(8,128)(2,1)S(1)}, bf16[512,128]{1,0:T(8,128)(2,1)S(1)}) custom-call(f32[128,128]{1,0:T(8,128)S(1)} %bitcast.86, f32[2,512,128]{2,1,0:T(8,128)S(1)} %bitcast.84, f32[2,512,128]{2,1,0:T(8,128)S(1)} %bitcast.85, f32[4,512,128]{2,1,0:T(8,128)S(1)} %bitcast.78, ...), custom_call_target="tpu_custom_call" | custom-call | flops 10485760 | bytes 4718592 | tf_op jit(solution)/shard_map/pallas_call | solution.py:262
  102.4 0.8 collective-permute-start.28
  103.2 1.1 collective-permute-start.20
  104.3 0.8 collective-permute-start.16
  105.1 1.8 %collective-permute-done.24.two = bf16[1,512,128]{2,1,0:T(8,128)(2,1)S(1)} collective-permute-done((bf16[1,512,128]{2,1,0:T(8,128)(2,1)S(1)}, bf16[1,512,128]{2,1,0:T(8,128)(2,1)S(1)}, u32[]{:S(2)}, u32[]{:S(2)}) %collective-permute-start.24) | collective-permute-done | bytes 131104 | tf_op jit(solution)/shard_map/ppermute | solution.py:307
  107.3 0.8 collective-permute-start.25
  108.4 0.8 collective-permute-start.29
  109.7 2.1 %collective-permute-start.21 = (bf16[2,512,128]{2,1,0:T(8,128)(2,1)S(1)}, bf16[2,512,128]{2,1,0:T(8,128)(2,1)S(1)}, u32[]{:S(2)}, u32[]{:S(2)}) collective-permute-start(bf16[2,512,128]{2,1,0:T(8,128)(2,1)S(1)} %shard_map.88.one), channel_id=1, source_target_pairs={{0,24},{8,16},{16,8},{24,0},{1,25},{9,17},{17,9},{25,1},{2,26},{10... | collective-permute-start | bytes 786440 | tf_op jit(solution)/shard_map/ppermute | solution.py:307
  112.3 3.4 %collective-permute-done.25.two = bf16[2,512,128]{2,1,0:T(8,128)(2,1)S(1)} collective-permute-done((bf16[2,512,128]{2,1,0:T(8,128)(2,1)S(1)}, bf16[2,512,128]{2,1,0:T(8,128)(2,1)S(1)}, u32[]{:S(2)}, u32[]{:S(2)}) %collective-permute-start.25) | collective-permute-done | bytes 262176 | tf_op jit(solution)/shard_map/ppermute | solution.py:307
  115.7 1.4 collective-permute-start.26
  117.2 1.2 collective-permute-start.30
  118.5 1.1 collective-permute-start.22
  119.7 0.8 collective-permute-start.18
  120.5 8.3 %collective-permute-done.26.two = bf16[4,512,128]{2,1,0:T(8,128)(2,1)S(1)} collective-permute-done((bf16[4,512,128]{2,1,0:T(8,128)(2,1)S(1)}, bf16[4,512,128]{2,1,0:T(8,128)(2,1)S(1)}, u32[]{:S(2)}, u32[]{:S(2)}) %collective-permute-start.26) | collective-permute-done | bytes 524320 | tf_op jit(solution)/shard_map/ppermute | solution.py:307
  128.9 0.7 collective-permute-start.27
  130.3 1.9 %collective-permute-start.31 = (bf16[8,512,128]{2,1,0:T(8,128)(2,1)S(1)}, bf16[8,512,128]{2,1,0:T(8,128)(2,1)S(1)}, u32[]{:S(2)}, u32[]{:S(2)}) collective-permute-start(bf16[8,512,128]{2,1,0:T(8,128)(2,1)S(1)} %shard_map.96.refs_0_), channel_id=1, source_target_pairs={{0,24},{8,16},{16,8},{24,0},{1,25},{9,17},{17,9},{25,1},{2,26},{10... | collective-permute-start | bytes 3145736 | tf_op jit(solution)/shard_map/ppermute | solution.py:307
  132.5 1.2 collective-permute-start.19
  133.8 3.3 %shard_map.102 = (f32[2,1024,128]{2,1,0:T(8,128)}, f32[2,1024,128]{2,1,0:T(8,128)}, f32[2,1024,128]{2,1,0:T(8,128)}) custom-call(f32[128,128]{1,0:T(8,128)S(1)} %bitcast.87, f32[1024,128]{1,0:T(8,128)S(1)} %get-tuple-element.43.mean_a, f32[1024,128]{1,0:T(8,128)S(1)} %get-tuple-element.44.mean_b, f32[2,1024,128]{2,1,0:T(8,128)S(1)} %bitcast.79, ...), custom_call_target="tpu_custom_call" | custom-call | flops 5242880 | bytes 7864320 | tf_op jit(solution)/shard_map/pallas_call | solution.py:290
  137.0 2.3 %shard_map.97.refs_1_ = bf16[4,4,4,512,128]{4,3,2,1,0:T(8,128)(2,1)} custom-call(bf16[8,512,128]{2,1,0:T(8,128)(2,1)S(1)} %shard_map.96.refs_0_, bf16[8,512,128]{2,1,0:T(8,128)(2,1)S(1)} %shard_map.93.refs_1_, bf16[8,512,128]{2,1,0:T(8,128)(2,1)S(1)} %shard_map.90.refs_2_, bf16[8,512,128]{2,1,0:T(8,128)(2,1)S(1)} %shard_map.87.refs_3_), custom_call_target="tpu_custom_call" | custom-call | bytes 8388608 | tf_op jit(solution)/shard_map/pallas_call | solution.py:359
  139.3 14.8 %collective-permute-done.31.refs_0_ = bf16[8,512,128]{2,1,0:T(8,128)(2,1)S(1)} collective-permute-done((bf16[8,512,128]{2,1,0:T(8,128)(2,1)S(1)}, bf16[8,512,128]{2,1,0:T(8,128)(2,1)S(1)}, u32[]{:S(2)}, u32[]{:S(2)}) %collective-permute-start.31) | collective-permute-done | bytes 1048608 | tf_op jit(solution)/shard_map/ppermute | solution.py:307
  154.0 1.0 shard_map.98.refs_1_
  155.1 1.0 shard_map.99.refs_1_
  156.1 1.0 shard_map.100.refs_1_
  157.2 1.0 shard_map.101
  (56 shorter events, 7.1 us)
Async XLA Ops:
  3.6 38.6 %collective-permute-start = (bf16[6,1024,128]{2,1,0:T(8,128)(2,1)S(1)}, bf16[6,1024,128]{2,1,0:T(8,128)(2,1)S(1)}, u32[]{:S(2)}, u32[]{:S(2)}) collective-permute-start(bf16[6,1024,128]{2,1,0:T(8,128)(2,1)S(1)} %get-tuple-element.28), channel_id=1, source_target_pairs={{0,32},{32,64},{64,96},{96,0},{1,33},{33,65},{65,97},{97,1},{2,34}... | collective-permute-start | bytes 4718600 | tf_op jit(solution)/shard_map/ppermute | solution.py:30
  5.6 36.6 %collective-permute-start.1 = (bf16[6,1024,128]{2,1,0:T(8,128)(2,1)S(1)}, bf16[6,1024,128]{2,1,0:T(8,128)(2,1)S(1)}, u32[]{:S(2)}, u32[]{:S(2)}) collective-permute-start(bf16[6,1024,128]{2,1,0:T(8,128)(2,1)S(1)} %get-tuple-element.29), channel_id=1, source_target_pairs={{0,96},{32,0},{64,32},{96,64},{1,97},{33,1},{65,33},{97,65},{2,98}... | collective-permute-start | bytes 4718600 | tf_op jit(solution)/shard_map/ppermute | solution.py:30
  7.8 37.8 %collective-permute-start.4 = (bf16[6,1024,128]{2,1,0:T(8,128)(2,1)S(1)}, bf16[6,1024,128]{2,1,0:T(8,128)(2,1)S(1)}, u32[]{:S(2)}, u32[]{:S(2)}) collective-permute-start(bf16[6,1024,128]{2,1,0:T(8,128)(2,1)S(1)} %get-tuple-element.30), channel_id=1, source_target_pairs={{0,8},{8,16},{16,24},{24,0},{1,9},{9,17},{17,25},{25,1},{2,10},{10... | collective-permute-start | bytes 4718600 | tf_op jit(solution)/shard_map/ppermute | solution.py:30
  9.3 37.9 %collective-permute-start.5 = (bf16[6,1024,128]{2,1,0:T(8,128)(2,1)S(1)}, bf16[6,1024,128]{2,1,0:T(8,128)(2,1)S(1)}, u32[]{:S(2)}, u32[]{:S(2)}) collective-permute-start(bf16[6,1024,128]{2,1,0:T(8,128)(2,1)S(1)} %get-tuple-element.31), channel_id=1, source_target_pairs={{0,24},{8,0},{16,8},{24,16},{1,25},{9,1},{17,9},{25,17},{2,26},{10... | collective-permute-start | bytes 4718600 | tf_op jit(solution)/shard_map/ppermute | solution.py:30
  42.2 14.4 %collective-permute-start.2 = (bf16[2,1024,128]{2,1,0:T(8,128)(2,1)S(1)}, bf16[2,1024,128]{2,1,0:T(8,128)(2,1)S(1)}, u32[]{:S(2)}, u32[]{:S(2)}) collective-permute-start(bf16[2,1024,128]{2,1,0:T(8,128)(2,1)S(1)} %slice.16), channel_id=1, source_target_pairs={{0,32},{32,64},{64,96},{96,0},{1,33},{33,65},{65,97},{97,1},{2,34}... | collective-permute-start | bytes 1572872 | tf_op jit(solution)/shard_map/ppermute | solution.py:30
  42.3 14.3 %collective-permute-start.3 = (bf16[2,1024,128]{2,1,0:T(8,128)(2,1)S(1)}, bf16[2,1024,128]{2,1,0:T(8,128)(2,1)S(1)}, u32[]{:S(2)}, u32[]{:S(2)}) collective-permute-start(bf16[2,1024,128]{2,1,0:T(8,128)(2,1)S(1)} %slice.17), channel_id=1, source_target_pairs={{0,96},{32,0},{64,32},{96,64},{1,97},{33,1},{65,33},{97,65},{2,98}... | collective-permute-start | bytes 1572872 | tf_op jit(solution)/shard_map/ppermute | solution.py:30
  45.6 14.9 %collective-permute-start.6 = (bf16[2,1024,128]{2,1,0:T(8,128)(2,1)S(1)}, bf16[2,1024,128]{2,1,0:T(8,128)(2,1)S(1)}, u32[]{:S(2)}, u32[]{:S(2)}) collective-permute-start(bf16[2,1024,128]{2,1,0:T(8,128)(2,1)S(1)} %slice.18), channel_id=1, source_target_pairs={{0,8},{8,16},{16,24},{24,0},{1,9},{9,17},{17,25},{25,1},{2,10},{10... | collective-permute-start | bytes 1572872 | tf_op jit(solution)/shard_map/ppermute | solution.py:30
  47.2 13.3 %collective-permute-start.7 = (bf16[2,1024,128]{2,1,0:T(8,128)(2,1)S(1)}, bf16[2,1024,128]{2,1,0:T(8,128)(2,1)S(1)}, u32[]{:S(2)}, u32[]{:S(2)}) collective-permute-start(bf16[2,1024,128]{2,1,0:T(8,128)(2,1)S(1)} %slice.19), channel_id=1, source_target_pairs={{0,24},{8,0},{16,8},{24,16},{1,25},{9,1},{17,9},{25,17},{2,26},{10... | collective-permute-start | bytes 1572872 | tf_op jit(solution)/shard_map/ppermute | solution.py:30
  57.2 7.9 %collective-permute-start.8 = (f32[512,128]{1,0:T(8,128)S(1)}, f32[512,128]{1,0:T(8,128)S(1)}, u32[]{:S(2)}, u32[]{:S(2)}) collective-permute-start(f32[512,128]{1,0:T(8,128)S(1)} %get-tuple-element.33), channel_id=1, source_target_pairs={{0,8},{8,16},{16,24},{24,0},{1,9},{9,17},{17,25},{25,1},{2,10},{10... | collective-permute-start | bytes 786440 | tf_op jit(solution)/shard_map/ppermute | solution.py:30
  58.8 6.4 %collective-permute-start.9 = (f32[512,128]{1,0:T(8,128)S(1)}, f32[512,128]{1,0:T(8,128)S(1)}, u32[]{:S(2)}, u32[]{:S(2)}) collective-permute-start(f32[512,128]{1,0:T(8,128)S(1)} %get-tuple-element.34), channel_id=1, source_target_pairs={{0,24},{8,0},{16,8},{24,16},{1,25},{9,1},{17,9},{25,17},{2,26},{10... | collective-permute-start | bytes 786440 | tf_op jit(solution)/shard_map/ppermute | solution.py:30
  61.2 8.0 %collective-permute-start.12 = (f32[512,128]{1,0:T(8,128)S(1)}, f32[512,128]{1,0:T(8,128)S(1)}, u32[]{:S(2)}, u32[]{:S(2)}) collective-permute-start(f32[512,128]{1,0:T(8,128)S(1)} %get-tuple-element.38), channel_id=1, source_target_pairs={{0,32},{32,64},{64,96},{96,0},{1,33},{33,65},{65,97},{97,1},{2,34}... | collective-permute-start | bytes 786440 | tf_op jit(solution)/shard_map/ppermute | solution.py:30
  61.3 8.0 %collective-permute-start.13 = (f32[512,128]{1,0:T(8,128)S(1)}, f32[512,128]{1,0:T(8,128)S(1)}, u32[]{:S(2)}, u32[]{:S(2)}) collective-permute-start(f32[512,128]{1,0:T(8,128)S(1)} %get-tuple-element.39), channel_id=1, source_target_pairs={{0,96},{32,0},{64,32},{96,64},{1,97},{33,1},{65,33},{97,65},{2,98}... | collective-permute-start | bytes 786440 | tf_op jit(solution)/shard_map/ppermute | solution.py:30
  65.9 12.4 %collective-permute-start.10 = (f32[1024,128]{1,0:T(8,128)S(1)}, f32[1024,128]{1,0:T(8,128)S(1)}, u32[]{:S(2)}, u32[]{:S(2)}) collective-permute-start(f32[1024,128]{1,0:T(8,128)S(1)} %get-tuple-element.35), channel_id=1, source_target_pairs={{0,8},{8,16},{16,24},{24,0},{1,9},{9,17},{17,25},{25,1},{2,10},{10... | collective-permute-start | bytes 1572872 | tf_op jit(solution)/shard_map/ppermute | solution.py:30
  67.5 10.9 %collective-permute-start.11 = (f32[1024,128]{1,0:T(8,128)S(1)}, f32[1024,128]{1,0:T(8,128)S(1)}, u32[]{:S(2)}, u32[]{:S(2)}) collective-permute-start(f32[1024,128]{1,0:T(8,128)S(1)} %get-tuple-element.36), channel_id=1, source_target_pairs={{0,24},{8,0},{16,8},{24,16},{1,25},{9,1},{17,9},{25,17},{2,26},{10... | collective-permute-start | bytes 1572872 | tf_op jit(solution)/shard_map/ppermute | solution.py:30
  70.0 11.9 %collective-permute-start.14 = (f32[1024,128]{1,0:T(8,128)S(1)}, f32[1024,128]{1,0:T(8,128)S(1)}, u32[]{:S(2)}, u32[]{:S(2)}) collective-permute-start(f32[1024,128]{1,0:T(8,128)S(1)} %get-tuple-element.40), channel_id=1, source_target_pairs={{0,32},{32,64},{64,96},{96,0},{1,33},{33,65},{65,97},{97,1},{2,34}... | collective-permute-start | bytes 1572872 | tf_op jit(solution)/shard_map/ppermute | solution.py:30
  70.9 11.0 %collective-permute-start.15 = (f32[1024,128]{1,0:T(8,128)S(1)}, f32[1024,128]{1,0:T(8,128)S(1)}, u32[]{:S(2)}, u32[]{:S(2)}) collective-permute-start(f32[1024,128]{1,0:T(8,128)S(1)} %get-tuple-element.41), channel_id=1, source_target_pairs={{0,96},{32,0},{64,32},{96,64},{1,97},{33,1},{65,33},{97,65},{2,98}... | collective-permute-start | bytes 1572872 | tf_op jit(solution)/shard_map/ppermute | solution.py:30
  74.0 25.9 %copy-start = (f32[1,4,65536]{2,1,0:T(4,128)S(1)}, f32[1,4,65536]{2,1,0:T(4,128)}, u32[]{:S(2)}) copy-start(f32[1,4,65536]{2,1,0:T(4,128)} %param.5) | copy-start | bytes 3145732
  74.0 25.9 %copy-start.1 = (f32[1,4,65536]{2,1,0:T(4,128)S(1)}, f32[1,4,65536]{2,1,0:T(4,128)}, u32[]{:S(2)}) copy-start(f32[1,4,65536]{2,1,0:T(4,128)} %param.6) | copy-start | bytes 3145732
  74.0 25.9 %copy-start.2 = (f32[1,4,65536]{2,1,0:T(4,128)S(1)}, f32[1,4,65536]{2,1,0:T(4,128)}, u32[]{:S(2)}) copy-start(f32[1,4,65536]{2,1,0:T(4,128)} %param.7) | copy-start | bytes 3145732
  101.7 5.2 %collective-permute-start.24 = (bf16[1,512,128]{2,1,0:T(8,128)(2,1)S(1)}, bf16[1,512,128]{2,1,0:T(8,128)(2,1)S(1)}, u32[]{:S(2)}, u32[]{:S(2)}) collective-permute-start(bf16[1,512,128]{2,1,0:T(8,128)(2,1)S(1)} %bitcast.94), channel_id=1, source_target_pairs={{0,8},{8,0},{16,24},{24,16},{1,9},{9,1},{17,25},{25,17},{2,10},{10... | collective-permute-start | bytes 393224 | tf_op jit(solution)/shard_map/ppermute | solution.py:307
  102.4 5.7 %collective-permute-start.28 = (bf16[1,512,128]{2,1,0:T(8,128)(2,1)S(1)}, bf16[1,512,128]{2,1,0:T(8,128)(2,1)S(1)}, u32[]{:S(2)}, u32[]{:S(2)}) collective-permute-start(bf16[1,512,128]{2,1,0:T(8,128)(2,1)S(1)} %bitcast.92), channel_id=1, source_target_pairs={{0,32},{32,0},{64,96},{96,64},{1,33},{33,1},{65,97},{97,65},{2,34}... | collective-permute-start | bytes 393224 | tf_op jit(solution)/shard_map/ppermute | solution.py:307
  103.2 6.2 %collective-permute-start.20 = (bf16[1,512,128]{2,1,0:T(8,128)(2,1)S(1)}, bf16[1,512,128]{2,1,0:T(8,128)(2,1)S(1)}, u32[]{:S(2)}, u32[]{:S(2)}) collective-permute-start(bf16[1,512,128]{2,1,0:T(8,128)(2,1)S(1)} %bitcast.90), channel_id=1, source_target_pairs={{0,96},{32,64},{64,32},{96,0},{1,97},{33,65},{65,33},{97,1},{2,98}... | collective-permute-start | bytes 393224 | tf_op jit(solution)/shard_map/ppermute | solution.py:307
  104.3 7.5 %collective-permute-start.16 = (bf16[1,512,128]{2,1,0:T(8,128)(2,1)S(1)}, bf16[1,512,128]{2,1,0:T(8,128)(2,1)S(1)}, u32[]{:S(2)}, u32[]{:S(2)}) collective-permute-start(bf16[1,512,128]{2,1,0:T(8,128)(2,1)S(1)} %bitcast.88), channel_id=1, source_target_pairs={{0,24},{8,16},{16,8},{24,0},{1,25},{9,17},{17,9},{25,1},{2,26},{10... | collective-permute-start | bytes 393224 | tf_op jit(solution)/shard_map/ppermute | solution.py:307
  107.3 8.4 %collective-permute-start.25 = (bf16[2,512,128]{2,1,0:T(8,128)(2,1)S(1)}, bf16[2,512,128]{2,1,0:T(8,128)(2,1)S(1)}, u32[]{:S(2)}, u32[]{:S(2)}) collective-permute-start(bf16[2,512,128]{2,1,0:T(8,128)(2,1)S(1)} %shard_map.91.one), channel_id=1, source_target_pairs={{0,96},{32,64},{64,32},{96,0},{1,97},{33,65},{65,33},{97,1},{2,98}... | collective-permute-start | bytes 786440 | tf_op jit(solution)/shard_map/ppermute | solution.py:307
  108.4 8.7 %collective-permute-start.29 = (bf16[2,512,128]{2,1,0:T(8,128)(2,1)S(1)}, bf16[2,512,128]{2,1,0:T(8,128)(2,1)S(1)}, u32[]{:S(2)}, u32[]{:S(2)}) collective-permute-start(bf16[2,512,128]{2,1,0:T(8,128)(2,1)S(1)} %shard_map.94.one), channel_id=1, source_target_pairs={{0,8},{8,0},{16,24},{24,16},{1,9},{9,1},{17,25},{25,17},{2,10},{10... | collective-permute-start | bytes 786440 | tf_op jit(solution)/shard_map/ppermute | solution.py:307
  109.7 8.7 %collective-permute-start.21 = (bf16[2,512,128]{2,1,0:T(8,128)(2,1)S(1)}, bf16[2,512,128]{2,1,0:T(8,128)(2,1)S(1)}, u32[]{:S(2)}, u32[]{:S(2)}) collective-permute-start(bf16[2,512,128]{2,1,0:T(8,128)(2,1)S(1)} %shard_map.88.one), channel_id=1, source_target_pairs={{0,24},{8,16},{16,8},{24,0},{1,25},{9,17},{17,9},{25,1},{2,26},{10... | collective-permute-start | bytes 786440 | tf_op jit(solution)/shard_map/ppermute | solution.py:307
  112.2 7.4 %collective-permute-start.17 = (bf16[2,512,128]{2,1,0:T(8,128)(2,1)S(1)}, bf16[2,512,128]{2,1,0:T(8,128)(2,1)S(1)}, u32[]{:S(2)}, u32[]{:S(2)}) collective-permute-start(bf16[2,512,128]{2,1,0:T(8,128)(2,1)S(1)} %shard_map.85.one), channel_id=1, source_target_pairs={{0,32},{32,0},{64,96},{96,64},{1,33},{33,1},{65,97},{97,65},{2,34}... | collective-permute-start | bytes 786440 | tf_op jit(solution)/shard_map/ppermute | solution.py:307
  115.7 13.1 %collective-permute-start.26 = (bf16[4,512,128]{2,1,0:T(8,128)(2,1)S(1)}, bf16[4,512,128]{2,1,0:T(8,128)(2,1)S(1)}, u32[]{:S(2)}, u32[]{:S(2)}) collective-permute-start(bf16[4,512,128]{2,1,0:T(8,128)(2,1)S(1)} %shard_map.92.one), channel_id=1, source_target_pairs={{0,24},{8,16},{16,8},{24,0},{1,25},{9,17},{17,9},{25,1},{2,26},{10... | collective-permute-start | bytes 1572872 | tf_op jit(solution)/shard_map/ppermute | solution.py:307
  117.2 13.1 %collective-permute-start.30 = (bf16[4,512,128]{2,1,0:T(8,128)(2,1)S(1)}, bf16[4,512,128]{2,1,0:T(8,128)(2,1)S(1)}, u32[]{:S(2)}, u32[]{:S(2)}) collective-permute-start(bf16[4,512,128]{2,1,0:T(8,128)(2,1)S(1)} %shard_map.95.one), channel_id=1, source_target_pairs={{0,96},{32,64},{64,32},{96,0},{1,97},{33,65},{65,33},{97,1},{2,98}... | collective-permute-start | bytes 1572872 | tf_op jit(solution)/shard_map/ppermute | solution.py:307
  118.5 13.7 %collective-permute-start.22 = (bf16[4,512,128]{2,1,0:T(8,128)(2,1)S(1)}, bf16[4,512,128]{2,1,0:T(8,128)(2,1)S(1)}, u32[]{:S(2)}, u32[]{:S(2)}) collective-permute-start(bf16[4,512,128]{2,1,0:T(8,128)(2,1)S(1)} %shard_map.89.one), channel_id=1, source_target_pairs={{0,32},{32,0},{64,96},{96,64},{1,33},{33,1},{65,97},{97,65},{2,34}... | collective-permute-start | bytes 1572872 | tf_op jit(solution)/shard_map/ppermute | solution.py:307
  119.7 12.8 %collective-permute-start.18 = (bf16[4,512,128]{2,1,0:T(8,128)(2,1)S(1)}, bf16[4,512,128]{2,1,0:T(8,128)(2,1)S(1)}, u32[]{:S(2)}, u32[]{:S(2)}) collective-permute-start(bf16[4,512,128]{2,1,0:T(8,128)(2,1)S(1)} %shard_map.86.one), channel_id=1, source_target_pairs={{0,8},{8,0},{16,24},{24,16},{1,9},{9,1},{17,25},{25,17},{2,10},{10... | collective-permute-start | bytes 1572872 | tf_op jit(solution)/shard_map/ppermute | solution.py:307
  128.9 26.2 %collective-permute-start.27 = (bf16[8,512,128]{2,1,0:T(8,128)(2,1)S(1)}, bf16[8,512,128]{2,1,0:T(8,128)(2,1)S(1)}, u32[]{:S(2)}, u32[]{:S(2)}) collective-permute-start(bf16[8,512,128]{2,1,0:T(8,128)(2,1)S(1)} %shard_map.93.refs_1_), channel_id=1, source_target_pairs={{0,32},{32,0},{64,96},{96,64},{1,33},{33,1},{65,97},{97,65},{2,34}... | collective-permute-start | bytes 3145736 | tf_op jit(solution)/shard_map/ppermute | solution.py:307
  130.3 23.7 %collective-permute-start.31 = (bf16[8,512,128]{2,1,0:T(8,128)(2,1)S(1)}, bf16[8,512,128]{2,1,0:T(8,128)(2,1)S(1)}, u32[]{:S(2)}, u32[]{:S(2)}) collective-permute-start(bf16[8,512,128]{2,1,0:T(8,128)(2,1)S(1)} %shard_map.96.refs_0_), channel_id=1, source_target_pairs={{0,24},{8,16},{16,8},{24,0},{1,25},{9,17},{17,9},{25,1},{2,26},{10... | collective-permute-start | bytes 3145736 | tf_op jit(solution)/shard_map/ppermute | solution.py:307
  132.3 23.8 %collective-permute-start.23 = (bf16[8,512,128]{2,1,0:T(8,128)(2,1)S(1)}, bf16[8,512,128]{2,1,0:T(8,128)(2,1)S(1)}, u32[]{:S(2)}, u32[]{:S(2)}) collective-permute-start(bf16[8,512,128]{2,1,0:T(8,128)(2,1)S(1)} %shard_map.90.refs_2_), channel_id=1, source_target_pairs={{0,8},{8,0},{16,24},{24,16},{1,9},{9,1},{17,25},{25,17},{2,10},{10... | collective-permute-start | bytes 3145736 | tf_op jit(solution)/shard_map/ppermute | solution.py:307
  132.5 24.7 %collective-permute-start.19 = (bf16[8,512,128]{2,1,0:T(8,128)(2,1)S(1)}, bf16[8,512,128]{2,1,0:T(8,128)(2,1)S(1)}, u32[]{:S(2)}, u32[]{:S(2)}) collective-permute-start(bf16[8,512,128]{2,1,0:T(8,128)(2,1)S(1)} %shard_map.87.refs_3_), channel_id=1, source_target_pairs={{0,96},{32,64},{64,32},{96,0},{1,97},{33,65},{65,33},{97,1},{2,98}... | collective-permute-start | bytes 3145736 | tf_op jit(solution)/shard_map/ppermute | solution.py:307

commit v5 on v4

--- a/solution.py
+++ b/solution.py
@@ -21,6 +21,7 @@
 
 LANES = 128
 BLOCK = 256
+CHUNK = 64
 VMEM_LIMIT = 12 * 2**20
 f32, bf16 = jnp.float32, jnp.bfloat16
 
@@ -99,132 +100,113 @@
     )(where, pltpu.with_memory_space_constraint(pieces, pltpu.HBM), behind, ahead)
 
 
-def on_half(low_part, high_part):
-    pl.when(pl.program_id(0) < pl.num_programs(0) // 2)(low_part)
-    pl.when(pl.program_id(0) >= pl.num_programs(0) // 2)(high_part)
-
-
-def far_sum_kernel(where, base, far_low, far_high, low, high):
-    def low_part():
-        low[...] = base[...] + far_low[...].astype(f32)
-
-    def high_part():
-        high[...] = base[...] + far_high[...].astype(f32)
-
-    on_half(low_part, high_part)
-
-
-def far_sum(where, base, far_low, far_high):
+def chunks_of(size):
+    def run(body):
+        @pl.loop(0, size // CHUNK)
+        def _(i):
+            body(pl.multiple_of(i * CHUNK, CHUNK))
+
+    return run
+
+
+def far_sum_kernel(axis, base, far_low, far_high, low, high):
+    quarter = low.shape[0]
+    at = lax.rem(lax.axis_index(axis) + 2, 4)
+
+    @chunks_of(quarter)
+    def _(start):
+        rows, upper = pl.ds(start, CHUNK), pl.ds(quarter + start, CHUNK)
+        low[rows] = base[at, rows] + far_low[at, rows].astype(f32)
+        high[rows] = base[at, upper] + far_high[at, rows].astype(f32)
+
+
+def far_sum(axis, base, far_low, far_high):
     quarter = far_low.shape[1]
-    out = pl.BlockSpec((quarter, LANES), lambda i, w: (0, 0))
-    far = pl.BlockSpec((None, quarter, LANES), lambda i, w: (lax.rem(w[1] + 2, 4), 0, 0))
-    return pl.pallas_call(
-        far_sum_kernel,
-        grid_spec=pltpu.PrefetchScalarGridSpec(
-            num_scalar_prefetch=1,
-            grid=(2,),
-            in_specs=[pl.BlockSpec((None, quarter, LANES), lambda i, w: (lax.rem(w[1] + 2, 4), i, 0)), far, far],
-            out_specs=[out, out],
-        ),
+    here = pl.BlockSpec(memory_space=pltpu.VMEM)
+    return pl.pallas_call(
+        functools.partial(far_sum_kernel, axis),
+        in_specs=[here] * 3,
+        out_specs=[here] * 2,
         out_shape=[jax.ShapeDtypeStruct((quarter, LANES), f32)] * 2,
         compiler_params=pltpu.CompilerParams(vmem_limit_bytes=VMEM_LIMIT),
         cost_estimate=cost(2 * quarter * LANES, 20 * quarter * LANES),
-    )(where, base, far_low, far_high)
-
-
-def near_sum_kernel(where, base_1, base_3, low_1, low_3, high_1, high_3, came_low, came_high, to_next, to_last):
-    def low_part():
-        to_next[...] = base_1[...] + low_1[...].astype(f32) + came_low[...]
-        to_last[...] = base_3[...] + low_3[...].astype(f32)
-
-    def high_part():
-        to_next[...] = base_1[...] + high_1[...].astype(f32)
-        to_last[...] = base_3[...] + high_3[...].astype(f32) + came_high[...]
-
-    on_half(low_part, high_part)
-
-
-def near_sum(where, base, far_low, far_high, came_low, came_high):
+    )(base, far_low, far_high)
+
+
+def near_sum_kernel(axis, base, far_low, far_high, came_low, came_high, to_next, to_last):
+    quarter = came_low.shape[0]
+    after = lax.rem(lax.axis_index(axis) + 1, 4)
+    before = lax.rem(lax.axis_index(axis) + 3, 4)
+
+    @chunks_of(quarter)
+    def _(start):
+        rows, upper = pl.ds(start, CHUNK), pl.ds(quarter + start, CHUNK)
+        to_next[rows] = base[after, rows] + far_low[after, rows].astype(f32) + came_low[rows]
+        to_next[upper] = base[after, upper] + far_high[after, rows].astype(f32)
+        to_last[rows] = base[before, rows] + far_low[before, rows].astype(f32)
+        to_last[upper] = base[before, upper] + far_high[before, rows].astype(f32) + came_high[rows]
+
+
+def near_sum(axis, base, far_low, far_high, came_low, came_high):
     quarter = far_low.shape[1]
-    whole = pl.BlockSpec((quarter, LANES), lambda i, w: (0, 0))
-    out = pl.BlockSpec((quarter, LANES), lambda i, w: (i, 0))
-
-    def base_at(by):
-        return pl.BlockSpec((None, quarter, LANES), lambda i, w: (lax.rem(w[1] + by, 4), i, 0))
-
-    def far_at(by):
-        return pl.BlockSpec((None, quarter, LANES), lambda i, w: (lax.rem(w[1] + by, 4), 0, 0))
-
-    return pl.pallas_call(
-        near_sum_kernel,
-        grid_spec=pltpu.PrefetchScalarGridSpec(
-            num_scalar_prefetch=1,
-            grid=(2,),
-            in_specs=[base_at(1), base_at(3), far_at(1), far_at(3), far_at(1), far_at(3), whole, whole],
-            out_specs=[out, out],
-        ),
+    here = pl.BlockSpec(memory_space=pltpu.VMEM)
+    return pl.pallas_call(
+        functools.partial(near_sum_kernel, axis),
+        in_specs=[here] * 5,
+        out_specs=[here] * 2,
         out_shape=[jax.ShapeDtypeStruct((2 * quarter, LANES), f32)] * 2,
         compiler_params=pltpu.CompilerParams(vmem_limit_bytes=VMEM_LIMIT),
         cost_estimate=cost(10 * quarter * LANES, 48 * quarter * LANES),
-    )(where, base, base, far_low, far_low, far_high, far_high, came_low, came_high)
-
-
-def here_sum_kernel(zx, *refs):
-    sets, outs = (refs[:3], refs[3:6]), refs[6:]
-
-    def add(which):
-        for parts, out in zip(sets, outs):
-            out[...] = parts[0][...] + parts[which][...].astype(f32)
-
-    on_half(lambda: add(1), lambda: add(2))
-
-
-def here_sum(zx, base_a, low_a, high_a, base_b, low_b, high_b):
+    )(base, far_low, far_high, came_low, came_high)
+
+
+def here_sum_kernel(*refs):
+    for axis, (base, far_low, far_high), out in zip((X, Z), (refs[:3], refs[3:6]), refs[6:]):
+        quarter = far_low.shape[1]
+        at = lax.axis_index(axis)
+
+        @chunks_of(quarter)
+        def _(start):
+            rows, upper = pl.ds(start, CHUNK), pl.ds(quarter + start, CHUNK)
+            out[rows] = base[at, rows] + far_low[at, rows].astype(f32)
+            out[upper] = base[at, upper] + far_high[at, rows].astype(f32)
+
+
+def here_sum(base_a, low_a, high_a, base_b, low_b, high_b):
     quarter = low_a.shape[1]
-
-    def set_specs(at):
-        far = pl.BlockSpec((None, quarter, LANES), lambda i, w: (w[at], 0, 0))
-        return [pl.BlockSpec((None, quarter, LANES), lambda i, w: (w[at], i, 0)), far, far]
-
+    here = pl.BlockSpec(memory_space=pltpu.VMEM)
     return pl.pallas_call(
         here_sum_kernel,
-        grid_spec=pltpu.PrefetchScalarGridSpec(
-            num_scalar_prefetch=1,
-            grid=(2,),
-            in_specs=set_specs(1) + set_specs(0),
-            out_specs=[pl.BlockSpec((quarter, LANES), lambda i, w: (i, 0))] * 2,
-        ),
+        in_specs=[here] * 6,
+        out_specs=[here] * 2,
         out_shape=[jax.ShapeDtypeStruct((2 * quarter, LANES), f32)] * 2,
         compiler_params=pltpu.CompilerParams(vmem_limit_bytes=VMEM_LIMIT),
         cost_estimate=cost(4 * quarter * LANES, 40 * quarter * LANES),
-    )(zx, base_a, low_a, high_a, base_b, low_b, high_b)
+    )(base_a, low_a, high_a, base_b, low_b, high_b)
 
 
 def last_sum_kernel(*refs):
     parts_a, parts_b, (mean_a, mean_b, squares, held) = refs[:3], refs[3:6], refs[6:]
-
-    @pl.when(pl.program_id(0) == 0)
-    def _():
-        held[...] = jnp.zeros_like(held)
-
-    for parts, mean in ((parts_a, mean_a), (parts_b, mean_b)):
-        total = (parts[0][...] + parts[1][...] + parts[2][...]) * (1.0 / 16.0)
-        mean[...] = total
-        held[...] += jnp.sum((total * total).reshape(BLOCK // 8, 8, LANES), axis=0)
-
-    @pl.when(pl.program_id(0) == pl.num_programs(0) - 1)
-    def _():
-        squares[...] = jnp.broadcast_to(jnp.sum(held[...], axis=0, keepdims=True), squares.shape)
+    held[...] = jnp.zeros_like(held)
+
+    @chunks_of(mean_a.shape[0])
+    def _(start):
+        rows = pl.ds(start, CHUNK)
+        for parts, mean in ((parts_a, mean_a), (parts_b, mean_b)):
+            total = (parts[0][rows] + parts[1][rows] + parts[2][rows]) * (1.0 / 16.0)
+            mean[rows] = total
+            held[...] += jnp.sum((total * total).reshape(CHUNK // 8, 8, LANES), axis=0)
+
+    squares[...] = jnp.broadcast_to(jnp.sum(held[...], axis=0, keepdims=True), squares.shape)
 
 
 def last_sum(parts_a, parts_b, devices):
     half = parts_a[0].shape[0]
-    block = pl.BlockSpec((BLOCK, LANES), lambda i: (i, 0))
+    here = pl.BlockSpec(memory_space=pltpu.VMEM)
     return pl.pallas_call(
         last_sum_kernel,
-        grid=(half // BLOCK,),
-        in_specs=[block] * 6,
-        out_specs=[block, block, pl.BlockSpec((devices, LANES), lambda i: (0, 0))],
+        in_specs=[here] * 6,
+        out_specs=[here] * 3,
         out_shape=[jax.ShapeDtypeStruct((half, LANES), f32)] * 2 + [jax.ShapeDtypeStruct((devices, LANES), f32)],
         scratch_shapes=[pltpu.VMEM((8, LANES), f32)],
         compiler_params=pltpu.CompilerParams(vmem_limit_bytes=VMEM_LIMIT),
@@ -248,30 +230,30 @@
 
 def params_kernel(squares, mean_a, mean_b, master, first, second, *outs):
     clip_factor = clip_of(squares)
+    quarter = outs[0].shape[0]
     for at, out in enumerate(outs):
         mean = (mean_a, mean_b)[at // 2]
-        new_master, _, _ = adam_update(mean[at % 2], master[at], first[at], second[at], clip_factor)
-        out[...] = new_master.astype(bf16)
+
+        @pl.loop(0, quarter // CHUNK)
+        def _(i):
+            rows = pl.ds(pl.multiple_of(at * quarter + i * CHUNK, CHUNK), CHUNK)
+            mean_rows = pl.ds(pl.multiple_of(at % 2 * quarter + i * CHUNK, CHUNK), CHUNK)
+            new_master, _, _ = adam_update(mean[mean_rows], master[rows], first[rows], second[rows], clip_factor)
+            out[pl.ds(pl.multiple_of(i * CHUNK, CHUNK), CHUNK)] = new_master.astype(bf16)
 
 
 def new_params(squares, means, states):
     quarter = means[0].shape[0] // 2
-    whole = pl.BlockSpec(squares.shape, lambda i: (0, 0))
-    two = pl.BlockSpec((2, BLOCK, LANES), lambda i: (0, i, 0))
-    four = pl.BlockSpec((4, BLOCK, LANES), lambda i: (0, i, 0))
+    here = pl.BlockSpec(memory_space=pltpu.VMEM)
+    operands = [value for value in (squares, *means, *states)]
     return pl.pallas_call(
         params_kernel,
-        grid=(quarter // BLOCK,),
-        in_specs=[whole, two, two, four, four, four],
-        out_specs=[pl.BlockSpec((BLOCK, LANES), lambda i: (i, 0))] * 4,
+        in_specs=[here] * 6,
+        out_specs=[here] * 4,
         out_shape=[jax.ShapeDtypeStruct((quarter, LANES), bf16)] * 4,
         compiler_params=pltpu.CompilerParams(vmem_limit_bytes=VMEM_LIMIT),
         cost_estimate=cost(160 * quarter * LANES, 72 * quarter * LANES),
-    )(
-        squares,
-        *(m.reshape(2, quarter, LANES) for m in means),
-        *(s.reshape(4, quarter, LANES) for s in states),
-    )
+    )(*operands)
 
 
 def states_both_kernel(squares, mean_a, mean_b, master, first, second, *outs):
@@ -307,25 +289,19 @@
     return lax.ppermute(value, axis, [(i, i ^ mask) for i in range(4)])
 
 
-def join_kernel(one, two, out, sems):
+def join_kernel(one, two, out):
     size = one.shape[0]
-    copies = [
-        pltpu.make_async_copy(one, out.at[pl.ds(0, size)], sems.at[0]),
-        pltpu.make_async_copy(two, out.at[pl.ds(size, size)], sems.at[1]),
-    ]
-    for copy in copies:
-        copy.start()
-    for copy in copies:
-        copy.wait()
+    for i in range(size):
+        out[i] = one[i]
+        out[size + i] = two[i]
 
 
 def join(one, two):
-    any_ = pl.BlockSpec(memory_space=pl.ANY)
+    here = pl.BlockSpec(memory_space=pltpu.VMEM)
     return pl.pallas_call(
         join_kernel,
-        in_specs=[any_, any_],
-        out_specs=any_,
-        scratch_shapes=[pltpu.SemaphoreType.DMA((2,))],
+        in_specs=[here, here],
+        out_specs=here,
         out_shape=jax.ShapeDtypeStruct((2 * one.shape[0],) + one.shape[1:], one.dtype),
         compiler_params=pltpu.CompilerParams(vmem_limit_bytes=VMEM_LIMIT),
         cost_estimate=cost(0, 4 * one.size),
@@ -406,13 +382,13 @@
     far = [shift(v[4:], axis, by).reshape(4, half // 2, LANES) for v, axis, by in zip(got, axes, ways)]
     base_a = base_sum(zx, pieces, got[0], got[1], True)
     base_b = base_sum(xz, pieces, got[2], got[3], False)
-    low_a, high_a = far_sum(zx, base_a, far[0], far[1])
-    low_b, high_b = far_sum(xz, base_b, far[2], far[3])
+    low_a, high_a = far_sum(X, base_a, far[0], far[1])
+    low_b, high_b = far_sum(Z, base_b, far[2], far[3])
     low_a, high_a = shift(low_a, X, 1), shift(high_a, X, 3)
     low_b, high_b = shift(low_b, Z, 1), shift(high_b, Z, 3)
-    next_a, last_a = near_sum(zx, base_a, far[0], far[1], low_a, high_a)
-    next_b, last_b = near_sum(xz, base_b, far[2], far[3], low_b, high_b)
-    here_a, here_b = here_sum(zx, base_a, far[0], far[1], base_b, far[2], far[3])
+    next_a, last_a = near_sum(X, base_a, far[0], far[1], low_a, high_a)
+    next_b, last_b = near_sum(Z, base_b, far[2], far[3], low_b, high_b)
+    here_a, here_b = here_sum(base_a, far[0], far[1], base_b, far[2], far[3])
     parts_a = here_a, shift(next_a, X, 1), shift(last_a, X, 3)
     parts_b = here_b, shift(next_b, Z, 1), shift(last_b, Z, 3)
     devices = lax.axis_size((Z, X, Y, CORE))

time: 159 us -> 157 us (0.987)
  Pallas kernels: 26 us -> 21.2 us
  waiting for transfers between devices: 70.3 us -> 73 us
    pallas_call x19, Pallas kernels: 7.55 us -> 2.78 us  [the longest x1 1.36 us: new_params(): pl.pallas_call(params_kernel, in_specs=[here] * 6, out_specs=[here] * 4,...]
    ppermute x16, waiting for transfers between devices: 41.2 us -> 43.5 us  [shift(): lax.ppermute(value, axis, [(i, (i + by) % size) for i in range(size)])]
  transfers between devices with their start and end apart: 32 -> 32, of which waited for: 12 -> 13; matrix products, arithmetic and copies ran while one was open for 0% -> 0% of each run, Pallas kernels for 13% -> 10%
where the time goes in v5:
time: 157 us
  waiting for transfers between devices  73 us (46%)
  starting transfers between devices  43.8 us (28%)
  Pallas kernels  21.2 us (14%)
  blocking collectives  17.7 us (11%)
    ppermute x16, waiting for transfers between devices, shift(): lax.ppermute(value, axis, [(i, (i + by) % size) for i in range(size)])  43.5 us
    ppermute x16, waiting for transfers between devices, partner(): return lax.ppermute(value, axis, [(i, i ^ mask) for i in range(4)])  29.5 us
    ppermute x16, starting transfers between devices, shift(): lax.ppermute(value, axis, [(i, (i + by) % size) for i in range(size)])  27.5 us
    all_to_all x1, blocking collectives, shards(): squares = lax.all_to_all(squares, (Z, X, Y, CORE), 0, 0, tiled=True)  17.7 us
    ppermute x16, starting transfers between devices, partner(): return lax.ppermute(value, axis, [(i, i ^ mask) for i in range(4)])  16.3 us
    pallas_call x5, Pallas kernels, set_blocks(): pl.pallas_call(functools.partial(set_kernel, jobs, len(parts)), in_specs=...  6.41 us
    pallas_call x2, Pallas kernels, base_sum(): pl.pallas_call(base_kernel, grid_spec=pltpu.PrefetchScalarGridSpec(num_sc...  5.86 us
    pallas_call x1, Pallas kernels, both_states(): pl.pallas_call(states_both_kernel, grid=(half // BLOCK,), in_specs=[whole...  3.26 us
  transfers between devices with their start and end apart: 32, of which 13 were waited for; matrix products, arithmetic and copies ran while one was open for 0% of the time, Pallas kernels for 10%

profile of v5, /device:TPU:0, one launch (start us, length us, event | category | flops | bytes accessed | tf_op | source)
XLA Modules:
  0.0 156.9 jit_solution(11961463963641492115)
XLA Ops:
  0.6 2.9 %shard_map.75 = (bf16[6,1024,128]{2,1,0:T(8,128)(2,1)S(1)}, bf16[6,1024,128]{2,1,0:T(8,128)(2,1)S(1)}, bf16[6,1024,128]{2,1,0:T(8,128)(2,1)S(1)}, bf16[6,1024,128]{2,1,0:T(8,128)(2,1)S(1)}) custom-call(s32[1]{0:T(128)} %bitcast.at_z, s32[1]{0:T(128)} %bitcast.1.at_x, bf16[4,4,2048,128]{3,2,1,0:T(8,128)(2,1)} %bitcast.90), custom_call_target="tpu_custom_call" | custom-call | bytes 12582912 | tf_op jit(solution)/shard_map/pallas_call | solution.py:65
  3.6 2.1 %collective-permute-start = (bf16[6,1024,128]{2,1,0:T(8,128)(2,1)S(1)}, bf16[6,1024,128]{2,1,0:T(8,128)(2,1)S(1)}, u32[]{:S(2)}, u32[]{:S(2)}) collective-permute-start(bf16[6,1024,128]{2,1,0:T(8,128)(2,1)S(1)} %get-tuple-element.28), channel_id=1, source_target_pairs={{0,32},{32,64},{64,96},{96,0},{1,33},{33,65},{65,97},{97,1},{2,34}... | collective-permute-start | bytes 4718600 | tf_op jit(solution)/shard_map/ppermute | solution.py:31
  5.6 2.2 %collective-permute-start.1 = (bf16[6,1024,128]{2,1,0:T(8,128)(2,1)S(1)}, bf16[6,1024,128]{2,1,0:T(8,128)(2,1)S(1)}, u32[]{:S(2)}, u32[]{:S(2)}) collective-permute-start(bf16[6,1024,128]{2,1,0:T(8,128)(2,1)S(1)} %get-tuple-element.29), channel_id=1, source_target_pairs={{0,96},{32,0},{64,32},{96,64},{1,97},{33,1},{65,33},{97,65},{2,98}... | collective-permute-start | bytes 4718600 | tf_op jit(solution)/shard_map/ppermute | solution.py:31
  7.8 1.5 collective-permute-start.4
  9.3 1.7 %collective-permute-start.5 = (bf16[6,1024,128]{2,1,0:T(8,128)(2,1)S(1)}, bf16[6,1024,128]{2,1,0:T(8,128)(2,1)S(1)}, u32[]{:S(2)}, u32[]{:S(2)}) collective-permute-start(bf16[6,1024,128]{2,1,0:T(8,128)(2,1)S(1)} %get-tuple-element.31), channel_id=1, source_target_pairs={{0,24},{8,0},{16,8},{24,16},{1,25},{9,1},{17,9},{25,17},{2,26},{10... | collective-permute-start | bytes 4718600 | tf_op jit(solution)/shard_map/ppermute | solution.py:31
  11.1 31.1 %collective-permute-done.behind = bf16[6,1024,128]{2,1,0:T(8,128)(2,1)S(1)} collective-permute-done((bf16[6,1024,128]{2,1,0:T(8,128)(2,1)S(1)}, bf16[6,1024,128]{2,1,0:T(8,128)(2,1)S(1)}, u32[]{:S(2)}, u32[]{:S(2)}) %collective-permute-start) | collective-permute-done | bytes 1572896 | tf_op jit(solution)/shard_map/ppermute | solution.py:31
  42.3 3.3 %collective-permute-start.3 = (bf16[2,1024,128]{2,1,0:T(8,128)(2,1)S(1)}, bf16[2,1024,128]{2,1,0:T(8,128)(2,1)S(1)}, u32[]{:S(2)}, u32[]{:S(2)}) collective-permute-start(bf16[2,1024,128]{2,1,0:T(8,128)(2,1)S(1)} %slice.17), channel_id=1, source_target_pairs={{0,96},{32,0},{64,32},{96,64},{1,97},{33,1},{65,33},{97,65},{2,98}... | collective-permute-start | bytes 1572872 | tf_op jit(solution)/shard_map/ppermute | solution.py:31
  45.6 1.6 collective-permute-start.6
  47.2 1.8 %collective-permute-start.7 = (bf16[2,1024,128]{2,1,0:T(8,128)(2,1)S(1)}, bf16[2,1024,128]{2,1,0:T(8,128)(2,1)S(1)}, u32[]{:S(2)}, u32[]{:S(2)}) collective-permute-start(bf16[2,1024,128]{2,1,0:T(8,128)(2,1)S(1)} %slice.19), channel_id=1, source_target_pairs={{0,24},{8,0},{16,8},{24,16},{1,25},{9,1},{17,9},{25,17},{2,26},{10... | collective-permute-start | bytes 1572872 | tf_op jit(solution)/shard_map/ppermute | solution.py:31
  49.1 2.9 %shard_map.76.refs_0_.base = f32[4,1024,128]{2,1,0:T(8,128)S(1)} custom-call(s32[2]{0:T(128)S(1)} %get-tuple-element.52.where, bf16[4,4,2048,128]{3,2,1,0:T(8,128)(2,1)} %bitcast.91, bf16[6,1024,128]{2,1,0:T(8,128)(2,1)S(1)} %collective-permute-done.behind, bf16[6,1024,128]{2,1,0:T(8,128)(2,1)S(1)} %collective-permute-done.1.ahead), custom_call_target="tpu_custom_call" | custom-call | flops 1048576 | bytes 5242880 | tf_op jit(solution)/shard_map/pallas_call | solution.py:92
  52.1 2.9 %shard_map.77.refs_3_.base = f32[4,1024,128]{2,1,0:T(8,128)S(1)} custom-call(s32[2]{0:T(128)S(1)} %get-tuple-element.53.where, bf16[4,4,2048,128]{3,2,1,0:T(8,128)(2,1)} %bitcast.92, bf16[6,1024,128]{2,1,0:T(8,128)(2,1)S(1)} %collective-permute-done.4.behind, bf16[6,1024,128]{2,1,0:T(8,128)(2,1)S(1)} %collective-permute-done.5.ahead), custom_call_target="tpu_custom_call" | custom-call | flops 1048576 | bytes 5242880 | tf_op jit(solution)/shard_map/pallas_call | solution.py:92
  55.0 1.6 collective-permute-done.2
  56.7 1.6 collective-permute-start.8
  58.2 1.7 %collective-permute-start.9 = (f32[512,128]{1,0:T(8,128)S(1)}, f32[512,128]{1,0:T(8,128)S(1)}, u32[]{:S(2)}, u32[]{:S(2)}) collective-permute-start(f32[512,128]{1,0:T(8,128)S(1)} %get-tuple-element.34), channel_id=1, source_target_pairs={{0,24},{8,0},{16,8},{24,16},{1,25},{9,1},{17,9},{25,17},{2,26},{10... | collective-permute-start | bytes 786440 | tf_op jit(solution)/shard_map/ppermute | solution.py:31
  60.4 3.2 %collective-permute-start.13 = (f32[512,128]{1,0:T(8,128)S(1)}, f32[512,128]{1,0:T(8,128)S(1)}, u32[]{:S(2)}, u32[]{:S(2)}) collective-permute-start(f32[512,128]{1,0:T(8,128)S(1)} %get-tuple-element.39), channel_id=1, source_target_pairs={{0,96},{32,0},{64,32},{96,64},{1,97},{33,1},{65,33},{97,65},{2,98}... | collective-permute-start | bytes 786440 | tf_op jit(solution)/shard_map/ppermute | solution.py:31
  63.6 1.5 collective-permute-done.8.came_low
  65.4 1.6 collective-permute-start.10
  66.9 1.7 %collective-permute-start.11 = (f32[1024,128]{1,0:T(8,128)S(1)}, f32[1024,128]{1,0:T(8,128)S(1)}, u32[]{:S(2)}, u32[]{:S(2)}) collective-permute-start(f32[1024,128]{1,0:T(8,128)S(1)} %get-tuple-element.36), channel_id=1, source_target_pairs={{0,24},{8,0},{16,8},{24,16},{1,25},{9,1},{17,9},{25,17},{2,26},{10... | collective-permute-start | bytes 1572872 | tf_op jit(solution)/shard_map/ppermute | solution.py:31
  69.2 2.9 %collective-permute-start.15 = (f32[1024,128]{1,0:T(8,128)S(1)}, f32[1024,128]{1,0:T(8,128)S(1)}, u32[]{:S(2)}, u32[]{:S(2)}) collective-permute-start(f32[1024,128]{1,0:T(8,128)S(1)} %get-tuple-element.41), channel_id=1, source_target_pairs={{0,96},{32,0},{64,32},{96,64},{1,97},{33,1},{65,33},{97,65},{2,98}... | collective-permute-start | bytes 1572872 | tf_op jit(solution)/shard_map/ppermute | solution.py:31
  72.3 6.0 %collective-permute-done.10.refs_1_ = f32[1024,128]{1,0:T(8,128)S(1)} collective-permute-done((f32[1024,128]{1,0:T(8,128)S(1)}, f32[1024,128]{1,0:T(8,128)S(1)}, u32[]{:S(2)}, u32[]{:S(2)}) %collective-permute-start.10) | collective-permute-done | bytes 524320 | tf_op jit(solution)/shard_map/ppermute | solution.py:31
  78.4 2.9 %collective-permute-done.14.refs_4_ = f32[1024,128]{1,0:T(8,128)S(1)} collective-permute-done((f32[1024,128]{1,0:T(8,128)S(1)}, f32[1024,128]{1,0:T(8,128)S(1)}, u32[]{:S(2)}, u32[]{:S(2)}) %collective-permute-start.14) | collective-permute-done | bytes 524320 | tf_op jit(solution)/shard_map/ppermute | solution.py:31
  81.6 17.7 %all_to_all.11 = f32[128,1,128]{2,1,0:T(1,128)S(1)} all-to-all(f32[128,1,128]{2,1,0:T(1,128)S(1)} %bitcast.88), channel_id=1, replica_groups=mesh['z'=4,'x'=4,'y'=4,'core'=2] {'z','x','y','core'}, dimensions={0} | all-to-all | bytes 131072 | tf_op jit(solution)/shard_map/all_to_all | solution.py:396
  99.4 1.4 shard_map.84
  100.7 0.7 collective-permute-start.24
  101.4 0.8 collective-permute-start.28
  102.2 1.1 collective-permute-start.20
  103.3 0.8 collective-permute-start.16
  104.1 1.8 %collective-permute-done.24.two = bf16[1,512,128]{2,1,0:T(8,128)(2,1)S(1)} collective-permute-done((bf16[1,512,128]{2,1,0:T(8,128)(2,1)S(1)}, bf16[1,512,128]{2,1,0:T(8,128)(2,1)S(1)}, u32[]{:S(2)}, u32[]{:S(2)}) %collective-permute-start.24) | collective-permute-done | bytes 131104 | tf_op jit(solution)/shard_map/ppermute | solution.py:289
  106.0 0.8 collective-permute-start.25
  106.8 1.1 collective-permute-start.29
  108.4 1.4 collective-permute-start.21
  110.1 4.3 %collective-permute-done.25.two = bf16[2,512,128]{2,1,0:T(8,128)(2,1)S(1)} collective-permute-done((bf16[2,512,128]{2,1,0:T(8,128)(2,1)S(1)}, bf16[2,512,128]{2,1,0:T(8,128)(2,1)S(1)}, u32[]{:S(2)}, u32[]{:S(2)}) %collective-permute-start.25) | collective-permute-done | bytes 262176 | tf_op jit(solution)/shard_map/ppermute | solution.py:289
  114.4 1.4 collective-permute-start.26
  115.8 1.1 collective-permute-start.30
  116.9 1.0 collective-permute-start.22
  118.0 1.2 collective-permute-start.18
  119.2 8.2 %collective-permute-done.26.two = bf16[4,512,128]{2,1,0:T(8,128)(2,1)S(1)} collective-permute-done((bf16[4,512,128]{2,1,0:T(8,128)(2,1)S(1)}, bf16[4,512,128]{2,1,0:T(8,128)(2,1)S(1)}, u32[]{:S(2)}, u32[]{:S(2)}) %collective-permute-start.26) | collective-permute-done | bytes 524320 | tf_op jit(solution)/shard_map/ppermute | solution.py:289
  127.5 0.9 collective-permute-start.27
  128.8 1.9 %collective-permute-start.31 = (bf16[8,512,128]{2,1,0:T(8,128)(2,1)S(1)}, bf16[8,512,128]{2,1,0:T(8,128)(2,1)S(1)}, u32[]{:S(2)}, u32[]{:S(2)}) collective-permute-start(bf16[8,512,128]{2,1,0:T(8,128)(2,1)S(1)} %shard_map.96.refs_0_), channel_id=1, source_target_pairs={{0,24},{8,16},{16,8},{24,0},{1,25},{9,17},{17,9},{25,1},{2,26},{10... | collective-permute-start | bytes 3145736 | tf_op jit(solution)/shard_map/ppermute | solution.py:289
  130.7 0.6 collective-permute-start.23
  131.4 1.4 collective-permute-start.19
  132.8 3.3 %shard_map.102 = (f32[2,1024,128]{2,1,0:T(8,128)}, f32[2,1024,128]{2,1,0:T(8,128)}, f32[2,1024,128]{2,1,0:T(8,128)}) custom-call(f32[128,128]{1,0:T(8,128)S(1)} %bitcast.79, f32[1024,128]{1,0:T(8,128)S(1)} %get-tuple-element.43.mean_a, f32[1024,128]{1,0:T(8,128)S(1)} %get-tuple-element.44.mean_b, f32[2,1024,128]{2,1,0:T(8,128)S(1)} %bitcast.73, ...), custom_call_target="tpu_custom_call" | custom-call | flops 5242880 | bytes 7864320 | tf_op jit(solution)/shard_map/pallas_call | solution.py:272
  136.0 2.3 %shard_map.97.refs_1_ = bf16[4,4,4,512,128]{4,3,2,1,0:T(8,128)(2,1)} custom-call(bf16[8,512,128]{2,1,0:T(8,128)(2,1)S(1)} %shard_map.96.refs_0_, bf16[8,512,128]{2,1,0:T(8,128)(2,1)S(1)} %shard_map.93.refs_1_, bf16[8,512,128]{2,1,0:T(8,128)(2,1)S(1)} %shard_map.90.refs_2_, bf16[8,512,128]{2,1,0:T(8,128)(2,1)S(1)} %shard_map.87.refs_3_), custom_call_target="tpu_custom_call" | custom-call | bytes 8388608 | tf_op jit(solution)/shard_map/pallas_call | solution.py:335
  138.3 14.4 %collective-permute-done.31.refs_0_ = bf16[8,512,128]{2,1,0:T(8,128)(2,1)S(1)} collective-permute-done((bf16[8,512,128]{2,1,0:T(8,128)(2,1)S(1)}, bf16[8,512,128]{2,1,0:T(8,128)(2,1)S(1)}, u32[]{:S(2)}, u32[]{:S(2)}) %collective-permute-start.31) | collective-permute-done | bytes 1048608 | tf_op jit(solution)/shard_map/ppermute | solution.py:289
  152.7 1.0 shard_map.98.refs_1_
  153.7 1.0 shard_map.99.refs_1_
  154.8 1.0 shard_map.100.refs_1_
  155.8 1.0 shard_map.101
  (56 shorter events, 3.5 us)
Async XLA Ops:
  3.6 38.6 %collective-permute-start = (bf16[6,1024,128]{2,1,0:T(8,128)(2,1)S(1)}, bf16[6,1024,128]{2,1,0:T(8,128)(2,1)S(1)}, u32[]{:S(2)}, u32[]{:S(2)}) collective-permute-start(bf16[6,1024,128]{2,1,0:T(8,128)(2,1)S(1)} %get-tuple-element.28), channel_id=1, source_target_pairs={{0,32},{32,64},{64,96},{96,0},{1,33},{33,65},{65,97},{97,1},{2,34}... | collective-permute-start | bytes 4718600 | tf_op jit(solution)/shard_map/ppermute | solution.py:31
  5.6 36.6 %collective-permute-start.1 = (bf16[6,1024,128]{2,1,0:T(8,128)(2,1)S(1)}, bf16[6,1024,128]{2,1,0:T(8,128)(2,1)S(1)}, u32[]{:S(2)}, u32[]{:S(2)}) collective-permute-start(bf16[6,1024,128]{2,1,0:T(8,128)(2,1)S(1)} %get-tuple-element.29), channel_id=1, source_target_pairs={{0,96},{32,0},{64,32},{96,64},{1,97},{33,1},{65,33},{97,65},{2,98}... | collective-permute-start | bytes 4718600 | tf_op jit(solution)/shard_map/ppermute | solution.py:31
  7.8 37.8 %collective-permute-start.4 = (bf16[6,1024,128]{2,1,0:T(8,128)(2,1)S(1)}, bf16[6,1024,128]{2,1,0:T(8,128)(2,1)S(1)}, u32[]{:S(2)}, u32[]{:S(2)}) collective-permute-start(bf16[6,1024,128]{2,1,0:T(8,128)(2,1)S(1)} %get-tuple-element.30), channel_id=1, source_target_pairs={{0,8},{8,16},{16,24},{24,0},{1,9},{9,17},{17,25},{25,1},{2,10},{10... | collective-permute-start | bytes 4718600 | tf_op jit(solution)/shard_map/ppermute | solution.py:31
  9.3 37.9 %collective-permute-start.5 = (bf16[6,1024,128]{2,1,0:T(8,128)(2,1)S(1)}, bf16[6,1024,128]{2,1,0:T(8,128)(2,1)S(1)}, u32[]{:S(2)}, u32[]{:S(2)}) collective-permute-start(bf16[6,1024,128]{2,1,0:T(8,128)(2,1)S(1)} %get-tuple-element.31), channel_id=1, source_target_pairs={{0,24},{8,0},{16,8},{24,16},{1,25},{9,1},{17,9},{25,17},{2,26},{10... | collective-permute-start | bytes 4718600 | tf_op jit(solution)/shard_map/ppermute | solution.py:31
  42.2 14.4 %collective-permute-start.2 = (bf16[2,1024,128]{2,1,0:T(8,128)(2,1)S(1)}, bf16[2,1024,128]{2,1,0:T(8,128)(2,1)S(1)}, u32[]{:S(2)}, u32[]{:S(2)}) collective-permute-start(bf16[2,1024,128]{2,1,0:T(8,128)(2,1)S(1)} %slice.16), channel_id=1, source_target_pairs={{0,32},{32,64},{64,96},{96,0},{1,33},{33,65},{65,97},{97,1},{2,34}... | collective-permute-start | bytes 1572872 | tf_op jit(solution)/shard_map/ppermute | solution.py:31
  42.3 14.3 %collective-permute-start.3 = (bf16[2,1024,128]{2,1,0:T(8,128)(2,1)S(1)}, bf16[2,1024,128]{2,1,0:T(8,128)(2,1)S(1)}, u32[]{:S(2)}, u32[]{:S(2)}) collective-permute-start(bf16[2,1024,128]{2,1,0:T(8,128)(2,1)S(1)} %slice.17), channel_id=1, source_target_pairs={{0,96},{32,0},{64,32},{96,64},{1,97},{33,1},{65,33},{97,65},{2,98}... | collective-permute-start | bytes 1572872 | tf_op jit(solution)/shard_map/ppermute | solution.py:31
  45.6 14.3 %collective-permute-start.6 = (bf16[2,1024,128]{2,1,0:T(8,128)(2,1)S(1)}, bf16[2,1024,128]{2,1,0:T(8,128)(2,1)S(1)}, u32[]{:S(2)}, u32[]{:S(2)}) collective-permute-start(bf16[2,1024,128]{2,1,0:T(8,128)(2,1)S(1)} %slice.18), channel_id=1, source_target_pairs={{0,8},{8,16},{16,24},{24,0},{1,9},{9,17},{17,25},{25,1},{2,10},{10... | collective-permute-start | bytes 1572872 | tf_op jit(solution)/shard_map/ppermute | solution.py:31
  47.2 13.0 %collective-permute-start.7 = (bf16[2,1024,128]{2,1,0:T(8,128)(2,1)S(1)}, bf16[2,1024,128]{2,1,0:T(8,128)(2,1)S(1)}, u32[]{:S(2)}, u32[]{:S(2)}) collective-permute-start(bf16[2,1024,128]{2,1,0:T(8,128)(2,1)S(1)} %slice.19), channel_id=1, source_target_pairs={{0,24},{8,0},{16,8},{24,16},{1,25},{9,1},{17,9},{25,17},{2,26},{10... | collective-permute-start | bytes 1572872 | tf_op jit(solution)/shard_map/ppermute | solution.py:31
  56.7 8.4 %collective-permute-start.8 = (f32[512,128]{1,0:T(8,128)S(1)}, f32[512,128]{1,0:T(8,128)S(1)}, u32[]{:S(2)}, u32[]{:S(2)}) collective-permute-start(f32[512,128]{1,0:T(8,128)S(1)} %get-tuple-element.33), channel_id=1, source_target_pairs={{0,8},{8,16},{16,24},{24,0},{1,9},{9,17},{17,25},{25,1},{2,10},{10... | collective-permute-start | bytes 786440 | tf_op jit(solution)/shard_map/ppermute | solution.py:31
  58.2 7.0 %collective-permute-start.9 = (f32[512,128]{1,0:T(8,128)S(1)}, f32[512,128]{1,0:T(8,128)S(1)}, u32[]{:S(2)}, u32[]{:S(2)}) collective-permute-start(f32[512,128]{1,0:T(8,128)S(1)} %get-tuple-element.34), channel_id=1, source_target_pairs={{0,24},{8,0},{16,8},{24,16},{1,25},{9,1},{17,9},{25,17},{2,26},{10... | collective-permute-start | bytes 786440 | tf_op jit(solution)/shard_map/ppermute | solution.py:31
  60.3 8.4 %collective-permute-start.12 = (f32[512,128]{1,0:T(8,128)S(1)}, f32[512,128]{1,0:T(8,128)S(1)}, u32[]{:S(2)}, u32[]{:S(2)}) collective-permute-start(f32[512,128]{1,0:T(8,128)S(1)} %get-tuple-element.38), channel_id=1, source_target_pairs={{0,32},{32,64},{64,96},{96,0},{1,33},{33,65},{65,97},{97,1},{2,34}... | collective-permute-start | bytes 786440 | tf_op jit(solution)/shard_map/ppermute | solution.py:31
  60.4 8.3 %collective-permute-start.13 = (f32[512,128]{1,0:T(8,128)S(1)}, f32[512,128]{1,0:T(8,128)S(1)}, u32[]{:S(2)}, u32[]{:S(2)}) collective-permute-start(f32[512,128]{1,0:T(8,128)S(1)} %get-tuple-element.39), channel_id=1, source_target_pairs={{0,96},{32,0},{64,32},{96,64},{1,97},{33,1},{65,33},{97,65},{2,98}... | collective-permute-start | bytes 786440 | tf_op jit(solution)/shard_map/ppermute | solution.py:31
  65.4 13.0 %collective-permute-start.10 = (f32[1024,128]{1,0:T(8,128)S(1)}, f32[1024,128]{1,0:T(8,128)S(1)}, u32[]{:S(2)}, u32[]{:S(2)}) collective-permute-start(f32[1024,128]{1,0:T(8,128)S(1)} %get-tuple-element.35), channel_id=1, source_target_pairs={{0,8},{8,16},{16,24},{24,0},{1,9},{9,17},{17,25},{25,1},{2,10},{10... | collective-permute-start | bytes 1572872 | tf_op jit(solution)/shard_map/ppermute | solution.py:31
  66.9 11.5 %collective-permute-start.11 = (f32[1024,128]{1,0:T(8,128)S(1)}, f32[1024,128]{1,0:T(8,128)S(1)}, u32[]{:S(2)}, u32[]{:S(2)}) collective-permute-start(f32[1024,128]{1,0:T(8,128)S(1)} %get-tuple-element.36), channel_id=1, source_target_pairs={{0,24},{8,0},{16,8},{24,16},{1,25},{9,1},{17,9},{25,17},{2,26},{10... | collective-permute-start | bytes 1572872 | tf_op jit(solution)/shard_map/ppermute | solution.py:31
  68.8 12.5 %collective-permute-start.14 = (f32[1024,128]{1,0:T(8,128)S(1)}, f32[1024,128]{1,0:T(8,128)S(1)}, u32[]{:S(2)}, u32[]{:S(2)}) collective-permute-start(f32[1024,128]{1,0:T(8,128)S(1)} %get-tuple-element.40), channel_id=1, source_target_pairs={{0,32},{32,64},{64,96},{96,0},{1,33},{33,65},{65,97},{97,1},{2,34}... | collective-permute-start | bytes 1572872 | tf_op jit(solution)/shard_map/ppermute | solution.py:31
  69.2 12.1 %collective-permute-start.15 = (f32[1024,128]{1,0:T(8,128)S(1)}, f32[1024,128]{1,0:T(8,128)S(1)}, u32[]{:S(2)}, u32[]{:S(2)}) collective-permute-start(f32[1024,128]{1,0:T(8,128)S(1)} %get-tuple-element.41), channel_id=1, source_target_pairs={{0,96},{32,0},{64,32},{96,64},{1,97},{33,1},{65,33},{97,65},{2,98}... | collective-permute-start | bytes 1572872 | tf_op jit(solution)/shard_map/ppermute | solution.py:31
  72.3 27.1 %copy-start = (f32[1,4,65536]{2,1,0:T(4,128)S(1)}, f32[1,4,65536]{2,1,0:T(4,128)}, u32[]{:S(2)}) copy-start(f32[1,4,65536]{2,1,0:T(4,128)} %param.5) | copy-start | bytes 3145732
  72.3 27.1 %copy-start.1 = (f32[1,4,65536]{2,1,0:T(4,128)S(1)}, f32[1,4,65536]{2,1,0:T(4,128)}, u32[]{:S(2)}) copy-start(f32[1,4,65536]{2,1,0:T(4,128)} %param.6) | copy-start | bytes 3145732
  72.3 27.1 %copy-start.2 = (f32[1,4,65536]{2,1,0:T(4,128)S(1)}, f32[1,4,65536]{2,1,0:T(4,128)}, u32[]{:S(2)}) copy-start(f32[1,4,65536]{2,1,0:T(4,128)} %param.7) | copy-start | bytes 3145732
  100.7 5.2 %collective-permute-start.24 = (bf16[1,512,128]{2,1,0:T(8,128)(2,1)S(1)}, bf16[1,512,128]{2,1,0:T(8,128)(2,1)S(1)}, u32[]{:S(2)}, u32[]{:S(2)}) collective-permute-start(bf16[1,512,128]{2,1,0:T(8,128)(2,1)S(1)} %bitcast.86), channel_id=1, source_target_pairs={{0,8},{8,0},{16,24},{24,16},{1,9},{9,1},{17,25},{25,17},{2,10},{10... | collective-permute-start | bytes 393224 | tf_op jit(solution)/shard_map/ppermute | solution.py:289
  101.4 5.4 %collective-permute-start.28 = (bf16[1,512,128]{2,1,0:T(8,128)(2,1)S(1)}, bf16[1,512,128]{2,1,0:T(8,128)(2,1)S(1)}, u32[]{:S(2)}, u32[]{:S(2)}) collective-permute-start(bf16[1,512,128]{2,1,0:T(8,128)(2,1)S(1)} %bitcast.84), channel_id=1, source_target_pairs={{0,32},{32,0},{64,96},{96,64},{1,33},{33,1},{65,97},{97,65},{2,34}... | collective-permute-start | bytes 393224 | tf_op jit(solution)/shard_map/ppermute | solution.py:289
  102.2 6.2 %collective-permute-start.20 = (bf16[1,512,128]{2,1,0:T(8,128)(2,1)S(1)}, bf16[1,512,128]{2,1,0:T(8,128)(2,1)S(1)}, u32[]{:S(2)}, u32[]{:S(2)}) collective-permute-start(bf16[1,512,128]{2,1,0:T(8,128)(2,1)S(1)} %bitcast.82), channel_id=1, source_target_pairs={{0,96},{32,64},{64,32},{96,0},{1,97},{33,65},{65,33},{97,1},{2,98}... | collective-permute-start | bytes 393224 | tf_op jit(solution)/shard_map/ppermute | solution.py:289
  103.3 6.6 %collective-permute-start.16 = (bf16[1,512,128]{2,1,0:T(8,128)(2,1)S(1)}, bf16[1,512,128]{2,1,0:T(8,128)(2,1)S(1)}, u32[]{:S(2)}, u32[]{:S(2)}) collective-permute-start(bf16[1,512,128]{2,1,0:T(8,128)(2,1)S(1)} %bitcast.80), channel_id=1, source_target_pairs={{0,24},{8,16},{16,8},{24,0},{1,25},{9,17},{17,9},{25,1},{2,26},{10... | collective-permute-start | bytes 393224 | tf_op jit(solution)/shard_map/ppermute | solution.py:289
  106.0 8.4 %collective-permute-start.25 = (bf16[2,512,128]{2,1,0:T(8,128)(2,1)S(1)}, bf16[2,512,128]{2,1,0:T(8,128)(2,1)S(1)}, u32[]{:S(2)}, u32[]{:S(2)}) collective-permute-start(bf16[2,512,128]{2,1,0:T(8,128)(2,1)S(1)} %shard_map.91.one), channel_id=1, source_target_pairs={{0,96},{32,64},{64,32},{96,0},{1,97},{33,65},{65,33},{97,1},{2,98}... | collective-permute-start | bytes 786440 | tf_op jit(solution)/shard_map/ppermute | solution.py:289
  106.8 9.0 %collective-permute-start.29 = (bf16[2,512,128]{2,1,0:T(8,128)(2,1)S(1)}, bf16[2,512,128]{2,1,0:T(8,128)(2,1)S(1)}, u32[]{:S(2)}, u32[]{:S(2)}) collective-permute-start(bf16[2,512,128]{2,1,0:T(8,128)(2,1)S(1)} %shard_map.94.one), channel_id=1, source_target_pairs={{0,8},{8,0},{16,24},{24,16},{1,9},{9,1},{17,25},{25,17},{2,10},{10... | collective-permute-start | bytes 786440 | tf_op jit(solution)/shard_map/ppermute | solution.py:289
  108.4 8.4 %collective-permute-start.21 = (bf16[2,512,128]{2,1,0:T(8,128)(2,1)S(1)}, bf16[2,512,128]{2,1,0:T(8,128)(2,1)S(1)}, u32[]{:S(2)}, u32[]{:S(2)}) collective-permute-start(bf16[2,512,128]{2,1,0:T(8,128)(2,1)S(1)} %shard_map.88.one), channel_id=1, source_target_pairs={{0,24},{8,16},{16,8},{24,0},{1,25},{9,17},{17,9},{25,1},{2,26},{10... | collective-permute-start | bytes 786440 | tf_op jit(solution)/shard_map/ppermute | solution.py:289
  109.9 8.1 %collective-permute-start.17 = (bf16[2,512,128]{2,1,0:T(8,128)(2,1)S(1)}, bf16[2,512,128]{2,1,0:T(8,128)(2,1)S(1)}, u32[]{:S(2)}, u32[]{:S(2)}) collective-permute-start(bf16[2,512,128]{2,1,0:T(8,128)(2,1)S(1)} %shard_map.85.one), channel_id=1, source_target_pairs={{0,32},{32,0},{64,96},{96,64},{1,33},{33,1},{65,97},{97,65},{2,34}... | collective-permute-start | bytes 786440 | tf_op jit(solution)/shard_map/ppermute | solution.py:289
  114.4 13.1 %collective-permute-start.26 = (bf16[4,512,128]{2,1,0:T(8,128)(2,1)S(1)}, bf16[4,512,128]{2,1,0:T(8,128)(2,1)S(1)}, u32[]{:S(2)}, u32[]{:S(2)}) collective-permute-start(bf16[4,512,128]{2,1,0:T(8,128)(2,1)S(1)} %shard_map.92.one), channel_id=1, source_target_pairs={{0,24},{8,16},{16,8},{24,0},{1,25},{9,17},{17,9},{25,1},{2,26},{10... | collective-permute-start | bytes 1572872 | tf_op jit(solution)/shard_map/ppermute | solution.py:289
  115.8 12.9 %collective-permute-start.30 = (bf16[4,512,128]{2,1,0:T(8,128)(2,1)S(1)}, bf16[4,512,128]{2,1,0:T(8,128)(2,1)S(1)}, u32[]{:S(2)}, u32[]{:S(2)}) collective-permute-start(bf16[4,512,128]{2,1,0:T(8,128)(2,1)S(1)} %shard_map.95.one), channel_id=1, source_target_pairs={{0,96},{32,64},{64,32},{96,0},{1,97},{33,65},{65,33},{97,1},{2,98}... | collective-permute-start | bytes 1572872 | tf_op jit(solution)/shard_map/ppermute | solution.py:289
  116.9 13.7 %collective-permute-start.22 = (bf16[4,512,128]{2,1,0:T(8,128)(2,1)S(1)}, bf16[4,512,128]{2,1,0:T(8,128)(2,1)S(1)}, u32[]{:S(2)}, u32[]{:S(2)}) collective-permute-start(bf16[4,512,128]{2,1,0:T(8,128)(2,1)S(1)} %shard_map.89.one), channel_id=1, source_target_pairs={{0,32},{32,0},{64,96},{96,64},{1,33},{33,1},{65,97},{97,65},{2,34}... | collective-permute-start | bytes 1572872 | tf_op jit(solution)/shard_map/ppermute | solution.py:289
  118.0 13.3 %collective-permute-start.18 = (bf16[4,512,128]{2,1,0:T(8,128)(2,1)S(1)}, bf16[4,512,128]{2,1,0:T(8,128)(2,1)S(1)}, u32[]{:S(2)}, u32[]{:S(2)}) collective-permute-start(bf16[4,512,128]{2,1,0:T(8,128)(2,1)S(1)} %shard_map.86.one), channel_id=1, source_target_pairs={{0,8},{8,0},{16,24},{24,16},{1,9},{9,1},{17,25},{25,17},{2,10},{10... | collective-permute-start | bytes 1572872 | tf_op jit(solution)/shard_map/ppermute | solution.py:289
  127.5 26.2 %collective-permute-start.27 = (bf16[8,512,128]{2,1,0:T(8,128)(2,1)S(1)}, bf16[8,512,128]{2,1,0:T(8,128)(2,1)S(1)}, u32[]{:S(2)}, u32[]{:S(2)}) collective-permute-start(bf16[8,512,128]{2,1,0:T(8,128)(2,1)S(1)} %shard_map.93.refs_1_), channel_id=1, source_target_pairs={{0,32},{32,0},{64,96},{96,64},{1,33},{33,1},{65,97},{97,65},{2,34}... | collective-permute-start | bytes 3145736 | tf_op jit(solution)/shard_map/ppermute | solution.py:289
  128.8 23.9 %collective-permute-start.31 = (bf16[8,512,128]{2,1,0:T(8,128)(2,1)S(1)}, bf16[8,512,128]{2,1,0:T(8,128)(2,1)S(1)}, u32[]{:S(2)}, u32[]{:S(2)}) collective-permute-start(bf16[8,512,128]{2,1,0:T(8,128)(2,1)S(1)} %shard_map.96.refs_0_), channel_id=1, source_target_pairs={{0,24},{8,16},{16,8},{24,0},{1,25},{9,17},{17,9},{25,1},{2,26},{10... | collective-permute-start | bytes 3145736 | tf_op jit(solution)/shard_map/ppermute | solution.py:289
  130.7 24.0 %collective-permute-start.23 = (bf16[8,512,128]{2,1,0:T(8,128)(2,1)S(1)}, bf16[8,512,128]{2,1,0:T(8,128)(2,1)S(1)}, u32[]{:S(2)}, u32[]{:S(2)}) collective-permute-start(bf16[8,512,128]{2,1,0:T(8,128)(2,1)S(1)} %shard_map.90.refs_2_), channel_id=1, source_target_pairs={{0,8},{8,0},{16,24},{24,16},{1,9},{9,1},{17,25},{25,17},{2,10},{10... | collective-permute-start | bytes 3145736 | tf_op jit(solution)/shard_map/ppermute | solution.py:289
  131.4 24.5 %collective-permute-start.19 = (bf16[8,512,128]{2,1,0:T(8,128)(2,1)S(1)}, bf16[8,512,128]{2,1,0:T(8,128)(2,1)S(1)}, u32[]{:S(2)}, u32[]{:S(2)}) collective-permute-start(bf16[8,512,128]{2,1,0:T(8,128)(2,1)S(1)} %shard_map.87.refs_3_), channel_id=1, source_target_pairs={{0,96},{32,64},{64,32},{96,0},{1,97},{33,65},{65,33},{97,1},{2,98}... | collective-permute-start | bytes 3145736 | tf_op jit(solution)/shard_map/ppermute | solution.py:289

commit v6 on v5

--- a/solution.py
+++ b/solution.py
@@ -21,7 +21,6 @@
 
 LANES = 128
 BLOCK = 256
-CHUNK = 64
 VMEM_LIMIT = 12 * 2**20
 f32, bf16 = jnp.float32, jnp.bfloat16
 
@@ -37,15 +36,17 @@
 
 def pick_kernel(at_z, at_x, pieces, *refs):
     outs, sems = refs[:4], refs[4]
-    quarter = outs[0].shape[1] // 2
     z, x = at_z[0], at_x[0]
+    half_a = outs[0].shape[1]
     copies = []
     for k, (out, along_z, by) in enumerate(zip(outs, (True, True, False, False), (1, 3, 1, 3))):
+        half = out.shape[1]
+        quarter = half // 2
         me = z if along_z else x
-        low = 0 if along_z else 2 * quarter
+        low = 0 if along_z else half_a
         far_low = low if by == 1 else low + quarter
         near, far = lax.rem(me + by, 4), lax.rem(me + 2, 4)
-        rows = pl.ds(low, 2 * quarter)
+        rows = pl.ds(low, half)
         piece = pieces.at[near, :, rows] if along_z else pieces.at[:, near, rows]
         copies.append(pltpu.make_async_copy(piece, out.at[pl.ds(0, 4)], sems.at[k, 0]))
         for j in range(4):
@@ -59,8 +60,7 @@
         copy.wait()
 
 
-def pick(pieces, z, x):
-    half = pieces.shape[2] // 2
+def pick(pieces, z, x, halves):
     any_ = pl.BlockSpec(memory_space=pl.ANY)
     return pl.pallas_call(
         pick_kernel,
@@ -71,40 +71,65 @@
             out_specs=[any_] * 4,
             scratch_shapes=[pltpu.SemaphoreType.DMA((4, 5))],
         ),
-        out_shape=[jax.ShapeDtypeStruct((6, half, LANES), bf16)] * 4,
-        compiler_params=pltpu.CompilerParams(vmem_limit_bytes=VMEM_LIMIT),
-        cost_estimate=cost(0, 96 * half * LANES),
+        out_shape=[jax.ShapeDtypeStruct((6, half, LANES), bf16) for half in halves for _ in range(2)],
+        compiler_params=pltpu.CompilerParams(vmem_limit_bytes=VMEM_LIMIT),
+        cost_estimate=cost(0, 48 * sum(halves) * LANES),
     )(z.reshape(1), x.reshape(1), pltpu.with_memory_space_constraint(pieces, pltpu.HBM))
 
 
-def base_kernel(where, own, behind, ahead, out):
-    out[...] = own[...].astype(f32) + behind[...].astype(f32) + ahead[...].astype(f32)
-
-
-def base_sum(where, pieces, behind, ahead, along_z):
-    half = behind.shape[1]
-    steps = half // BLOCK
-    part = pl.BlockSpec((4, BLOCK, LANES), lambda i, w: (0, i, 0))
-    if along_z:
-        own = pl.BlockSpec((None, 4, BLOCK, LANES), lambda i, w: (w[0], 0, i, 0))
-    else:
-        own = pl.BlockSpec((4, None, BLOCK, LANES), lambda i, w: (0, w[0], steps + i, 0))
+def own_kernel(pieces, out_a, out_b, sems):
+    half_a, half_b = out_a.shape[1], out_b.shape[1]
+    z, x = lax.axis_index(Z), lax.axis_index(X)
+    copies = [
+        pltpu.make_async_copy(pieces.at[z, :, pl.ds(0, half_a)], out_a, sems.at[0]),
+        pltpu.make_async_copy(pieces.at[:, x, pl.ds(half_a, half_b)], out_b, sems.at[1]),
+    ]
+    for copy in copies:
+        copy.start()
+    for copy in copies:
+        copy.wait()
+
+
+def own_pieces(pieces, halves):
+    any_ = pl.BlockSpec(memory_space=pl.ANY)
+    return pl.pallas_call(
+        own_kernel,
+        in_specs=[any_],
+        out_specs=[any_] * 2,
+        scratch_shapes=[pltpu.SemaphoreType.DMA((2,))],
+        out_shape=[jax.ShapeDtypeStruct((4, half, LANES), bf16) for half in halves],
+        compiler_params=pltpu.CompilerParams(vmem_limit_bytes=VMEM_LIMIT),
+        cost_estimate=cost(0, 16 * sum(halves) * LANES),
+    )(pltpu.with_memory_space_constraint(pieces, pltpu.HBM))
+
+
+def base_kernel(own, behind, ahead, out):
+    for j in range(4):
+
+        @chunks_of(out.shape[1])
+        def _(rows):
+            out[j, rows] = own[j, rows].astype(f32) + behind[j, rows].astype(f32) + ahead[j, rows].astype(f32)
+
+
+def base_sum(own, behind, ahead):
+    here = pl.BlockSpec(memory_space=pltpu.VMEM)
     return pl.pallas_call(
         base_kernel,
-        grid_spec=pltpu.PrefetchScalarGridSpec(
-            num_scalar_prefetch=1, grid=(steps,), in_specs=[own, part, part], out_specs=part
-        ),
-        out_shape=jax.ShapeDtypeStruct((4, half, LANES), f32),
-        compiler_params=pltpu.CompilerParams(vmem_limit_bytes=VMEM_LIMIT),
-        cost_estimate=cost(8 * half * LANES, 40 * half * LANES),
-    )(where, pltpu.with_memory_space_constraint(pieces, pltpu.HBM), behind, ahead)
-
-
-def chunks_of(size):
+        in_specs=[here] * 3,
+        out_specs=here,
+        out_shape=jax.ShapeDtypeStruct(own.shape, f32),
+        compiler_params=pltpu.CompilerParams(vmem_limit_bytes=VMEM_LIMIT),
+        cost_estimate=cost(2 * own.size, 60 * own.size),
+    )(own, behind, ahead)
+
+
+def chunks_of(size, *starts):
+    step = max(n for n in (64, 48, 32, 16) if size % n == 0)
+
     def run(body):
-        @pl.loop(0, size // CHUNK)
+        @pl.loop(0, size // step)
         def _(i):
-            body(pl.multiple_of(i * CHUNK, CHUNK))
+            body(*(pl.ds(pl.multiple_of(at + i * step, 16), step) for at in (0, *starts)))
 
     return run
 
@@ -113,9 +138,8 @@
     quarter = low.shape[0]
     at = lax.rem(lax.axis_index(axis) + 2, 4)
 
-    @chunks_of(quarter)
-    def _(start):
-        rows, upper = pl.ds(start, CHUNK), pl.ds(quarter + start, CHUNK)
+    @chunks_of(quarter, quarter)
+    def _(rows, upper):
         low[rows] = base[at, rows] + far_low[at, rows].astype(f32)
         high[rows] = base[at, upper] + far_high[at, rows].astype(f32)
 
@@ -138,9 +162,8 @@
     after = lax.rem(lax.axis_index(axis) + 1, 4)
     before = lax.rem(lax.axis_index(axis) + 3, 4)
 
-    @chunks_of(quarter)
-    def _(start):
-        rows, upper = pl.ds(start, CHUNK), pl.ds(quarter + start, CHUNK)
+    @chunks_of(quarter, quarter)
+    def _(rows, upper):
         to_next[rows] = base[after, rows] + far_low[after, rows].astype(f32) + came_low[rows]
         to_next[upper] = base[after, upper] + far_high[after, rows].astype(f32)
         to_last[rows] = base[before, rows] + far_low[before, rows].astype(f32)
@@ -165,52 +188,49 @@
         quarter = far_low.shape[1]
         at = lax.axis_index(axis)
 
-        @chunks_of(quarter)
-        def _(start):
-            rows, upper = pl.ds(start, CHUNK), pl.ds(quarter + start, CHUNK)
+        @chunks_of(quarter, quarter)
+        def _(rows, upper):
             out[rows] = base[at, rows] + far_low[at, rows].astype(f32)
             out[upper] = base[at, upper] + far_high[at, rows].astype(f32)
 
 
 def here_sum(base_a, low_a, high_a, base_b, low_b, high_b):
-    quarter = low_a.shape[1]
     here = pl.BlockSpec(memory_space=pltpu.VMEM)
     return pl.pallas_call(
         here_sum_kernel,
         in_specs=[here] * 6,
         out_specs=[here] * 2,
-        out_shape=[jax.ShapeDtypeStruct((2 * quarter, LANES), f32)] * 2,
-        compiler_params=pltpu.CompilerParams(vmem_limit_bytes=VMEM_LIMIT),
-        cost_estimate=cost(4 * quarter * LANES, 40 * quarter * LANES),
+        out_shape=[jax.ShapeDtypeStruct(base.shape[1:], f32) for base in (base_a, base_b)],
+        compiler_params=pltpu.CompilerParams(vmem_limit_bytes=VMEM_LIMIT),
+        cost_estimate=cost(base_a.size // 2, 5 * base_a.size),
     )(base_a, low_a, high_a, base_b, low_b, high_b)
 
 
 def last_sum_kernel(*refs):
-    parts_a, parts_b, (mean_a, mean_b, squares, held) = refs[:3], refs[3:6], refs[6:]
+    parts_a, parts_b, (mean, squares, held) = refs[:3], refs[3:6], refs[6:]
     held[...] = jnp.zeros_like(held)
-
-    @chunks_of(mean_a.shape[0])
-    def _(start):
-        rows = pl.ds(start, CHUNK)
-        for parts, mean in ((parts_a, mean_a), (parts_b, mean_b)):
+    for parts, first in ((parts_a, 0), (parts_b, parts_a[0].shape[0])):
+
+        @chunks_of(parts[0].shape[0], first)
+        def _(rows, target):
             total = (parts[0][rows] + parts[1][rows] + parts[2][rows]) * (1.0 / 16.0)
-            mean[rows] = total
-            held[...] += jnp.sum((total * total).reshape(CHUNK // 8, 8, LANES), axis=0)
+            mean[target] = total
+            held[...] += jnp.sum((total * total).reshape(-1, 8, LANES), axis=0)
 
     squares[...] = jnp.broadcast_to(jnp.sum(held[...], axis=0, keepdims=True), squares.shape)
 
 
 def last_sum(parts_a, parts_b, devices):
-    half = parts_a[0].shape[0]
+    rows = parts_a[0].shape[0] + parts_b[0].shape[0]
     here = pl.BlockSpec(memory_space=pltpu.VMEM)
     return pl.pallas_call(
         last_sum_kernel,
         in_specs=[here] * 6,
-        out_specs=[here] * 3,
-        out_shape=[jax.ShapeDtypeStruct((half, LANES), f32)] * 2 + [jax.ShapeDtypeStruct((devices, LANES), f32)],
+        out_specs=[here] * 2,
+        out_shape=[jax.ShapeDtypeStruct((rows, LANES), f32), jax.ShapeDtypeStruct((devices, LANES), f32)],
         scratch_shapes=[pltpu.VMEM((8, LANES), f32)],
         compiler_params=pltpu.CompilerParams(vmem_limit_bytes=VMEM_LIMIT),
-        cost_estimate=cost(16 * half * LANES, 10 * 4 * half * LANES),
+        cost_estimate=cost(8 * rows * LANES, 20 * rows * LANES),
     )(*parts_a, *parts_b)
 
 
@@ -228,56 +248,49 @@
     return jnp.minimum(1.0, clip_limit / (jnp.sqrt(total) + norm_eps))
 
 
-def params_kernel(squares, mean_a, mean_b, master, first, second, *outs):
+def params_kernel(squares, mean, master, first, second, *outs):
     clip_factor = clip_of(squares)
-    quarter = outs[0].shape[0]
+    size = outs[0].shape[0]
     for at, out in enumerate(outs):
-        mean = (mean_a, mean_b)[at // 2]
-
-        @pl.loop(0, quarter // CHUNK)
-        def _(i):
-            rows = pl.ds(pl.multiple_of(at * quarter + i * CHUNK, CHUNK), CHUNK)
-            mean_rows = pl.ds(pl.multiple_of(at % 2 * quarter + i * CHUNK, CHUNK), CHUNK)
-            new_master, _, _ = adam_update(mean[mean_rows], master[rows], first[rows], second[rows], clip_factor)
-            out[pl.ds(pl.multiple_of(i * CHUNK, CHUNK), CHUNK)] = new_master.astype(bf16)
-
-
-def new_params(squares, means, states):
-    quarter = means[0].shape[0] // 2
-    here = pl.BlockSpec(memory_space=pltpu.VMEM)
-    operands = [value for value in (squares, *means, *states)]
+
+        @chunks_of(size, at * size)
+        def _(target, rows):
+            new_master, _, _ = adam_update(mean[rows], master[rows], first[rows], second[rows], clip_factor)
+            out[target] = new_master.astype(bf16)
+
+
+def new_params(squares, mean, states):
+    quarter = mean.shape[0] // 4
+    here = pl.BlockSpec(memory_space=pltpu.VMEM)
     return pl.pallas_call(
         params_kernel,
-        in_specs=[here] * 6,
+        in_specs=[here] * 5,
         out_specs=[here] * 4,
         out_shape=[jax.ShapeDtypeStruct((quarter, LANES), bf16)] * 4,
         compiler_params=pltpu.CompilerParams(vmem_limit_bytes=VMEM_LIMIT),
         cost_estimate=cost(160 * quarter * LANES, 72 * quarter * LANES),
-    )(*operands)
-
-
-def states_both_kernel(squares, mean_a, mean_b, master, first, second, *outs):
-    clip_factor = clip_of(squares)
-    for at, mean in enumerate((mean_a, mean_b)):
-        values = adam_update(mean[...], master[at], first[at], second[at], clip_factor)
-        for out, value in zip(outs, values):
-            out[at] = value
-
-
-def both_states(squares, means, states):
-    half = means[0].shape[0]
+    )(squares, mean, *states)
+
+
+def states_kernel(squares, mean, master, first, second, *outs):
+    values = adam_update(mean[...], master[...], first[...], second[...], clip_of(squares))
+    for out, value in zip(outs, values):
+        out[...] = value
+
+
+def new_states(squares, mean, states):
+    rows = mean.shape[0]
     whole = pl.BlockSpec(squares.shape, lambda i: (0, 0))
-    low = pl.BlockSpec((BLOCK, LANES), lambda i: (i, 0))
-    pair = pl.BlockSpec((2, BLOCK, LANES), lambda i: (0, i, 0))
-    return pl.pallas_call(
-        states_both_kernel,
-        grid=(half // BLOCK,),
-        in_specs=[whole, low, low, pair, pair, pair],
-        out_specs=[pair] * 3,
-        out_shape=[jax.ShapeDtypeStruct((2, half, LANES), f32)] * 3,
-        compiler_params=pltpu.CompilerParams(vmem_limit_bytes=VMEM_LIMIT),
-        cost_estimate=cost(40 * half * LANES, 60 * half * LANES),
-    )(squares, *means, *(s.reshape(2, half, LANES) for s in states))
+    block = pl.BlockSpec((2 * BLOCK, LANES), lambda i: (i, 0))
+    return pl.pallas_call(
+        states_kernel,
+        grid=(rows // BLOCK // 2,),
+        in_specs=[whole, block, block, block, block],
+        out_specs=[block] * 3,
+        out_shape=[jax.ShapeDtypeStruct((rows, LANES), f32)] * 3,
+        compiler_params=pltpu.CompilerParams(vmem_limit_bytes=VMEM_LIMIT),
+        cost_estimate=cost(20 * rows * LANES, 28 * rows * LANES),
+    )(squares, mean, *states)
 
 
 DIMS = {"zA": (Z, 1), "zB": (Z, 3), "xA": (X, 1), "xB": (X, 3)}
@@ -361,7 +374,7 @@
 def shards(local_grads, master_weights, first_moment, second_moment):
     layers, flat = local_grads.shape[2:]
     rows = layers * flat // LANES // 16
-    half = rows // 2
+    halves = rows // 2, rows // 2
     z, x = lax.axis_index(Z), lax.axis_index(X)
 
     def to_rows(value):
@@ -372,16 +385,14 @@
 
     pieces = to_rows(local_grads[0, 0]).reshape(4, 4, rows, LANES)
     states = [to_rows(s[0]) for s in (master_weights, first_moment, second_moment)]
-    zx = jnp.stack([z, x]).astype(jnp.int32)
-    xz = jnp.stack([x, z]).astype(jnp.int32)
-
-    sends = pick(pieces, z, x)
+    sends = pick(pieces, z, x, halves)
     axes = (Z, Z, X, X)
     ways = (1, 3, 1, 3)
     got = [shift(v, axis, by) for v, axis, by in zip(sends, axes, ways)]
-    far = [shift(v[4:], axis, by).reshape(4, half // 2, LANES) for v, axis, by in zip(got, axes, ways)]
-    base_a = base_sum(zx, pieces, got[0], got[1], True)
-    base_b = base_sum(xz, pieces, got[2], got[3], False)
+    far = [shift(v[4:], axis, by).reshape(4, -1, LANES) for v, axis, by in zip(got, axes, ways)]
+    own_a, own_b = own_pieces(pieces, halves)
+    base_a = base_sum(own_a, got[0], got[1])
+    base_b = base_sum(own_b, got[2], got[3])
     low_a, high_a = far_sum(X, base_a, far[0], far[1])
     low_b, high_b = far_sum(Z, base_b, far[2], far[3])
     low_a, high_a = shift(low_a, X, 1), shift(high_a, X, 3)
@@ -392,12 +403,11 @@
     parts_a = here_a, shift(next_a, X, 1), shift(last_a, X, 3)
     parts_b = here_b, shift(next_b, Z, 1), shift(last_b, Z, 3)
     devices = lax.axis_size((Z, X, Y, CORE))
-    mean_a, mean_b, squares = last_sum(parts_a, parts_b, devices)
+    mean, squares = last_sum(parts_a, parts_b, devices)
     squares = lax.all_to_all(squares, (Z, X, Y, CORE), 0, 0, tiled=True)
 
-    blocks = new_params(squares, (mean_a, mean_b), states)
-    outs = both_states(squares, (mean_a, mean_b), states)
-    outs = [from_rows(o.reshape(rows, LANES)) for o in outs]
+    blocks = new_params(squares, mean, states)
+    outs = [from_rows(o) for o in new_states(squares, mean, states)]
     out = gather_blocks(blocks)
     return (from_rows(out.reshape(-1, LANES)), *outs)
 

time: 157 us -> 155 us (0.987)
  Pallas kernels: 21.2 us -> 18 us
  waiting for transfers between devices: 73 us -> 74.7 us
    pallas_call x5 -> x6, Pallas kernels: 10.8 us -> 7.59 us  [the longest x1 2.8 us: new_states(): pl.pallas_call(states_kernel, grid=(rows // BLOCK // 2,), in_specs=[whole...]
    ppermute x16, waiting for transfers between devices: 43.5 us -> 45.6 us  [shift(): lax.ppermute(value, axis, [(i, (i + by) % size) for i in range(size)])]
    ppermute x16, starting transfers between devices: 16.3 us -> 14.6 us  [partner(): return lax.ppermute(value, axis, [(i, i ^ mask) for i in range(4)])]
  transfers between devices with their start and end apart: 32 -> 32, of which waited for: 13 -> 15; matrix products, arithmetic and copies ran while one was open for 0% -> 0% of each run, Pallas kernels for 10% -> 8%
where the time goes in v6:
time: 155 us
  waiting for transfers between devices  74.7 us (48%)
  starting transfers between devices  43.3 us (28%)
  Pallas kernels  18 us (12%)
  blocking collectives  17.8 us (11%)
    ppermute x16, waiting for transfers between devices, shift(): lax.ppermute(value, axis, [(i, (i + by) % size) for i in range(size)])  45.6 us
    ppermute x16, waiting for transfers between devices, partner(): return lax.ppermute(value, axis, [(i, i ^ mask) for i in range(4)])  29 us
    ppermute x16, starting transfers between devices, shift(): lax.ppermute(value, axis, [(i, (i + by) % size) for i in range(size)])  28.7 us
    all_to_all x1, blocking collectives, shards(): squares = lax.all_to_all(squares, (Z, X, Y, CORE), 0, 0, tiled=True)  17.8 us
    ppermute x16, starting transfers between devices, partner(): return lax.ppermute(value, axis, [(i, i ^ mask) for i in range(4)])  14.6 us
    pallas_call x5, Pallas kernels, set_blocks(): pl.pallas_call(functools.partial(set_kernel, jobs, len(parts)), in_specs=...  6.41 us
  transfers between devices with their start and end apart: 32, of which 15 were waited for; matrix products, arithmetic and copies ran while one was open for 0% of the time, Pallas kernels for 8%

profile of v6, /device:TPU:0, one launch (start us, length us, event | category | flops | bytes accessed | tf_op | source)
XLA Modules:
  0.0 154.8 jit_solution(7815543266627037901)
XLA Ops:
  0.6 2.9 %shard_map.76 = (bf16[6,1024,128]{2,1,0:T(8,128)(2,1)S(1)}, bf16[6,1024,128]{2,1,0:T(8,128)(2,1)S(1)}, bf16[6,1024,128]{2,1,0:T(8,128)(2,1)S(1)}, bf16[6,1024,128]{2,1,0:T(8,128)(2,1)S(1)}) custom-call(s32[1]{0:T(128)} %bitcast.3.at_z, s32[1]{0:T(128)} %bitcast.4.at_x, bf16[4,4,2048,128]{3,2,1,0:T(8,128)(2,1)} %bitcast.84), custom_call_target="tpu_custom_call" | custom-call | bytes 12582912 | tf_op jit(solution)/shard_map/pallas_call | solution.py:65
  3.6 2.9 %collective-permute-start.5 = (bf16[6,1024,128]{2,1,0:T(8,128)(2,1)S(1)}, bf16[6,1024,128]{2,1,0:T(8,128)(2,1)S(1)}, u32[]{:S(2)}, u32[]{:S(2)}) collective-permute-start(bf16[6,1024,128]{2,1,0:T(8,128)(2,1)S(1)} %get-tuple-element.34), channel_id=1, source_target_pairs={{0,24},{8,0},{16,8},{24,16},{1,25},{9,1},{17,9},{25,17},{2,26},{10... | collective-permute-start | bytes 4718600 | tf_op jit(solution)/shard_map/ppermute | solution.py:30
  6.5 1.9 %collective-permute-start = (bf16[6,1024,128]{2,1,0:T(8,128)(2,1)S(1)}, bf16[6,1024,128]{2,1,0:T(8,128)(2,1)S(1)}, u32[]{:S(2)}, u32[]{:S(2)}) collective-permute-start(bf16[6,1024,128]{2,1,0:T(8,128)(2,1)S(1)} %get-tuple-element.30), channel_id=1, source_target_pairs={{0,32},{32,64},{64,96},{96,0},{1,33},{33,65},{65,97},{97,1},{2,34}... | collective-permute-start | bytes 4718600 | tf_op jit(solution)/shard_map/ppermute | solution.py:30
  8.4 2.1 %collective-permute-start.1 = (bf16[6,1024,128]{2,1,0:T(8,128)(2,1)S(1)}, bf16[6,1024,128]{2,1,0:T(8,128)(2,1)S(1)}, u32[]{:S(2)}, u32[]{:S(2)}) collective-permute-start(bf16[6,1024,128]{2,1,0:T(8,128)(2,1)S(1)} %get-tuple-element.31), channel_id=1, source_target_pairs={{0,96},{32,0},{64,32},{96,64},{1,97},{33,1},{65,33},{97,65},{2,98}... | collective-permute-start | bytes 4718600 | tf_op jit(solution)/shard_map/ppermute | solution.py:30
  10.5 29.6 %collective-permute-done.5.ahead = bf16[6,1024,128]{2,1,0:T(8,128)(2,1)S(1)} collective-permute-done((bf16[6,1024,128]{2,1,0:T(8,128)(2,1)S(1)}, bf16[6,1024,128]{2,1,0:T(8,128)(2,1)S(1)}, u32[]{:S(2)}, u32[]{:S(2)}) %collective-permute-start.5) | collective-permute-done | bytes 1572896 | tf_op jit(solution)/shard_map/ppermute | solution.py:30
  40.2 3.8 %collective-permute-start.7 = (bf16[2,1024,128]{2,1,0:T(8,128)(2,1)S(1)}, bf16[2,1024,128]{2,1,0:T(8,128)(2,1)S(1)}, u32[]{:S(2)}, u32[]{:S(2)}) collective-permute-start(bf16[2,1024,128]{2,1,0:T(8,128)(2,1)S(1)} %slice.19), channel_id=1, source_target_pairs={{0,24},{8,0},{16,8},{24,16},{1,25},{9,1},{17,9},{25,17},{2,26},{10... | collective-permute-start | bytes 1572872 | tf_op jit(solution)/shard_map/ppermute | solution.py:30
  44.1 0.6 collective-permute-done.behind
  44.7 1.4 collective-permute-start.2
  46.1 2.2 %collective-permute-start.3 = (bf16[2,1024,128]{2,1,0:T(8,128)(2,1)S(1)}, bf16[2,1024,128]{2,1,0:T(8,128)(2,1)S(1)}, u32[]{:S(2)}, u32[]{:S(2)}) collective-permute-start(bf16[2,1024,128]{2,1,0:T(8,128)(2,1)S(1)} %slice.17), channel_id=1, source_target_pairs={{0,96},{32,0},{64,32},{96,64},{1,97},{33,1},{65,33},{97,65},{2,98}... | collective-permute-start | bytes 1572872 | tf_op jit(solution)/shard_map/ppermute | solution.py:30
  48.4 1.6 %shard_map.75 = (bf16[4,1024,128]{2,1,0:T(8,128)(2,1)S(1)}, bf16[4,1024,128]{2,1,0:T(8,128)(2,1)S(1)}) custom-call(bf16[4,4,2048,128]{3,2,1,0:T(8,128)(2,1)} %bitcast.85), custom_call_target="tpu_custom_call" | custom-call | bytes 4194304 | tf_op jit(solution)/shard_map/pallas_call | solution.py:95
  49.9 0.7 shard_map.78.refs_3_.base
  50.6 0.7 shard_map.77.refs_0_.base
  51.3 3.0 %collective-permute-done.7 = bf16[2,1024,128]{2,1,0:T(8,128)(2,1)S(1)} collective-permute-done((bf16[2,1024,128]{2,1,0:T(8,128)(2,1)S(1)}, bf16[2,1024,128]{2,1,0:T(8,128)(2,1)S(1)}, u32[]{:S(2)}, u32[]{:S(2)}) %collective-permute-start.7) | collective-permute-done | bytes 524320 | tf_op jit(solution)/shard_map/ppermute | solution.py:30
  54.2 3.5 %collective-permute-done.6 = bf16[2,1024,128]{2,1,0:T(8,128)(2,1)S(1)} collective-permute-done((bf16[2,1024,128]{2,1,0:T(8,128)(2,1)S(1)}, bf16[2,1024,128]{2,1,0:T(8,128)(2,1)S(1)}, u32[]{:S(2)}, u32[]{:S(2)}) %collective-permute-start.6) | collective-permute-done | bytes 524320 | tf_op jit(solution)/shard_map/ppermute | solution.py:30
  57.8 2.0 %collective-permute-start.12 = (f32[512,128]{1,0:T(8,128)S(1)}, f32[512,128]{1,0:T(8,128)S(1)}, u32[]{:S(2)}, u32[]{:S(2)}) collective-permute-start(f32[512,128]{1,0:T(8,128)S(1)} %get-tuple-element.41), channel_id=1, source_target_pairs={{0,32},{32,64},{64,96},{96,0},{1,33},{33,65},{65,97},{97,1},{2,34}... | collective-permute-start | bytes 786440 | tf_op jit(solution)/shard_map/ppermute | solution.py:30
  59.8 2.2 %collective-permute-start.13 = (f32[512,128]{1,0:T(8,128)S(1)}, f32[512,128]{1,0:T(8,128)S(1)}, u32[]{:S(2)}, u32[]{:S(2)}) collective-permute-start(f32[512,128]{1,0:T(8,128)S(1)} %get-tuple-element.42), channel_id=1, source_target_pairs={{0,96},{32,0},{64,32},{96,64},{1,97},{33,1},{65,33},{97,65},{2,98}... | collective-permute-start | bytes 786440 | tf_op jit(solution)/shard_map/ppermute | solution.py:30
  62.2 3.2 %collective-permute-start.9 = (f32[512,128]{1,0:T(8,128)S(1)}, f32[512,128]{1,0:T(8,128)S(1)}, u32[]{:S(2)}, u32[]{:S(2)}) collective-permute-start(f32[512,128]{1,0:T(8,128)S(1)} %get-tuple-element.37), channel_id=1, source_target_pairs={{0,24},{8,0},{16,8},{24,16},{1,25},{9,1},{17,9},{25,17},{2,26},{10... | collective-permute-start | bytes 786440 | tf_op jit(solution)/shard_map/ppermute | solution.py:30
  65.4 0.9 collective-permute-done.12.came_low
  66.5 1.9 %collective-permute-start.14 = (f32[1024,128]{1,0:T(8,128)S(1)}, f32[1024,128]{1,0:T(8,128)S(1)}, u32[]{:S(2)}, u32[]{:S(2)}) collective-permute-start(f32[1024,128]{1,0:T(8,128)S(1)} %get-tuple-element.43), channel_id=1, source_target_pairs={{0,32},{32,64},{64,96},{96,0},{1,33},{33,65},{65,97},{97,1},{2,34}... | collective-permute-start | bytes 1572872 | tf_op jit(solution)/shard_map/ppermute | solution.py:30
  68.3 1.6 %collective-permute-start.15 = (f32[1024,128]{1,0:T(8,128)S(1)}, f32[1024,128]{1,0:T(8,128)S(1)}, u32[]{:S(2)}, u32[]{:S(2)}) collective-permute-start(f32[1024,128]{1,0:T(8,128)S(1)} %get-tuple-element.44), channel_id=1, source_target_pairs={{0,96},{32,0},{64,32},{96,64},{1,97},{33,1},{65,33},{97,65},{2,98}... | collective-permute-start | bytes 1572872 | tf_op jit(solution)/shard_map/ppermute | solution.py:30
  70.1 3.2 %collective-permute-start.11 = (f32[1024,128]{1,0:T(8,128)S(1)}, f32[1024,128]{1,0:T(8,128)S(1)}, u32[]{:S(2)}, u32[]{:S(2)}) collective-permute-start(f32[1024,128]{1,0:T(8,128)S(1)} %get-tuple-element.39), channel_id=1, source_target_pairs={{0,24},{8,0},{16,8},{24,16},{1,25},{9,1},{17,9},{25,17},{2,26},{10... | collective-permute-start | bytes 1572872 | tf_op jit(solution)/shard_map/ppermute | solution.py:30
  73.6 5.0 %collective-permute-done.14.refs_4_ = f32[1024,128]{1,0:T(8,128)S(1)} collective-permute-done((f32[1024,128]{1,0:T(8,128)S(1)}, f32[1024,128]{1,0:T(8,128)S(1)}, u32[]{:S(2)}, u32[]{:S(2)}) %collective-permute-start.14) | collective-permute-done | bytes 524320 | tf_op jit(solution)/shard_map/ppermute | solution.py:30
  78.5 3.1 %collective-permute-done.10.refs_1_ = f32[1024,128]{1,0:T(8,128)S(1)} collective-permute-done((f32[1024,128]{1,0:T(8,128)S(1)}, f32[1024,128]{1,0:T(8,128)S(1)}, u32[]{:S(2)}, u32[]{:S(2)}) %collective-permute-start.10) | collective-permute-done | bytes 524320 | tf_op jit(solution)/shard_map/ppermute | solution.py:30
  82.2 17.8 %all_to_all.11 = f32[128,1,128]{2,1,0:T(1,128)S(1)} all-to-all(f32[128,1,128]{2,1,0:T(1,128)S(1)} %bitcast.82), channel_id=1, replica_groups=mesh['z'=4,'x'=4,'y'=4,'core'=2] {'z','x','y','core'}, dimensions={0} | all-to-all | bytes 131072 | tf_op jit(solution)/shard_map/all_to_all | solution.py:407
  100.0 1.4 shard_map.85
  101.3 0.9 collective-permute-start.28
  102.2 0.6 collective-permute-start.24
  102.8 1.1 collective-permute-start.20
  103.9 0.8 collective-permute-start.16
  104.7 1.8 %collective-permute-done.28.two = bf16[1,512,128]{2,1,0:T(8,128)(2,1)S(1)} collective-permute-done((bf16[1,512,128]{2,1,0:T(8,128)(2,1)S(1)}, bf16[1,512,128]{2,1,0:T(8,128)(2,1)S(1)}, u32[]{:S(2)}, u32[]{:S(2)}) %collective-permute-start.28) | collective-permute-done | bytes 131104 | tf_op jit(solution)/shard_map/ppermute | solution.py:302
  106.6 0.7 collective-permute-start.29
  107.3 1.2 collective-permute-start.25
  109.0 1.4 collective-permute-start.21
  110.6 3.1 %collective-permute-done.29.two = bf16[2,512,128]{2,1,0:T(8,128)(2,1)S(1)} collective-permute-done((bf16[2,512,128]{2,1,0:T(8,128)(2,1)S(1)}, bf16[2,512,128]{2,1,0:T(8,128)(2,1)S(1)}, u32[]{:S(2)}, u32[]{:S(2)}) %collective-permute-start.29) | collective-permute-done | bytes 262176 | tf_op jit(solution)/shard_map/ppermute | solution.py:302
  113.8 0.7 collective-permute-start.30
  114.5 0.9 collective-permute-done.25.two
  115.4 1.6 %collective-permute-start.26 = (bf16[4,512,128]{2,1,0:T(8,128)(2,1)S(1)}, bf16[4,512,128]{2,1,0:T(8,128)(2,1)S(1)}, u32[]{:S(2)}, u32[]{:S(2)}) collective-permute-start(bf16[4,512,128]{2,1,0:T(8,128)(2,1)S(1)} %shard_map.93.one), channel_id=1, source_target_pairs={{0,24},{8,16},{16,8},{24,0},{1,25},{9,17},{17,9},{25,1},{2,26},{10... | collective-permute-start | bytes 1572872 | tf_op jit(solution)/shard_map/ppermute | solution.py:302
  117.2 0.9 collective-permute-start.18
  118.0 8.8 %collective-permute-done.30.two = bf16[4,512,128]{2,1,0:T(8,128)(2,1)S(1)} collective-permute-done((bf16[4,512,128]{2,1,0:T(8,128)(2,1)S(1)}, bf16[4,512,128]{2,1,0:T(8,128)(2,1)S(1)}, u32[]{:S(2)}, u32[]{:S(2)}) %collective-permute-start.30) | collective-permute-done | bytes 524320 | tf_op jit(solution)/shard_map/ppermute | solution.py:302
  126.9 1.5 collective-permute-start.31
  129.4 2.4 %collective-permute-start.19 = (bf16[8,512,128]{2,1,0:T(8,128)(2,1)S(1)}, bf16[8,512,128]{2,1,0:T(8,128)(2,1)S(1)}, u32[]{:S(2)}, u32[]{:S(2)}) collective-permute-start(bf16[8,512,128]{2,1,0:T(8,128)(2,1)S(1)} %shard_map.88.refs_3_), channel_id=1, source_target_pairs={{0,96},{32,64},{64,32},{96,0},{1,97},{33,65},{65,33},{97,1},{2,98}... | collective-permute-start | bytes 3145736 | tf_op jit(solution)/shard_map/ppermute | solution.py:302
  131.9 2.8 %shard_map.103 = (f32[2048,128]{1,0:T(8,128)}, f32[2048,128]{1,0:T(8,128)}, f32[2048,128]{1,0:T(8,128)}) custom-call(f32[128,128]{1,0:T(8,128)S(1)} %bitcast.73, f32[2048,128]{1,0:T(8,128)S(1)} %get-tuple-element.46.mean, f32[2048,128]{1,0:T(8,128)S(1)} %bitcast.67, f32[2048,128]{1,0:T(8,128)S(1)} %bitcast.69, f32[2048,128]{1,0:T(8,128)S(1)} %bitcast.71), custom_call_target="tpu_custom_call" | custom-call | flops 5242880 | bytes 7340032 | tf_op jit(solution)/shard_map/pallas_call | solution.py:285
  134.7 2.3 %shard_map.98.refs_1_ = bf16[4,4,4,512,128]{4,3,2,1,0:T(8,128)(2,1)} custom-call(bf16[8,512,128]{2,1,0:T(8,128)(2,1)S(1)} %shard_map.97.refs_0_, bf16[8,512,128]{2,1,0:T(8,128)(2,1)S(1)} %shard_map.94.refs_1_, bf16[8,512,128]{2,1,0:T(8,128)(2,1)S(1)} %shard_map.91.refs_2_, bf16[8,512,128]{2,1,0:T(8,128)(2,1)S(1)} %shard_map.88.refs_3_), custom_call_target="tpu_custom_call" | custom-call | bytes 8388608 | tf_op jit(solution)/shard_map/pallas_call | solution.py:348
  136.9 13.7 %collective-permute-done.31.refs_0_ = bf16[8,512,128]{2,1,0:T(8,128)(2,1)S(1)} collective-permute-done((bf16[8,512,128]{2,1,0:T(8,128)(2,1)S(1)}, bf16[8,512,128]{2,1,0:T(8,128)(2,1)S(1)}, u32[]{:S(2)}, u32[]{:S(2)}) %collective-permute-start.31) | collective-permute-done | bytes 1048608 | tf_op jit(solution)/shard_map/ppermute | solution.py:302
  150.6 1.0 shard_map.99.refs_1_
  151.7 1.0 shard_map.100.refs_1_
  152.7 1.0 shard_map.101.refs_1_
  153.8 1.0 shard_map.102
  (56 shorter events, 3.6 us)
Async XLA Ops:
  3.6 36.6 %collective-permute-start.5 = (bf16[6,1024,128]{2,1,0:T(8,128)(2,1)S(1)}, bf16[6,1024,128]{2,1,0:T(8,128)(2,1)S(1)}, u32[]{:S(2)}, u32[]{:S(2)}) collective-permute-start(bf16[6,1024,128]{2,1,0:T(8,128)(2,1)S(1)} %get-tuple-element.34), channel_id=1, source_target_pairs={{0,24},{8,0},{16,8},{24,16},{1,25},{9,1},{17,9},{25,17},{2,26},{10... | collective-permute-start | bytes 4718600 | tf_op jit(solution)/shard_map/ppermute | solution.py:30
  6.5 37.5 %collective-permute-start.4 = (bf16[6,1024,128]{2,1,0:T(8,128)(2,1)S(1)}, bf16[6,1024,128]{2,1,0:T(8,128)(2,1)S(1)}, u32[]{:S(2)}, u32[]{:S(2)}) collective-permute-start(bf16[6,1024,128]{2,1,0:T(8,128)(2,1)S(1)} %get-tuple-element.33), channel_id=1, source_target_pairs={{0,8},{8,16},{16,24},{24,0},{1,9},{9,17},{17,25},{25,1},{2,10},{10... | collective-permute-start | bytes 4718600 | tf_op jit(solution)/shard_map/ppermute | solution.py:30
  6.5 38.1 %collective-permute-start = (bf16[6,1024,128]{2,1,0:T(8,128)(2,1)S(1)}, bf16[6,1024,128]{2,1,0:T(8,128)(2,1)S(1)}, u32[]{:S(2)}, u32[]{:S(2)}) collective-permute-start(bf16[6,1024,128]{2,1,0:T(8,128)(2,1)S(1)} %get-tuple-element.30), channel_id=1, source_target_pairs={{0,32},{32,64},{64,96},{96,0},{1,33},{33,65},{65,97},{97,1},{2,34}... | collective-permute-start | bytes 4718600 | tf_op jit(solution)/shard_map/ppermute | solution.py:30
  8.4 37.7 %collective-permute-start.1 = (bf16[6,1024,128]{2,1,0:T(8,128)(2,1)S(1)}, bf16[6,1024,128]{2,1,0:T(8,128)(2,1)S(1)}, u32[]{:S(2)}, u32[]{:S(2)}) collective-permute-start(bf16[6,1024,128]{2,1,0:T(8,128)(2,1)S(1)} %get-tuple-element.31), channel_id=1, source_target_pairs={{0,96},{32,0},{64,32},{96,64},{1,97},{33,1},{65,33},{97,65},{2,98}... | collective-permute-start | bytes 4718600 | tf_op jit(solution)/shard_map/ppermute | solution.py:30
  40.2 14.1 %collective-permute-start.7 = (bf16[2,1024,128]{2,1,0:T(8,128)(2,1)S(1)}, bf16[2,1024,128]{2,1,0:T(8,128)(2,1)S(1)}, u32[]{:S(2)}, u32[]{:S(2)}) collective-permute-start(bf16[2,1024,128]{2,1,0:T(8,128)(2,1)S(1)} %slice.19), channel_id=1, source_target_pairs={{0,24},{8,0},{16,8},{24,16},{1,25},{9,1},{17,9},{25,17},{2,26},{10... | collective-permute-start | bytes 1572872 | tf_op jit(solution)/shard_map/ppermute | solution.py:30
  44.0 13.8 %collective-permute-start.6 = (bf16[2,1024,128]{2,1,0:T(8,128)(2,1)S(1)}, bf16[2,1024,128]{2,1,0:T(8,128)(2,1)S(1)}, u32[]{:S(2)}, u32[]{:S(2)}) collective-permute-start(bf16[2,1024,128]{2,1,0:T(8,128)(2,1)S(1)} %slice.18), channel_id=1, source_target_pairs={{0,8},{8,16},{16,24},{24,0},{1,9},{9,17},{17,25},{25,1},{2,10},{10... | collective-permute-start | bytes 1572872 | tf_op jit(solution)/shard_map/ppermute | solution.py:30
  44.7 17.4 %collective-permute-start.2 = (bf16[2,1024,128]{2,1,0:T(8,128)(2,1)S(1)}, bf16[2,1024,128]{2,1,0:T(8,128)(2,1)S(1)}, u32[]{:S(2)}, u32[]{:S(2)}) collective-permute-start(bf16[2,1024,128]{2,1,0:T(8,128)(2,1)S(1)} %slice.16), channel_id=1, source_target_pairs={{0,32},{32,64},{64,96},{96,0},{1,33},{33,65},{65,97},{97,1},{2,34}... | collective-permute-start | bytes 1572872 | tf_op jit(solution)/shard_map/ppermute | solution.py:30
  46.1 15.9 %collective-permute-start.3 = (bf16[2,1024,128]{2,1,0:T(8,128)(2,1)S(1)}, bf16[2,1024,128]{2,1,0:T(8,128)(2,1)S(1)}, u32[]{:S(2)}, u32[]{:S(2)}) collective-permute-start(bf16[2,1024,128]{2,1,0:T(8,128)(2,1)S(1)} %slice.17), channel_id=1, source_target_pairs={{0,96},{32,0},{64,32},{96,64},{1,97},{33,1},{65,33},{97,65},{2,98}... | collective-permute-start | bytes 1572872 | tf_op jit(solution)/shard_map/ppermute | solution.py:30
  57.8 8.5 %collective-permute-start.12 = (f32[512,128]{1,0:T(8,128)S(1)}, f32[512,128]{1,0:T(8,128)S(1)}, u32[]{:S(2)}, u32[]{:S(2)}) collective-permute-start(f32[512,128]{1,0:T(8,128)S(1)} %get-tuple-element.41), channel_id=1, source_target_pairs={{0,32},{32,64},{64,96},{96,0},{1,33},{33,65},{65,97},{97,1},{2,34}... | collective-permute-start | bytes 786440 | tf_op jit(solution)/shard_map/ppermute | solution.py:30
  59.8 6.5 %collective-permute-start.13 = (f32[512,128]{1,0:T(8,128)S(1)}, f32[512,128]{1,0:T(8,128)S(1)}, u32[]{:S(2)}, u32[]{:S(2)}) collective-permute-start(f32[512,128]{1,0:T(8,128)S(1)} %get-tuple-element.42), channel_id=1, source_target_pairs={{0,96},{32,0},{64,32},{96,64},{1,97},{33,1},{65,33},{97,65},{2,98}... | collective-permute-start | bytes 786440 | tf_op jit(solution)/shard_map/ppermute | solution.py:30
  62.1 7.8 %collective-permute-start.8 = (f32[512,128]{1,0:T(8,128)S(1)}, f32[512,128]{1,0:T(8,128)S(1)}, u32[]{:S(2)}, u32[]{:S(2)}) collective-permute-start(f32[512,128]{1,0:T(8,128)S(1)} %get-tuple-element.36), channel_id=1, source_target_pairs={{0,8},{8,16},{16,24},{24,0},{1,9},{9,17},{17,25},{25,1},{2,10},{10... | collective-permute-start | bytes 786440 | tf_op jit(solution)/shard_map/ppermute | solution.py:30
  62.2 7.7 %collective-permute-start.9 = (f32[512,128]{1,0:T(8,128)S(1)}, f32[512,128]{1,0:T(8,128)S(1)}, u32[]{:S(2)}, u32[]{:S(2)}) collective-permute-start(f32[512,128]{1,0:T(8,128)S(1)} %get-tuple-element.37), channel_id=1, source_target_pairs={{0,24},{8,0},{16,8},{24,16},{1,25},{9,1},{17,9},{25,17},{2,26},{10... | collective-permute-start | bytes 786440 | tf_op jit(solution)/shard_map/ppermute | solution.py:30
  66.5 12.1 %collective-permute-start.14 = (f32[1024,128]{1,0:T(8,128)S(1)}, f32[1024,128]{1,0:T(8,128)S(1)}, u32[]{:S(2)}, u32[]{:S(2)}) collective-permute-start(f32[1024,128]{1,0:T(8,128)S(1)} %get-tuple-element.43), channel_id=1, source_target_pairs={{0,32},{32,64},{64,96},{96,0},{1,33},{33,65},{65,97},{97,1},{2,34}... | collective-permute-start | bytes 1572872 | tf_op jit(solution)/shard_map/ppermute | solution.py:30
  68.3 10.2 %collective-permute-start.15 = (f32[1024,128]{1,0:T(8,128)S(1)}, f32[1024,128]{1,0:T(8,128)S(1)}, u32[]{:S(2)}, u32[]{:S(2)}) collective-permute-start(f32[1024,128]{1,0:T(8,128)S(1)} %get-tuple-element.44), channel_id=1, source_target_pairs={{0,96},{32,0},{64,32},{96,64},{1,97},{33,1},{65,33},{97,65},{2,98}... | collective-permute-start | bytes 1572872 | tf_op jit(solution)/shard_map/ppermute | solution.py:30
  70.1 11.6 %collective-permute-start.10 = (f32[1024,128]{1,0:T(8,128)S(1)}, f32[1024,128]{1,0:T(8,128)S(1)}, u32[]{:S(2)}, u32[]{:S(2)}) collective-permute-start(f32[1024,128]{1,0:T(8,128)S(1)} %get-tuple-element.38), channel_id=1, source_target_pairs={{0,8},{8,16},{16,24},{24,0},{1,9},{9,17},{17,25},{25,1},{2,10},{10... | collective-permute-start | bytes 1572872 | tf_op jit(solution)/shard_map/ppermute | solution.py:30
  70.1 11.5 %collective-permute-start.11 = (f32[1024,128]{1,0:T(8,128)S(1)}, f32[1024,128]{1,0:T(8,128)S(1)}, u32[]{:S(2)}, u32[]{:S(2)}) collective-permute-start(f32[1024,128]{1,0:T(8,128)S(1)} %get-tuple-element.39), channel_id=1, source_target_pairs={{0,24},{8,0},{16,8},{24,16},{1,25},{9,1},{17,9},{25,17},{2,26},{10... | collective-permute-start | bytes 1572872 | tf_op jit(solution)/shard_map/ppermute | solution.py:30
  73.5 26.4 %copy-start = (f32[1,4,65536]{2,1,0:T(4,128)S(1)}, f32[1,4,65536]{2,1,0:T(4,128)}, u32[]{:S(2)}) copy-start(f32[1,4,65536]{2,1,0:T(4,128)} %param.5) | copy-start | bytes 3145732
  73.6 26.4 %copy-start.1 = (f32[1,4,65536]{2,1,0:T(4,128)S(1)}, f32[1,4,65536]{2,1,0:T(4,128)}, u32[]{:S(2)}) copy-start(f32[1,4,65536]{2,1,0:T(4,128)} %param.6) | copy-start | bytes 3145732
  73.6 26.4 %copy-start.2 = (f32[1,4,65536]{2,1,0:T(4,128)S(1)}, f32[1,4,65536]{2,1,0:T(4,128)}, u32[]{:S(2)}) copy-start(f32[1,4,65536]{2,1,0:T(4,128)} %param.7) | copy-start | bytes 3145732
  101.3 5.2 %collective-permute-start.28 = (bf16[1,512,128]{2,1,0:T(8,128)(2,1)S(1)}, bf16[1,512,128]{2,1,0:T(8,128)(2,1)S(1)}, u32[]{:S(2)}, u32[]{:S(2)}) collective-permute-start(bf16[1,512,128]{2,1,0:T(8,128)(2,1)S(1)} %bitcast.80), channel_id=1, source_target_pairs={{0,32},{32,0},{64,96},{96,64},{1,33},{33,1},{65,97},{97,65},{2,34}... | collective-permute-start | bytes 393224 | tf_op jit(solution)/shard_map/ppermute | solution.py:302
  102.2 5.0 %collective-permute-start.24 = (bf16[1,512,128]{2,1,0:T(8,128)(2,1)S(1)}, bf16[1,512,128]{2,1,0:T(8,128)(2,1)S(1)}, u32[]{:S(2)}, u32[]{:S(2)}) collective-permute-start(bf16[1,512,128]{2,1,0:T(8,128)(2,1)S(1)} %bitcast.78), channel_id=1, source_target_pairs={{0,8},{8,0},{16,24},{24,16},{1,9},{9,1},{17,25},{25,17},{2,10},{10... | collective-permute-start | bytes 393224 | tf_op jit(solution)/shard_map/ppermute | solution.py:302
  102.8 6.2 %collective-permute-start.20 = (bf16[1,512,128]{2,1,0:T(8,128)(2,1)S(1)}, bf16[1,512,128]{2,1,0:T(8,128)(2,1)S(1)}, u32[]{:S(2)}, u32[]{:S(2)}) collective-permute-start(bf16[1,512,128]{2,1,0:T(8,128)(2,1)S(1)} %bitcast.76), channel_id=1, source_target_pairs={{0,96},{32,64},{64,32},{96,0},{1,97},{33,65},{65,33},{97,1},{2,98}... | collective-permute-start | bytes 393224 | tf_op jit(solution)/shard_map/ppermute | solution.py:302
  103.9 6.6 %collective-permute-start.16 = (bf16[1,512,128]{2,1,0:T(8,128)(2,1)S(1)}, bf16[1,512,128]{2,1,0:T(8,128)(2,1)S(1)}, u32[]{:S(2)}, u32[]{:S(2)}) collective-permute-start(bf16[1,512,128]{2,1,0:T(8,128)(2,1)S(1)} %bitcast.74), channel_id=1, source_target_pairs={{0,24},{8,16},{16,8},{24,0},{1,25},{9,17},{17,9},{25,1},{2,26},{10... | collective-permute-start | bytes 393224 | tf_op jit(solution)/shard_map/ppermute | solution.py:302
  106.6 7.1 %collective-permute-start.29 = (bf16[2,512,128]{2,1,0:T(8,128)(2,1)S(1)}, bf16[2,512,128]{2,1,0:T(8,128)(2,1)S(1)}, u32[]{:S(2)}, u32[]{:S(2)}) collective-permute-start(bf16[2,512,128]{2,1,0:T(8,128)(2,1)S(1)} %shard_map.95.one), channel_id=1, source_target_pairs={{0,8},{8,0},{16,24},{24,16},{1,9},{9,1},{17,25},{25,17},{2,10},{10... | collective-permute-start | bytes 786440 | tf_op jit(solution)/shard_map/ppermute | solution.py:302
  107.3 8.1 %collective-permute-start.25 = (bf16[2,512,128]{2,1,0:T(8,128)(2,1)S(1)}, bf16[2,512,128]{2,1,0:T(8,128)(2,1)S(1)}, u32[]{:S(2)}, u32[]{:S(2)}) collective-permute-start(bf16[2,512,128]{2,1,0:T(8,128)(2,1)S(1)} %shard_map.92.one), channel_id=1, source_target_pairs={{0,96},{32,64},{64,32},{96,0},{1,97},{33,65},{65,33},{97,1},{2,98}... | collective-permute-start | bytes 786440 | tf_op jit(solution)/shard_map/ppermute | solution.py:302
  109.0 8.0 %collective-permute-start.21 = (bf16[2,512,128]{2,1,0:T(8,128)(2,1)S(1)}, bf16[2,512,128]{2,1,0:T(8,128)(2,1)S(1)}, u32[]{:S(2)}, u32[]{:S(2)}) collective-permute-start(bf16[2,512,128]{2,1,0:T(8,128)(2,1)S(1)} %shard_map.89.one), channel_id=1, source_target_pairs={{0,24},{8,16},{16,8},{24,0},{1,25},{9,17},{17,9},{25,1},{2,26},{10... | collective-permute-start | bytes 786440 | tf_op jit(solution)/shard_map/ppermute | solution.py:302
  110.5 6.6 %collective-permute-start.17 = (bf16[2,512,128]{2,1,0:T(8,128)(2,1)S(1)}, bf16[2,512,128]{2,1,0:T(8,128)(2,1)S(1)}, u32[]{:S(2)}, u32[]{:S(2)}) collective-permute-start(bf16[2,512,128]{2,1,0:T(8,128)(2,1)S(1)} %shard_map.86.one), channel_id=1, source_target_pairs={{0,32},{32,0},{64,96},{96,64},{1,33},{33,1},{65,97},{97,65},{2,34}... | collective-permute-start | bytes 786440 | tf_op jit(solution)/shard_map/ppermute | solution.py:302
  113.8 13.1 %collective-permute-start.30 = (bf16[4,512,128]{2,1,0:T(8,128)(2,1)S(1)}, bf16[4,512,128]{2,1,0:T(8,128)(2,1)S(1)}, u32[]{:S(2)}, u32[]{:S(2)}) collective-permute-start(bf16[4,512,128]{2,1,0:T(8,128)(2,1)S(1)} %shard_map.96.one), channel_id=1, source_target_pairs={{0,96},{32,64},{64,32},{96,0},{1,97},{33,65},{65,33},{97,1},{2,98}... | collective-permute-start | bytes 1572872 | tf_op jit(solution)/shard_map/ppermute | solution.py:302
  115.4 13.1 %collective-permute-start.26 = (bf16[4,512,128]{2,1,0:T(8,128)(2,1)S(1)}, bf16[4,512,128]{2,1,0:T(8,128)(2,1)S(1)}, u32[]{:S(2)}, u32[]{:S(2)}) collective-permute-start(bf16[4,512,128]{2,1,0:T(8,128)(2,1)S(1)} %shard_map.93.one), channel_id=1, source_target_pairs={{0,24},{8,16},{16,8},{24,0},{1,25},{9,17},{17,9},{25,1},{2,26},{10... | collective-permute-start | bytes 1572872 | tf_op jit(solution)/shard_map/ppermute | solution.py:302
  117.0 11.9 %collective-permute-start.22 = (bf16[4,512,128]{2,1,0:T(8,128)(2,1)S(1)}, bf16[4,512,128]{2,1,0:T(8,128)(2,1)S(1)}, u32[]{:S(2)}, u32[]{:S(2)}) collective-permute-start(bf16[4,512,128]{2,1,0:T(8,128)(2,1)S(1)} %shard_map.90.one), channel_id=1, source_target_pairs={{0,32},{32,0},{64,96},{96,64},{1,33},{33,1},{65,97},{97,65},{2,34}... | collective-permute-start | bytes 1572872 | tf_op jit(solution)/shard_map/ppermute | solution.py:302
  117.2 12.2 %collective-permute-start.18 = (bf16[4,512,128]{2,1,0:T(8,128)(2,1)S(1)}, bf16[4,512,128]{2,1,0:T(8,128)(2,1)S(1)}, u32[]{:S(2)}, u32[]{:S(2)}) collective-permute-start(bf16[4,512,128]{2,1,0:T(8,128)(2,1)S(1)} %shard_map.87.one), channel_id=1, source_target_pairs={{0,8},{8,0},{16,24},{24,16},{1,9},{9,1},{17,25},{25,17},{2,10},{10... | collective-permute-start | bytes 1572872 | tf_op jit(solution)/shard_map/ppermute | solution.py:302
  126.9 23.7 %collective-permute-start.31 = (bf16[8,512,128]{2,1,0:T(8,128)(2,1)S(1)}, bf16[8,512,128]{2,1,0:T(8,128)(2,1)S(1)}, u32[]{:S(2)}, u32[]{:S(2)}) collective-permute-start(bf16[8,512,128]{2,1,0:T(8,128)(2,1)S(1)} %shard_map.97.refs_0_), channel_id=1, source_target_pairs={{0,24},{8,16},{16,8},{24,0},{1,25},{9,17},{17,9},{25,1},{2,26},{10... | collective-permute-start | bytes 3145736 | tf_op jit(solution)/shard_map/ppermute | solution.py:302
  128.5 23.1 %collective-permute-start.27 = (bf16[8,512,128]{2,1,0:T(8,128)(2,1)S(1)}, bf16[8,512,128]{2,1,0:T(8,128)(2,1)S(1)}, u32[]{:S(2)}, u32[]{:S(2)}) collective-permute-start(bf16[8,512,128]{2,1,0:T(8,128)(2,1)S(1)} %shard_map.94.refs_1_), channel_id=1, source_target_pairs={{0,32},{32,0},{64,96},{96,64},{1,33},{33,1},{65,97},{97,65},{2,34}... | collective-permute-start | bytes 3145736 | tf_op jit(solution)/shard_map/ppermute | solution.py:302
  129.0 23.7 %collective-permute-start.23 = (bf16[8,512,128]{2,1,0:T(8,128)(2,1)S(1)}, bf16[8,512,128]{2,1,0:T(8,128)(2,1)S(1)}, u32[]{:S(2)}, u32[]{:S(2)}) collective-permute-start(bf16[8,512,128]{2,1,0:T(8,128)(2,1)S(1)} %shard_map.91.refs_2_), channel_id=1, source_target_pairs={{0,8},{8,0},{16,24},{24,16},{1,9},{9,1},{17,25},{25,17},{2,10},{10... | collective-permute-start | bytes 3145736 | tf_op jit(solution)/shard_map/ppermute | solution.py:302
  129.4 24.3 %collective-permute-start.19 = (bf16[8,512,128]{2,1,0:T(8,128)(2,1)S(1)}, bf16[8,512,128]{2,1,0:T(8,128)(2,1)S(1)}, u32[]{:S(2)}, u32[]{:S(2)}) collective-permute-start(bf16[8,512,128]{2,1,0:T(8,128)(2,1)S(1)} %shard_map.88.refs_3_), channel_id=1, source_target_pairs={{0,96},{32,64},{64,32},{96,0},{1,97},{33,65},{65,33},{97,1},{2,98}... | collective-permute-start | bytes 3145736 | tf_op jit(solution)/shard_map/ppermute | solution.py:302

commit v7 on v6

--- a/solution.py
+++ b/solution.py
@@ -208,16 +208,18 @@
 
 def last_sum_kernel(*refs):
     parts_a, parts_b, (mean, squares, held) = refs[:3], refs[3:6], refs[6:]
+    half = parts_a[0].shape[0]
     held[...] = jnp.zeros_like(held)
-    for parts, first in ((parts_a, 0), (parts_b, parts_a[0].shape[0])):
-
-        @chunks_of(parts[0].shape[0], first)
-        def _(rows, target):
+
+    @chunks_of(half, half)
+    def _(rows, upper):
+        for parts, target in ((parts_a, rows), (parts_b, upper)):
             total = (parts[0][rows] + parts[1][rows] + parts[2][rows]) * (1.0 / 16.0)
             mean[target] = total
-            held[...] += jnp.sum((total * total).reshape(-1, 8, LANES), axis=0)
-
-    squares[...] = jnp.broadcast_to(jnp.sum(held[...], axis=0, keepdims=True), squares.shape)
+            held[...] += total * total
+
+    total = jnp.sum(held[...], axis=0, keepdims=True)
+    squares[...] = jnp.broadcast_to(total, squares.shape)
 
 
 def last_sum(parts_a, parts_b, devices):
@@ -228,7 +230,7 @@
         in_specs=[here] * 6,
         out_specs=[here] * 2,
         out_shape=[jax.ShapeDtypeStruct((rows, LANES), f32), jax.ShapeDtypeStruct((devices, LANES), f32)],
-        scratch_shapes=[pltpu.VMEM((8, LANES), f32)],
+        scratch_shapes=[pltpu.VMEM((64, LANES), f32)],
         compiler_params=pltpu.CompilerParams(vmem_limit_bytes=VMEM_LIMIT),
         cost_estimate=cost(8 * rows * LANES, 20 * rows * LANES),
     )(*parts_a, *parts_b)
@@ -239,7 +241,7 @@
     new_first = beta_first * first + (1.0 - beta_first) * scaled
     new_second = beta_second * second + (1.0 - beta_second) * scaled * scaled
     direction = (new_first * (1.0 / correct_first)) / (jnp.sqrt(new_second * (1.0 / correct_second)) + tiny_eps)
-    new_master = master - learn_rate * (decay_rate * master + direction)
+    new_master = (1.0 - learn_rate * decay_rate) * master - learn_rate * direction
     return (new_master, new_first, new_second)
 
 

time: 155 us -> 155 us (level)
  no operation moved by 1% of the time
where the time goes in v7:
time: 155 us
  waiting for transfers between devices  74.7 us (48%)
  starting transfers between devices  43.3 us (28%)
  blocking collectives  17.8 us (11%)
  Pallas kernels  17.7 us (11%)
    ppermute x16, waiting for transfers between devices, shift(): lax.ppermute(value, axis, [(i, (i + by) % size) for i in range(size)])  45.6 us
    ppermute x16, waiting for transfers between devices, partner(): return lax.ppermute(value, axis, [(i, i ^ mask) for i in range(4)])  29 us
    ppermute x16, starting transfers between devices, shift(): lax.ppermute(value, axis, [(i, (i + by) % size) for i in range(size)])  28.7 us
    all_to_all x1, blocking collectives, shards(): squares = lax.all_to_all(squares, (Z, X, Y, CORE), 0, 0, tiled=True)  17.8 us
    ppermute x16, starting transfers between devices, partner(): return lax.ppermute(value, axis, [(i, i ^ mask) for i in range(4)])  14.6 us
    pallas_call x5, Pallas kernels, set_blocks(): pl.pallas_call(functools.partial(set_kernel, jobs, len(parts)), in_specs=...  6.41 us
  transfers between devices with their start and end apart: 32, of which 15 were waited for; matrix products, arithmetic and copies ran while one was open for 0% of the time, Pallas kernels for 8%

profile of v7, /device:TPU:0, one launch (start us, length us, event | category | flops | bytes accessed | tf_op | source)
XLA Modules:
  0.0 154.5 jit_solution(7723044677446343286)
XLA Ops:
  0.6 2.9 %shard_map.76 = (bf16[6,1024,128]{2,1,0:T(8,128)(2,1)S(1)}, bf16[6,1024,128]{2,1,0:T(8,128)(2,1)S(1)}, bf16[6,1024,128]{2,1,0:T(8,128)(2,1)S(1)}, bf16[6,1024,128]{2,1,0:T(8,128)(2,1)S(1)}) custom-call(s32[1]{0:T(128)} %bitcast.3.at_z, s32[1]{0:T(128)} %bitcast.4.at_x, bf16[4,4,2048,128]{3,2,1,0:T(8,128)(2,1)} %bitcast.84), custom_call_target="tpu_custom_call" | custom-call | bytes 12582912 | tf_op jit(solution)/shard_map/pallas_call | solution.py:65
  3.6 2.9 %collective-permute-start.5 = (bf16[6,1024,128]{2,1,0:T(8,128)(2,1)S(1)}, bf16[6,1024,128]{2,1,0:T(8,128)(2,1)S(1)}, u32[]{:S(2)}, u32[]{:S(2)}) collective-permute-start(bf16[6,1024,128]{2,1,0:T(8,128)(2,1)S(1)} %get-tuple-element.34), channel_id=1, source_target_pairs={{0,24},{8,0},{16,8},{24,16},{1,25},{9,1},{17,9},{25,17},{2,26},{10... | collective-permute-start | bytes 4718600 | tf_op jit(solution)/shard_map/ppermute | solution.py:30
  6.5 1.9 %collective-permute-start = (bf16[6,1024,128]{2,1,0:T(8,128)(2,1)S(1)}, bf16[6,1024,128]{2,1,0:T(8,128)(2,1)S(1)}, u32[]{:S(2)}, u32[]{:S(2)}) collective-permute-start(bf16[6,1024,128]{2,1,0:T(8,128)(2,1)S(1)} %get-tuple-element.30), channel_id=1, source_target_pairs={{0,32},{32,64},{64,96},{96,0},{1,33},{33,65},{65,97},{97,1},{2,34}... | collective-permute-start | bytes 4718600 | tf_op jit(solution)/shard_map/ppermute | solution.py:30
  8.4 2.1 %collective-permute-start.1 = (bf16[6,1024,128]{2,1,0:T(8,128)(2,1)S(1)}, bf16[6,1024,128]{2,1,0:T(8,128)(2,1)S(1)}, u32[]{:S(2)}, u32[]{:S(2)}) collective-permute-start(bf16[6,1024,128]{2,1,0:T(8,128)(2,1)S(1)} %get-tuple-element.31), channel_id=1, source_target_pairs={{0,96},{32,0},{64,32},{96,64},{1,97},{33,1},{65,33},{97,65},{2,98}... | collective-permute-start | bytes 4718600 | tf_op jit(solution)/shard_map/ppermute | solution.py:30
  10.5 29.6 %collective-permute-done.5.ahead = bf16[6,1024,128]{2,1,0:T(8,128)(2,1)S(1)} collective-permute-done((bf16[6,1024,128]{2,1,0:T(8,128)(2,1)S(1)}, bf16[6,1024,128]{2,1,0:T(8,128)(2,1)S(1)}, u32[]{:S(2)}, u32[]{:S(2)}) %collective-permute-start.5) | collective-permute-done | bytes 1572896 | tf_op jit(solution)/shard_map/ppermute | solution.py:30
  40.2 3.8 %collective-permute-start.7 = (bf16[2,1024,128]{2,1,0:T(8,128)(2,1)S(1)}, bf16[2,1024,128]{2,1,0:T(8,128)(2,1)S(1)}, u32[]{:S(2)}, u32[]{:S(2)}) collective-permute-start(bf16[2,1024,128]{2,1,0:T(8,128)(2,1)S(1)} %slice.19), channel_id=1, source_target_pairs={{0,24},{8,0},{16,8},{24,16},{1,25},{9,1},{17,9},{25,17},{2,26},{10... | collective-permute-start | bytes 1572872 | tf_op jit(solution)/shard_map/ppermute | solution.py:30
  44.1 0.6 collective-permute-done.behind
  44.7 1.4 collective-permute-start.2
  46.1 2.2 %collective-permute-start.3 = (bf16[2,1024,128]{2,1,0:T(8,128)(2,1)S(1)}, bf16[2,1024,128]{2,1,0:T(8,128)(2,1)S(1)}, u32[]{:S(2)}, u32[]{:S(2)}) collective-permute-start(bf16[2,1024,128]{2,1,0:T(8,128)(2,1)S(1)} %slice.17), channel_id=1, source_target_pairs={{0,96},{32,0},{64,32},{96,64},{1,97},{33,1},{65,33},{97,65},{2,98}... | collective-permute-start | bytes 1572872 | tf_op jit(solution)/shard_map/ppermute | solution.py:30
  48.4 1.6 %shard_map.75 = (bf16[4,1024,128]{2,1,0:T(8,128)(2,1)S(1)}, bf16[4,1024,128]{2,1,0:T(8,128)(2,1)S(1)}) custom-call(bf16[4,4,2048,128]{3,2,1,0:T(8,128)(2,1)} %bitcast.85), custom_call_target="tpu_custom_call" | custom-call | bytes 4194304 | tf_op jit(solution)/shard_map/pallas_call | solution.py:95
  49.9 0.7 shard_map.78.refs_3_.base
  50.6 0.7 shard_map.77.refs_0_.base
  51.3 3.0 %collective-permute-done.7 = bf16[2,1024,128]{2,1,0:T(8,128)(2,1)S(1)} collective-permute-done((bf16[2,1024,128]{2,1,0:T(8,128)(2,1)S(1)}, bf16[2,1024,128]{2,1,0:T(8,128)(2,1)S(1)}, u32[]{:S(2)}, u32[]{:S(2)}) %collective-permute-start.7) | collective-permute-done | bytes 524320 | tf_op jit(solution)/shard_map/ppermute | solution.py:30
  54.2 3.5 %collective-permute-done.6 = bf16[2,1024,128]{2,1,0:T(8,128)(2,1)S(1)} collective-permute-done((bf16[2,1024,128]{2,1,0:T(8,128)(2,1)S(1)}, bf16[2,1024,128]{2,1,0:T(8,128)(2,1)S(1)}, u32[]{:S(2)}, u32[]{:S(2)}) %collective-permute-start.6) | collective-permute-done | bytes 524320 | tf_op jit(solution)/shard_map/ppermute | solution.py:30
  57.8 2.0 %collective-permute-start.12 = (f32[512,128]{1,0:T(8,128)S(1)}, f32[512,128]{1,0:T(8,128)S(1)}, u32[]{:S(2)}, u32[]{:S(2)}) collective-permute-start(f32[512,128]{1,0:T(8,128)S(1)} %get-tuple-element.41), channel_id=1, source_target_pairs={{0,32},{32,64},{64,96},{96,0},{1,33},{33,65},{65,97},{97,1},{2,34}... | collective-permute-start | bytes 786440 | tf_op jit(solution)/shard_map/ppermute | solution.py:30
  59.8 2.2 %collective-permute-start.13 = (f32[512,128]{1,0:T(8,128)S(1)}, f32[512,128]{1,0:T(8,128)S(1)}, u32[]{:S(2)}, u32[]{:S(2)}) collective-permute-start(f32[512,128]{1,0:T(8,128)S(1)} %get-tuple-element.42), channel_id=1, source_target_pairs={{0,96},{32,0},{64,32},{96,64},{1,97},{33,1},{65,33},{97,65},{2,98}... | collective-permute-start | bytes 786440 | tf_op jit(solution)/shard_map/ppermute | solution.py:30
  62.2 3.2 %collective-permute-start.9 = (f32[512,128]{1,0:T(8,128)S(1)}, f32[512,128]{1,0:T(8,128)S(1)}, u32[]{:S(2)}, u32[]{:S(2)}) collective-permute-start(f32[512,128]{1,0:T(8,128)S(1)} %get-tuple-element.37), channel_id=1, source_target_pairs={{0,24},{8,0},{16,8},{24,16},{1,25},{9,1},{17,9},{25,17},{2,26},{10... | collective-permute-start | bytes 786440 | tf_op jit(solution)/shard_map/ppermute | solution.py:30
  65.4 0.9 collective-permute-done.12.came_low
  66.5 1.9 %collective-permute-start.14 = (f32[1024,128]{1,0:T(8,128)S(1)}, f32[1024,128]{1,0:T(8,128)S(1)}, u32[]{:S(2)}, u32[]{:S(2)}) collective-permute-start(f32[1024,128]{1,0:T(8,128)S(1)} %get-tuple-element.43), channel_id=1, source_target_pairs={{0,32},{32,64},{64,96},{96,0},{1,33},{33,65},{65,97},{97,1},{2,34}... | collective-permute-start | bytes 1572872 | tf_op jit(solution)/shard_map/ppermute | solution.py:30
  68.3 1.6 %collective-permute-start.15 = (f32[1024,128]{1,0:T(8,128)S(1)}, f32[1024,128]{1,0:T(8,128)S(1)}, u32[]{:S(2)}, u32[]{:S(2)}) collective-permute-start(f32[1024,128]{1,0:T(8,128)S(1)} %get-tuple-element.44), channel_id=1, source_target_pairs={{0,96},{32,0},{64,32},{96,64},{1,97},{33,1},{65,33},{97,65},{2,98}... | collective-permute-start | bytes 1572872 | tf_op jit(solution)/shard_map/ppermute | solution.py:30
  70.1 3.2 %collective-permute-start.11 = (f32[1024,128]{1,0:T(8,128)S(1)}, f32[1024,128]{1,0:T(8,128)S(1)}, u32[]{:S(2)}, u32[]{:S(2)}) collective-permute-start(f32[1024,128]{1,0:T(8,128)S(1)} %get-tuple-element.39), channel_id=1, source_target_pairs={{0,24},{8,0},{16,8},{24,16},{1,25},{9,1},{17,9},{25,17},{2,26},{10... | collective-permute-start | bytes 1572872 | tf_op jit(solution)/shard_map/ppermute | solution.py:30
  73.6 5.0 %collective-permute-done.14.refs_4_ = f32[1024,128]{1,0:T(8,128)S(1)} collective-permute-done((f32[1024,128]{1,0:T(8,128)S(1)}, f32[1024,128]{1,0:T(8,128)S(1)}, u32[]{:S(2)}, u32[]{:S(2)}) %collective-permute-start.14) | collective-permute-done | bytes 524320 | tf_op jit(solution)/shard_map/ppermute | solution.py:30
  78.5 3.1 %collective-permute-done.10.refs_1_ = f32[1024,128]{1,0:T(8,128)S(1)} collective-permute-done((f32[1024,128]{1,0:T(8,128)S(1)}, f32[1024,128]{1,0:T(8,128)S(1)}, u32[]{:S(2)}, u32[]{:S(2)}) %collective-permute-start.10) | collective-permute-done | bytes 524320 | tf_op jit(solution)/shard_map/ppermute | solution.py:30
  82.0 17.8 %all_to_all.11 = f32[128,1,128]{2,1,0:T(1,128)S(1)} all-to-all(f32[128,1,128]{2,1,0:T(1,128)S(1)} %bitcast.82), channel_id=1, replica_groups=mesh['z'=4,'x'=4,'y'=4,'core'=2] {'z','x','y','core'}, dimensions={0} | all-to-all | bytes 131072 | tf_op jit(solution)/shard_map/all_to_all | solution.py:409
  99.7 1.3 shard_map.85
  101.1 0.9 collective-permute-start.28
  102.0 0.6 collective-permute-start.24
  102.5 1.1 collective-permute-start.20
  103.6 0.8 collective-permute-start.16
  104.4 1.8 %collective-permute-done.28.two = bf16[1,512,128]{2,1,0:T(8,128)(2,1)S(1)} collective-permute-done((bf16[1,512,128]{2,1,0:T(8,128)(2,1)S(1)}, bf16[1,512,128]{2,1,0:T(8,128)(2,1)S(1)}, u32[]{:S(2)}, u32[]{:S(2)}) %collective-permute-start.28) | collective-permute-done | bytes 131104 | tf_op jit(solution)/shard_map/ppermute | solution.py:304
  106.3 0.7 collective-permute-start.29
  107.0 1.2 collective-permute-start.25
  108.7 1.4 collective-permute-start.21
  110.3 3.1 %collective-permute-done.29.two = bf16[2,512,128]{2,1,0:T(8,128)(2,1)S(1)} collective-permute-done((bf16[2,512,128]{2,1,0:T(8,128)(2,1)S(1)}, bf16[2,512,128]{2,1,0:T(8,128)(2,1)S(1)}, u32[]{:S(2)}, u32[]{:S(2)}) %collective-permute-start.29) | collective-permute-done | bytes 262176 | tf_op jit(solution)/shard_map/ppermute | solution.py:304
  113.5 0.7 collective-permute-start.30
  114.2 0.9 collective-permute-done.25.two
  115.1 1.6 %collective-permute-start.26 = (bf16[4,512,128]{2,1,0:T(8,128)(2,1)S(1)}, bf16[4,512,128]{2,1,0:T(8,128)(2,1)S(1)}, u32[]{:S(2)}, u32[]{:S(2)}) collective-permute-start(bf16[4,512,128]{2,1,0:T(8,128)(2,1)S(1)} %shard_map.93.one), channel_id=1, source_target_pairs={{0,24},{8,16},{16,8},{24,0},{1,25},{9,17},{17,9},{25,1},{2,26},{10... | collective-permute-start | bytes 1572872 | tf_op jit(solution)/shard_map/ppermute | solution.py:304
  116.9 0.9 collective-permute-start.18
  117.8 8.8 %collective-permute-done.30.two = bf16[4,512,128]{2,1,0:T(8,128)(2,1)S(1)} collective-permute-done((bf16[4,512,128]{2,1,0:T(8,128)(2,1)S(1)}, bf16[4,512,128]{2,1,0:T(8,128)(2,1)S(1)}, u32[]{:S(2)}, u32[]{:S(2)}) %collective-permute-start.30) | collective-permute-done | bytes 524320 | tf_op jit(solution)/shard_map/ppermute | solution.py:304
  126.6 1.5 collective-permute-start.31
  129.2 2.4 %collective-permute-start.19 = (bf16[8,512,128]{2,1,0:T(8,128)(2,1)S(1)}, bf16[8,512,128]{2,1,0:T(8,128)(2,1)S(1)}, u32[]{:S(2)}, u32[]{:S(2)}) collective-permute-start(bf16[8,512,128]{2,1,0:T(8,128)(2,1)S(1)} %shard_map.88.refs_3_), channel_id=1, source_target_pairs={{0,96},{32,64},{64,32},{96,0},{1,97},{33,65},{65,33},{97,1},{2,98}... | collective-permute-start | bytes 3145736 | tf_op jit(solution)/shard_map/ppermute | solution.py:304
  131.6 2.8 %shard_map.103 = (f32[2048,128]{1,0:T(8,128)}, f32[2048,128]{1,0:T(8,128)}, f32[2048,128]{1,0:T(8,128)}) custom-call(f32[128,128]{1,0:T(8,128)S(1)} %bitcast.73, f32[2048,128]{1,0:T(8,128)S(1)} %get-tuple-element.46.mean, f32[2048,128]{1,0:T(8,128)S(1)} %bitcast.67, f32[2048,128]{1,0:T(8,128)S(1)} %bitcast.69, f32[2048,128]{1,0:T(8,128)S(1)} %bitcast.71), custom_call_target="tpu_custom_call" | custom-call | flops 5242880 | bytes 7340032 | tf_op jit(solution)/shard_map/pallas_call | solution.py:287
  134.4 2.3 %shard_map.98.refs_1_ = bf16[4,4,4,512,128]{4,3,2,1,0:T(8,128)(2,1)} custom-call(bf16[8,512,128]{2,1,0:T(8,128)(2,1)S(1)} %shard_map.97.refs_0_, bf16[8,512,128]{2,1,0:T(8,128)(2,1)S(1)} %shard_map.94.refs_1_, bf16[8,512,128]{2,1,0:T(8,128)(2,1)S(1)} %shard_map.91.refs_2_, bf16[8,512,128]{2,1,0:T(8,128)(2,1)S(1)} %shard_map.88.refs_3_), custom_call_target="tpu_custom_call" | custom-call | bytes 8388608 | tf_op jit(solution)/shard_map/pallas_call | solution.py:350
  136.7 13.7 %collective-permute-done.31.refs_0_ = bf16[8,512,128]{2,1,0:T(8,128)(2,1)S(1)} collective-permute-done((bf16[8,512,128]{2,1,0:T(8,128)(2,1)S(1)}, bf16[8,512,128]{2,1,0:T(8,128)(2,1)S(1)}, u32[]{:S(2)}, u32[]{:S(2)}) %collective-permute-start.31) | collective-permute-done | bytes 1048608 | tf_op jit(solution)/shard_map/ppermute | solution.py:304
  150.3 1.0 shard_map.99.refs_1_
  151.4 1.0 shard_map.100.refs_1_
  152.4 1.0 shard_map.101.refs_1_
  153.5 1.0 shard_map.102
  (56 shorter events, 3.4 us)
Async XLA Ops:
  3.6 36.6 %collective-permute-start.5 = (bf16[6,1024,128]{2,1,0:T(8,128)(2,1)S(1)}, bf16[6,1024,128]{2,1,0:T(8,128)(2,1)S(1)}, u32[]{:S(2)}, u32[]{:S(2)}) collective-permute-start(bf16[6,1024,128]{2,1,0:T(8,128)(2,1)S(1)} %get-tuple-element.34), channel_id=1, source_target_pairs={{0,24},{8,0},{16,8},{24,16},{1,25},{9,1},{17,9},{25,17},{2,26},{10... | collective-permute-start | bytes 4718600 | tf_op jit(solution)/shard_map/ppermute | solution.py:30
  6.5 37.5 %collective-permute-start.4 = (bf16[6,1024,128]{2,1,0:T(8,128)(2,1)S(1)}, bf16[6,1024,128]{2,1,0:T(8,128)(2,1)S(1)}, u32[]{:S(2)}, u32[]{:S(2)}) collective-permute-start(bf16[6,1024,128]{2,1,0:T(8,128)(2,1)S(1)} %get-tuple-element.33), channel_id=1, source_target_pairs={{0,8},{8,16},{16,24},{24,0},{1,9},{9,17},{17,25},{25,1},{2,10},{10... | collective-permute-start | bytes 4718600 | tf_op jit(solution)/shard_map/ppermute | solution.py:30
  6.5 38.1 %collective-permute-start = (bf16[6,1024,128]{2,1,0:T(8,128)(2,1)S(1)}, bf16[6,1024,128]{2,1,0:T(8,128)(2,1)S(1)}, u32[]{:S(2)}, u32[]{:S(2)}) collective-permute-start(bf16[6,1024,128]{2,1,0:T(8,128)(2,1)S(1)} %get-tuple-element.30), channel_id=1, source_target_pairs={{0,32},{32,64},{64,96},{96,0},{1,33},{33,65},{65,97},{97,1},{2,34}... | collective-permute-start | bytes 4718600 | tf_op jit(solution)/shard_map/ppermute | solution.py:30
  8.4 37.7 %collective-permute-start.1 = (bf16[6,1024,128]{2,1,0:T(8,128)(2,1)S(1)}, bf16[6,1024,128]{2,1,0:T(8,128)(2,1)S(1)}, u32[]{:S(2)}, u32[]{:S(2)}) collective-permute-start(bf16[6,1024,128]{2,1,0:T(8,128)(2,1)S(1)} %get-tuple-element.31), channel_id=1, source_target_pairs={{0,96},{32,0},{64,32},{96,64},{1,97},{33,1},{65,33},{97,65},{2,98}... | collective-permute-start | bytes 4718600 | tf_op jit(solution)/shard_map/ppermute | solution.py:30
  40.2 14.1 %collective-permute-start.7 = (bf16[2,1024,128]{2,1,0:T(8,128)(2,1)S(1)}, bf16[2,1024,128]{2,1,0:T(8,128)(2,1)S(1)}, u32[]{:S(2)}, u32[]{:S(2)}) collective-permute-start(bf16[2,1024,128]{2,1,0:T(8,128)(2,1)S(1)} %slice.19), channel_id=1, source_target_pairs={{0,24},{8,0},{16,8},{24,16},{1,25},{9,1},{17,9},{25,17},{2,26},{10... | collective-permute-start | bytes 1572872 | tf_op jit(solution)/shard_map/ppermute | solution.py:30
  44.0 13.8 %collective-permute-start.6 = (bf16[2,1024,128]{2,1,0:T(8,128)(2,1)S(1)}, bf16[2,1024,128]{2,1,0:T(8,128)(2,1)S(1)}, u32[]{:S(2)}, u32[]{:S(2)}) collective-permute-start(bf16[2,1024,128]{2,1,0:T(8,128)(2,1)S(1)} %slice.18), channel_id=1, source_target_pairs={{0,8},{8,16},{16,24},{24,0},{1,9},{9,17},{17,25},{25,1},{2,10},{10... | collective-permute-start | bytes 1572872 | tf_op jit(solution)/shard_map/ppermute | solution.py:30
  44.7 17.4 %collective-permute-start.2 = (bf16[2,1024,128]{2,1,0:T(8,128)(2,1)S(1)}, bf16[2,1024,128]{2,1,0:T(8,128)(2,1)S(1)}, u32[]{:S(2)}, u32[]{:S(2)}) collective-permute-start(bf16[2,1024,128]{2,1,0:T(8,128)(2,1)S(1)} %slice.16), channel_id=1, source_target_pairs={{0,32},{32,64},{64,96},{96,0},{1,33},{33,65},{65,97},{97,1},{2,34}... | collective-permute-start | bytes 1572872 | tf_op jit(solution)/shard_map/ppermute | solution.py:30
  46.1 15.9 %collective-permute-start.3 = (bf16[2,1024,128]{2,1,0:T(8,128)(2,1)S(1)}, bf16[2,1024,128]{2,1,0:T(8,128)(2,1)S(1)}, u32[]{:S(2)}, u32[]{:S(2)}) collective-permute-start(bf16[2,1024,128]{2,1,0:T(8,128)(2,1)S(1)} %slice.17), channel_id=1, source_target_pairs={{0,96},{32,0},{64,32},{96,64},{1,97},{33,1},{65,33},{97,65},{2,98}... | collective-permute-start | bytes 1572872 | tf_op jit(solution)/shard_map/ppermute | solution.py:30
  57.8 8.5 %collective-permute-start.12 = (f32[512,128]{1,0:T(8,128)S(1)}, f32[512,128]{1,0:T(8,128)S(1)}, u32[]{:S(2)}, u32[]{:S(2)}) collective-permute-start(f32[512,128]{1,0:T(8,128)S(1)} %get-tuple-element.41), channel_id=1, source_target_pairs={{0,32},{32,64},{64,96},{96,0},{1,33},{33,65},{65,97},{97,1},{2,34}... | collective-permute-start | bytes 786440 | tf_op jit(solution)/shard_map/ppermute | solution.py:30
  59.8 6.5 %collective-permute-start.13 = (f32[512,128]{1,0:T(8,128)S(1)}, f32[512,128]{1,0:T(8,128)S(1)}, u32[]{:S(2)}, u32[]{:S(2)}) collective-permute-start(f32[512,128]{1,0:T(8,128)S(1)} %get-tuple-element.42), channel_id=1, source_target_pairs={{0,96},{32,0},{64,32},{96,64},{1,97},{33,1},{65,33},{97,65},{2,98}... | collective-permute-start | bytes 786440 | tf_op jit(solution)/shard_map/ppermute | solution.py:30
  62.1 7.8 %collective-permute-start.8 = (f32[512,128]{1,0:T(8,128)S(1)}, f32[512,128]{1,0:T(8,128)S(1)}, u32[]{:S(2)}, u32[]{:S(2)}) collective-permute-start(f32[512,128]{1,0:T(8,128)S(1)} %get-tuple-element.36), channel_id=1, source_target_pairs={{0,8},{8,16},{16,24},{24,0},{1,9},{9,17},{17,25},{25,1},{2,10},{10... | collective-permute-start | bytes 786440 | tf_op jit(solution)/shard_map/ppermute | solution.py:30
  62.2 7.7 %collective-permute-start.9 = (f32[512,128]{1,0:T(8,128)S(1)}, f32[512,128]{1,0:T(8,128)S(1)}, u32[]{:S(2)}, u32[]{:S(2)}) collective-permute-start(f32[512,128]{1,0:T(8,128)S(1)} %get-tuple-element.37), channel_id=1, source_target_pairs={{0,24},{8,0},{16,8},{24,16},{1,25},{9,1},{17,9},{25,17},{2,26},{10... | collective-permute-start | bytes 786440 | tf_op jit(solution)/shard_map/ppermute | solution.py:30
  66.5 12.1 %collective-permute-start.14 = (f32[1024,128]{1,0:T(8,128)S(1)}, f32[1024,128]{1,0:T(8,128)S(1)}, u32[]{:S(2)}, u32[]{:S(2)}) collective-permute-start(f32[1024,128]{1,0:T(8,128)S(1)} %get-tuple-element.43), channel_id=1, source_target_pairs={{0,32},{32,64},{64,96},{96,0},{1,33},{33,65},{65,97},{97,1},{2,34}... | collective-permute-start | bytes 1572872 | tf_op jit(solution)/shard_map/ppermute | solution.py:30
  68.3 10.2 %collective-permute-start.15 = (f32[1024,128]{1,0:T(8,128)S(1)}, f32[1024,128]{1,0:T(8,128)S(1)}, u32[]{:S(2)}, u32[]{:S(2)}) collective-permute-start(f32[1024,128]{1,0:T(8,128)S(1)} %get-tuple-element.44), channel_id=1, source_target_pairs={{0,96},{32,0},{64,32},{96,64},{1,97},{33,1},{65,33},{97,65},{2,98}... | collective-permute-start | bytes 1572872 | tf_op jit(solution)/shard_map/ppermute | solution.py:30
  70.1 11.6 %collective-permute-start.10 = (f32[1024,128]{1,0:T(8,128)S(1)}, f32[1024,128]{1,0:T(8,128)S(1)}, u32[]{:S(2)}, u32[]{:S(2)}) collective-permute-start(f32[1024,128]{1,0:T(8,128)S(1)} %get-tuple-element.38), channel_id=1, source_target_pairs={{0,8},{8,16},{16,24},{24,0},{1,9},{9,17},{17,25},{25,1},{2,10},{10... | collective-permute-start | bytes 1572872 | tf_op jit(solution)/shard_map/ppermute | solution.py:30
  70.1 11.5 %collective-permute-start.11 = (f32[1024,128]{1,0:T(8,128)S(1)}, f32[1024,128]{1,0:T(8,128)S(1)}, u32[]{:S(2)}, u32[]{:S(2)}) collective-permute-start(f32[1024,128]{1,0:T(8,128)S(1)} %get-tuple-element.39), channel_id=1, source_target_pairs={{0,24},{8,0},{16,8},{24,16},{1,25},{9,1},{17,9},{25,17},{2,26},{10... | collective-permute-start | bytes 1572872 | tf_op jit(solution)/shard_map/ppermute | solution.py:30
  73.5 26.2 %copy-start = (f32[1,4,65536]{2,1,0:T(4,128)S(1)}, f32[1,4,65536]{2,1,0:T(4,128)}, u32[]{:S(2)}) copy-start(f32[1,4,65536]{2,1,0:T(4,128)} %param.5) | copy-start | bytes 3145732
  73.6 26.2 %copy-start.1 = (f32[1,4,65536]{2,1,0:T(4,128)S(1)}, f32[1,4,65536]{2,1,0:T(4,128)}, u32[]{:S(2)}) copy-start(f32[1,4,65536]{2,1,0:T(4,128)} %param.6) | copy-start | bytes 3145732
  73.6 26.2 %copy-start.2 = (f32[1,4,65536]{2,1,0:T(4,128)S(1)}, f32[1,4,65536]{2,1,0:T(4,128)}, u32[]{:S(2)}) copy-start(f32[1,4,65536]{2,1,0:T(4,128)} %param.7) | copy-start | bytes 3145732
  101.1 5.2 %collective-permute-start.28 = (bf16[1,512,128]{2,1,0:T(8,128)(2,1)S(1)}, bf16[1,512,128]{2,1,0:T(8,128)(2,1)S(1)}, u32[]{:S(2)}, u32[]{:S(2)}) collective-permute-start(bf16[1,512,128]{2,1,0:T(8,128)(2,1)S(1)} %bitcast.80), channel_id=1, source_target_pairs={{0,32},{32,0},{64,96},{96,64},{1,33},{33,1},{65,97},{97,65},{2,34}... | collective-permute-start | bytes 393224 | tf_op jit(solution)/shard_map/ppermute | solution.py:304
  102.0 5.0 %collective-permute-start.24 = (bf16[1,512,128]{2,1,0:T(8,128)(2,1)S(1)}, bf16[1,512,128]{2,1,0:T(8,128)(2,1)S(1)}, u32[]{:S(2)}, u32[]{:S(2)}) collective-permute-start(bf16[1,512,128]{2,1,0:T(8,128)(2,1)S(1)} %bitcast.78), channel_id=1, source_target_pairs={{0,8},{8,0},{16,24},{24,16},{1,9},{9,1},{17,25},{25,17},{2,10},{10... | collective-permute-start | bytes 393224 | tf_op jit(solution)/shard_map/ppermute | solution.py:304
  102.5 6.2 %collective-permute-start.20 = (bf16[1,512,128]{2,1,0:T(8,128)(2,1)S(1)}, bf16[1,512,128]{2,1,0:T(8,128)(2,1)S(1)}, u32[]{:S(2)}, u32[]{:S(2)}) collective-permute-start(bf16[1,512,128]{2,1,0:T(8,128)(2,1)S(1)} %bitcast.76), channel_id=1, source_target_pairs={{0,96},{32,64},{64,32},{96,0},{1,97},{33,65},{65,33},{97,1},{2,98}... | collective-permute-start | bytes 393224 | tf_op jit(solution)/shard_map/ppermute | solution.py:304
  103.6 6.6 %collective-permute-start.16 = (bf16[1,512,128]{2,1,0:T(8,128)(2,1)S(1)}, bf16[1,512,128]{2,1,0:T(8,128)(2,1)S(1)}, u32[]{:S(2)}, u32[]{:S(2)}) collective-permute-start(bf16[1,512,128]{2,1,0:T(8,128)(2,1)S(1)} %bitcast.74), channel_id=1, source_target_pairs={{0,24},{8,16},{16,8},{24,0},{1,25},{9,17},{17,9},{25,1},{2,26},{10... | collective-permute-start | bytes 393224 | tf_op jit(solution)/shard_map/ppermute | solution.py:304
  106.3 7.1 %collective-permute-start.29 = (bf16[2,512,128]{2,1,0:T(8,128)(2,1)S(1)}, bf16[2,512,128]{2,1,0:T(8,128)(2,1)S(1)}, u32[]{:S(2)}, u32[]{:S(2)}) collective-permute-start(bf16[2,512,128]{2,1,0:T(8,128)(2,1)S(1)} %shard_map.95.one), channel_id=1, source_target_pairs={{0,8},{8,0},{16,24},{24,16},{1,9},{9,1},{17,25},{25,17},{2,10},{10... | collective-permute-start | bytes 786440 | tf_op jit(solution)/shard_map/ppermute | solution.py:304
  107.0 8.1 %collective-permute-start.25 = (bf16[2,512,128]{2,1,0:T(8,128)(2,1)S(1)}, bf16[2,512,128]{2,1,0:T(8,128)(2,1)S(1)}, u32[]{:S(2)}, u32[]{:S(2)}) collective-permute-start(bf16[2,512,128]{2,1,0:T(8,128)(2,1)S(1)} %shard_map.92.one), channel_id=1, source_target_pairs={{0,96},{32,64},{64,32},{96,0},{1,97},{33,65},{65,33},{97,1},{2,98}... | collective-permute-start | bytes 786440 | tf_op jit(solution)/shard_map/ppermute | solution.py:304
  108.7 8.0 %collective-permute-start.21 = (bf16[2,512,128]{2,1,0:T(8,128)(2,1)S(1)}, bf16[2,512,128]{2,1,0:T(8,128)(2,1)S(1)}, u32[]{:S(2)}, u32[]{:S(2)}) collective-permute-start(bf16[2,512,128]{2,1,0:T(8,128)(2,1)S(1)} %shard_map.89.one), channel_id=1, source_target_pairs={{0,24},{8,16},{16,8},{24,0},{1,25},{9,17},{17,9},{25,1},{2,26},{10... | collective-permute-start | bytes 786440 | tf_op jit(solution)/shard_map/ppermute | solution.py:304
  110.2 6.6 %collective-permute-start.17 = (bf16[2,512,128]{2,1,0:T(8,128)(2,1)S(1)}, bf16[2,512,128]{2,1,0:T(8,128)(2,1)S(1)}, u32[]{:S(2)}, u32[]{:S(2)}) collective-permute-start(bf16[2,512,128]{2,1,0:T(8,128)(2,1)S(1)} %shard_map.86.one), channel_id=1, source_target_pairs={{0,32},{32,0},{64,96},{96,64},{1,33},{33,1},{65,97},{97,65},{2,34}... | collective-permute-start | bytes 786440 | tf_op jit(solution)/shard_map/ppermute | solution.py:304
  113.5 13.1 %collective-permute-start.30 = (bf16[4,512,128]{2,1,0:T(8,128)(2,1)S(1)}, bf16[4,512,128]{2,1,0:T(8,128)(2,1)S(1)}, u32[]{:S(2)}, u32[]{:S(2)}) collective-permute-start(bf16[4,512,128]{2,1,0:T(8,128)(2,1)S(1)} %shard_map.96.one), channel_id=1, source_target_pairs={{0,96},{32,64},{64,32},{96,0},{1,97},{33,65},{65,33},{97,1},{2,98}... | collective-permute-start | bytes 1572872 | tf_op jit(solution)/shard_map/ppermute | solution.py:304
  115.1 13.1 %collective-permute-start.26 = (bf16[4,512,128]{2,1,0:T(8,128)(2,1)S(1)}, bf16[4,512,128]{2,1,0:T(8,128)(2,1)S(1)}, u32[]{:S(2)}, u32[]{:S(2)}) collective-permute-start(bf16[4,512,128]{2,1,0:T(8,128)(2,1)S(1)} %shard_map.93.one), channel_id=1, source_target_pairs={{0,24},{8,16},{16,8},{24,0},{1,25},{9,17},{17,9},{25,1},{2,26},{10... | collective-permute-start | bytes 1572872 | tf_op jit(solution)/shard_map/ppermute | solution.py:304
  116.7 11.9 %collective-permute-start.22 = (bf16[4,512,128]{2,1,0:T(8,128)(2,1)S(1)}, bf16[4,512,128]{2,1,0:T(8,128)(2,1)S(1)}, u32[]{:S(2)}, u32[]{:S(2)}) collective-permute-start(bf16[4,512,128]{2,1,0:T(8,128)(2,1)S(1)} %shard_map.90.one), channel_id=1, source_target_pairs={{0,32},{32,0},{64,96},{96,64},{1,33},{33,1},{65,97},{97,65},{2,34}... | collective-permute-start | bytes 1572872 | tf_op jit(solution)/shard_map/ppermute | solution.py:304
  116.9 12.2 %collective-permute-start.18 = (bf16[4,512,128]{2,1,0:T(8,128)(2,1)S(1)}, bf16[4,512,128]{2,1,0:T(8,128)(2,1)S(1)}, u32[]{:S(2)}, u32[]{:S(2)}) collective-permute-start(bf16[4,512,128]{2,1,0:T(8,128)(2,1)S(1)} %shard_map.87.one), channel_id=1, source_target_pairs={{0,8},{8,0},{16,24},{24,16},{1,9},{9,1},{17,25},{25,17},{2,10},{10... | collective-permute-start | bytes 1572872 | tf_op jit(solution)/shard_map/ppermute | solution.py:304
  126.6 23.7 %collective-permute-start.31 = (bf16[8,512,128]{2,1,0:T(8,128)(2,1)S(1)}, bf16[8,512,128]{2,1,0:T(8,128)(2,1)S(1)}, u32[]{:S(2)}, u32[]{:S(2)}) collective-permute-start(bf16[8,512,128]{2,1,0:T(8,128)(2,1)S(1)} %shard_map.97.refs_0_), channel_id=1, source_target_pairs={{0,24},{8,16},{16,8},{24,0},{1,25},{9,17},{17,9},{25,1},{2,26},{10... | collective-permute-start | bytes 3145736 | tf_op jit(solution)/shard_map/ppermute | solution.py:304
  128.2 23.1 %collective-permute-start.27 = (bf16[8,512,128]{2,1,0:T(8,128)(2,1)S(1)}, bf16[8,512,128]{2,1,0:T(8,128)(2,1)S(1)}, u32[]{:S(2)}, u32[]{:S(2)}) collective-permute-start(bf16[8,512,128]{2,1,0:T(8,128)(2,1)S(1)} %shard_map.94.refs_1_), channel_id=1, source_target_pairs={{0,32},{32,0},{64,96},{96,64},{1,33},{33,1},{65,97},{97,65},{2,34}... | collective-permute-start | bytes 3145736 | tf_op jit(solution)/shard_map/ppermute | solution.py:304
  128.7 23.7 %collective-permute-start.23 = (bf16[8,512,128]{2,1,0:T(8,128)(2,1)S(1)}, bf16[8,512,128]{2,1,0:T(8,128)(2,1)S(1)}, u32[]{:S(2)}, u32[]{:S(2)}) collective-permute-start(bf16[8,512,128]{2,1,0:T(8,128)(2,1)S(1)} %shard_map.91.refs_2_), channel_id=1, source_target_pairs={{0,8},{8,0},{16,24},{24,16},{1,9},{9,1},{17,25},{25,17},{2,10},{10... | collective-permute-start | bytes 3145736 | tf_op jit(solution)/shard_map/ppermute | solution.py:304
  129.2 24.3 %collective-permute-start.19 = (bf16[8,512,128]{2,1,0:T(8,128)(2,1)S(1)}, bf16[8,512,128]{2,1,0:T(8,128)(2,1)S(1)}, u32[]{:S(2)}, u32[]{:S(2)}) collective-permute-start(bf16[8,512,128]{2,1,0:T(8,128)(2,1)S(1)} %shard_map.88.refs_3_), channel_id=1, source_target_pairs={{0,96},{32,64},{64,32},{96,0},{1,97},{33,65},{65,33},{97,1},{2,98}... | collective-permute-start | bytes 3145736 | tf_op jit(solution)/shard_map/ppermute | solution.py:304

commit v8 on v7

--- a/solution.py
+++ b/solution.py
@@ -124,7 +124,7 @@
 
 
 def chunks_of(size, *starts):
-    step = max(n for n in (64, 48, 32, 16) if size % n == 0)
+    step = max(n for n in (128, 64, 48, 32, 16) if size % n == 0)
 
     def run(body):
         @pl.loop(0, size // step)
@@ -230,7 +230,7 @@
         in_specs=[here] * 6,
         out_specs=[here] * 2,
         out_shape=[jax.ShapeDtypeStruct((rows, LANES), f32), jax.ShapeDtypeStruct((devices, LANES), f32)],
-        scratch_shapes=[pltpu.VMEM((64, LANES), f32)],
+        scratch_shapes=[pltpu.VMEM((128, LANES), f32)],
         compiler_params=pltpu.CompilerParams(vmem_limit_bytes=VMEM_LIMIT),
         cost_estimate=cost(8 * rows * LANES, 20 * rows * LANES),
     )(*parts_a, *parts_b)

time: 155 us -> 154 us (level)
  no operation moved by 1% of the time
where the time goes in v8:
time: 154 us
  waiting for transfers between devices  75 us (49%)
  starting transfers between devices  43.3 us (28%)
  blocking collectives  17.8 us (12%)
  Pallas kernels  17.1 us (11%)
    ppermute x16, waiting for transfers between devices, shift(): lax.ppermute(value, axis, [(i, (i + by) % size) for i in range(size)])  46 us
    ppermute x16, waiting for transfers between devices, partner(): return lax.ppermute(value, axis, [(i, i ^ mask) for i in range(4)])  29 us
    ppermute x16, starting transfers between devices, shift(): lax.ppermute(value, axis, [(i, (i + by) % size) for i in range(size)])  28.7 us
    all_to_all x1, blocking collectives, shards(): squares = lax.all_to_all(squares, (Z, X, Y, CORE), 0, 0, tiled=True)  17.8 us
    ppermute x16, starting transfers between devices, partner(): return lax.ppermute(value, axis, [(i, i ^ mask) for i in range(4)])  14.6 us
    pallas_call x5, Pallas kernels, set_blocks(): pl.pallas_call(functools.partial(set_kernel, jobs, len(parts)), in_specs=...  6.41 us
  transfers between devices with their start and end apart: 32, of which 15 were waited for; matrix products, arithmetic and copies ran while one was open for 0% of the time, Pallas kernels for 8%

profile of v8, /device:TPU:0, one launch (start us, length us, event | category | flops | bytes accessed | tf_op | source)
XLA Modules:
  0.0 154.3 jit_solution(4850906780760862235)
XLA Ops:
  0.6 2.9 %shard_map.76 = (bf16[6,1024,128]{2,1,0:T(8,128)(2,1)S(1)}, bf16[6,1024,128]{2,1,0:T(8,128)(2,1)S(1)}, bf16[6,1024,128]{2,1,0:T(8,128)(2,1)S(1)}, bf16[6,1024,128]{2,1,0:T(8,128)(2,1)S(1)}) custom-call(s32[1]{0:T(128)} %bitcast.3.at_z, s32[1]{0:T(128)} %bitcast.4.at_x, bf16[4,4,2048,128]{3,2,1,0:T(8,128)(2,1)} %bitcast.84), custom_call_target="tpu_custom_call" | custom-call | bytes 12582912 | tf_op jit(solution)/shard_map/pallas_call | solution.py:65
  3.6 2.9 %collective-permute-start.5 = (bf16[6,1024,128]{2,1,0:T(8,128)(2,1)S(1)}, bf16[6,1024,128]{2,1,0:T(8,128)(2,1)S(1)}, u32[]{:S(2)}, u32[]{:S(2)}) collective-permute-start(bf16[6,1024,128]{2,1,0:T(8,128)(2,1)S(1)} %get-tuple-element.34), channel_id=1, source_target_pairs={{0,24},{8,0},{16,8},{24,16},{1,25},{9,1},{17,9},{25,17},{2,26},{10... | collective-permute-start | bytes 4718600 | tf_op jit(solution)/shard_map/ppermute | solution.py:30
  6.5 1.9 %collective-permute-start = (bf16[6,1024,128]{2,1,0:T(8,128)(2,1)S(1)}, bf16[6,1024,128]{2,1,0:T(8,128)(2,1)S(1)}, u32[]{:S(2)}, u32[]{:S(2)}) collective-permute-start(bf16[6,1024,128]{2,1,0:T(8,128)(2,1)S(1)} %get-tuple-element.30), channel_id=1, source_target_pairs={{0,32},{32,64},{64,96},{96,0},{1,33},{33,65},{65,97},{97,1},{2,34}... | collective-permute-start | bytes 4718600 | tf_op jit(solution)/shard_map/ppermute | solution.py:30
  8.4 2.1 %collective-permute-start.1 = (bf16[6,1024,128]{2,1,0:T(8,128)(2,1)S(1)}, bf16[6,1024,128]{2,1,0:T(8,128)(2,1)S(1)}, u32[]{:S(2)}, u32[]{:S(2)}) collective-permute-start(bf16[6,1024,128]{2,1,0:T(8,128)(2,1)S(1)} %get-tuple-element.31), channel_id=1, source_target_pairs={{0,96},{32,0},{64,32},{96,64},{1,97},{33,1},{65,33},{97,65},{2,98}... | collective-permute-start | bytes 4718600 | tf_op jit(solution)/shard_map/ppermute | solution.py:30
  10.5 29.6 %collective-permute-done.5.ahead = bf16[6,1024,128]{2,1,0:T(8,128)(2,1)S(1)} collective-permute-done((bf16[6,1024,128]{2,1,0:T(8,128)(2,1)S(1)}, bf16[6,1024,128]{2,1,0:T(8,128)(2,1)S(1)}, u32[]{:S(2)}, u32[]{:S(2)}) %collective-permute-start.5) | collective-permute-done | bytes 1572896 | tf_op jit(solution)/shard_map/ppermute | solution.py:30
  40.2 3.8 %collective-permute-start.7 = (bf16[2,1024,128]{2,1,0:T(8,128)(2,1)S(1)}, bf16[2,1024,128]{2,1,0:T(8,128)(2,1)S(1)}, u32[]{:S(2)}, u32[]{:S(2)}) collective-permute-start(bf16[2,1024,128]{2,1,0:T(8,128)(2,1)S(1)} %slice.19), channel_id=1, source_target_pairs={{0,24},{8,0},{16,8},{24,16},{1,25},{9,1},{17,9},{25,17},{2,26},{10... | collective-permute-start | bytes 1572872 | tf_op jit(solution)/shard_map/ppermute | solution.py:30
  44.1 0.6 collective-permute-done.behind
  44.7 1.4 collective-permute-start.2
  46.1 2.2 %collective-permute-start.3 = (bf16[2,1024,128]{2,1,0:T(8,128)(2,1)S(1)}, bf16[2,1024,128]{2,1,0:T(8,128)(2,1)S(1)}, u32[]{:S(2)}, u32[]{:S(2)}) collective-permute-start(bf16[2,1024,128]{2,1,0:T(8,128)(2,1)S(1)} %slice.17), channel_id=1, source_target_pairs={{0,96},{32,0},{64,32},{96,64},{1,97},{33,1},{65,33},{97,65},{2,98}... | collective-permute-start | bytes 1572872 | tf_op jit(solution)/shard_map/ppermute | solution.py:30
  48.4 1.6 %shard_map.75 = (bf16[4,1024,128]{2,1,0:T(8,128)(2,1)S(1)}, bf16[4,1024,128]{2,1,0:T(8,128)(2,1)S(1)}) custom-call(bf16[4,4,2048,128]{3,2,1,0:T(8,128)(2,1)} %bitcast.85), custom_call_target="tpu_custom_call" | custom-call | bytes 4194304 | tf_op jit(solution)/shard_map/pallas_call | solution.py:95
  49.9 0.5 shard_map.78.refs_3_.base
  50.9 3.3 %collective-permute-done.7 = bf16[2,1024,128]{2,1,0:T(8,128)(2,1)S(1)} collective-permute-done((bf16[2,1024,128]{2,1,0:T(8,128)(2,1)S(1)}, bf16[2,1024,128]{2,1,0:T(8,128)(2,1)S(1)}, u32[]{:S(2)}, u32[]{:S(2)}) %collective-permute-start.7) | collective-permute-done | bytes 524320 | tf_op jit(solution)/shard_map/ppermute | solution.py:30
  54.2 3.5 %collective-permute-done.6 = bf16[2,1024,128]{2,1,0:T(8,128)(2,1)S(1)} collective-permute-done((bf16[2,1024,128]{2,1,0:T(8,128)(2,1)S(1)}, bf16[2,1024,128]{2,1,0:T(8,128)(2,1)S(1)}, u32[]{:S(2)}, u32[]{:S(2)}) %collective-permute-start.6) | collective-permute-done | bytes 524320 | tf_op jit(solution)/shard_map/ppermute | solution.py:30
  57.8 2.0 %collective-permute-start.12 = (f32[512,128]{1,0:T(8,128)S(1)}, f32[512,128]{1,0:T(8,128)S(1)}, u32[]{:S(2)}, u32[]{:S(2)}) collective-permute-start(f32[512,128]{1,0:T(8,128)S(1)} %get-tuple-element.41), channel_id=1, source_target_pairs={{0,32},{32,64},{64,96},{96,0},{1,33},{33,65},{65,97},{97,1},{2,34}... | collective-permute-start | bytes 786440 | tf_op jit(solution)/shard_map/ppermute | solution.py:30
  59.8 2.2 %collective-permute-start.13 = (f32[512,128]{1,0:T(8,128)S(1)}, f32[512,128]{1,0:T(8,128)S(1)}, u32[]{:S(2)}, u32[]{:S(2)}) collective-permute-start(f32[512,128]{1,0:T(8,128)S(1)} %get-tuple-element.42), channel_id=1, source_target_pairs={{0,96},{32,0},{64,32},{96,64},{1,97},{33,1},{65,33},{97,65},{2,98}... | collective-permute-start | bytes 786440 | tf_op jit(solution)/shard_map/ppermute | solution.py:30
  62.2 3.2 %collective-permute-start.9 = (f32[512,128]{1,0:T(8,128)S(1)}, f32[512,128]{1,0:T(8,128)S(1)}, u32[]{:S(2)}, u32[]{:S(2)}) collective-permute-start(f32[512,128]{1,0:T(8,128)S(1)} %get-tuple-element.37), channel_id=1, source_target_pairs={{0,24},{8,0},{16,8},{24,16},{1,25},{9,1},{17,9},{25,17},{2,26},{10... | collective-permute-start | bytes 786440 | tf_op jit(solution)/shard_map/ppermute | solution.py:30
  65.4 0.9 collective-permute-done.12.came_low
  66.4 1.9 %collective-permute-start.14 = (f32[1024,128]{1,0:T(8,128)S(1)}, f32[1024,128]{1,0:T(8,128)S(1)}, u32[]{:S(2)}, u32[]{:S(2)}) collective-permute-start(f32[1024,128]{1,0:T(8,128)S(1)} %get-tuple-element.43), channel_id=1, source_target_pairs={{0,32},{32,64},{64,96},{96,0},{1,33},{33,65},{65,97},{97,1},{2,34}... | collective-permute-start | bytes 1572872 | tf_op jit(solution)/shard_map/ppermute | solution.py:30
  68.3 1.6 %collective-permute-start.15 = (f32[1024,128]{1,0:T(8,128)S(1)}, f32[1024,128]{1,0:T(8,128)S(1)}, u32[]{:S(2)}, u32[]{:S(2)}) collective-permute-start(f32[1024,128]{1,0:T(8,128)S(1)} %get-tuple-element.44), channel_id=1, source_target_pairs={{0,96},{32,0},{64,32},{96,64},{1,97},{33,1},{65,33},{97,65},{2,98}... | collective-permute-start | bytes 1572872 | tf_op jit(solution)/shard_map/ppermute | solution.py:30
  70.1 3.2 %collective-permute-start.11 = (f32[1024,128]{1,0:T(8,128)S(1)}, f32[1024,128]{1,0:T(8,128)S(1)}, u32[]{:S(2)}, u32[]{:S(2)}) collective-permute-start(f32[1024,128]{1,0:T(8,128)S(1)} %get-tuple-element.39), channel_id=1, source_target_pairs={{0,24},{8,0},{16,8},{24,16},{1,25},{9,1},{17,9},{25,17},{2,26},{10... | collective-permute-start | bytes 1572872 | tf_op jit(solution)/shard_map/ppermute | solution.py:30
  73.5 5.0 %collective-permute-done.14.refs_4_ = f32[1024,128]{1,0:T(8,128)S(1)} collective-permute-done((f32[1024,128]{1,0:T(8,128)S(1)}, f32[1024,128]{1,0:T(8,128)S(1)}, u32[]{:S(2)}, u32[]{:S(2)}) %collective-permute-start.14) | collective-permute-done | bytes 524320 | tf_op jit(solution)/shard_map/ppermute | solution.py:30
  78.5 3.1 %collective-permute-done.10.refs_1_ = f32[1024,128]{1,0:T(8,128)S(1)} collective-permute-done((f32[1024,128]{1,0:T(8,128)S(1)}, f32[1024,128]{1,0:T(8,128)S(1)}, u32[]{:S(2)}, u32[]{:S(2)}) %collective-permute-start.10) | collective-permute-done | bytes 524320 | tf_op jit(solution)/shard_map/ppermute | solution.py:30
  81.9 17.8 %all_to_all.11 = f32[128,1,128]{2,1,0:T(1,128)S(1)} all-to-all(f32[128,1,128]{2,1,0:T(1,128)S(1)} %bitcast.82), channel_id=1, replica_groups=mesh['z'=4,'x'=4,'y'=4,'core'=2] {'z','x','y','core'}, dimensions={0} | all-to-all | bytes 131072 | tf_op jit(solution)/shard_map/all_to_all | solution.py:409
  99.7 1.1 shard_map.85
  100.8 0.9 collective-permute-start.28
  101.7 0.6 collective-permute-start.24
  102.3 1.1 collective-permute-start.20
  103.4 0.8 collective-permute-start.16
  104.2 1.8 %collective-permute-done.28.two = bf16[1,512,128]{2,1,0:T(8,128)(2,1)S(1)} collective-permute-done((bf16[1,512,128]{2,1,0:T(8,128)(2,1)S(1)}, bf16[1,512,128]{2,1,0:T(8,128)(2,1)S(1)}, u32[]{:S(2)}, u32[]{:S(2)}) %collective-permute-start.28) | collective-permute-done | bytes 131104 | tf_op jit(solution)/shard_map/ppermute | solution.py:304
  106.1 0.7 collective-permute-start.29
  106.8 1.2 collective-permute-start.25
  107.9 0.6 collective-permute-done.20.two
  108.5 1.4 collective-permute-start.21
  110.1 3.1 %collective-permute-done.29.two = bf16[2,512,128]{2,1,0:T(8,128)(2,1)S(1)} collective-permute-done((bf16[2,512,128]{2,1,0:T(8,128)(2,1)S(1)}, bf16[2,512,128]{2,1,0:T(8,128)(2,1)S(1)}, u32[]{:S(2)}, u32[]{:S(2)}) %collective-permute-start.29) | collective-permute-done | bytes 262176 | tf_op jit(solution)/shard_map/ppermute | solution.py:304
  113.3 0.7 collective-permute-start.30
  114.0 0.9 collective-permute-done.25.two
  114.9 1.6 %collective-permute-start.26 = (bf16[4,512,128]{2,1,0:T(8,128)(2,1)S(1)}, bf16[4,512,128]{2,1,0:T(8,128)(2,1)S(1)}, u32[]{:S(2)}, u32[]{:S(2)}) collective-permute-start(bf16[4,512,128]{2,1,0:T(8,128)(2,1)S(1)} %shard_map.93.one), channel_id=1, source_target_pairs={{0,24},{8,16},{16,8},{24,0},{1,25},{9,17},{17,9},{25,1},{2,26},{10... | collective-permute-start | bytes 1572872 | tf_op jit(solution)/shard_map/ppermute | solution.py:304
  116.7 0.9 collective-permute-start.18
  117.6 8.8 %collective-permute-done.30.two = bf16[4,512,128]{2,1,0:T(8,128)(2,1)S(1)} collective-permute-done((bf16[4,512,128]{2,1,0:T(8,128)(2,1)S(1)}, bf16[4,512,128]{2,1,0:T(8,128)(2,1)S(1)}, u32[]{:S(2)}, u32[]{:S(2)}) %collective-permute-start.30) | collective-permute-done | bytes 524320 | tf_op jit(solution)/shard_map/ppermute | solution.py:304
  126.4 1.5 collective-permute-start.31
  129.0 2.4 %collective-permute-start.19 = (bf16[8,512,128]{2,1,0:T(8,128)(2,1)S(1)}, bf16[8,512,128]{2,1,0:T(8,128)(2,1)S(1)}, u32[]{:S(2)}, u32[]{:S(2)}) collective-permute-start(bf16[8,512,128]{2,1,0:T(8,128)(2,1)S(1)} %shard_map.88.refs_3_), channel_id=1, source_target_pairs={{0,96},{32,64},{64,32},{96,0},{1,97},{33,65},{65,33},{97,1},{2,98}... | collective-permute-start | bytes 3145736 | tf_op jit(solution)/shard_map/ppermute | solution.py:304
  131.4 2.8 %shard_map.103 = (f32[2048,128]{1,0:T(8,128)}, f32[2048,128]{1,0:T(8,128)}, f32[2048,128]{1,0:T(8,128)}) custom-call(f32[128,128]{1,0:T(8,128)S(1)} %bitcast.73, f32[2048,128]{1,0:T(8,128)S(1)} %get-tuple-element.46.mean, f32[2048,128]{1,0:T(8,128)S(1)} %bitcast.67, f32[2048,128]{1,0:T(8,128)S(1)} %bitcast.69, f32[2048,128]{1,0:T(8,128)S(1)} %bitcast.71), custom_call_target="tpu_custom_call" | custom-call | flops 5242880 | bytes 7340032 | tf_op jit(solution)/shard_map/pallas_call | solution.py:287
  134.2 2.3 %shard_map.98.refs_1_ = bf16[4,4,4,512,128]{4,3,2,1,0:T(8,128)(2,1)} custom-call(bf16[8,512,128]{2,1,0:T(8,128)(2,1)S(1)} %shard_map.97.refs_0_, bf16[8,512,128]{2,1,0:T(8,128)(2,1)S(1)} %shard_map.94.refs_1_, bf16[8,512,128]{2,1,0:T(8,128)(2,1)S(1)} %shard_map.91.refs_2_, bf16[8,512,128]{2,1,0:T(8,128)(2,1)S(1)} %shard_map.88.refs_3_), custom_call_target="tpu_custom_call" | custom-call | bytes 8388608 | tf_op jit(solution)/shard_map/pallas_call | solution.py:350
  136.4 13.7 %collective-permute-done.31.refs_0_ = bf16[8,512,128]{2,1,0:T(8,128)(2,1)S(1)} collective-permute-done((bf16[8,512,128]{2,1,0:T(8,128)(2,1)S(1)}, bf16[8,512,128]{2,1,0:T(8,128)(2,1)S(1)}, u32[]{:S(2)}, u32[]{:S(2)}) %collective-permute-start.31) | collective-permute-done | bytes 1048608 | tf_op jit(solution)/shard_map/ppermute | solution.py:304
  150.1 1.0 shard_map.99.refs_1_
  151.2 1.0 shard_map.100.refs_1_
  152.2 1.0 shard_map.101.refs_1_
  153.3 1.0 shard_map.102
  (56 shorter events, 3.2 us)
Async XLA Ops:
  3.6 36.6 %collective-permute-start.5 = (bf16[6,1024,128]{2,1,0:T(8,128)(2,1)S(1)}, bf16[6,1024,128]{2,1,0:T(8,128)(2,1)S(1)}, u32[]{:S(2)}, u32[]{:S(2)}) collective-permute-start(bf16[6,1024,128]{2,1,0:T(8,128)(2,1)S(1)} %get-tuple-element.34), channel_id=1, source_target_pairs={{0,24},{8,0},{16,8},{24,16},{1,25},{9,1},{17,9},{25,17},{2,26},{10... | collective-permute-start | bytes 4718600 | tf_op jit(solution)/shard_map/ppermute | solution.py:30
  6.5 37.5 %collective-permute-start.4 = (bf16[6,1024,128]{2,1,0:T(8,128)(2,1)S(1)}, bf16[6,1024,128]{2,1,0:T(8,128)(2,1)S(1)}, u32[]{:S(2)}, u32[]{:S(2)}) collective-permute-start(bf16[6,1024,128]{2,1,0:T(8,128)(2,1)S(1)} %get-tuple-element.33), channel_id=1, source_target_pairs={{0,8},{8,16},{16,24},{24,0},{1,9},{9,17},{17,25},{25,1},{2,10},{10... | collective-permute-start | bytes 4718600 | tf_op jit(solution)/shard_map/ppermute | solution.py:30
  6.5 38.1 %collective-permute-start = (bf16[6,1024,128]{2,1,0:T(8,128)(2,1)S(1)}, bf16[6,1024,128]{2,1,0:T(8,128)(2,1)S(1)}, u32[]{:S(2)}, u32[]{:S(2)}) collective-permute-start(bf16[6,1024,128]{2,1,0:T(8,128)(2,1)S(1)} %get-tuple-element.30), channel_id=1, source_target_pairs={{0,32},{32,64},{64,96},{96,0},{1,33},{33,65},{65,97},{97,1},{2,34}... | collective-permute-start | bytes 4718600 | tf_op jit(solution)/shard_map/ppermute | solution.py:30
  8.4 37.7 %collective-permute-start.1 = (bf16[6,1024,128]{2,1,0:T(8,128)(2,1)S(1)}, bf16[6,1024,128]{2,1,0:T(8,128)(2,1)S(1)}, u32[]{:S(2)}, u32[]{:S(2)}) collective-permute-start(bf16[6,1024,128]{2,1,0:T(8,128)(2,1)S(1)} %get-tuple-element.31), channel_id=1, source_target_pairs={{0,96},{32,0},{64,32},{96,64},{1,97},{33,1},{65,33},{97,65},{2,98}... | collective-permute-start | bytes 4718600 | tf_op jit(solution)/shard_map/ppermute | solution.py:30
  40.2 14.1 %collective-permute-start.7 = (bf16[2,1024,128]{2,1,0:T(8,128)(2,1)S(1)}, bf16[2,1024,128]{2,1,0:T(8,128)(2,1)S(1)}, u32[]{:S(2)}, u32[]{:S(2)}) collective-permute-start(bf16[2,1024,128]{2,1,0:T(8,128)(2,1)S(1)} %slice.19), channel_id=1, source_target_pairs={{0,24},{8,0},{16,8},{24,16},{1,25},{9,1},{17,9},{25,17},{2,26},{10... | collective-permute-start | bytes 1572872 | tf_op jit(solution)/shard_map/ppermute | solution.py:30
  44.0 13.8 %collective-permute-start.6 = (bf16[2,1024,128]{2,1,0:T(8,128)(2,1)S(1)}, bf16[2,1024,128]{2,1,0:T(8,128)(2,1)S(1)}, u32[]{:S(2)}, u32[]{:S(2)}) collective-permute-start(bf16[2,1024,128]{2,1,0:T(8,128)(2,1)S(1)} %slice.18), channel_id=1, source_target_pairs={{0,8},{8,16},{16,24},{24,0},{1,9},{9,17},{17,25},{25,1},{2,10},{10... | collective-permute-start | bytes 1572872 | tf_op jit(solution)/shard_map/ppermute | solution.py:30
  44.7 17.4 %collective-permute-start.2 = (bf16[2,1024,128]{2,1,0:T(8,128)(2,1)S(1)}, bf16[2,1024,128]{2,1,0:T(8,128)(2,1)S(1)}, u32[]{:S(2)}, u32[]{:S(2)}) collective-permute-start(bf16[2,1024,128]{2,1,0:T(8,128)(2,1)S(1)} %slice.16), channel_id=1, source_target_pairs={{0,32},{32,64},{64,96},{96,0},{1,33},{33,65},{65,97},{97,1},{2,34}... | collective-permute-start | bytes 1572872 | tf_op jit(solution)/shard_map/ppermute | solution.py:30
  46.1 15.9 %collective-permute-start.3 = (bf16[2,1024,128]{2,1,0:T(8,128)(2,1)S(1)}, bf16[2,1024,128]{2,1,0:T(8,128)(2,1)S(1)}, u32[]{:S(2)}, u32[]{:S(2)}) collective-permute-start(bf16[2,1024,128]{2,1,0:T(8,128)(2,1)S(1)} %slice.17), channel_id=1, source_target_pairs={{0,96},{32,0},{64,32},{96,64},{1,97},{33,1},{65,33},{97,65},{2,98}... | collective-permute-start | bytes 1572872 | tf_op jit(solution)/shard_map/ppermute | solution.py:30
  57.8 8.5 %collective-permute-start.12 = (f32[512,128]{1,0:T(8,128)S(1)}, f32[512,128]{1,0:T(8,128)S(1)}, u32[]{:S(2)}, u32[]{:S(2)}) collective-permute-start(f32[512,128]{1,0:T(8,128)S(1)} %get-tuple-element.41), channel_id=1, source_target_pairs={{0,32},{32,64},{64,96},{96,0},{1,33},{33,65},{65,97},{97,1},{2,34}... | collective-permute-start | bytes 786440 | tf_op jit(solution)/shard_map/ppermute | solution.py:30
  59.8 6.5 %collective-permute-start.13 = (f32[512,128]{1,0:T(8,128)S(1)}, f32[512,128]{1,0:T(8,128)S(1)}, u32[]{:S(2)}, u32[]{:S(2)}) collective-permute-start(f32[512,128]{1,0:T(8,128)S(1)} %get-tuple-element.42), channel_id=1, source_target_pairs={{0,96},{32,0},{64,32},{96,64},{1,97},{33,1},{65,33},{97,65},{2,98}... | collective-permute-start | bytes 786440 | tf_op jit(solution)/shard_map/ppermute | solution.py:30
  62.1 7.8 %collective-permute-start.8 = (f32[512,128]{1,0:T(8,128)S(1)}, f32[512,128]{1,0:T(8,128)S(1)}, u32[]{:S(2)}, u32[]{:S(2)}) collective-permute-start(f32[512,128]{1,0:T(8,128)S(1)} %get-tuple-element.36), channel_id=1, source_target_pairs={{0,8},{8,16},{16,24},{24,0},{1,9},{9,17},{17,25},{25,1},{2,10},{10... | collective-permute-start | bytes 786440 | tf_op jit(solution)/shard_map/ppermute | solution.py:30
  62.2 7.7 %collective-permute-start.9 = (f32[512,128]{1,0:T(8,128)S(1)}, f32[512,128]{1,0:T(8,128)S(1)}, u32[]{:S(2)}, u32[]{:S(2)}) collective-permute-start(f32[512,128]{1,0:T(8,128)S(1)} %get-tuple-element.37), channel_id=1, source_target_pairs={{0,24},{8,0},{16,8},{24,16},{1,25},{9,1},{17,9},{25,17},{2,26},{10... | collective-permute-start | bytes 786440 | tf_op jit(solution)/shard_map/ppermute | solution.py:30
  66.4 12.1 %collective-permute-start.14 = (f32[1024,128]{1,0:T(8,128)S(1)}, f32[1024,128]{1,0:T(8,128)S(1)}, u32[]{:S(2)}, u32[]{:S(2)}) collective-permute-start(f32[1024,128]{1,0:T(8,128)S(1)} %get-tuple-element.43), channel_id=1, source_target_pairs={{0,32},{32,64},{64,96},{96,0},{1,33},{33,65},{65,97},{97,1},{2,34}... | collective-permute-start | bytes 1572872 | tf_op jit(solution)/shard_map/ppermute | solution.py:30
  68.3 10.2 %collective-permute-start.15 = (f32[1024,128]{1,0:T(8,128)S(1)}, f32[1024,128]{1,0:T(8,128)S(1)}, u32[]{:S(2)}, u32[]{:S(2)}) collective-permute-start(f32[1024,128]{1,0:T(8,128)S(1)} %get-tuple-element.44), channel_id=1, source_target_pairs={{0,96},{32,0},{64,32},{96,64},{1,97},{33,1},{65,33},{97,65},{2,98}... | collective-permute-start | bytes 1572872 | tf_op jit(solution)/shard_map/ppermute | solution.py:30
  70.0 11.6 %collective-permute-start.10 = (f32[1024,128]{1,0:T(8,128)S(1)}, f32[1024,128]{1,0:T(8,128)S(1)}, u32[]{:S(2)}, u32[]{:S(2)}) collective-permute-start(f32[1024,128]{1,0:T(8,128)S(1)} %get-tuple-element.38), channel_id=1, source_target_pairs={{0,8},{8,16},{16,24},{24,0},{1,9},{9,17},{17,25},{25,1},{2,10},{10... | collective-permute-start | bytes 1572872 | tf_op jit(solution)/shard_map/ppermute | solution.py:30
  70.1 11.5 %collective-permute-start.11 = (f32[1024,128]{1,0:T(8,128)S(1)}, f32[1024,128]{1,0:T(8,128)S(1)}, u32[]{:S(2)}, u32[]{:S(2)}) collective-permute-start(f32[1024,128]{1,0:T(8,128)S(1)} %get-tuple-element.39), channel_id=1, source_target_pairs={{0,24},{8,0},{16,8},{24,16},{1,25},{9,1},{17,9},{25,17},{2,26},{10... | collective-permute-start | bytes 1572872 | tf_op jit(solution)/shard_map/ppermute | solution.py:30
  73.4 26.2 %copy-start = (f32[1,4,65536]{2,1,0:T(4,128)S(1)}, f32[1,4,65536]{2,1,0:T(4,128)}, u32[]{:S(2)}) copy-start(f32[1,4,65536]{2,1,0:T(4,128)} %param.5) | copy-start | bytes 3145732
  73.5 26.2 %copy-start.1 = (f32[1,4,65536]{2,1,0:T(4,128)S(1)}, f32[1,4,65536]{2,1,0:T(4,128)}, u32[]{:S(2)}) copy-start(f32[1,4,65536]{2,1,0:T(4,128)} %param.6) | copy-start | bytes 3145732
  73.5 26.2 %copy-start.2 = (f32[1,4,65536]{2,1,0:T(4,128)S(1)}, f32[1,4,65536]{2,1,0:T(4,128)}, u32[]{:S(2)}) copy-start(f32[1,4,65536]{2,1,0:T(4,128)} %param.7) | copy-start | bytes 3145732
  100.8 5.2 %collective-permute-start.28 = (bf16[1,512,128]{2,1,0:T(8,128)(2,1)S(1)}, bf16[1,512,128]{2,1,0:T(8,128)(2,1)S(1)}, u32[]{:S(2)}, u32[]{:S(2)}) collective-permute-start(bf16[1,512,128]{2,1,0:T(8,128)(2,1)S(1)} %bitcast.80), channel_id=1, source_target_pairs={{0,32},{32,0},{64,96},{96,64},{1,33},{33,1},{65,97},{97,65},{2,34}... | collective-permute-start | bytes 393224 | tf_op jit(solution)/shard_map/ppermute | solution.py:304
  101.7 5.0 %collective-permute-start.24 = (bf16[1,512,128]{2,1,0:T(8,128)(2,1)S(1)}, bf16[1,512,128]{2,1,0:T(8,128)(2,1)S(1)}, u32[]{:S(2)}, u32[]{:S(2)}) collective-permute-start(bf16[1,512,128]{2,1,0:T(8,128)(2,1)S(1)} %bitcast.78), channel_id=1, source_target_pairs={{0,8},{8,0},{16,24},{24,16},{1,9},{9,1},{17,25},{25,17},{2,10},{10... | collective-permute-start | bytes 393224 | tf_op jit(solution)/shard_map/ppermute | solution.py:304
  102.3 6.2 %collective-permute-start.20 = (bf16[1,512,128]{2,1,0:T(8,128)(2,1)S(1)}, bf16[1,512,128]{2,1,0:T(8,128)(2,1)S(1)}, u32[]{:S(2)}, u32[]{:S(2)}) collective-permute-start(bf16[1,512,128]{2,1,0:T(8,128)(2,1)S(1)} %bitcast.76), channel_id=1, source_target_pairs={{0,96},{32,64},{64,32},{96,0},{1,97},{33,65},{65,33},{97,1},{2,98}... | collective-permute-start | bytes 393224 | tf_op jit(solution)/shard_map/ppermute | solution.py:304
  103.4 6.6 %collective-permute-start.16 = (bf16[1,512,128]{2,1,0:T(8,128)(2,1)S(1)}, bf16[1,512,128]{2,1,0:T(8,128)(2,1)S(1)}, u32[]{:S(2)}, u32[]{:S(2)}) collective-permute-start(bf16[1,512,128]{2,1,0:T(8,128)(2,1)S(1)} %bitcast.74), channel_id=1, source_target_pairs={{0,24},{8,16},{16,8},{24,0},{1,25},{9,17},{17,9},{25,1},{2,26},{10... | collective-permute-start | bytes 393224 | tf_op jit(solution)/shard_map/ppermute | solution.py:304
  106.1 7.1 %collective-permute-start.29 = (bf16[2,512,128]{2,1,0:T(8,128)(2,1)S(1)}, bf16[2,512,128]{2,1,0:T(8,128)(2,1)S(1)}, u32[]{:S(2)}, u32[]{:S(2)}) collective-permute-start(bf16[2,512,128]{2,1,0:T(8,128)(2,1)S(1)} %shard_map.95.one), channel_id=1, source_target_pairs={{0,8},{8,0},{16,24},{24,16},{1,9},{9,1},{17,25},{25,17},{2,10},{10... | collective-permute-start | bytes 786440 | tf_op jit(solution)/shard_map/ppermute | solution.py:304
  106.8 8.1 %collective-permute-start.25 = (bf16[2,512,128]{2,1,0:T(8,128)(2,1)S(1)}, bf16[2,512,128]{2,1,0:T(8,128)(2,1)S(1)}, u32[]{:S(2)}, u32[]{:S(2)}) collective-permute-start(bf16[2,512,128]{2,1,0:T(8,128)(2,1)S(1)} %shard_map.92.one), channel_id=1, source_target_pairs={{0,96},{32,64},{64,32},{96,0},{1,97},{33,65},{65,33},{97,1},{2,98}... | collective-permute-start | bytes 786440 | tf_op jit(solution)/shard_map/ppermute | solution.py:304
  108.5 8.0 %collective-permute-start.21 = (bf16[2,512,128]{2,1,0:T(8,128)(2,1)S(1)}, bf16[2,512,128]{2,1,0:T(8,128)(2,1)S(1)}, u32[]{:S(2)}, u32[]{:S(2)}) collective-permute-start(bf16[2,512,128]{2,1,0:T(8,128)(2,1)S(1)} %shard_map.89.one), channel_id=1, source_target_pairs={{0,24},{8,16},{16,8},{24,0},{1,25},{9,17},{17,9},{25,1},{2,26},{10... | collective-permute-start | bytes 786440 | tf_op jit(solution)/shard_map/ppermute | solution.py:304
  110.0 6.6 %collective-permute-start.17 = (bf16[2,512,128]{2,1,0:T(8,128)(2,1)S(1)}, bf16[2,512,128]{2,1,0:T(8,128)(2,1)S(1)}, u32[]{:S(2)}, u32[]{:S(2)}) collective-permute-start(bf16[2,512,128]{2,1,0:T(8,128)(2,1)S(1)} %shard_map.86.one), channel_id=1, source_target_pairs={{0,32},{32,0},{64,96},{96,64},{1,33},{33,1},{65,97},{97,65},{2,34}... | collective-permute-start | bytes 786440 | tf_op jit(solution)/shard_map/ppermute | solution.py:304
  113.3 13.1 %collective-permute-start.30 = (bf16[4,512,128]{2,1,0:T(8,128)(2,1)S(1)}, bf16[4,512,128]{2,1,0:T(8,128)(2,1)S(1)}, u32[]{:S(2)}, u32[]{:S(2)}) collective-permute-start(bf16[4,512,128]{2,1,0:T(8,128)(2,1)S(1)} %shard_map.96.one), channel_id=1, source_target_pairs={{0,96},{32,64},{64,32},{96,0},{1,97},{33,65},{65,33},{97,1},{2,98}... | collective-permute-start | bytes 1572872 | tf_op jit(solution)/shard_map/ppermute | solution.py:304
  114.9 13.1 %collective-permute-start.26 = (bf16[4,512,128]{2,1,0:T(8,128)(2,1)S(1)}, bf16[4,512,128]{2,1,0:T(8,128)(2,1)S(1)}, u32[]{:S(2)}, u32[]{:S(2)}) collective-permute-start(bf16[4,512,128]{2,1,0:T(8,128)(2,1)S(1)} %shard_map.93.one), channel_id=1, source_target_pairs={{0,24},{8,16},{16,8},{24,0},{1,25},{9,17},{17,9},{25,1},{2,26},{10... | collective-permute-start | bytes 1572872 | tf_op jit(solution)/shard_map/ppermute | solution.py:304
  116.5 11.9 %collective-permute-start.22 = (bf16[4,512,128]{2,1,0:T(8,128)(2,1)S(1)}, bf16[4,512,128]{2,1,0:T(8,128)(2,1)S(1)}, u32[]{:S(2)}, u32[]{:S(2)}) collective-permute-start(bf16[4,512,128]{2,1,0:T(8,128)(2,1)S(1)} %shard_map.90.one), channel_id=1, source_target_pairs={{0,32},{32,0},{64,96},{96,64},{1,33},{33,1},{65,97},{97,65},{2,34}... | collective-permute-start | bytes 1572872 | tf_op jit(solution)/shard_map/ppermute | solution.py:304
  116.7 12.2 %collective-permute-start.18 = (bf16[4,512,128]{2,1,0:T(8,128)(2,1)S(1)}, bf16[4,512,128]{2,1,0:T(8,128)(2,1)S(1)}, u32[]{:S(2)}, u32[]{:S(2)}) collective-permute-start(bf16[4,512,128]{2,1,0:T(8,128)(2,1)S(1)} %shard_map.87.one), channel_id=1, source_target_pairs={{0,8},{8,0},{16,24},{24,16},{1,9},{9,1},{17,25},{25,17},{2,10},{10... | collective-permute-start | bytes 1572872 | tf_op jit(solution)/shard_map/ppermute | solution.py:304
  126.4 23.7 %collective-permute-start.31 = (bf16[8,512,128]{2,1,0:T(8,128)(2,1)S(1)}, bf16[8,512,128]{2,1,0:T(8,128)(2,1)S(1)}, u32[]{:S(2)}, u32[]{:S(2)}) collective-permute-start(bf16[8,512,128]{2,1,0:T(8,128)(2,1)S(1)} %shard_map.97.refs_0_), channel_id=1, source_target_pairs={{0,24},{8,16},{16,8},{24,0},{1,25},{9,17},{17,9},{25,1},{2,26},{10... | collective-permute-start | bytes 3145736 | tf_op jit(solution)/shard_map/ppermute | solution.py:304
  128.0 23.1 %collective-permute-start.27 = (bf16[8,512,128]{2,1,0:T(8,128)(2,1)S(1)}, bf16[8,512,128]{2,1,0:T(8,128)(2,1)S(1)}, u32[]{:S(2)}, u32[]{:S(2)}) collective-permute-start(bf16[8,512,128]{2,1,0:T(8,128)(2,1)S(1)} %shard_map.94.refs_1_), channel_id=1, source_target_pairs={{0,32},{32,0},{64,96},{96,64},{1,33},{33,1},{65,97},{97,65},{2,34}... | collective-permute-start | bytes 3145736 | tf_op jit(solution)/shard_map/ppermute | solution.py:304
  128.5 23.7 %collective-permute-start.23 = (bf16[8,512,128]{2,1,0:T(8,128)(2,1)S(1)}, bf16[8,512,128]{2,1,0:T(8,128)(2,1)S(1)}, u32[]{:S(2)}, u32[]{:S(2)}) collective-permute-start(bf16[8,512,128]{2,1,0:T(8,128)(2,1)S(1)} %shard_map.91.refs_2_), channel_id=1, source_target_pairs={{0,8},{8,0},{16,24},{24,16},{1,9},{9,1},{17,25},{25,17},{2,10},{10... | collective-permute-start | bytes 3145736 | tf_op jit(solution)/shard_map/ppermute | solution.py:304
  129.0 24.3 %collective-permute-start.19 = (bf16[8,512,128]{2,1,0:T(8,128)(2,1)S(1)}, bf16[8,512,128]{2,1,0:T(8,128)(2,1)S(1)}, u32[]{:S(2)}, u32[]{:S(2)}) collective-permute-start(bf16[8,512,128]{2,1,0:T(8,128)(2,1)S(1)} %shard_map.88.refs_3_), channel_id=1, source_target_pairs={{0,96},{32,64},{64,32},{96,0},{1,97},{33,65},{65,33},{97,1},{2,98}... | collective-permute-start | bytes 3145736 | tf_op jit(solution)/shard_map/ppermute | solution.py:304
